TPU v7x, 32 devices: a whole 2x2x4 slice. The times are simulated.
32 devices in a mesh: ctx: 16 (over z, y, x), tp: 2 (over core).
Axes of the slice: x: 2, y: 2, z: 4, core: 2. Of those that a mesh axis runs over, the one named last changes fastest.
Arguments:
- hyena_q: bfloat16 [4096, 4096], P('ctx', 'tp'), may hold values from -6 to 6
- hyena_k: bfloat16 [4096, 4096], P('ctx', 'tp'), may hold values from -6 to 6
- hyena_v: bfloat16 [4096, 4096], P('ctx', 'tp'), may hold values from -6 to 6
- filters: bfloat16 [256, 128], P('tp'), may hold values from -0.5 to 0.5
- direct: bfloat16 [4096], P('tp'), may hold values from -4 to 4
- queries: bfloat16 [4096, 2048], P('ctx', 'tp'), may hold values from -64 to 64
- keys: bfloat16 [4096, 2048], P('ctx', 'tp'), may hold values from -4 to 4
- values: bfloat16 [4096, 2048], P('ctx', 'tp'), may hold values from -6 to 6
- segment_ids: int32 [4096], P('ctx'), may hold values from 0 to 7, never falling along the last dimension, each value on 1 to 1793 neighbouring positions
- out_weight: bfloat16 [2048, 4096], P(None, 'tp'), may hold values from -0.125 to 0.125
Outputs:
- hyena_out: bfloat16 [4096, 4096], P('ctx', 'tp')
- attn_out: bfloat16 [4096, 4096], P('ctx', 'tp')
Inputs may be any that keep to these rules, and one draw needn't show every extreme that they name: `segment_ids`: ids never fall along the sequence; each document holds 1 to 1793 tokens and one holds exactly 1793.
All inputs are finite; a program needn't handle non-finite values.
Results may differ from a plain program's by a relative error of at most 0.006.
Values may be sent and summed in bfloat16 or wider, within the bound.
No kernel may reach another device: no remote copies, remote signals or barrier semaphores. Data moves between devices by JAX's collectives and lax.ppermute only.
A program may use at most 64 MiB of HBM per device.

v0:
```python
import functools
import math

import jax
import jax.numpy as jnp
from jax import lax
from jax.experimental import pallas as pl
from jax.experimental.pallas import tpu as pltpu
from jax.sharding import PartitionSpec as P

HD = 128
SQUAD = 4
NEG = -1e30
TAG = 16
LANES = 128
VMEM_LIMIT = 32 * 1024 * 1024
ALL_VMEM = 62 * 1024 * 1024
VMEM = pl.BlockSpec(memory_space=pltpu.VMEM)
SMEM = pl.BlockSpec(memory_space=pltpu.SMEM)


def corner_of(place_ref):
    return lax.rem(place_ref[0], SQUAD)


def kernel_call(kernel, args, shapes, name, scratch=(), flops=0, exps=0):
    total = sum(math.prod(x.shape) * x.dtype.itemsize for x in (*args, *shapes))
    return list(pl.pallas_call(
        kernel,
        in_specs=[SMEM] + [VMEM] * (len(args) - 1),
        out_specs=[VMEM] * len(shapes),
        out_shape=shapes,
        scratch_shapes=scratch,
        compiler_params=pltpu.CompilerParams(vmem_limit_bytes=VMEM_LIMIT),
        cost_estimate=pl.CostEstimate(flops=flops, bytes_accessed=total, transcendentals=exps),
        name=name,
    )(*args))


def hyena_kernel(q_ref, k_ref, v_ref, rim_ref, taps_ref, direct_ref, out_ref):
    rows, width = q_ref.shape
    per_tile = taps_ref.shape[0] * LANES // width
    group = LANES // per_tile
    windows = rows // LANES
    shape = (LANES, 2 * LANES)
    turn = lax.broadcasted_iota(jnp.int32, shape, 0) + lax.broadcasted_iota(jnp.int32, shape, 1)
    turn = jnp.where(turn == LANES, 1.0, 0.0).astype(jnp.bfloat16)
    taps = jnp.dot(taps_ref[...], turn, preferred_element_type=jnp.float32)
    lane_group = lax.broadcasted_iota(jnp.int32, (LANES, windows * LANES), 1) % LANES // group
    for tile in range(width // LANES):
        cols = slice(tile * LANES, (tile + 1) * LANES)
        mixed = (k_ref[:, cols].astype(jnp.float32) * v_ref[:, cols].astype(jnp.float32)).astype(
            jnp.bfloat16
        )
        full = jnp.concatenate([rim_ref[:, cols], mixed], axis=0)
        stacked = jnp.concatenate(
            [full[w * LANES : (w + 2) * LANES] for w in range(windows)], axis=1
        )
        conv = jnp.zeros((LANES, windows * LANES), jnp.float32)
        for g in range(per_tile):
            at = tile * per_tile + g
            row = taps[at : at + 1]
            first = pltpu.roll(
                jnp.broadcast_to(row, (TAG, 2 * LANES)), 0, 1, stride=1, stride_axis=0
            ).astype(jnp.bfloat16)
            table = jnp.concatenate(
                [first] + [pltpu.roll(first, t, 1) for t in range(TAG, LANES, TAG)], axis=0
            )
            part = jnp.dot(table, stacked, preferred_element_type=jnp.float32)
            conv = jnp.where(lane_group == g, part, conv)
        conv = jnp.concatenate(
            [conv[:, w * LANES : (w + 1) * LANES] for w in range(windows)], axis=0
        )
        out_ref[:, cols] = (
            q_ref[:, cols].astype(jnp.float32)
            * (conv + direct_ref[:, cols].astype(jnp.float32) * mixed.astype(jnp.float32))
        ).astype(jnp.bfloat16)


def hyena(hyena_q, hyena_k, hyena_v, rim, filters, direct):
    rows, chans = hyena_q.shape
    groups, kernel = filters.shape
    taps = jnp.pad(filters, ((0, 0), (0, LANES - kernel)))
    block = 2 * LANES
    steps = chans // block
    wide = pl.BlockSpec((rows, block), lambda i: (0, i))
    return pl.pallas_call(
        hyena_kernel,
        grid=(steps,),
        in_specs=[
            wide,
            wide,
            wide,
            pl.BlockSpec((LANES, block), lambda i: (0, i)),
            pl.BlockSpec((groups // steps, LANES), lambda i: (i, 0)),
            pl.BlockSpec((1, block), lambda i: (0, i)),
        ],
        out_specs=wide,
        out_shape=jax.ShapeDtypeStruct((rows, chans), jnp.bfloat16),
        compiler_params=pltpu.CompilerParams(vmem_limit_bytes=VMEM_LIMIT),
        cost_estimate=pl.CostEstimate(
            flops=4 * rows * chans * 2 * LANES * 8,
            bytes_accessed=10 * rows * chans,
            transcendentals=0,
        ),
        name="hyena",
    )(hyena_q, hyena_k, hyena_v, rim, taps, direct[None])


def deal_kernel(place_ref, q_ref, k_ref, v_ref, id_ref, *refs):
    outs, held, (arrive, leave) = refs[: SQUAD + 1], refs[SQUAD + 1 : -2], refs[-2:]
    rows, feat = q_ref.shape
    width = feat // SQUAD
    corner = corner_of(place_ref)
    order = list(range(1, SQUAD)) + [0]
    copies = {}
    for k in order:
        cols = pl.ds(pl.multiple_of(jnp.bitwise_xor(corner, k) * width, width), width)
        base = rows if k else 0
        places = (
            (q_ref, held[k + 1] if k else held[0], 0),
            (k_ref, held[k + 1], base + TAG),
            (v_ref, held[k + 1], base + TAG + rows),
        )
        copies[k] = [
            pltpu.make_async_copy(
                source.at[:, cols], target.at[pl.ds(begin, rows)], arrive.at[k, i]
            )
            for i, (source, target, begin) in enumerate(places)
        ]
        for copy in copies[k]:
            copy.start()
    ids = (id_ref[...] + 1).astype(jnp.float32)
    spare = jnp.zeros((TAG - ids.shape[0], LANES), jnp.float32)
    ids = jnp.concatenate([ids, spare], axis=0)
    tag = jnp.concatenate([ids] * (width // LANES), axis=1).astype(jnp.bfloat16)
    for i, target in enumerate(held):
        begin = 0 if i == 1 else rows
        target[begin : begin + TAG, :] = tag
    leaving = [
        pltpu.make_async_copy(source, out, leave.at[i])
        for i, (source, out) in enumerate(zip(held, outs))
    ]
    for k in order:
        for copy in copies[k]:
            copy.wait()
        leaving[k + 1].start()
    leaving[0].start()
    for copy in leaving:
        copy.wait()


def deal(place, queries, keys, values, ids):
    rows, feat = queries.shape
    tall = [rows + TAG, 2 * rows + TAG] + [3 * rows + TAG] * (SQUAD - 1)
    shapes = [(x, feat // SQUAD) for x in tall]
    anywhere = pl.BlockSpec(memory_space=pl.ANY)
    return list(
        pl.pallas_call(
            deal_kernel,
            in_specs=[SMEM] + [anywhere] * 3 + [VMEM],
            out_specs=[anywhere] * len(tall),
            out_shape=[jax.ShapeDtypeStruct(x, jnp.bfloat16) for x in shapes],
            scratch_shapes=[pltpu.VMEM(x, jnp.bfloat16) for x in shapes]
            + [pltpu.SemaphoreType.DMA((SQUAD, 3)), pltpu.SemaphoreType.DMA((SQUAD + 1,))],
            compiler_params=pltpu.CompilerParams(vmem_limit_bytes=ALL_VMEM),
            cost_estimate=pl.CostEstimate(
                flops=0, bytes_accessed=12 * rows * feat, transcendentals=0
            ),
            name="deal",
        )(place, queries, keys, values, ids)
    )


def id_columns(tag_ref, rows):
    tag = tag_ref[:, :LANES].astype(jnp.float32)
    tiles = [jnp.broadcast_to(tag[t : t + 1], (LANES, LANES)).T for t in range(rows // LANES)]
    return jnp.concatenate(tiles, axis=0)


def place_keys(parts, corner, base, rows, keys, values):
    heads = keys.shape[0]
    marks = lax.broadcasted_iota(jnp.int32, (rows, LANES), 1).astype(jnp.float32) + 1.0
    for k, part in enumerate(parts):
        begin = pl.multiple_of((jnp.bitwise_xor(corner, k) + base) * rows, rows)
        span = pl.ds(begin, rows)
        ids = id_columns(part.at[:TAG], rows)
        mask = jnp.where(ids == marks, 0.0, -NEG).astype(jnp.bfloat16)
        for h in range(heads):
            cols = slice(h * HD, (h + 1) * HD)
            keys[h, span, :HD] = part[TAG : TAG + rows, cols]
            keys[h, span, HD:] = mask
            values[h, span, :] = part[TAG + rows : TAG + 2 * rows, cols]


def near_parts(near, rows):
    tall = 2 * rows + TAG
    return [near[0], near[1].at[:tall], near[1].at[tall:], near[2]]


def place_queries(parts, corner, rows, queries):
    heads = queries.shape[0]
    marks = lax.broadcasted_iota(jnp.int32, (rows, LANES), 1).astype(jnp.float32) + 1.0
    for k, part in enumerate(parts):
        begin = pl.multiple_of(jnp.bitwise_xor(corner, k) * rows, rows)
        span = pl.ds(begin, rows)
        ids = id_columns(part.at[rows : rows + TAG], rows)
        mask = jnp.where(ids == marks, -1.0, 0.0).astype(jnp.bfloat16)
        for h in range(heads):
            queries[h, span, :HD] = part[:rows, h * HD : (h + 1) * HD]
            queries[h, span, HD:] = mask


def attend(query, keys, values, diagonal):
    factor = math.log2(math.e) / math.sqrt(HD)
    rows = query.shape[0]
    score = lax.dot_general(
        keys, query, (((1,), (1,)), ((), ())), preferred_element_type=jnp.float32
    )
    if diagonal:
        older = lax.broadcasted_iota(jnp.int32, (rows, rows), 0) <= lax.broadcasted_iota(
            jnp.int32, (rows, rows), 1
        )
        score = jnp.concatenate(
            [score[:-rows], jnp.where(older, score[-rows:], NEG)], axis=0
        )
    high = jnp.max(score, axis=0, keepdims=True)
    expo = jnp.exp2((score - high) * factor)
    total = jnp.sum(expo, axis=0, keepdims=True)
    summed = lax.dot_general(
        values,
        expo.astype(jnp.bfloat16),
        (((0,), (0,)), ((), ())),
        preferred_element_type=jnp.float32,
    )
    return summed / total, high * factor + jnp.log2(total)


def main_kernel(place_ref, *refs):
    own, near, out, (queries, keys, values) = refs[:5], refs[5:8], refs[8], refs[9:]
    heads, span, _ = queries.shape
    rows = span // SQUAD
    width = heads * HD
    corner = corner_of(place_ref)
    asked = [own[0]] + [p.at[: rows + TAG] for p in own[2:]]
    held = [own[1]] + [p.at[rows:] for p in own[2:]]
    place_queries(asked, corner, rows, queries)
    place_keys(held, corner, SQUAD, rows, keys, values)
    place_keys(near_parts(near, rows), corner, 0, rows, keys, values)
    for j in range(SQUAD):
        cols = slice(j * rows, (j + 1) * rows)
        reach = (SQUAD + 1 + j) * rows
        for h in range(heads):
            mixed, lse = attend(queries[h, cols], keys[h, :reach], values[h, :reach], True)
            out[h * HD : (h + 1) * HD, cols] = mixed
            out[width + h : width + h + 1, cols] = lse
        out[width + heads :, cols] = jnp.zeros((TAG - heads, rows), jnp.float32)


def far_kernel(place_ref, *refs):
    asked, near, out, (queries, keys, values) = refs[:2], refs[2:5], refs[5], refs[6:]
    heads, span, _ = queries.shape
    rows = span // SQUAD
    width = heads * HD
    corner = corner_of(place_ref)
    tall = rows + TAG
    asked = [asked[0].at[k * tall : (k + 1) * tall] for k in range(SQUAD - 1)] + [asked[1]]
    place_queries(asked, corner, rows, queries)
    place_keys(near_parts(near, rows), corner, 0, rows, keys, values)
    for j in range(SQUAD - 1):
        cols = slice(j * rows, (j + 1) * rows)
        stats = []
        for h in range(heads):
            mixed, lse = attend(
                queries[h, cols], keys[h, cols.stop :], values[h, cols.stop :], False
            )
            out[h * HD : (h + 1) * HD, cols] = mixed.astype(out.dtype)
            top = lse.astype(jnp.bfloat16).astype(jnp.float32)
            mid = (lse - top).astype(jnp.bfloat16).astype(jnp.float32)
            stats += [top, mid, lse - top - mid]
        stats.append(jnp.zeros((TAG - len(stats), rows), jnp.float32))
        out[width:, cols] = jnp.concatenate(stats, axis=0).astype(out.dtype)


def merge_kernel(place_ref, main_ref, far_ref, *refs):
    outs, ready = refs[:-1], refs[-1]
    _, rows, width = ready.shape
    corner = corner_of(place_ref)
    served = place_ref[0] >= 2 * SQUAD
    for j in range(SQUAD):
        cols = slice(j * rows, (j + 1) * rows)
        for h in range(width // HD):
            feats = slice(h * HD, (h + 1) * HD)
            mixed = main_ref[feats, cols]
            if j < SQUAD - 1:
                here = main_ref[width + h : width + h + 1, cols]
                stats = far_ref[width:, cols].astype(jnp.float32)
                there = stats[3 * h : 3 * h + 1] + stats[3 * h + 1 : 3 * h + 2]
                there = jnp.where(served, there + stats[3 * h + 2 : 3 * h + 3], NEG)
                high = jnp.maximum(here, there)
                here, there = jnp.exp2(here - high), jnp.exp2(there - high)
                total = here + there
                mixed = mixed * (here / total) + far_ref[feats, cols].astype(jnp.float32) * (
                    there / total
                )
            ready[j, :, feats] = mixed.T.astype(ready.dtype)
    for k, out in enumerate(outs):
        out[...] = ready[jnp.bitwise_xor(corner, k)]


def project_kernel(ranks, place_ref, *refs):
    parts, weight_ref, out_ref, whole = refs[:-3], refs[-3], refs[-2], refs[-1]
    mine, corner = place_ref[1], corner_of(place_ref)
    width = parts[0].shape[1]
    for r in range(ranks):
        source = lax.rem(mine + ranks - r, ranks)
        for k in range(SQUAD):
            begin = (source * SQUAD + jnp.bitwise_xor(corner, k)) * width
            whole[:, pl.ds(pl.multiple_of(begin, width), width)] = parts[r * SQUAD + k][...]
    block = 2 * LANES
    for c in range(out_ref.shape[1] // block):
        cols = slice(c * block, (c + 1) * block)
        out_ref[:, cols] = jnp.dot(
            whole[...], weight_ref[:, cols], preferred_element_type=jnp.float32
        ).astype(out_ref.dtype)


def local(
    hyena_q, hyena_k, hyena_v, filters, direct, queries, keys, values, segment_ids, out_weight
):
    rows, feat = queries.shape
    count, ranks = lax.axis_size("ctx"), lax.axis_size("tp")
    width = feat // SQUAD
    heads = width // HD
    bf16, f32 = jnp.bfloat16, jnp.float32
    place = jnp.stack([lax.axis_index("ctx"), lax.axis_index("tp")]).astype(jnp.int32)

    def swap(value, mask):
        return lax.ppermute(value, "ctx", [(i, i ^ mask) for i in range(count)])

    def climb(value, first=0):
        return lax.ppermute(value, "ctx", [(i, i + SQUAD) for i in range(first, count - SQUAD)])

    def descend(value):
        return lax.ppermute(
            value, "ctx", [(i, i - SQUAD) for i in range(2 * SQUAD, count)]
        )

    asked, kept, *sent = deal(
        place, queries, keys, values, segment_ids.reshape(rows // LANES, LANES)
    )
    tall = rows + TAG
    near = [climb(kept)]
    beside = [swap(sent[0], 1), swap(sent[1], 2)]
    sent[2], beside[0] = lax.optimization_barrier((sent[2], beside[0]))
    across = swap(sent[2], 3)
    near.append(climb(jnp.concatenate([x[rows:] for x in beside], axis=0)))
    back = [descend(jnp.concatenate([asked] + [x[:tall] for x in beside], axis=0))]
    near.append(climb(across[rows:]))
    back.append(descend(across[:tall]))
    own = [asked, kept, *beside, across]
    tail_k = hyena_k[rows - LANES :].astype(f32)
    tail_v = hyena_v[rows - LANES :].astype(f32)
    rim = lax.ppermute(
        (tail_k * tail_v).astype(bf16), "ctx", [(i, i + 1) for i in range(count - 1)]
    )

    def store(blocks):
        return [
            pltpu.VMEM((heads, SQUAD * rows, 2 * HD), bf16),
            pltpu.VMEM((heads, blocks * rows, 2 * HD), bf16),
            pltpu.VMEM((heads, blocks * rows, HD), bf16),
        ]

    (far,) = kernel_call(
        far_kernel,
        (place, *back, *near),
        [jax.ShapeDtypeStruct((width + TAG, (SQUAD - 1) * rows), bf16)],
        "far",
        store(SQUAD),
        flops=6 * 4 * rows * rows * width,
        exps=6 * rows * rows * heads,
    )
    far = climb(far, SQUAD)
    (main,) = kernel_call(
        main_kernel,
        (place, *own, *near),
        [jax.ShapeDtypeStruct((width + TAG, SQUAD * rows), f32)],
        "main",
        store(2 * SQUAD),
        flops=26 * 4 * rows * rows * width,
        exps=26 * rows * rows * heads,
    )
    done = kernel_call(
        merge_kernel,
        (place, main, far),
        [jax.ShapeDtypeStruct((rows, width), bf16)] * SQUAD,
        "merge",
        [pltpu.VMEM((SQUAD, rows, width), bf16)],
    )
    rim, done[0] = lax.optimization_barrier((rim, done[0]))
    hyena_out = hyena(hyena_q, hyena_k, hyena_v, rim, filters, direct)

    def turn(value, r):
        return lax.ppermute(value, "tp", [(t, (t + r) % ranks) for t in range(ranks)])

    pieces = [swap(done[k], k) for k in range(1, SQUAD)]
    hyena_out, *pieces = lax.optimization_barrier((hyena_out, done[0], *pieces))
    pieces += [turn(piece, r) for r in range(1, ranks) for piece in pieces]
    (attn_out,) = kernel_call(
        functools.partial(project_kernel, ranks),
        (place, *pieces, out_weight),
        [jax.ShapeDtypeStruct((rows, out_weight.shape[1]), bf16)],
        "project",
        [pltpu.VMEM((rows, ranks * feat), bf16)],
        flops=2 * rows * math.prod(out_weight.shape),
    )
    return (hyena_out, attn_out)


def solution(mesh):
    placed = (
        P("ctx", "tp"),
        P("ctx", "tp"),
        P("ctx", "tp"),
        P("tp", None),
        P("tp"),
        P("ctx", "tp"),
        P("ctx", "tp"),
        P("ctx", "tp"),
        P("ctx"),
        P(None, "tp"),
    )
    return jax.shard_map(
        local,
        mesh=mesh,
        in_specs=placed,
        out_specs=(P("ctx", "tp"), P("ctx", "tp")),
        check_vma=False,
    )
```

profile of v0, /device:TPU:17, one launch (start us, length us, event | category | flops | bytes accessed | tf_op | source)
XLA Modules:
  0.0 82.2 jit_solution(1491318893867329645)
XLA Ops:
  0.6 0.7 pad_add_fusion.place_ref
  1.3 3.1 %deal.1 = (bf16[272,256]{1,0:T(8,128)(2,1)}, bf16[528,256]{1,0:T(8,128)(2,1)}, bf16[784,256]{1,0:T(8,128)(2,1)}, bf16[784,256]{1,0:T(8,128)(2,1)}, bf16[784,256]{1,0:T(8,128)(2,1)}) custom-call(s32[2]{0:T(128)} %pad_add_fusion.place_ref, bf16[256,1024]{1,0:T(8,128)(2,1)} %q_ref.2, bf16[256,1024]{1,0:T(8,128)(2,1)} %k_ref.2, bf16[256,1024]{1,0:T(8,128)(2,1)} %v_ref.2, ...), custom_call_target="tpu_custom_call" | custom-call | bytes 3145728 | tf_op jit(solution)/shard_map/deal/pallas_call | solution.py:159
  4.4 1.3 %collective-permute-start.1 = (bf16[784,256]{1,0:T(8,128)(2,1)}, bf16[784,256]{1,0:T(8,128)(2,1)S(1)}, u32[]{:S(2)}, u32[]{:S(2)}) collective-permute-start(bf16[784,256]{1,0:T(8,128)(2,1)} %get-tuple-element.23), channel_id=1, source_target_pairs={{0,2},{2,0},{4,6},{6,4},{8,10},{10,8},{12,14},{14,12},{16,18},{18,... | collective-permute-start | bytes 1204232 | tf_op jit(solution)/shard_map/ppermute | solution.py:339
  5.7 1.2 %collective-permute-start.2 = (bf16[784,256]{1,0:T(8,128)(2,1)}, bf16[784,256]{1,0:T(8,128)(2,1)S(1)}, u32[]{:S(2)}, u32[]{:S(2)}) collective-permute-start(bf16[784,256]{1,0:T(8,128)(2,1)} %get-tuple-element.25), channel_id=1, source_target_pairs={{0,4},{2,6},{4,0},{6,2},{8,12},{10,14},{12,8},{14,10},{16,20},{18,... | collective-permute-start | bytes 1204232 | tf_op jit(solution)/shard_map/ppermute | solution.py:339
  6.9 7.9 %collective-permute-done.1.refs_2_ = bf16[784,256]{1,0:T(8,128)(2,1)S(1)} collective-permute-done((bf16[784,256]{1,0:T(8,128)(2,1)}, bf16[784,256]{1,0:T(8,128)(2,1)S(1)}, u32[]{:S(2)}, u32[]{:S(2)}) %collective-permute-start.1) | collective-permute-done | bytes 401440 | tf_op jit(solution)/shard_map/ppermute | solution.py:339
  14.8 2.2 %collective-permute-start.3 = (bf16[784,256]{1,0:T(8,128)(2,1)}, bf16[784,256]{1,0:T(8,128)(2,1)S(1)}, u32[]{:S(2)}, u32[]{:S(2)}) collective-permute-start(bf16[784,256]{1,0:T(8,128)(2,1)} %get-tuple-element.26), channel_id=1, source_target_pairs={{0,6},{2,4},{4,2},{6,0},{8,14},{10,12},{12,10},{14,8},{16,22},{18,... | collective-permute-start | bytes 1204232 | tf_op jit(solution)/shard_map/ppermute | solution.py:339
  17.0 3.2 %collective-permute-start.4 = (bf16[528,256]{1,0:T(8,128)(2,1)}, bf16[528,256]{1,0:T(8,128)(2,1)S(1)}, u32[]{:S(2)}, u32[]{:S(2)}) collective-permute-start(bf16[528,256]{1,0:T(8,128)(2,1)} %get-tuple-element.21.refs_1_), channel_id=1, source_target_pairs={{0,8},{2,10},{4,12},{6,14},{8,16},{10,18},{12,20},{14,22},{16,24},... | collective-permute-start | bytes 811016 | tf_op jit(solution)/shard_map/ppermute | solution.py:342
  20.3 2.1 %collective-permute-start.7 = (bf16[816,256]{1,0:T(8,128)(2,1)S(1)}, bf16[816,256]{1,0:T(8,128)(2,1)S(1)}, u32[]{:S(2)}, u32[]{:S(2)}) collective-permute-start(bf16[816,256]{1,0:T(8,128)(2,1)S(1)} %pad_maximum_fusion.1), channel_id=1, source_target_pairs={{16,8},{18,10},{20,12},{22,14},{24,16},{26,18},{28,20},{30,22},{17... | collective-permute-start | bytes 1253384 | tf_op jit(solution)/shard_map/ppermute | solution.py:345
  22.5 3.4 %collective-permute-start.5 = (bf16[1056,256]{1,0:T(8,128)(2,1)S(1)}, bf16[1056,256]{1,0:T(8,128)(2,1)S(1)}, u32[]{:S(2)}, u32[]{:S(2)}) collective-permute-start(bf16[1056,256]{1,0:T(8,128)(2,1)S(1)} %pad_maximum_fusion), channel_id=1, source_target_pairs={{0,8},{2,10},{4,12},{6,14},{8,16},{10,18},{12,20},{14,22},{16,24},... | collective-permute-start | bytes 1622024 | tf_op jit(solution)/shard_map/ppermute | solution.py:342
  25.9 2.5 %collective-permute-start.6 = (bf16[528,256]{1,0:T(8,128)(2,1)S(1)}, bf16[528,256]{1,0:T(8,128)(2,1)S(1)}, u32[]{:S(2)}, u32[]{:S(2)}) collective-permute-start(bf16[528,256]{1,0:T(8,128)(2,1)S(1)} %slice.33), channel_id=1, source_target_pairs={{0,8},{2,10},{4,12},{6,14},{8,16},{10,18},{12,20},{14,22},{16,24},... | collective-permute-start | bytes 811016 | tf_op jit(solution)/shard_map/ppermute | solution.py:342
  28.4 2.8 %collective-permute-start.8 = (bf16[272,256]{1,0:T(8,128)(2,1)S(1)}, bf16[272,256]{1,0:T(8,128)(2,1)S(1)}, u32[]{:S(2)}, u32[]{:S(2)}) collective-permute-start(bf16[272,256]{1,0:T(8,128)(2,1)S(1)} %slice.35), channel_id=1, source_target_pairs={{16,8},{18,10},{20,12},{22,14},{24,16},{26,18},{28,20},{30,22},{17... | collective-permute-start | bytes 417800 | tf_op jit(solution)/shard_map/ppermute | solution.py:345
  31.4 2.5 %collective-permute-start = (bf16[128,2048]{1,0:T(8,128)(2,1)S(1)}, bf16[128,2048]{1,0:T(8,128)(2,1)S(1)}, u32[]{:S(2)}, u32[]{:S(2)}) collective-permute-start(bf16[128,2048]{1,0:T(8,128)(2,1)S(1)} %multiply_convert_fusion), channel_id=1, source_target_pairs={{0,2},{2,4},{4,6},{6,8},{8,10},{10,12},{12,14},{14,16},{16,18},{18... | collective-permute-start | bytes 1572872 | tf_op jit(solution)/shard_map/ppermute | solution.py:364
  34.0 2.6 %collective-permute-done.5.refs_6_.refs_3_ = bf16[1056,256]{1,0:T(8,128)(2,1)S(1)} collective-permute-done((bf16[1056,256]{1,0:T(8,128)(2,1)S(1)}, bf16[1056,256]{1,0:T(8,128)(2,1)S(1)}, u32[]{:S(2)}, u32[]{:S(2)}) %collective-permute-start.5) | collective-permute-done | bytes 540704 | tf_op jit(solution)/shard_map/ppermute | solution.py:342
  36.6 5.8 %collective-permute-done.6.refs_7_.refs_4_ = bf16[528,256]{1,0:T(8,128)(2,1)S(1)} collective-permute-done((bf16[528,256]{1,0:T(8,128)(2,1)S(1)}, bf16[528,256]{1,0:T(8,128)(2,1)S(1)}, u32[]{:S(2)}, u32[]{:S(2)}) %collective-permute-start.6) | collective-permute-done | bytes 270368 | tf_op jit(solution)/shard_map/ppermute | solution.py:342
  42.4 3.2 %far.1 = bf16[272,768]{1,0:T(8,128)(2,1)S(1)} custom-call(s32[2]{0:T(128)S(1)} %copy-done.3, bf16[816,256]{1,0:T(8,128)(2,1)S(1)} %collective-permute-done.7.refs_0_, bf16[272,256]{1,0:T(8,128)(2,1)S(1)} %collective-permute-done.8.refs_1_, bf16[528,256]{1,0:T(8,128)(2,1)S(1)} %collective-permute-done.4.refs_5_.refs_2_, ...), custom_call_target="tpu_custom_call" | custom-call | flops 402653184 | bytes 2056200 | tf_op jit(solution)/shard_map/far/pallas_call | solution.py:28
  45.6 3.4 %collective-permute-start.9 = (bf16[272,768]{1,0:T(8,128)(2,1)S(1)}, bf16[272,768]{1,0:T(8,128)(2,1)S(1)}, u32[]{:S(2)}, u32[]{:S(2)}) collective-permute-start(bf16[272,768]{1,0:T(8,128)(2,1)S(1)} %far.1), channel_id=1, source_target_pairs={{8,16},{10,18},{12,20},{14,22},{16,24},{18,26},{20,28},{22,30},{9,... | collective-permute-start | bytes 1253384 | tf_op jit(solution)/shard_map/ppermute | solution.py:342
  49.0 8.6 %main.1.main_ref = f32[272,1024]{1,0:T(8,128)S(1)} custom-call(s32[2]{0:T(128)S(1)} %copy-done.3, bf16[272,256]{1,0:T(8,128)(2,1)S(1)} %copy-done.2, bf16[528,256]{1,0:T(8,128)(2,1)S(1)} %copy-done.5, bf16[784,256]{1,0:T(8,128)(2,1)S(1)} %collective-permute-done.1.refs_2_, bf16[784,256]{1,0:T(8,128)(2,1)S(1)} %collective-permute-done.2.refs_3_, ...), custom_call_target="tpu_custom_call" | custom-call | flops 1744830464 | bytes 3809288 | tf_op jit(solution)/shard_map/main/pallas_call | solution.py:28
  57.6 0.9 %merge.1 = (bf16[256,256]{1,0:T(8,128)(2,1)S(1)}, bf16[256,256]{1,0:T(8,128)(2,1)S(1)}, bf16[256,256]{1,0:T(8,128)(2,1)S(1)}, bf16[256,256]{1,0:T(8,128)(2,1)S(1)}) custom-call(s32[2]{0:T(128)S(1)} %copy-done.3, f32[272,1024]{1,0:T(8,128)S(1)} %main.1.main_ref, bf16[272,768]{1,0:T(8,128)(2,1)S(1)} %collective-permute-done.9.far_ref), custom_call_target="tpu_custom_call" | custom-call | bytes 2056200 | tf_op jit(solution)/shard_map/merge/pallas_call | solution.py:28
  58.8 5.2 %collective-permute-start.11 = (bf16[256,256]{1,0:T(8,128)(2,1)S(1)}, bf16[256,256]{1,0:T(8,128)(2,1)S(1)}, u32[]{:S(2)}, u32[]{:S(2)}) collective-permute-start(bf16[256,256]{1,0:T(8,128)(2,1)S(1)} %get-tuple-element.31), channel_id=1, source_target_pairs={{0,4},{2,6},{4,0},{6,2},{8,12},{10,14},{12,8},{14,10},{16,20},{18,... | collective-permute-start | bytes 393224 | tf_op jit(solution)/shard_map/ppermute | solution.py:339
  64.1 8.7 %hyena.1 = bf16[256,2048]{1,0:T(8,128)(2,1)} custom-call(bf16[256,2048]{1,0:T(8,128)(2,1)S(1)} %copy-done.4, bf16[256,2048]{1,0:T(8,128)(2,1)S(1)} %copy-done, bf16[256,2048]{1,0:T(8,128)(2,1)S(1)} %copy-done.1, bf16[128,2048]{1,0:T(8,128)(2,1)S(1)} %collective-permute-done.rim_ref, bf16[128,128]{1,0:T(8,128)(2,1)S(1)} %copy-done.6, ...), custom_call_target="tpu_custom_call" | custom-call | flops 4294967296 | bytes 5242880 | tf_op jit(solution)/shard_map/hyena/pallas_call | solution.py:87
  72.7 3.6 %collective-permute-start.13 = (bf16[256,256]{1,0:T(8,128)(2,1)S(1)}, bf16[256,256]{1,0:T(8,128)(2,1)S(1)}, u32[]{:S(2)}, u32[]{:S(2)}) collective-permute-start(bf16[256,256]{1,0:T(8,128)(2,1)S(1)} %get-tuple-element.34.refs_0_), channel_id=1, source_target_pairs={{0,1},{1,0},{2,3},{3,2},{4,5},{5,4},{6,7},{7,6},{8,9},{9,8},{10,11... | collective-permute-start | bytes 393224 | tf_op jit(solution)/shard_map/ppermute | solution.py:405
  76.4 0.4 collective-permute-start.15
  76.9 0.4 collective-permute-done.13.refs_4_
  78.2 4.0 %project.1 = bf16[256,2048]{1,0:T(8,128)(2,1)} custom-call(s32[2]{0:T(128)S(1)} %copy-done.3, bf16[256,256]{1,0:T(8,128)(2,1)S(1)} %get-tuple-element.34.refs_0_, bf16[256,256]{1,0:T(8,128)(2,1)S(1)} %collective-permute-done.10.refs_1_, bf16[256,256]{1,0:T(8,128)(2,1)S(1)} %collective-permute-done.11.refs_2_, ...), custom_call_target="tpu_custom_call" | custom-call | flops 2147483648 | bytes 10485768 | tf_op jit(solution)/shard_map/project/pallas_call | solution.py:28
  (48 shorter events, 1.8 us)
Async XLA Ops:
  4.4 15.9 %copy-start.2 = (bf16[272,256]{1,0:T(8,128)(2,1)S(1)}, bf16[272,256]{1,0:T(8,128)(2,1)}, u32[]{:S(2)}) copy-start(bf16[272,256]{1,0:T(8,128)(2,1)} %get-tuple-element.20.refs_0_) | copy-start | bytes 417796
  4.4 10.4 %collective-permute-start.1 = (bf16[784,256]{1,0:T(8,128)(2,1)}, bf16[784,256]{1,0:T(8,128)(2,1)S(1)}, u32[]{:S(2)}, u32[]{:S(2)}) collective-permute-start(bf16[784,256]{1,0:T(8,128)(2,1)} %get-tuple-element.23), channel_id=1, source_target_pairs={{0,2},{2,0},{4,6},{6,4},{8,10},{10,8},{12,14},{14,12},{16,18},{18,... | collective-permute-start | bytes 1204232 | tf_op jit(solution)/shard_map/ppermute | solution.py:339
  5.7 14.6 %collective-permute-start.2 = (bf16[784,256]{1,0:T(8,128)(2,1)}, bf16[784,256]{1,0:T(8,128)(2,1)S(1)}, u32[]{:S(2)}, u32[]{:S(2)}) collective-permute-start(bf16[784,256]{1,0:T(8,128)(2,1)} %get-tuple-element.25), channel_id=1, source_target_pairs={{0,4},{2,6},{4,0},{6,2},{8,12},{10,14},{12,8},{14,10},{16,20},{18,... | collective-permute-start | bytes 1204232 | tf_op jit(solution)/shard_map/ppermute | solution.py:339
  14.8 11.1 %collective-permute-start.3 = (bf16[784,256]{1,0:T(8,128)(2,1)}, bf16[784,256]{1,0:T(8,128)(2,1)S(1)}, u32[]{:S(2)}, u32[]{:S(2)}) collective-permute-start(bf16[784,256]{1,0:T(8,128)(2,1)} %get-tuple-element.26), channel_id=1, source_target_pairs={{0,6},{2,4},{4,2},{6,0},{8,14},{10,12},{12,10},{14,8},{16,22},{18,... | collective-permute-start | bytes 1204232 | tf_op jit(solution)/shard_map/ppermute | solution.py:339
  17.0 14.4 %collective-permute-start.4 = (bf16[528,256]{1,0:T(8,128)(2,1)}, bf16[528,256]{1,0:T(8,128)(2,1)S(1)}, u32[]{:S(2)}, u32[]{:S(2)}) collective-permute-start(bf16[528,256]{1,0:T(8,128)(2,1)} %get-tuple-element.21.refs_1_), channel_id=1, source_target_pairs={{0,8},{2,10},{4,12},{6,14},{8,16},{10,18},{12,20},{14,22},{16,24},... | collective-permute-start | bytes 811016 | tf_op jit(solution)/shard_map/ppermute | solution.py:342
  20.3 13.7 %collective-permute-start.7 = (bf16[816,256]{1,0:T(8,128)(2,1)S(1)}, bf16[816,256]{1,0:T(8,128)(2,1)S(1)}, u32[]{:S(2)}, u32[]{:S(2)}) collective-permute-start(bf16[816,256]{1,0:T(8,128)(2,1)S(1)} %pad_maximum_fusion.1), channel_id=1, source_target_pairs={{16,8},{18,10},{20,12},{22,14},{24,16},{26,18},{28,20},{30,22},{17... | collective-permute-start | bytes 1253384 | tf_op jit(solution)/shard_map/ppermute | solution.py:345
  22.4 8.8 %copy-start.1 = (bf16[256,2048]{1,0:T(8,128)(2,1)S(1)}, bf16[256,2048]{1,0:T(8,128)(2,1)}, u32[]{:S(2)}) copy-start(bf16[256,2048]{1,0:T(8,128)(2,1)} %v_ref.3) | copy-start | bytes 3145732
  22.5 19.9 %copy-start.3 = (s32[2]{0:T(128)S(1)}, s32[2]{0:T(128)}, u32[]{:S(2)}) copy-start(s32[2]{0:T(128)} %pad_add_fusion.place_ref) | copy-start | bytes 28
  22.5 14.1 %collective-permute-start.5 = (bf16[1056,256]{1,0:T(8,128)(2,1)S(1)}, bf16[1056,256]{1,0:T(8,128)(2,1)S(1)}, u32[]{:S(2)}, u32[]{:S(2)}) collective-permute-start(bf16[1056,256]{1,0:T(8,128)(2,1)S(1)} %pad_maximum_fusion), channel_id=1, source_target_pairs={{0,8},{2,10},{4,12},{6,14},{8,16},{10,18},{12,20},{14,22},{16,24},... | collective-permute-start | bytes 1622024 | tf_op jit(solution)/shard_map/ppermute | solution.py:342
  25.9 16.5 %collective-permute-start.6 = (bf16[528,256]{1,0:T(8,128)(2,1)S(1)}, bf16[528,256]{1,0:T(8,128)(2,1)S(1)}, u32[]{:S(2)}, u32[]{:S(2)}) collective-permute-start(bf16[528,256]{1,0:T(8,128)(2,1)S(1)} %slice.33), channel_id=1, source_target_pairs={{0,8},{2,10},{4,12},{6,14},{8,16},{10,18},{12,20},{14,22},{16,24},... | collective-permute-start | bytes 811016 | tf_op jit(solution)/shard_map/ppermute | solution.py:342
  28.4 8.2 %collective-permute-start.8 = (bf16[272,256]{1,0:T(8,128)(2,1)S(1)}, bf16[272,256]{1,0:T(8,128)(2,1)S(1)}, u32[]{:S(2)}, u32[]{:S(2)}) collective-permute-start(bf16[272,256]{1,0:T(8,128)(2,1)S(1)} %slice.35), channel_id=1, source_target_pairs={{16,8},{18,10},{20,12},{22,14},{24,16},{26,18},{28,20},{30,22},{17... | collective-permute-start | bytes 417800 | tf_op jit(solution)/shard_map/ppermute | solution.py:345
  31.4 17.5 %copy-start.7 = (bf16[2048]{0:T(1024)(128)(2,1)S(1)}, bf16[2048]{0:T(1024)(128)(2,1)}, u32[]{:S(2)}) copy-start(bf16[2048]{0:T(1024)(128)(2,1)} %param.14) | copy-start | bytes 12292
  31.4 17.6 %copy-start.5 = (bf16[528,256]{1,0:T(8,128)(2,1)S(1)}, bf16[528,256]{1,0:T(8,128)(2,1)}, u32[]{:S(2)}) copy-start(bf16[528,256]{1,0:T(8,128)(2,1)} %get-tuple-element.21.refs_1_) | copy-start | bytes 811012
  31.4 27.1 %collective-permute-start = (bf16[128,2048]{1,0:T(8,128)(2,1)S(1)}, bf16[128,2048]{1,0:T(8,128)(2,1)S(1)}, u32[]{:S(2)}, u32[]{:S(2)}) collective-permute-start(bf16[128,2048]{1,0:T(8,128)(2,1)S(1)} %multiply_convert_fusion), channel_id=1, source_target_pairs={{0,2},{2,4},{4,6},{6,8},{8,10},{10,12},{12,14},{14,16},{16,18},{18... | collective-permute-start | bytes 1572872 | tf_op jit(solution)/shard_map/ppermute | solution.py:364
  45.6 12.0 %collective-permute-start.9 = (bf16[272,768]{1,0:T(8,128)(2,1)S(1)}, bf16[272,768]{1,0:T(8,128)(2,1)S(1)}, u32[]{:S(2)}, u32[]{:S(2)}) collective-permute-start(bf16[272,768]{1,0:T(8,128)(2,1)S(1)} %far.1), channel_id=1, source_target_pairs={{8,16},{10,18},{12,20},{14,22},{16,24},{18,26},{20,28},{22,30},{9,... | collective-permute-start | bytes 1253384 | tf_op jit(solution)/shard_map/ppermute | solution.py:342
  58.5 14.2 %collective-permute-start.10 = (bf16[256,256]{1,0:T(8,128)(2,1)S(1)}, bf16[256,256]{1,0:T(8,128)(2,1)S(1)}, u32[]{:S(2)}, u32[]{:S(2)}) collective-permute-start(bf16[256,256]{1,0:T(8,128)(2,1)S(1)} %get-tuple-element.30), channel_id=1, source_target_pairs={{0,2},{2,0},{4,6},{6,4},{8,10},{10,8},{12,14},{14,12},{16,18},{18,... | collective-permute-start | bytes 393224 | tf_op jit(solution)/shard_map/ppermute | solution.py:339
  58.8 13.9 %collective-permute-start.11 = (bf16[256,256]{1,0:T(8,128)(2,1)S(1)}, bf16[256,256]{1,0:T(8,128)(2,1)S(1)}, u32[]{:S(2)}, u32[]{:S(2)}) collective-permute-start(bf16[256,256]{1,0:T(8,128)(2,1)S(1)} %get-tuple-element.31), channel_id=1, source_target_pairs={{0,4},{2,6},{4,0},{6,2},{8,12},{10,14},{12,8},{14,10},{16,20},{18,... | collective-permute-start | bytes 393224 | tf_op jit(solution)/shard_map/ppermute | solution.py:339
  64.0 14.2 %slice-start = ((s8[8388608]{0:T(1024)(128)(4,1)}), s8[4194304]{0:T(1024)(128)(4,1)S(1)}, s32[]{:S(2)}) async-start(s8[8388608]{0:T(1024)(128)(4,1)} %bitcast.3), calls=%async_computation | async-start | bytes 8388608
  64.0 14.2 %slice-start.1 = ((s8[8388608]{0:T(1024)(128)(4,1)}), s8[4194304]{0:T(1024)(128)(4,1)S(1)}, s32[]{:S(2)}) async-start(s8[8388608]{0:T(1024)(128)(4,1)} %bitcast.3), calls=%async_computation.1 | async-start | bytes 8388608
  64.0 8.7 %collective-permute-start.12 = (bf16[256,256]{1,0:T(8,128)(2,1)S(1)}, bf16[256,256]{1,0:T(8,128)(2,1)S(1)}, u32[]{:S(2)}, u32[]{:S(2)}) collective-permute-start(bf16[256,256]{1,0:T(8,128)(2,1)S(1)} %get-tuple-element.32), channel_id=1, source_target_pairs={{0,6},{2,4},{4,2},{6,0},{8,14},{10,12},{12,10},{14,8},{16,22},{18,... | collective-permute-start | bytes 393224 | tf_op jit(solution)/shard_map/ppermute | solution.py:339
  72.7 4.6 %collective-permute-start.13 = (bf16[256,256]{1,0:T(8,128)(2,1)S(1)}, bf16[256,256]{1,0:T(8,128)(2,1)S(1)}, u32[]{:S(2)}, u32[]{:S(2)}) collective-permute-start(bf16[256,256]{1,0:T(8,128)(2,1)S(1)} %get-tuple-element.34.refs_0_), channel_id=1, source_target_pairs={{0,1},{1,0},{2,3},{3,2},{4,5},{5,4},{6,7},{7,6},{8,9},{9,8},{10,11... | collective-permute-start | bytes 393224 | tf_op jit(solution)/shard_map/ppermute | solution.py:405
  76.3 1.3 %collective-permute-start.14 = (bf16[256,256]{1,0:T(8,128)(2,1)S(1)}, bf16[256,256]{1,0:T(8,128)(2,1)S(1)}, u32[]{:S(2)}, u32[]{:S(2)}) collective-permute-start(bf16[256,256]{1,0:T(8,128)(2,1)S(1)} %collective-permute-done.10.refs_1_), channel_id=1, source_target_pairs={{0,1},{1,0},{2,3},{3,2},{4,5},{5,4},{6,7},{7,6},{8,9},{9,8},{10,11... | collective-permute-start | bytes 393224 | tf_op jit(solution)/shard_map/ppermute | solution.py:405
  76.4 1.5 %collective-permute-start.15 = (bf16[256,256]{1,0:T(8,128)(2,1)S(1)}, bf16[256,256]{1,0:T(8,128)(2,1)S(1)}, u32[]{:S(2)}, u32[]{:S(2)}) collective-permute-start(bf16[256,256]{1,0:T(8,128)(2,1)S(1)} %collective-permute-done.11.refs_2_), channel_id=1, source_target_pairs={{0,1},{1,0},{2,3},{3,2},{4,5},{5,4},{6,7},{7,6},{8,9},{9,8},{10,11... | collective-permute-start | bytes 393224 | tf_op jit(solution)/shard_map/ppermute | solution.py:405
  76.8 1.3 %collective-permute-start.16 = (bf16[256,256]{1,0:T(8,128)(2,1)S(1)}, bf16[256,256]{1,0:T(8,128)(2,1)S(1)}, u32[]{:S(2)}, u32[]{:S(2)}) collective-permute-start(bf16[256,256]{1,0:T(8,128)(2,1)S(1)} %collective-permute-done.12.refs_3_), channel_id=1, source_target_pairs={{0,1},{1,0},{2,3},{3,2},{4,5},{5,4},{6,7},{7,6},{8,9},{9,8},{10,11... | collective-permute-start | bytes 393224 | tf_op jit(solution)/shard_map/ppermute | solution.py:405
  (3 other events, 21.8 us)
where the time goes:
time: 83 us; the launch traced here: 82.2 us
  starting transfers between devices  34.2 us (41%)
  Pallas kernels  28.4 us (34%)
  waiting for transfers between devices  17.6 us (21%)
  between operations  0.98 us (1%)
  other arithmetic  0.87 us (1%)
    pallas_call x4, Pallas kernels, kernel_call(): pl.pallas_call(kernel, in_specs=[SMEM] + [VMEM] * (len(args) - 1), out_sp...  16.6 us
    ppermute x4, starting transfers between devices, climb(): lax.ppermute(value, 'ctx', [(i, i + SQUAD) for i in range(first, count -...  12.4 us
    ppermute x6, starting transfers between devices, swap(): return lax.ppermute(value, 'ctx', [(i, i ^ mask) for i in range(count)])  10.2 us
    pallas_call x1, Pallas kernels, hyena(): pl.pallas_call(hyena_kernel, grid=(steps,), in_specs=[wide, wide, wide, p...  8.67 us
    ppermute x4, waiting for transfers between devices, climb(): lax.ppermute(value, 'ctx', [(i, i + SQUAD) for i in range(first, count -...  8.4 us
    ppermute x6, waiting for transfers between devices, swap(): return lax.ppermute(value, 'ctx', [(i, i ^ mask) for i in range(count)])  7.93 us
    ppermute x2, starting transfers between devices, descend(): lax.ppermute(value, 'ctx', [(i, i - SQUAD) for i in range(2 * SQUAD, coun...  4.87 us
    ppermute x4, starting transfers between devices, turn(): lax.ppermute(value, 'tp', [(t, (t + r) % ranks) for t in range(ranks)])  4.18 us
  transfers between devices with their start and end apart: 17, of which 7 were waited for; matrix products, arithmetic and copies ran while one was open for 0% of the time, Pallas kernels for 26%

commit v1 on v0

--- a/solution.py
+++ b/solution.py
@@ -16,18 +16,17 @@
 VMEM_LIMIT = 32 * 1024 * 1024
 ALL_VMEM = 62 * 1024 * 1024
 VMEM = pl.BlockSpec(memory_space=pltpu.VMEM)
-SMEM = pl.BlockSpec(memory_space=pltpu.SMEM)
-
-
-def corner_of(place_ref):
-    return lax.rem(place_ref[0], SQUAD)
+
+
+def corner_of():
+    return lax.rem(lax.axis_index("ctx"), SQUAD)
 
 
 def kernel_call(kernel, args, shapes, name, scratch=(), flops=0, exps=0):
     total = sum(math.prod(x.shape) * x.dtype.itemsize for x in (*args, *shapes))
     return list(pl.pallas_call(
         kernel,
-        in_specs=[SMEM] + [VMEM] * (len(args) - 1),
+        in_specs=[VMEM] * len(args),
         out_specs=[VMEM] * len(shapes),
         out_shape=shapes,
         scratch_shapes=scratch,
@@ -42,9 +41,11 @@
     per_tile = taps_ref.shape[0] * LANES // width
     group = LANES // per_tile
     windows = rows // LANES
-    shape = (LANES, 2 * LANES)
-    turn = lax.broadcasted_iota(jnp.int32, shape, 0) + lax.broadcasted_iota(jnp.int32, shape, 1)
-    turn = jnp.where(turn == LANES, 1.0, 0.0).astype(jnp.bfloat16)
+    shape = (LANES, LANES)
+    down, along = (lax.broadcasted_iota(jnp.int32, shape, i) for i in range(2))
+    turn = jnp.where((down + along) % LANES == 0, 1.0, 0.0).astype(jnp.bfloat16)
+    before = jnp.where(along > down, 1.0, 0.0).astype(jnp.bfloat16)
+    within = jnp.where(along > down, 0.0, 1.0).astype(jnp.bfloat16)
     taps = jnp.dot(taps_ref[...], turn, preferred_element_type=jnp.float32)
     lane_group = lax.broadcasted_iota(jnp.int32, (LANES, windows * LANES), 1) % LANES // group
     for tile in range(width // LANES):
@@ -60,12 +61,10 @@
         for g in range(per_tile):
             at = tile * per_tile + g
             row = taps[at : at + 1]
-            first = pltpu.roll(
-                jnp.broadcast_to(row, (TAG, 2 * LANES)), 0, 1, stride=1, stride_axis=0
+            ring = pltpu.roll(
+                jnp.broadcast_to(row, shape), 0, 1, stride=1, stride_axis=0
             ).astype(jnp.bfloat16)
-            table = jnp.concatenate(
-                [first] + [pltpu.roll(first, t, 1) for t in range(TAG, LANES, TAG)], axis=0
-            )
+            table = jnp.concatenate([ring * before, ring * within], axis=1)
             part = jnp.dot(table, stacked, preferred_element_type=jnp.float32)
             conv = jnp.where(lane_group == g, part, conv)
         conv = jnp.concatenate(
@@ -107,11 +106,11 @@
     )(hyena_q, hyena_k, hyena_v, rim, taps, direct[None])
 
 
-def deal_kernel(place_ref, q_ref, k_ref, v_ref, id_ref, *refs):
+def deal_kernel(q_ref, k_ref, v_ref, id_ref, *refs):
     outs, held, (arrive, leave) = refs[: SQUAD + 1], refs[SQUAD + 1 : -2], refs[-2:]
     rows, feat = q_ref.shape
     width = feat // SQUAD
-    corner = corner_of(place_ref)
+    corner = corner_of()
     order = list(range(1, SQUAD)) + [0]
     copies = {}
     for k in order:
@@ -150,7 +149,7 @@
         copy.wait()
 
 
-def deal(place, queries, keys, values, ids):
+def deal(queries, keys, values, ids):
     rows, feat = queries.shape
     tall = [rows + TAG, 2 * rows + TAG] + [3 * rows + TAG] * (SQUAD - 1)
     shapes = [(x, feat // SQUAD) for x in tall]
@@ -158,7 +157,7 @@
     return list(
         pl.pallas_call(
             deal_kernel,
-            in_specs=[SMEM] + [anywhere] * 3 + [VMEM],
+            in_specs=[anywhere] * 3 + [VMEM],
             out_specs=[anywhere] * len(tall),
             out_shape=[jax.ShapeDtypeStruct(x, jnp.bfloat16) for x in shapes],
             scratch_shapes=[pltpu.VMEM(x, jnp.bfloat16) for x in shapes]
@@ -168,7 +167,7 @@
                 flops=0, bytes_accessed=12 * rows * feat, transcendentals=0
             ),
             name="deal",
-        )(place, queries, keys, values, ids)
+        )(queries, keys, values, ids)
     )
 
 
@@ -236,12 +235,12 @@
     return summed / total, high * factor + jnp.log2(total)
 
 
-def main_kernel(place_ref, *refs):
+def main_kernel(*refs):
     own, near, out, (queries, keys, values) = refs[:5], refs[5:8], refs[8], refs[9:]
     heads, span, _ = queries.shape
     rows = span // SQUAD
     width = heads * HD
-    corner = corner_of(place_ref)
+    corner = corner_of()
     asked = [own[0]] + [p.at[: rows + TAG] for p in own[2:]]
     held = [own[1]] + [p.at[rows:] for p in own[2:]]
     place_queries(asked, corner, rows, queries)
@@ -257,12 +256,12 @@
         out[width + heads :, cols] = jnp.zeros((TAG - heads, rows), jnp.float32)
 
 
-def far_kernel(place_ref, *refs):
+def far_kernel(*refs):
     asked, near, out, (queries, keys, values) = refs[:2], refs[2:5], refs[5], refs[6:]
     heads, span, _ = queries.shape
     rows = span // SQUAD
     width = heads * HD
-    corner = corner_of(place_ref)
+    corner = corner_of()
     tall = rows + TAG
     asked = [asked[0].at[k * tall : (k + 1) * tall] for k in range(SQUAD - 1)] + [asked[1]]
     place_queries(asked, corner, rows, queries)
@@ -282,11 +281,11 @@
         out[width:, cols] = jnp.concatenate(stats, axis=0).astype(out.dtype)
 
 
-def merge_kernel(place_ref, main_ref, far_ref, *refs):
+def merge_kernel(main_ref, far_ref, *refs):
     outs, ready = refs[:-1], refs[-1]
     _, rows, width = ready.shape
-    corner = corner_of(place_ref)
-    served = place_ref[0] >= 2 * SQUAD
+    corner = corner_of()
+    served = lax.axis_index("ctx") >= 2 * SQUAD
     for j in range(SQUAD):
         cols = slice(j * rows, (j + 1) * rows)
         for h in range(width // HD):
@@ -308,9 +307,9 @@
         out[...] = ready[jnp.bitwise_xor(corner, k)]
 
 
-def project_kernel(ranks, place_ref, *refs):
+def project_kernel(ranks, *refs):
     parts, weight_ref, out_ref, whole = refs[:-3], refs[-3], refs[-2], refs[-1]
-    mine, corner = place_ref[1], corner_of(place_ref)
+    mine, corner = lax.axis_index("tp"), corner_of()
     width = parts[0].shape[1]
     for r in range(ranks):
         source = lax.rem(mine + ranks - r, ranks)
@@ -333,7 +332,6 @@
     width = feat // SQUAD
     heads = width // HD
     bf16, f32 = jnp.bfloat16, jnp.float32
-    place = jnp.stack([lax.axis_index("ctx"), lax.axis_index("tp")]).astype(jnp.int32)
 
     def swap(value, mask):
         return lax.ppermute(value, "ctx", [(i, i ^ mask) for i in range(count)])
@@ -347,24 +345,26 @@
         )
 
     asked, kept, *sent = deal(
-        place, queries, keys, values, segment_ids.reshape(rows // LANES, LANES)
+        queries, keys, values, segment_ids.reshape(rows // LANES, LANES)
     )
     tall = rows + TAG
     near = [climb(kept)]
     beside = [swap(sent[0], 1), swap(sent[1], 2)]
     sent[2], beside[0] = lax.optimization_barrier((sent[2], beside[0]))
     across = swap(sent[2], 3)
+    beside[1], near[0] = lax.optimization_barrier((beside[1], near[0]))
     near.append(climb(jnp.concatenate([x[rows:] for x in beside], axis=0)))
     back = [descend(jnp.concatenate([asked] + [x[:tall] for x in beside], axis=0))]
     near.append(climb(across[rows:]))
     back.append(descend(across[:tall]))
-    own = [asked, kept, *beside, across]
     tail_k = hyena_k[rows - LANES :].astype(f32)
     tail_v = hyena_v[rows - LANES :].astype(f32)
     rim = lax.ppermute(
-        (tail_k * tail_v).astype(bf16), "ctx", [(i, i + 1) for i in range(count - 1)]
-    )
-
+        (tail_k * tail_v).astype(bf16),
+        "ctx",
+        [(i, i + 1) for i in range(count - 1)],
+    )
+    own = [asked, kept, *beside, across]
     def store(blocks):
         return [
             pltpu.VMEM((heads, SQUAD * rows, 2 * HD), bf16),
@@ -374,7 +374,7 @@
 
     (far,) = kernel_call(
         far_kernel,
-        (place, *back, *near),
+        (*back, *near),
         [jax.ShapeDtypeStruct((width + TAG, (SQUAD - 1) * rows), bf16)],
         "far",
         store(SQUAD),
@@ -384,7 +384,7 @@
     far = climb(far, SQUAD)
     (main,) = kernel_call(
         main_kernel,
-        (place, *own, *near),
+        (*own, *near),
         [jax.ShapeDtypeStruct((width + TAG, SQUAD * rows), f32)],
         "main",
         store(2 * SQUAD),
@@ -393,7 +393,7 @@
     )
     done = kernel_call(
         merge_kernel,
-        (place, main, far),
+        (main, far),
         [jax.ShapeDtypeStruct((rows, width), bf16)] * SQUAD,
         "merge",
         [pltpu.VMEM((SQUAD, rows, width), bf16)],
@@ -409,7 +409,7 @@
     pieces += [turn(piece, r) for r in range(1, ranks) for piece in pieces]
     (attn_out,) = kernel_call(
         functools.partial(project_kernel, ranks),
-        (place, *pieces, out_weight),
+        (*pieces, out_weight),
         [jax.ShapeDtypeStruct((rows, out_weight.shape[1]), bf16)],
         "project",
         [pltpu.VMEM((rows, ranks * feat), bf16)],

time: 83 us -> 73.4 us (0.88)
  waiting for transfers between devices: 17.6 us -> 11.5 us
  Pallas kernels: 28.4 us -> 24.1 us
  starting transfers between devices: 34.2 us -> 35.8 us
    ppermute x4, waiting for transfers between devices: 8.4 us -> 1.33 us  [climb(): lax.ppermute(value, 'ctx', [(i, i + SQUAD) for i in range(first, count -...]
    pallas_call x5, Pallas kernels: 19.7 us -> 17.6 us  [the longest x4 14.5 us: kernel_call(): pl.pallas_call(kernel, in_specs=[VMEM] * len(args), out_specs=[VMEM] * le...]
    pallas_call x1, Pallas kernels: 8.67 us -> 6.57 us  [hyena(): pl.pallas_call(hyena_kernel, grid=(steps,), in_specs=[wide, wide, wide, p...]
    ppermute x6, starting transfers between devices: 10.2 us -> 12 us  [swap(): return lax.ppermute(value, 'ctx', [(i, i ^ mask) for i in range(count)])]
    ppermute x2, waiting for transfers between devices: 0.01 us -> 1.64 us  [descend(): lax.ppermute(value, 'ctx', [(i, i - SQUAD) for i in range(2 * SQUAD, coun...]
    ppermute x4, starting transfers between devices: 4.18 us -> 3.26 us  [turn(): lax.ppermute(value, 'tp', [(t, (t + r) % ranks) for t in range(ranks)])]
  transfers between devices with their start and end apart: 17 -> 17, of which waited for: 7 -> 8; matrix products, arithmetic and copies ran while one was open for 0% -> 0% of each run, Pallas kernels for 26% -> 24%
where the time goes in v1:
time: 73.4 us; the launch traced here: 72.7 us
  starting transfers between devices  35.8 us (49%)
  Pallas kernels  24.1 us (33%)
  waiting for transfers between devices  11.5 us (16%)
  between operations  0.94 us (1%)
    pallas_call x4, Pallas kernels, kernel_call(): pl.pallas_call(kernel, in_specs=[VMEM] * len(args), out_specs=[VMEM] * le...  14.5 us
    ppermute x4, starting transfers between devices, climb(): lax.ppermute(value, 'ctx', [(i, i + SQUAD) for i in range(first, count -...  13.1 us
    ppermute x6, starting transfers between devices, swap(): return lax.ppermute(value, 'ctx', [(i, i ^ mask) for i in range(count)])  12 us
    ppermute x6, waiting for transfers between devices, swap(): return lax.ppermute(value, 'ctx', [(i, i ^ mask) for i in range(count)])  7.26 us
    pallas_call x1, Pallas kernels, hyena(): pl.pallas_call(hyena_kernel, grid=(steps,), in_specs=[wide, wide, wide, p...  6.57 us
    ppermute x2, starting transfers between devices, descend(): lax.ppermute(value, 'ctx', [(i, i - SQUAD) for i in range(2 * SQUAD, coun...  4.16 us
    ppermute x4, starting transfers between devices, turn(): lax.ppermute(value, 'tp', [(t, (t + r) % ranks) for t in range(ranks)])  3.26 us
    ppermute x1, starting transfers between devices, local(): lax.ppermute((tail_k * tail_v).astype(bf16), 'ctx', [(i, i + 1) for i in...  3.25 us
  transfers between devices with their start and end apart: 17, of which 8 were waited for; matrix products, arithmetic and copies ran while one was open for 0% of the time, Pallas kernels for 24%

profile of v1, /device:TPU:17, one launch (start us, length us, event | category | flops | bytes accessed | tf_op | source)
XLA Modules:
  0.0 72.7 jit_solution(5585417326953566851)
XLA Ops:
  0.6 3.1 %deal.1 = (bf16[272,256]{1,0:T(8,128)(2,1)}, bf16[528,256]{1,0:T(8,128)(2,1)}, bf16[784,256]{1,0:T(8,128)(2,1)}, bf16[784,256]{1,0:T(8,128)(2,1)}, bf16[784,256]{1,0:T(8,128)(2,1)}) custom-call(bf16[256,1024]{1,0:T(8,128)(2,1)} %q_ref.2, bf16[256,1024]{1,0:T(8,128)(2,1)} %k_ref.2, bf16[256,1024]{1,0:T(8,128)(2,1)} %v_ref.2, s32[2,128]{1,0:T(2,128)} %bitcast.3), custom_call_target="tpu_custom_call" | custom-call | bytes 3145728 | tf_op jit(solution)/shard_map/deal/pallas_call | solution.py:158
  3.7 1.3 %collective-permute-start.1 = (bf16[784,256]{1,0:T(8,128)(2,1)}, bf16[784,256]{1,0:T(8,128)(2,1)S(1)}, u32[]{:S(2)}, u32[]{:S(2)}) collective-permute-start(bf16[784,256]{1,0:T(8,128)(2,1)} %get-tuple-element.25), channel_id=1, source_target_pairs={{0,2},{2,0},{4,6},{6,4},{8,10},{10,8},{12,14},{14,12},{16,18},{18,... | collective-permute-start | bytes 1204232 | tf_op jit(solution)/shard_map/ppermute | solution.py:337
  5.0 1.2 %collective-permute-start.2 = (bf16[784,256]{1,0:T(8,128)(2,1)}, bf16[784,256]{1,0:T(8,128)(2,1)S(1)}, u32[]{:S(2)}, u32[]{:S(2)}) collective-permute-start(bf16[784,256]{1,0:T(8,128)(2,1)} %get-tuple-element.27), channel_id=1, source_target_pairs={{0,4},{2,6},{4,0},{6,2},{8,12},{10,14},{12,8},{14,10},{16,20},{18,... | collective-permute-start | bytes 1204232 | tf_op jit(solution)/shard_map/ppermute | solution.py:337
  6.2 3.2 %collective-permute-start.3 = (bf16[528,256]{1,0:T(8,128)(2,1)}, bf16[528,256]{1,0:T(8,128)(2,1)S(1)}, u32[]{:S(2)}, u32[]{:S(2)}) collective-permute-start(bf16[528,256]{1,0:T(8,128)(2,1)} %get-tuple-element.23.refs_1_), channel_id=1, source_target_pairs={{0,8},{2,10},{4,12},{6,14},{8,16},{10,18},{12,20},{14,22},{16,24},... | collective-permute-start | bytes 811016 | tf_op jit(solution)/shard_map/ppermute | solution.py:340
  9.4 4.7 %collective-permute-done.1.refs_2_ = bf16[784,256]{1,0:T(8,128)(2,1)S(1)} collective-permute-done((bf16[784,256]{1,0:T(8,128)(2,1)}, bf16[784,256]{1,0:T(8,128)(2,1)S(1)}, u32[]{:S(2)}, u32[]{:S(2)}) %collective-permute-start.1) | collective-permute-done | bytes 401440 | tf_op jit(solution)/shard_map/ppermute | solution.py:337
  14.1 2.2 %collective-permute-start.4 = (bf16[784,256]{1,0:T(8,128)(2,1)}, bf16[784,256]{1,0:T(8,128)(2,1)S(1)}, u32[]{:S(2)}, u32[]{:S(2)}) collective-permute-start(bf16[784,256]{1,0:T(8,128)(2,1)} %get-tuple-element.29), channel_id=1, source_target_pairs={{0,6},{2,4},{4,2},{6,0},{8,14},{10,12},{12,10},{14,8},{16,22},{18,... | collective-permute-start | bytes 1204232 | tf_op jit(solution)/shard_map/ppermute | solution.py:337
  16.5 3.3 %collective-permute-start.5 = (bf16[1056,256]{1,0:T(8,128)(2,1)S(1)}, bf16[1056,256]{1,0:T(8,128)(2,1)S(1)}, u32[]{:S(2)}, u32[]{:S(2)}) collective-permute-start(bf16[1056,256]{1,0:T(8,128)(2,1)S(1)} %pad_maximum_fusion), channel_id=1, source_target_pairs={{0,8},{2,10},{4,12},{6,14},{8,16},{10,18},{12,20},{14,22},{16,24},... | collective-permute-start | bytes 1622024 | tf_op jit(solution)/shard_map/ppermute | solution.py:340
  19.9 2.1 %collective-permute-start.7 = (bf16[816,256]{1,0:T(8,128)(2,1)S(1)}, bf16[816,256]{1,0:T(8,128)(2,1)S(1)}, u32[]{:S(2)}, u32[]{:S(2)}) collective-permute-start(bf16[816,256]{1,0:T(8,128)(2,1)S(1)} %pad_maximum_fusion.1), channel_id=1, source_target_pairs={{16,8},{18,10},{20,12},{22,14},{24,16},{26,18},{28,20},{30,22},{17... | collective-permute-start | bytes 1253384 | tf_op jit(solution)/shard_map/ppermute | solution.py:343
  22.0 2.5 %collective-permute-done.4.refs_4_ = bf16[784,256]{1,0:T(8,128)(2,1)S(1)} collective-permute-done((bf16[784,256]{1,0:T(8,128)(2,1)}, bf16[784,256]{1,0:T(8,128)(2,1)S(1)}, u32[]{:S(2)}, u32[]{:S(2)}) %collective-permute-start.4) | collective-permute-done | bytes 401440 | tf_op jit(solution)/shard_map/ppermute | solution.py:337
  24.5 3.2 %collective-permute-start.6 = (bf16[528,256]{1,0:T(8,128)(2,1)S(1)}, bf16[528,256]{1,0:T(8,128)(2,1)S(1)}, u32[]{:S(2)}, u32[]{:S(2)}) collective-permute-start(bf16[528,256]{1,0:T(8,128)(2,1)S(1)} %slice.32), channel_id=1, source_target_pairs={{0,8},{2,10},{4,12},{6,14},{8,16},{10,18},{12,20},{14,22},{16,24},... | collective-permute-start | bytes 811016 | tf_op jit(solution)/shard_map/ppermute | solution.py:340
  27.7 2.1 %collective-permute-start.8 = (bf16[272,256]{1,0:T(8,128)(2,1)S(1)}, bf16[272,256]{1,0:T(8,128)(2,1)S(1)}, u32[]{:S(2)}, u32[]{:S(2)}) collective-permute-start(bf16[272,256]{1,0:T(8,128)(2,1)S(1)} %slice.33), channel_id=1, source_target_pairs={{16,8},{18,10},{20,12},{22,14},{24,16},{26,18},{28,20},{30,22},{17... | collective-permute-start | bytes 417800 | tf_op jit(solution)/shard_map/ppermute | solution.py:343
  30.0 3.3 %collective-permute-start = (bf16[128,2048]{1,0:T(8,128)(2,1)S(1)}, bf16[128,2048]{1,0:T(8,128)(2,1)S(1)}, u32[]{:S(2)}, u32[]{:S(2)}) collective-permute-start(bf16[128,2048]{1,0:T(8,128)(2,1)S(1)} %multiply_convert_fusion), channel_id=1, source_target_pairs={{0,2},{2,4},{4,6},{6,8},{8,10},{10,12},{12,14},{14,16},{16,18},{18... | collective-permute-start | bytes 1572872 | tf_op jit(solution)/shard_map/ppermute | solution.py:362
  33.3 1.6 %collective-permute-done.8.refs_1_ = bf16[272,256]{1,0:T(8,128)(2,1)S(1)} collective-permute-done((bf16[272,256]{1,0:T(8,128)(2,1)S(1)}, bf16[272,256]{1,0:T(8,128)(2,1)S(1)}, u32[]{:S(2)}, u32[]{:S(2)}) %collective-permute-start.8) | collective-permute-done | bytes 139296 | tf_op jit(solution)/shard_map/ppermute | solution.py:343
  34.9 1.3 %collective-permute-done.6.refs_7_.refs_4_ = bf16[528,256]{1,0:T(8,128)(2,1)S(1)} collective-permute-done((bf16[528,256]{1,0:T(8,128)(2,1)S(1)}, bf16[528,256]{1,0:T(8,128)(2,1)S(1)}, u32[]{:S(2)}, u32[]{:S(2)}) %collective-permute-start.6) | collective-permute-done | bytes 270368 | tf_op jit(solution)/shard_map/ppermute | solution.py:340
  36.2 2.6 %far.1 = bf16[272,768]{1,0:T(8,128)(2,1)S(1)} custom-call(bf16[816,256]{1,0:T(8,128)(2,1)S(1)} %collective-permute-done.7.refs_0_, bf16[272,256]{1,0:T(8,128)(2,1)S(1)} %collective-permute-done.8.refs_1_, bf16[528,256]{1,0:T(8,128)(2,1)S(1)} %collective-permute-done.3.refs_5_.refs_2_, bf16[1056,256]{1,0:T(8,128)(2,1)S(1)} %collective-permute-done.5.refs_6_.refs_3_, ...), custom_call_target="tpu_custom_call" | custom-call | flops 402653184 | bytes 2056192 | tf_op jit(solution)/shard_map/far/pallas_call | solution.py:27
  38.9 3.4 %collective-permute-start.9 = (bf16[272,768]{1,0:T(8,128)(2,1)S(1)}, bf16[272,768]{1,0:T(8,128)(2,1)S(1)}, u32[]{:S(2)}, u32[]{:S(2)}) collective-permute-start(bf16[272,768]{1,0:T(8,128)(2,1)S(1)} %far.1), channel_id=1, source_target_pairs={{8,16},{10,18},{12,20},{14,22},{16,24},{18,26},{20,28},{22,30},{9,... | collective-permute-start | bytes 1253384 | tf_op jit(solution)/shard_map/ppermute | solution.py:340
  42.3 8.0 %main.1.main_ref = f32[272,1024]{1,0:T(8,128)S(1)} custom-call(bf16[272,256]{1,0:T(8,128)(2,1)S(1)} %copy-done.2, bf16[528,256]{1,0:T(8,128)(2,1)S(1)} %copy-done.4, bf16[784,256]{1,0:T(8,128)(2,1)S(1)} %collective-permute-done.1.refs_2_, bf16[784,256]{1,0:T(8,128)(2,1)S(1)} %collective-permute-done.2.refs_3_, ...), custom_call_target="tpu_custom_call" | custom-call | flops 1744830464 | bytes 3809280 | tf_op jit(solution)/shard_map/main/pallas_call | solution.py:27
  51.1 7.0 %collective-permute-start.11 = (bf16[256,256]{1,0:T(8,128)(2,1)S(1)}, bf16[256,256]{1,0:T(8,128)(2,1)S(1)}, u32[]{:S(2)}, u32[]{:S(2)}) collective-permute-start(bf16[256,256]{1,0:T(8,128)(2,1)S(1)} %get-tuple-element.35), channel_id=1, source_target_pairs={{0,4},{2,6},{4,0},{6,2},{8,12},{10,14},{12,8},{14,10},{16,20},{18,... | collective-permute-start | bytes 393224 | tf_op jit(solution)/shard_map/ppermute | solution.py:337
  58.1 6.6 %hyena.1 = bf16[256,2048]{1,0:T(8,128)(2,1)} custom-call(bf16[256,2048]{1,0:T(8,128)(2,1)S(1)} %copy-done.3, bf16[256,2048]{1,0:T(8,128)(2,1)S(1)} %copy-done, bf16[256,2048]{1,0:T(8,128)(2,1)S(1)} %copy-done.1, bf16[128,2048]{1,0:T(8,128)(2,1)S(1)} %collective-permute-done.rim_ref, bf16[128,128]{1,0:T(8,128)(2,1)S(1)} %copy-done.5, ...), custom_call_target="tpu_custom_call" | custom-call | flops 4294967296 | bytes 5242880 | tf_op jit(solution)/shard_map/hyena/pallas_call | solution.py:86
  64.7 2.7 %collective-permute-start.13 = (bf16[256,256]{1,0:T(8,128)(2,1)S(1)}, bf16[256,256]{1,0:T(8,128)(2,1)S(1)}, u32[]{:S(2)}, u32[]{:S(2)}) collective-permute-start(bf16[256,256]{1,0:T(8,128)(2,1)S(1)} %get-tuple-element.38.refs_0_), channel_id=1, source_target_pairs={{0,1},{1,0},{2,3},{3,2},{4,5},{5,4},{6,7},{7,6},{8,9},{9,8},{10,11... | collective-permute-start | bytes 393224 | tf_op jit(solution)/shard_map/ppermute | solution.py:405
  67.4 0.4 collective-permute-start.15
  67.9 0.4 collective-permute-done.13.refs_4_
  68.3 0.4 collective-permute-done.14.refs_5_
  69.2 3.5 %project.1 = bf16[256,2048]{1,0:T(8,128)(2,1)} custom-call(bf16[256,256]{1,0:T(8,128)(2,1)S(1)} %get-tuple-element.38.refs_0_, bf16[256,256]{1,0:T(8,128)(2,1)S(1)} %collective-permute-done.10.refs_1_, bf16[256,256]{1,0:T(8,128)(2,1)S(1)} %collective-permute-done.11.refs_2_, bf16[256,256]{1,0:T(8,128)(2,1)S(1)} %collective-permute-done.12.refs_3_, ...), custom_call_target="tpu_custom_call" | custom-call | flops 2147483648 | bytes 10485760 | tf_op jit(solution)/shard_map/project/pallas_call | solution.py:27
  (45 shorter events, 1.7 us)
Async XLA Ops:
  3.7 10.4 %collective-permute-start.1 = (bf16[784,256]{1,0:T(8,128)(2,1)}, bf16[784,256]{1,0:T(8,128)(2,1)S(1)}, u32[]{:S(2)}, u32[]{:S(2)}) collective-permute-start(bf16[784,256]{1,0:T(8,128)(2,1)} %get-tuple-element.25), channel_id=1, source_target_pairs={{0,2},{2,0},{4,6},{6,4},{8,10},{10,8},{12,14},{14,12},{16,18},{18,... | collective-permute-start | bytes 1204232 | tf_op jit(solution)/shard_map/ppermute | solution.py:337
  5.0 11.3 %collective-permute-start.2 = (bf16[784,256]{1,0:T(8,128)(2,1)}, bf16[784,256]{1,0:T(8,128)(2,1)S(1)}, u32[]{:S(2)}, u32[]{:S(2)}) collective-permute-start(bf16[784,256]{1,0:T(8,128)(2,1)} %get-tuple-element.27), channel_id=1, source_target_pairs={{0,4},{2,6},{4,0},{6,2},{8,12},{10,14},{12,8},{14,10},{16,20},{18,... | collective-permute-start | bytes 1204232 | tf_op jit(solution)/shard_map/ppermute | solution.py:337
  6.2 10.1 %collective-permute-start.3 = (bf16[528,256]{1,0:T(8,128)(2,1)}, bf16[528,256]{1,0:T(8,128)(2,1)S(1)}, u32[]{:S(2)}, u32[]{:S(2)}) collective-permute-start(bf16[528,256]{1,0:T(8,128)(2,1)} %get-tuple-element.23.refs_1_), channel_id=1, source_target_pairs={{0,8},{2,10},{4,12},{6,14},{8,16},{10,18},{12,20},{14,22},{16,24},... | collective-permute-start | bytes 811016 | tf_op jit(solution)/shard_map/ppermute | solution.py:340
  14.1 10.3 %collective-permute-start.4 = (bf16[784,256]{1,0:T(8,128)(2,1)}, bf16[784,256]{1,0:T(8,128)(2,1)S(1)}, u32[]{:S(2)}, u32[]{:S(2)}) collective-permute-start(bf16[784,256]{1,0:T(8,128)(2,1)} %get-tuple-element.29), channel_id=1, source_target_pairs={{0,6},{2,4},{4,2},{6,0},{8,14},{10,12},{12,10},{14,8},{16,22},{18,... | collective-permute-start | bytes 1204232 | tf_op jit(solution)/shard_map/ppermute | solution.py:337
  16.4 13.4 %copy-start.1 = (bf16[256,2048]{1,0:T(8,128)(2,1)S(1)}, bf16[256,2048]{1,0:T(8,128)(2,1)}, u32[]{:S(2)}) copy-start(bf16[256,2048]{1,0:T(8,128)(2,1)} %v_ref.3) | copy-start | bytes 3145732
  16.5 13.4 %copy-start = (bf16[256,2048]{1,0:T(8,128)(2,1)S(1)}, bf16[256,2048]{1,0:T(8,128)(2,1)}, u32[]{:S(2)}) copy-start(bf16[256,2048]{1,0:T(8,128)(2,1)} %k_ref.3) | copy-start | bytes 3145732
  16.5 16.8 %collective-permute-start.5 = (bf16[1056,256]{1,0:T(8,128)(2,1)S(1)}, bf16[1056,256]{1,0:T(8,128)(2,1)S(1)}, u32[]{:S(2)}, u32[]{:S(2)}) collective-permute-start(bf16[1056,256]{1,0:T(8,128)(2,1)S(1)} %pad_maximum_fusion), channel_id=1, source_target_pairs={{0,8},{2,10},{4,12},{6,14},{8,16},{10,18},{12,20},{14,22},{16,24},... | collective-permute-start | bytes 1622024 | tf_op jit(solution)/shard_map/ppermute | solution.py:340
  19.9 13.4 %collective-permute-start.7 = (bf16[816,256]{1,0:T(8,128)(2,1)S(1)}, bf16[816,256]{1,0:T(8,128)(2,1)S(1)}, u32[]{:S(2)}, u32[]{:S(2)}) collective-permute-start(bf16[816,256]{1,0:T(8,128)(2,1)S(1)} %pad_maximum_fusion.1), channel_id=1, source_target_pairs={{16,8},{18,10},{20,12},{22,14},{24,16},{26,18},{28,20},{30,22},{17... | collective-permute-start | bytes 1253384 | tf_op jit(solution)/shard_map/ppermute | solution.py:343
  24.5 11.7 %collective-permute-start.6 = (bf16[528,256]{1,0:T(8,128)(2,1)S(1)}, bf16[528,256]{1,0:T(8,128)(2,1)S(1)}, u32[]{:S(2)}, u32[]{:S(2)}) collective-permute-start(bf16[528,256]{1,0:T(8,128)(2,1)S(1)} %slice.32), channel_id=1, source_target_pairs={{0,8},{2,10},{4,12},{6,14},{8,16},{10,18},{12,20},{14,22},{16,24},... | collective-permute-start | bytes 811016 | tf_op jit(solution)/shard_map/ppermute | solution.py:340
  27.7 7.2 %collective-permute-start.8 = (bf16[272,256]{1,0:T(8,128)(2,1)S(1)}, bf16[272,256]{1,0:T(8,128)(2,1)S(1)}, u32[]{:S(2)}, u32[]{:S(2)}) collective-permute-start(bf16[272,256]{1,0:T(8,128)(2,1)S(1)} %slice.33), channel_id=1, source_target_pairs={{16,8},{18,10},{20,12},{22,14},{24,16},{26,18},{28,20},{30,22},{17... | collective-permute-start | bytes 417800 | tf_op jit(solution)/shard_map/ppermute | solution.py:343
  30.0 12.3 %copy-start.6 = (bf16[2048]{0:T(1024)(128)(2,1)S(1)}, bf16[2048]{0:T(1024)(128)(2,1)}, u32[]{:S(2)}) copy-start(bf16[2048]{0:T(1024)(128)(2,1)} %param.14) | copy-start | bytes 12292
  30.0 12.3 %copy-start.4 = (bf16[528,256]{1,0:T(8,128)(2,1)S(1)}, bf16[528,256]{1,0:T(8,128)(2,1)}, u32[]{:S(2)}) copy-start(bf16[528,256]{1,0:T(8,128)(2,1)} %get-tuple-element.23.refs_1_) | copy-start | bytes 811012
  30.0 20.8 %collective-permute-start = (bf16[128,2048]{1,0:T(8,128)(2,1)S(1)}, bf16[128,2048]{1,0:T(8,128)(2,1)S(1)}, u32[]{:S(2)}, u32[]{:S(2)}) collective-permute-start(bf16[128,2048]{1,0:T(8,128)(2,1)S(1)} %multiply_convert_fusion), channel_id=1, source_target_pairs={{0,2},{2,4},{4,6},{6,8},{8,10},{10,12},{12,14},{14,16},{16,18},{18... | collective-permute-start | bytes 1572872 | tf_op jit(solution)/shard_map/ppermute | solution.py:362
  38.9 11.5 %collective-permute-start.9 = (bf16[272,768]{1,0:T(8,128)(2,1)S(1)}, bf16[272,768]{1,0:T(8,128)(2,1)S(1)}, u32[]{:S(2)}, u32[]{:S(2)}) collective-permute-start(bf16[272,768]{1,0:T(8,128)(2,1)S(1)} %far.1), channel_id=1, source_target_pairs={{8,16},{10,18},{12,20},{14,22},{16,24},{18,26},{20,28},{22,30},{9,... | collective-permute-start | bytes 1253384 | tf_op jit(solution)/shard_map/ppermute | solution.py:340
  50.4 7.7 %copy-start.3 = (bf16[256,2048]{1,0:T(8,128)(2,1)S(1)}, bf16[256,2048]{1,0:T(8,128)(2,1)}, u32[]{:S(2)}) copy-start(bf16[256,2048]{1,0:T(8,128)(2,1)} %q_ref.3) | copy-start | bytes 3145732
  50.8 13.9 %collective-permute-start.10 = (bf16[256,256]{1,0:T(8,128)(2,1)S(1)}, bf16[256,256]{1,0:T(8,128)(2,1)S(1)}, u32[]{:S(2)}, u32[]{:S(2)}) collective-permute-start(bf16[256,256]{1,0:T(8,128)(2,1)S(1)} %get-tuple-element.34), channel_id=1, source_target_pairs={{0,2},{2,0},{4,6},{6,4},{8,10},{10,8},{12,14},{14,12},{16,18},{18,... | collective-permute-start | bytes 393224 | tf_op jit(solution)/shard_map/ppermute | solution.py:337
  51.1 13.6 %collective-permute-start.11 = (bf16[256,256]{1,0:T(8,128)(2,1)S(1)}, bf16[256,256]{1,0:T(8,128)(2,1)S(1)}, u32[]{:S(2)}, u32[]{:S(2)}) collective-permute-start(bf16[256,256]{1,0:T(8,128)(2,1)S(1)} %get-tuple-element.35), channel_id=1, source_target_pairs={{0,4},{2,6},{4,0},{6,2},{8,12},{10,14},{12,8},{14,10},{16,20},{18,... | collective-permute-start | bytes 393224 | tf_op jit(solution)/shard_map/ppermute | solution.py:337
  58.0 11.1 %slice-start = ((s8[8388608]{0:T(1024)(128)(4,1)}), s8[4194304]{0:T(1024)(128)(4,1)S(1)}, s32[]{:S(2)}) async-start(s8[8388608]{0:T(1024)(128)(4,1)} %bitcast.1), calls=%async_computation | async-start | bytes 8388608
  58.0 11.1 %slice-start.1 = ((s8[8388608]{0:T(1024)(128)(4,1)}), s8[4194304]{0:T(1024)(128)(4,1)S(1)}, s32[]{:S(2)}) async-start(s8[8388608]{0:T(1024)(128)(4,1)} %bitcast.1), calls=%async_computation.1 | async-start | bytes 8388608
  58.1 6.6 %collective-permute-start.12 = (bf16[256,256]{1,0:T(8,128)(2,1)S(1)}, bf16[256,256]{1,0:T(8,128)(2,1)S(1)}, u32[]{:S(2)}, u32[]{:S(2)}) collective-permute-start(bf16[256,256]{1,0:T(8,128)(2,1)S(1)} %get-tuple-element.36), channel_id=1, source_target_pairs={{0,6},{2,4},{4,2},{6,0},{8,14},{10,12},{12,10},{14,8},{16,22},{18,... | collective-permute-start | bytes 393224 | tf_op jit(solution)/shard_map/ppermute | solution.py:337
  64.7 3.7 %collective-permute-start.13 = (bf16[256,256]{1,0:T(8,128)(2,1)S(1)}, bf16[256,256]{1,0:T(8,128)(2,1)S(1)}, u32[]{:S(2)}, u32[]{:S(2)}) collective-permute-start(bf16[256,256]{1,0:T(8,128)(2,1)S(1)} %get-tuple-element.38.refs_0_), channel_id=1, source_target_pairs={{0,1},{1,0},{2,3},{3,2},{4,5},{5,4},{6,7},{7,6},{8,9},{9,8},{10,11... | collective-permute-start | bytes 393224 | tf_op jit(solution)/shard_map/ppermute | solution.py:405
  67.3 1.3 %collective-permute-start.14 = (bf16[256,256]{1,0:T(8,128)(2,1)S(1)}, bf16[256,256]{1,0:T(8,128)(2,1)S(1)}, u32[]{:S(2)}, u32[]{:S(2)}) collective-permute-start(bf16[256,256]{1,0:T(8,128)(2,1)S(1)} %collective-permute-done.10.refs_1_), channel_id=1, source_target_pairs={{0,1},{1,0},{2,3},{3,2},{4,5},{5,4},{6,7},{7,6},{8,9},{9,8},{10,11... | collective-permute-start | bytes 393224 | tf_op jit(solution)/shard_map/ppermute | solution.py:405
  67.4 1.5 %collective-permute-start.15 = (bf16[256,256]{1,0:T(8,128)(2,1)S(1)}, bf16[256,256]{1,0:T(8,128)(2,1)S(1)}, u32[]{:S(2)}, u32[]{:S(2)}) collective-permute-start(bf16[256,256]{1,0:T(8,128)(2,1)S(1)} %collective-permute-done.11.refs_2_), channel_id=1, source_target_pairs={{0,1},{1,0},{2,3},{3,2},{4,5},{5,4},{6,7},{7,6},{8,9},{9,8},{10,11... | collective-permute-start | bytes 393224 | tf_op jit(solution)/shard_map/ppermute | solution.py:405
  67.8 1.3 %collective-permute-start.16 = (bf16[256,256]{1,0:T(8,128)(2,1)S(1)}, bf16[256,256]{1,0:T(8,128)(2,1)S(1)}, u32[]{:S(2)}, u32[]{:S(2)}) collective-permute-start(bf16[256,256]{1,0:T(8,128)(2,1)S(1)} %collective-permute-done.12.refs_3_), channel_id=1, source_target_pairs={{0,1},{1,0},{2,3},{3,2},{4,5},{5,4},{6,7},{7,6},{8,9},{9,8},{10,11... | collective-permute-start | bytes 393224 | tf_op jit(solution)/shard_map/ppermute | solution.py:405
  (2 other events, 11.2 us)

commit v2 on v1

--- a/solution.py
+++ b/solution.py
@@ -57,16 +57,20 @@
         stacked = jnp.concatenate(
             [full[w * LANES : (w + 2) * LANES] for w in range(windows)], axis=1
         )
-        conv = jnp.zeros((LANES, windows * LANES), jnp.float32)
+        tables = []
         for g in range(per_tile):
             at = tile * per_tile + g
             row = taps[at : at + 1]
             ring = pltpu.roll(
                 jnp.broadcast_to(row, shape), 0, 1, stride=1, stride_axis=0
             ).astype(jnp.bfloat16)
-            table = jnp.concatenate([ring * before, ring * within], axis=1)
-            part = jnp.dot(table, stacked, preferred_element_type=jnp.float32)
-            conv = jnp.where(lane_group == g, part, conv)
+            tables.append(jnp.concatenate([ring * before, ring * within], axis=1))
+        parts = jnp.dot(
+            jnp.concatenate(tables, axis=0), stacked, preferred_element_type=jnp.float32
+        )
+        conv = parts[:LANES]
+        for g in range(1, per_tile):
+            conv = jnp.where(lane_group == g, parts[g * LANES : (g + 1) * LANES], conv)
         conv = jnp.concatenate(
             [conv[:, w * LANES : (w + 1) * LANES] for w in range(windows)], axis=0
         )
@@ -382,6 +386,7 @@
         exps=6 * rows * rows * heads,
     )
     far = climb(far, SQUAD)
+    own[1], rim = lax.optimization_barrier((own[1], rim))
     (main,) = kernel_call(
         main_kernel,
         (*own, *near),

time: 73.4 us -> 76.1 us (1.037)
  waiting for transfers between devices: 11.5 us -> 18.3 us
  starting transfers between devices: 35.8 us -> 32.1 us
    ppermute x1, waiting for transfers between devices: 0.01 us -> 5.78 us  [local(): lax.ppermute((tail_k * tail_v).astype(bf16), 'ctx', [(i, i + 1) for i in...]
    ppermute x6, starting transfers between devices: 12 us -> 7.39 us  [swap(): return lax.ppermute(value, 'ctx', [(i, i ^ mask) for i in range(count)])]
    ppermute x2, waiting for transfers between devices: 1.64 us -> 3.99 us  [descend(): lax.ppermute(value, 'ctx', [(i, i - SQUAD) for i in range(2 * SQUAD, coun...]
    ppermute x4, starting transfers between devices: 3.26 us -> 5.2 us  [turn(): lax.ppermute(value, 'tp', [(t, (t + r) % ranks) for t in range(ranks)])]
    ppermute x4, waiting for transfers between devices: 1.33 us -> 0.01 us  [climb(): lax.ppermute(value, 'ctx', [(i, i + SQUAD) for i in range(first, count -...]
    ppermute x4, starting transfers between devices: 13.1 us -> 12.1 us  [climb(): lax.ppermute(value, 'ctx', [(i, i + SQUAD) for i in range(first, count -...]
  transfers between devices with their start and end apart: 17 -> 17, of which waited for: 8 -> 8; matrix products, arithmetic and copies ran while one was open for 0% -> 0% of each run, Pallas kernels for 24% -> 23%
where the time goes in v2:
time: 76.1 us; the launch traced here: 75.7 us
  starting transfers between devices  32.1 us (42%)
  Pallas kernels  24.1 us (32%)
  waiting for transfers between devices  18.3 us (24%)
  between operations  0.93 us (1%)
    pallas_call x4, Pallas kernels, kernel_call(): pl.pallas_call(kernel, in_specs=[VMEM] * len(args), out_specs=[VMEM] * le...  14.5 us
    ppermute x4, starting transfers between devices, climb(): lax.ppermute(value, 'ctx', [(i, i + SQUAD) for i in range(first, count -...  12.1 us
    ppermute x6, starting transfers between devices, swap(): return lax.ppermute(value, 'ctx', [(i, i ^ mask) for i in range(count)])  7.39 us
    ppermute x6, waiting for transfers between devices, swap(): return lax.ppermute(value, 'ctx', [(i, i ^ mask) for i in range(count)])  7.26 us
    pallas_call x1, Pallas kernels, hyena(): pl.pallas_call(hyena_kernel, grid=(steps,), in_specs=[wide, wide, wide, p...  6.51 us
    ppermute x1, waiting for transfers between devices, local(): lax.ppermute((tail_k * tail_v).astype(bf16), 'ctx', [(i, i + 1) for i in...  5.78 us
    ppermute x4, starting transfers between devices, turn(): lax.ppermute(value, 'tp', [(t, (t + r) % ranks) for t in range(ranks)])  5.2 us
    ppermute x2, starting transfers between devices, descend(): lax.ppermute(value, 'ctx', [(i, i - SQUAD) for i in range(2 * SQUAD, coun...  4.29 us
  transfers between devices with their start and end apart: 17, of which 8 were waited for; matrix products, arithmetic and copies ran while one was open for 0% of the time, Pallas kernels for 23%

profile of v2, /device:TPU:17, one launch (start us, length us, event | category | flops | bytes accessed | tf_op | source)
XLA Modules:
  0.0 75.7 jit_solution(383941483216013508)
XLA Ops:
  0.6 3.1 %deal.1 = (bf16[272,256]{1,0:T(8,128)(2,1)}, bf16[528,256]{1,0:T(8,128)(2,1)}, bf16[784,256]{1,0:T(8,128)(2,1)}, bf16[784,256]{1,0:T(8,128)(2,1)}, bf16[784,256]{1,0:T(8,128)(2,1)}) custom-call(bf16[256,1024]{1,0:T(8,128)(2,1)} %q_ref.2, bf16[256,1024]{1,0:T(8,128)(2,1)} %k_ref.2, bf16[256,1024]{1,0:T(8,128)(2,1)} %v_ref.2, s32[2,128]{1,0:T(2,128)} %bitcast.3), custom_call_target="tpu_custom_call" | custom-call | bytes 3145728 | tf_op jit(solution)/shard_map/deal/pallas_call | solution.py:162
  3.7 1.3 %collective-permute-start.1 = (bf16[784,256]{1,0:T(8,128)(2,1)}, bf16[784,256]{1,0:T(8,128)(2,1)S(1)}, u32[]{:S(2)}, u32[]{:S(2)}) collective-permute-start(bf16[784,256]{1,0:T(8,128)(2,1)} %get-tuple-element.29), channel_id=1, source_target_pairs={{0,2},{2,0},{4,6},{6,4},{8,10},{10,8},{12,14},{14,12},{16,18},{18,... | collective-permute-start | bytes 1204232 | tf_op jit(solution)/shard_map/ppermute | solution.py:341
  5.0 1.2 %collective-permute-start.2 = (bf16[784,256]{1,0:T(8,128)(2,1)}, bf16[784,256]{1,0:T(8,128)(2,1)S(1)}, u32[]{:S(2)}, u32[]{:S(2)}) collective-permute-start(bf16[784,256]{1,0:T(8,128)(2,1)} %get-tuple-element.31), channel_id=1, source_target_pairs={{0,4},{2,6},{4,0},{6,2},{8,12},{10,14},{12,8},{14,10},{16,20},{18,... | collective-permute-start | bytes 1204232 | tf_op jit(solution)/shard_map/ppermute | solution.py:341
  6.2 3.2 %collective-permute-start.3 = (bf16[528,256]{1,0:T(8,128)(2,1)}, bf16[528,256]{1,0:T(8,128)(2,1)S(1)}, u32[]{:S(2)}, u32[]{:S(2)}) collective-permute-start(bf16[528,256]{1,0:T(8,128)(2,1)} %get-tuple-element.27.refs_1_), channel_id=1, source_target_pairs={{0,8},{2,10},{4,12},{6,14},{8,16},{10,18},{12,20},{14,22},{16,24},... | collective-permute-start | bytes 811016 | tf_op jit(solution)/shard_map/ppermute | solution.py:344
  9.4 4.7 %collective-permute-done.1.refs_2_ = bf16[784,256]{1,0:T(8,128)(2,1)S(1)} collective-permute-done((bf16[784,256]{1,0:T(8,128)(2,1)}, bf16[784,256]{1,0:T(8,128)(2,1)S(1)}, u32[]{:S(2)}, u32[]{:S(2)}) %collective-permute-start.1) | collective-permute-done | bytes 401440 | tf_op jit(solution)/shard_map/ppermute | solution.py:341
  14.1 2.2 %collective-permute-start.4 = (bf16[784,256]{1,0:T(8,128)(2,1)}, bf16[784,256]{1,0:T(8,128)(2,1)S(1)}, u32[]{:S(2)}, u32[]{:S(2)}) collective-permute-start(bf16[784,256]{1,0:T(8,128)(2,1)} %get-tuple-element.33), channel_id=1, source_target_pairs={{0,6},{2,4},{4,2},{6,0},{8,14},{10,12},{12,10},{14,8},{16,22},{18,... | collective-permute-start | bytes 1204232 | tf_op jit(solution)/shard_map/ppermute | solution.py:341
  16.5 3.3 %collective-permute-start.5 = (bf16[1056,256]{1,0:T(8,128)(2,1)S(1)}, bf16[1056,256]{1,0:T(8,128)(2,1)S(1)}, u32[]{:S(2)}, u32[]{:S(2)}) collective-permute-start(bf16[1056,256]{1,0:T(8,128)(2,1)S(1)} %pad_maximum_fusion), channel_id=1, source_target_pairs={{0,8},{2,10},{4,12},{6,14},{8,16},{10,18},{12,20},{14,22},{16,24},... | collective-permute-start | bytes 1622024 | tf_op jit(solution)/shard_map/ppermute | solution.py:344
  19.9 2.1 %collective-permute-start.7 = (bf16[816,256]{1,0:T(8,128)(2,1)S(1)}, bf16[816,256]{1,0:T(8,128)(2,1)S(1)}, u32[]{:S(2)}, u32[]{:S(2)}) collective-permute-start(bf16[816,256]{1,0:T(8,128)(2,1)S(1)} %pad_maximum_fusion.1), channel_id=1, source_target_pairs={{16,8},{18,10},{20,12},{22,14},{24,16},{26,18},{28,20},{30,22},{17... | collective-permute-start | bytes 1253384 | tf_op jit(solution)/shard_map/ppermute | solution.py:347
  22.0 2.5 %collective-permute-done.4.refs_4_ = bf16[784,256]{1,0:T(8,128)(2,1)S(1)} collective-permute-done((bf16[784,256]{1,0:T(8,128)(2,1)}, bf16[784,256]{1,0:T(8,128)(2,1)S(1)}, u32[]{:S(2)}, u32[]{:S(2)}) %collective-permute-start.4) | collective-permute-done | bytes 401440 | tf_op jit(solution)/shard_map/ppermute | solution.py:341
  24.5 3.2 %collective-permute-start.6 = (bf16[528,256]{1,0:T(8,128)(2,1)S(1)}, bf16[528,256]{1,0:T(8,128)(2,1)S(1)}, u32[]{:S(2)}, u32[]{:S(2)}) collective-permute-start(bf16[528,256]{1,0:T(8,128)(2,1)S(1)} %slice.32), channel_id=1, source_target_pairs={{0,8},{2,10},{4,12},{6,14},{8,16},{10,18},{12,20},{14,22},{16,24},... | collective-permute-start | bytes 811016 | tf_op jit(solution)/shard_map/ppermute | solution.py:344
  27.9 3.1 %collective-permute-start = (bf16[128,2048]{1,0:T(8,128)(2,1)S(1)}, bf16[128,2048]{1,0:T(8,128)(2,1)S(1)}, u32[]{:S(2)}, u32[]{:S(2)}) collective-permute-start(bf16[128,2048]{1,0:T(8,128)(2,1)S(1)} %multiply_convert_fusion), channel_id=1, source_target_pairs={{0,2},{2,4},{4,6},{6,8},{8,10},{10,12},{12,14},{14,16},{16,18},{18... | collective-permute-start | bytes 1572872 | tf_op jit(solution)/shard_map/ppermute | solution.py:366
  31.0 2.2 %collective-permute-start.8 = (bf16[272,256]{1,0:T(8,128)(2,1)S(1)}, bf16[272,256]{1,0:T(8,128)(2,1)S(1)}, u32[]{:S(2)}, u32[]{:S(2)}) collective-permute-start(bf16[272,256]{1,0:T(8,128)(2,1)S(1)} %slice.33), channel_id=1, source_target_pairs={{16,8},{18,10},{20,12},{22,14},{24,16},{26,18},{28,20},{30,22},{17... | collective-permute-start | bytes 417800 | tf_op jit(solution)/shard_map/ppermute | solution.py:347
  33.3 4.0 %collective-permute-done.8.refs_1_ = bf16[272,256]{1,0:T(8,128)(2,1)S(1)} collective-permute-done((bf16[272,256]{1,0:T(8,128)(2,1)S(1)}, bf16[272,256]{1,0:T(8,128)(2,1)S(1)}, u32[]{:S(2)}, u32[]{:S(2)}) %collective-permute-start.8) | collective-permute-done | bytes 139296 | tf_op jit(solution)/shard_map/ppermute | solution.py:347
  37.3 2.6 %far.1 = bf16[272,768]{1,0:T(8,128)(2,1)S(1)} custom-call(bf16[816,256]{1,0:T(8,128)(2,1)S(1)} %collective-permute-done.7.refs_0_, bf16[272,256]{1,0:T(8,128)(2,1)S(1)} %collective-permute-done.8.refs_1_, bf16[528,256]{1,0:T(8,128)(2,1)S(1)} %collective-permute-done.3.refs_5_.refs_2_, bf16[1056,256]{1,0:T(8,128)(2,1)S(1)} %collective-permute-done.5.refs_6_.refs_3_, ...), custom_call_target="tpu_custom_call" | custom-call | flops 402653184 | bytes 2056192 | tf_op jit(solution)/shard_map/far/pallas_call | solution.py:27
  39.9 2.4 %collective-permute-start.9 = (bf16[272,768]{1,0:T(8,128)(2,1)S(1)}, bf16[272,768]{1,0:T(8,128)(2,1)S(1)}, u32[]{:S(2)}, u32[]{:S(2)}) collective-permute-start(bf16[272,768]{1,0:T(8,128)(2,1)S(1)} %far.1), channel_id=1, source_target_pairs={{8,16},{10,18},{12,20},{14,22},{16,24},{18,26},{20,28},{22,30},{9,... | collective-permute-start | bytes 1253384 | tf_op jit(solution)/shard_map/ppermute | solution.py:344
  42.3 5.8 %collective-permute-done.rim_ref = bf16[128,2048]{1,0:T(8,128)(2,1)S(1)} collective-permute-done((bf16[128,2048]{1,0:T(8,128)(2,1)S(1)}, bf16[128,2048]{1,0:T(8,128)(2,1)S(1)}, u32[]{:S(2)}, u32[]{:S(2)}) %collective-permute-start) | collective-permute-done | bytes 524320 | tf_op jit(solution)/shard_map/ppermute | solution.py:366
  48.1 8.0 %main.1.main_ref = f32[272,1024]{1,0:T(8,128)S(1)} custom-call(bf16[272,256]{1,0:T(8,128)(2,1)S(1)} %copy-done.2, bf16[528,256]{1,0:T(8,128)(2,1)S(1)} %copy-done.4, bf16[784,256]{1,0:T(8,128)(2,1)S(1)} %collective-permute-done.1.refs_2_, bf16[784,256]{1,0:T(8,128)(2,1)S(1)} %collective-permute-done.2.refs_3_, ...), custom_call_target="tpu_custom_call" | custom-call | flops 1744830464 | bytes 3809280 | tf_op jit(solution)/shard_map/main/pallas_call | solution.py:27
  56.6 1.4 %collective-permute-start.11 = (bf16[256,256]{1,0:T(8,128)(2,1)S(1)}, bf16[256,256]{1,0:T(8,128)(2,1)S(1)}, u32[]{:S(2)}, u32[]{:S(2)}) collective-permute-start(bf16[256,256]{1,0:T(8,128)(2,1)S(1)} %get-tuple-element.39), channel_id=1, source_target_pairs={{0,4},{2,6},{4,0},{6,2},{8,12},{10,14},{12,8},{14,10},{16,20},{18,... | collective-permute-start | bytes 393224 | tf_op jit(solution)/shard_map/ppermute | solution.py:341
  58.0 1.2 %collective-permute-start.12 = (bf16[256,256]{1,0:T(8,128)(2,1)S(1)}, bf16[256,256]{1,0:T(8,128)(2,1)S(1)}, u32[]{:S(2)}, u32[]{:S(2)}) collective-permute-start(bf16[256,256]{1,0:T(8,128)(2,1)S(1)} %get-tuple-element.40), channel_id=1, source_target_pairs={{0,6},{2,4},{4,2},{6,0},{8,14},{10,12},{12,10},{14,8},{16,22},{18,... | collective-permute-start | bytes 393224 | tf_op jit(solution)/shard_map/ppermute | solution.py:341
  59.2 6.5 %hyena.1 = bf16[256,2048]{1,0:T(8,128)(2,1)} custom-call(bf16[256,2048]{1,0:T(8,128)(2,1)S(1)} %copy-done.3, bf16[256,2048]{1,0:T(8,128)(2,1)S(1)} %copy-done, bf16[256,2048]{1,0:T(8,128)(2,1)S(1)} %copy-done.1, bf16[128,2048]{1,0:T(8,128)(2,1)S(1)} %collective-permute-done.rim_ref, bf16[128,128]{1,0:T(8,128)(2,1)S(1)} %copy-done.5, ...), custom_call_target="tpu_custom_call" | custom-call | flops 4294967296 | bytes 5242880 | tf_op jit(solution)/shard_map/hyena/pallas_call | solution.py:90
  65.8 4.6 %collective-permute-start.13 = (bf16[256,256]{1,0:T(8,128)(2,1)S(1)}, bf16[256,256]{1,0:T(8,128)(2,1)S(1)}, u32[]{:S(2)}, u32[]{:S(2)}) collective-permute-start(bf16[256,256]{1,0:T(8,128)(2,1)S(1)} %get-tuple-element.42.refs_0_), channel_id=1, source_target_pairs={{0,1},{1,0},{2,3},{3,2},{4,5},{5,4},{6,7},{7,6},{8,9},{9,8},{10,11... | collective-permute-start | bytes 393224 | tf_op jit(solution)/shard_map/ppermute | solution.py:410
  70.5 0.4 collective-permute-start.15
  71.0 0.4 collective-permute-done.13.refs_4_
  72.3 3.5 %project.1 = bf16[256,2048]{1,0:T(8,128)(2,1)} custom-call(bf16[256,256]{1,0:T(8,128)(2,1)S(1)} %get-tuple-element.42.refs_0_, bf16[256,256]{1,0:T(8,128)(2,1)S(1)} %collective-permute-done.10.refs_1_, bf16[256,256]{1,0:T(8,128)(2,1)S(1)} %collective-permute-done.11.refs_2_, bf16[256,256]{1,0:T(8,128)(2,1)S(1)} %collective-permute-done.12.refs_3_, ...), custom_call_target="tpu_custom_call" | custom-call | flops 2147483648 | bytes 10485760 | tf_op jit(solution)/shard_map/project/pallas_call | solution.py:27
  (45 shorter events, 1.8 us)
Async XLA Ops:
  3.7 10.4 %collective-permute-start.1 = (bf16[784,256]{1,0:T(8,128)(2,1)}, bf16[784,256]{1,0:T(8,128)(2,1)S(1)}, u32[]{:S(2)}, u32[]{:S(2)}) collective-permute-start(bf16[784,256]{1,0:T(8,128)(2,1)} %get-tuple-element.29), channel_id=1, source_target_pairs={{0,2},{2,0},{4,6},{6,4},{8,10},{10,8},{12,14},{14,12},{16,18},{18,... | collective-permute-start | bytes 1204232 | tf_op jit(solution)/shard_map/ppermute | solution.py:341
  5.0 11.3 %collective-permute-start.2 = (bf16[784,256]{1,0:T(8,128)(2,1)}, bf16[784,256]{1,0:T(8,128)(2,1)S(1)}, u32[]{:S(2)}, u32[]{:S(2)}) collective-permute-start(bf16[784,256]{1,0:T(8,128)(2,1)} %get-tuple-element.31), channel_id=1, source_target_pairs={{0,4},{2,6},{4,0},{6,2},{8,12},{10,14},{12,8},{14,10},{16,20},{18,... | collective-permute-start | bytes 1204232 | tf_op jit(solution)/shard_map/ppermute | solution.py:341
  6.2 10.1 %collective-permute-start.3 = (bf16[528,256]{1,0:T(8,128)(2,1)}, bf16[528,256]{1,0:T(8,128)(2,1)S(1)}, u32[]{:S(2)}, u32[]{:S(2)}) collective-permute-start(bf16[528,256]{1,0:T(8,128)(2,1)} %get-tuple-element.27.refs_1_), channel_id=1, source_target_pairs={{0,8},{2,10},{4,12},{6,14},{8,16},{10,18},{12,20},{14,22},{16,24},... | collective-permute-start | bytes 811016 | tf_op jit(solution)/shard_map/ppermute | solution.py:344
  14.1 10.3 %collective-permute-start.4 = (bf16[784,256]{1,0:T(8,128)(2,1)}, bf16[784,256]{1,0:T(8,128)(2,1)S(1)}, u32[]{:S(2)}, u32[]{:S(2)}) collective-permute-start(bf16[784,256]{1,0:T(8,128)(2,1)} %get-tuple-element.33), channel_id=1, source_target_pairs={{0,6},{2,4},{4,2},{6,0},{8,14},{10,12},{12,10},{14,8},{16,22},{18,... | collective-permute-start | bytes 1204232 | tf_op jit(solution)/shard_map/ppermute | solution.py:341
  16.3 3.5 %copy-start.2 = (bf16[272,256]{1,0:T(8,128)(2,1)S(1)}, bf16[272,256]{1,0:T(8,128)(2,1)}, u32[]{:S(2)}) copy-start(bf16[272,256]{1,0:T(8,128)(2,1)} %get-tuple-element.26.refs_0_) | copy-start | bytes 417796
  16.4 11.3 %copy-start = (bf16[256,2048]{1,0:T(8,128)(2,1)S(1)}, bf16[256,2048]{1,0:T(8,128)(2,1)}, u32[]{:S(2)}) copy-start(bf16[256,2048]{1,0:T(8,128)(2,1)} %k_ref.3) | copy-start | bytes 3145732
  16.4 11.3 %copy-start.1 = (bf16[256,2048]{1,0:T(8,128)(2,1)S(1)}, bf16[256,2048]{1,0:T(8,128)(2,1)}, u32[]{:S(2)}) copy-start(bf16[256,2048]{1,0:T(8,128)(2,1)} %v_ref.3) | copy-start | bytes 3145732
  16.5 16.8 %collective-permute-start.5 = (bf16[1056,256]{1,0:T(8,128)(2,1)S(1)}, bf16[1056,256]{1,0:T(8,128)(2,1)S(1)}, u32[]{:S(2)}, u32[]{:S(2)}) collective-permute-start(bf16[1056,256]{1,0:T(8,128)(2,1)S(1)} %pad_maximum_fusion), channel_id=1, source_target_pairs={{0,8},{2,10},{4,12},{6,14},{8,16},{10,18},{12,20},{14,22},{16,24},... | collective-permute-start | bytes 1622024 | tf_op jit(solution)/shard_map/ppermute | solution.py:344
  19.9 13.4 %collective-permute-start.7 = (bf16[816,256]{1,0:T(8,128)(2,1)S(1)}, bf16[816,256]{1,0:T(8,128)(2,1)S(1)}, u32[]{:S(2)}, u32[]{:S(2)}) collective-permute-start(bf16[816,256]{1,0:T(8,128)(2,1)S(1)} %pad_maximum_fusion.1), channel_id=1, source_target_pairs={{16,8},{18,10},{20,12},{22,14},{24,16},{26,18},{28,20},{30,22},{17... | collective-permute-start | bytes 1253384 | tf_op jit(solution)/shard_map/ppermute | solution.py:347
  24.5 12.8 %collective-permute-start.6 = (bf16[528,256]{1,0:T(8,128)(2,1)S(1)}, bf16[528,256]{1,0:T(8,128)(2,1)S(1)}, u32[]{:S(2)}, u32[]{:S(2)}) collective-permute-start(bf16[528,256]{1,0:T(8,128)(2,1)S(1)} %slice.32), channel_id=1, source_target_pairs={{0,8},{2,10},{4,12},{6,14},{8,16},{10,18},{12,20},{14,22},{16,24},... | collective-permute-start | bytes 811016 | tf_op jit(solution)/shard_map/ppermute | solution.py:344
  27.9 20.2 %collective-permute-start = (bf16[128,2048]{1,0:T(8,128)(2,1)S(1)}, bf16[128,2048]{1,0:T(8,128)(2,1)S(1)}, u32[]{:S(2)}, u32[]{:S(2)}) collective-permute-start(bf16[128,2048]{1,0:T(8,128)(2,1)S(1)} %multiply_convert_fusion), channel_id=1, source_target_pairs={{0,2},{2,4},{4,6},{6,8},{8,10},{10,12},{12,14},{14,16},{16,18},{18... | collective-permute-start | bytes 1572872 | tf_op jit(solution)/shard_map/ppermute | solution.py:366
  31.0 11.3 %copy-start.6 = (bf16[2048]{0:T(1024)(128)(2,1)S(1)}, bf16[2048]{0:T(1024)(128)(2,1)}, u32[]{:S(2)}) copy-start(bf16[2048]{0:T(1024)(128)(2,1)} %param.14) | copy-start | bytes 12292
  31.0 17.1 %copy-start.4 = (bf16[528,256]{1,0:T(8,128)(2,1)S(1)}, bf16[528,256]{1,0:T(8,128)(2,1)}, u32[]{:S(2)}) copy-start(bf16[528,256]{1,0:T(8,128)(2,1)} %get-tuple-element.27.refs_1_) | copy-start | bytes 811012
  31.0 6.2 %collective-permute-start.8 = (bf16[272,256]{1,0:T(8,128)(2,1)S(1)}, bf16[272,256]{1,0:T(8,128)(2,1)S(1)}, u32[]{:S(2)}, u32[]{:S(2)}) collective-permute-start(bf16[272,256]{1,0:T(8,128)(2,1)S(1)} %slice.33), channel_id=1, source_target_pairs={{16,8},{18,10},{20,12},{22,14},{24,16},{26,18},{28,20},{30,22},{17... | collective-permute-start | bytes 417800 | tf_op jit(solution)/shard_map/ppermute | solution.py:347
  39.9 16.2 %collective-permute-start.9 = (bf16[272,768]{1,0:T(8,128)(2,1)S(1)}, bf16[272,768]{1,0:T(8,128)(2,1)S(1)}, u32[]{:S(2)}, u32[]{:S(2)}) collective-permute-start(bf16[272,768]{1,0:T(8,128)(2,1)S(1)} %far.1), channel_id=1, source_target_pairs={{8,16},{10,18},{12,20},{14,22},{16,24},{18,26},{20,28},{22,30},{9,... | collective-permute-start | bytes 1253384 | tf_op jit(solution)/shard_map/ppermute | solution.py:344
  56.5 9.2 %collective-permute-start.10 = (bf16[256,256]{1,0:T(8,128)(2,1)S(1)}, bf16[256,256]{1,0:T(8,128)(2,1)S(1)}, u32[]{:S(2)}, u32[]{:S(2)}) collective-permute-start(bf16[256,256]{1,0:T(8,128)(2,1)S(1)} %get-tuple-element.38), channel_id=1, source_target_pairs={{0,2},{2,0},{4,6},{6,4},{8,10},{10,8},{12,14},{14,12},{16,18},{18,... | collective-permute-start | bytes 393224 | tf_op jit(solution)/shard_map/ppermute | solution.py:341
  56.6 9.2 %collective-permute-start.11 = (bf16[256,256]{1,0:T(8,128)(2,1)S(1)}, bf16[256,256]{1,0:T(8,128)(2,1)S(1)}, u32[]{:S(2)}, u32[]{:S(2)}) collective-permute-start(bf16[256,256]{1,0:T(8,128)(2,1)S(1)} %get-tuple-element.39), channel_id=1, source_target_pairs={{0,4},{2,6},{4,0},{6,2},{8,12},{10,14},{12,8},{14,10},{16,20},{18,... | collective-permute-start | bytes 393224 | tf_op jit(solution)/shard_map/ppermute | solution.py:341
  58.0 14.2 %slice-start = ((s8[8388608]{0:T(1024)(128)(4,1)}), s8[4194304]{0:T(1024)(128)(4,1)S(1)}, s32[]{:S(2)}) async-start(s8[8388608]{0:T(1024)(128)(4,1)} %bitcast.1), calls=%async_computation | async-start | bytes 8388608
  58.0 14.2 %slice-start.1 = ((s8[8388608]{0:T(1024)(128)(4,1)}), s8[4194304]{0:T(1024)(128)(4,1)S(1)}, s32[]{:S(2)}) async-start(s8[8388608]{0:T(1024)(128)(4,1)} %bitcast.1), calls=%async_computation.1 | async-start | bytes 8388608
  58.0 7.7 %collective-permute-start.12 = (bf16[256,256]{1,0:T(8,128)(2,1)S(1)}, bf16[256,256]{1,0:T(8,128)(2,1)S(1)}, u32[]{:S(2)}, u32[]{:S(2)}) collective-permute-start(bf16[256,256]{1,0:T(8,128)(2,1)S(1)} %get-tuple-element.40), channel_id=1, source_target_pairs={{0,6},{2,4},{4,2},{6,0},{8,14},{10,12},{12,10},{14,8},{16,22},{18,... | collective-permute-start | bytes 393224 | tf_op jit(solution)/shard_map/ppermute | solution.py:341
  65.8 5.6 %collective-permute-start.13 = (bf16[256,256]{1,0:T(8,128)(2,1)S(1)}, bf16[256,256]{1,0:T(8,128)(2,1)S(1)}, u32[]{:S(2)}, u32[]{:S(2)}) collective-permute-start(bf16[256,256]{1,0:T(8,128)(2,1)S(1)} %get-tuple-element.42.refs_0_), channel_id=1, source_target_pairs={{0,1},{1,0},{2,3},{3,2},{4,5},{5,4},{6,7},{7,6},{8,9},{9,8},{10,11... | collective-permute-start | bytes 393224 | tf_op jit(solution)/shard_map/ppermute | solution.py:410
  70.4 1.3 %collective-permute-start.14 = (bf16[256,256]{1,0:T(8,128)(2,1)S(1)}, bf16[256,256]{1,0:T(8,128)(2,1)S(1)}, u32[]{:S(2)}, u32[]{:S(2)}) collective-permute-start(bf16[256,256]{1,0:T(8,128)(2,1)S(1)} %collective-permute-done.10.refs_1_), channel_id=1, source_target_pairs={{0,1},{1,0},{2,3},{3,2},{4,5},{5,4},{6,7},{7,6},{8,9},{9,8},{10,11... | collective-permute-start | bytes 393224 | tf_op jit(solution)/shard_map/ppermute | solution.py:410
  70.5 1.5 %collective-permute-start.15 = (bf16[256,256]{1,0:T(8,128)(2,1)S(1)}, bf16[256,256]{1,0:T(8,128)(2,1)S(1)}, u32[]{:S(2)}, u32[]{:S(2)}) collective-permute-start(bf16[256,256]{1,0:T(8,128)(2,1)S(1)} %collective-permute-done.11.refs_2_), channel_id=1, source_target_pairs={{0,1},{1,0},{2,3},{3,2},{4,5},{5,4},{6,7},{7,6},{8,9},{9,8},{10,11... | collective-permute-start | bytes 393224 | tf_op jit(solution)/shard_map/ppermute | solution.py:410
  70.9 1.3 %collective-permute-start.16 = (bf16[256,256]{1,0:T(8,128)(2,1)S(1)}, bf16[256,256]{1,0:T(8,128)(2,1)S(1)}, u32[]{:S(2)}, u32[]{:S(2)}) collective-permute-start(bf16[256,256]{1,0:T(8,128)(2,1)S(1)} %collective-permute-done.12.refs_3_), channel_id=1, source_target_pairs={{0,1},{1,0},{2,3},{3,2},{4,5},{5,4},{6,7},{7,6},{8,9},{9,8},{10,11... | collective-permute-start | bytes 393224 | tf_op jit(solution)/shard_map/ppermute | solution.py:410
  (2 other events, 6.2 us)

commit v3 on v1

--- a/solution.py
+++ b/solution.py
@@ -14,7 +14,6 @@
 TAG = 16
 LANES = 128
 VMEM_LIMIT = 32 * 1024 * 1024
-ALL_VMEM = 62 * 1024 * 1024
 VMEM = pl.BlockSpec(memory_space=pltpu.VMEM)
 
 
@@ -36,20 +35,24 @@
     )(*args))
 
 
-def hyena_kernel(q_ref, k_ref, v_ref, rim_ref, taps_ref, direct_ref, out_ref):
-    rows, width = q_ref.shape
-    per_tile = taps_ref.shape[0] * LANES // width
-    group = LANES // per_tile
+def hyena_kernel(q_ref, k_ref, v_ref, rim_ref, taps_ref, direct_ref, out_ref, taps):
+    rows, chans = q_ref.shape
+    groups = taps_ref.shape[0]
+    group = chans // groups
+    per_tile = LANES // group
     windows = rows // LANES
     shape = (LANES, LANES)
     down, along = (lax.broadcasted_iota(jnp.int32, shape, i) for i in range(2))
     turn = jnp.where((down + along) % LANES == 0, 1.0, 0.0).astype(jnp.bfloat16)
     before = jnp.where(along > down, 1.0, 0.0).astype(jnp.bfloat16)
     within = jnp.where(along > down, 0.0, 1.0).astype(jnp.bfloat16)
-    taps = jnp.dot(taps_ref[...], turn, preferred_element_type=jnp.float32)
+    taps[...] = jnp.dot(taps_ref[...], turn, preferred_element_type=jnp.float32)
     lane_group = lax.broadcasted_iota(jnp.int32, (LANES, windows * LANES), 1) % LANES // group
-    for tile in range(width // LANES):
-        cols = slice(tile * LANES, (tile + 1) * LANES)
+
+    @pl.loop(0, chans // LANES, unroll=2)
+    def _(tile):
+        cols = pl.ds(pl.multiple_of(tile * LANES, LANES), LANES)
+        rings = taps[pl.ds(pl.multiple_of(tile * per_tile, per_tile), per_tile), :]
         mixed = (k_ref[:, cols].astype(jnp.float32) * v_ref[:, cols].astype(jnp.float32)).astype(
             jnp.bfloat16
         )
@@ -59,10 +62,8 @@
         )
         conv = jnp.zeros((LANES, windows * LANES), jnp.float32)
         for g in range(per_tile):
-            at = tile * per_tile + g
-            row = taps[at : at + 1]
             ring = pltpu.roll(
-                jnp.broadcast_to(row, shape), 0, 1, stride=1, stride_axis=0
+                jnp.broadcast_to(rings[g : g + 1], shape), 0, 1, stride=1, stride_axis=0
             ).astype(jnp.bfloat16)
             table = jnp.concatenate([ring * before, ring * within], axis=1)
             part = jnp.dot(table, stacked, preferred_element_type=jnp.float32)
@@ -80,72 +81,47 @@
     rows, chans = hyena_q.shape
     groups, kernel = filters.shape
     taps = jnp.pad(filters, ((0, 0), (0, LANES - kernel)))
-    block = 2 * LANES
-    steps = chans // block
-    wide = pl.BlockSpec((rows, block), lambda i: (0, i))
-    return pl.pallas_call(
+    (out,) = kernel_call(
         hyena_kernel,
-        grid=(steps,),
-        in_specs=[
-            wide,
-            wide,
-            wide,
-            pl.BlockSpec((LANES, block), lambda i: (0, i)),
-            pl.BlockSpec((groups // steps, LANES), lambda i: (i, 0)),
-            pl.BlockSpec((1, block), lambda i: (0, i)),
-        ],
-        out_specs=wide,
-        out_shape=jax.ShapeDtypeStruct((rows, chans), jnp.bfloat16),
-        compiler_params=pltpu.CompilerParams(vmem_limit_bytes=VMEM_LIMIT),
-        cost_estimate=pl.CostEstimate(
-            flops=4 * rows * chans * 2 * LANES * 8,
-            bytes_accessed=10 * rows * chans,
-            transcendentals=0,
-        ),
-        name="hyena",
-    )(hyena_q, hyena_k, hyena_v, rim, taps, direct[None])
+        (hyena_q, hyena_k, hyena_v, rim, taps, direct[None]),
+        [jax.ShapeDtypeStruct((rows, chans), jnp.bfloat16)],
+        "hyena",
+        [pltpu.VMEM((groups, LANES), jnp.float32)],
+        flops=4 * rows * chans * 2 * LANES * 8,
+    )
+    return out
 
 
 def deal_kernel(q_ref, k_ref, v_ref, id_ref, *refs):
-    outs, held, (arrive, leave) = refs[: SQUAD + 1], refs[SQUAD + 1 : -2], refs[-2:]
+    outs, arrive = refs[:-1], refs[-1]
     rows, feat = q_ref.shape
     width = feat // SQUAD
     corner = corner_of()
-    order = list(range(1, SQUAD)) + [0]
-    copies = {}
-    for k in order:
+    copies = []
+    for k in (*range(1, SQUAD), 0):
         cols = pl.ds(pl.multiple_of(jnp.bitwise_xor(corner, k) * width, width), width)
         base = rows if k else 0
         places = (
-            (q_ref, held[k + 1] if k else held[0], 0),
-            (k_ref, held[k + 1], base + TAG),
-            (v_ref, held[k + 1], base + TAG + rows),
-        )
-        copies[k] = [
+            (q_ref, outs[k + 1] if k else outs[0], 0),
+            (k_ref, outs[k + 1], base + TAG),
+            (v_ref, outs[k + 1], base + TAG + rows),
+        )
+        copies += [
             pltpu.make_async_copy(
                 source.at[:, cols], target.at[pl.ds(begin, rows)], arrive.at[k, i]
             )
             for i, (source, target, begin) in enumerate(places)
         ]
-        for copy in copies[k]:
-            copy.start()
+    for copy in copies:
+        copy.start()
     ids = (id_ref[...] + 1).astype(jnp.float32)
     spare = jnp.zeros((TAG - ids.shape[0], LANES), jnp.float32)
     ids = jnp.concatenate([ids, spare], axis=0)
     tag = jnp.concatenate([ids] * (width // LANES), axis=1).astype(jnp.bfloat16)
-    for i, target in enumerate(held):
+    for i, target in enumerate(outs):
         begin = 0 if i == 1 else rows
         target[begin : begin + TAG, :] = tag
-    leaving = [
-        pltpu.make_async_copy(source, out, leave.at[i])
-        for i, (source, out) in enumerate(zip(held, outs))
-    ]
-    for k in order:
-        for copy in copies[k]:
-            copy.wait()
-        leaving[k + 1].start()
-    leaving[0].start()
-    for copy in leaving:
+    for copy in copies:
         copy.wait()
 
 
@@ -153,21 +129,20 @@
     rows, feat = queries.shape
     tall = [rows + TAG, 2 * rows + TAG] + [3 * rows + TAG] * (SQUAD - 1)
     shapes = [(x, feat // SQUAD) for x in tall]
-    anywhere = pl.BlockSpec(memory_space=pl.ANY)
+    held = [pltpu.with_memory_space_constraint(x, pltpu.HBM) for x in (queries, keys, values)]
     return list(
         pl.pallas_call(
             deal_kernel,
-            in_specs=[anywhere] * 3 + [VMEM],
-            out_specs=[anywhere] * len(tall),
+            in_specs=[pl.BlockSpec(memory_space=pl.ANY)] * 3 + [VMEM],
+            out_specs=[VMEM] * len(tall),
             out_shape=[jax.ShapeDtypeStruct(x, jnp.bfloat16) for x in shapes],
-            scratch_shapes=[pltpu.VMEM(x, jnp.bfloat16) for x in shapes]
-            + [pltpu.SemaphoreType.DMA((SQUAD, 3)), pltpu.SemaphoreType.DMA((SQUAD + 1,))],
-            compiler_params=pltpu.CompilerParams(vmem_limit_bytes=ALL_VMEM),
+            scratch_shapes=[pltpu.SemaphoreType.DMA((SQUAD, 3))],
+            compiler_params=pltpu.CompilerParams(vmem_limit_bytes=VMEM_LIMIT),
             cost_estimate=pl.CostEstimate(
                 flops=0, bytes_accessed=12 * rows * feat, transcendentals=0
             ),
             name="deal",
-        )(queries, keys, values, ids)
+        )(*held, ids)
     )
 
 

time: 73.4 us -> 71.2 us (0.970)
  Pallas kernels: 24.1 us -> 21.3 us
  waiting for transfers between devices: 11.5 us -> 12.3 us
    pallas_call x2 -> x1, Pallas kernels: 9.64 us -> 1.57 us  [deal(): pl.pallas_call(deal_kernel, in_specs=[pl.BlockSpec(memory_space=pl.ANY)]...]
    pallas_call x4 -> x5, Pallas kernels: 14.5 us -> 19.7 us  [kernel_call(): pl.pallas_call(kernel, in_specs=[VMEM] * len(args), out_specs=[VMEM] * le...]
  transfers between devices with their start and end apart: 17 -> 17, of which waited for: 8 -> 9; matrix products, arithmetic and copies ran while one was open for 0% -> 0% of each run, Pallas kernels for 24% -> 23%
where the time goes in v3:
time: 71.2 us; the launch traced here: 70.8 us
  starting transfers between devices  35.3 us (50%)
  Pallas kernels  21.3 us (30%)
  waiting for transfers between devices  12.3 us (17%)
  between operations  0.92 us (1%)
  local copies, waits for them, and re-layouts  0.81 us (1%)
    pallas_call x5, Pallas kernels, kernel_call(): pl.pallas_call(kernel, in_specs=[VMEM] * len(args), out_specs=[VMEM] * le...  19.7 us
    ppermute x4, starting transfers between devices, climb(): lax.ppermute(value, 'ctx', [(i, i + SQUAD) for i in range(first, count -...  13.1 us
    ppermute x6, starting transfers between devices, swap(): return lax.ppermute(value, 'ctx', [(i, i ^ mask) for i in range(count)])  11.8 us
    ppermute x6, waiting for transfers between devices, swap(): return lax.ppermute(value, 'ctx', [(i, i ^ mask) for i in range(count)])  7.64 us
    ppermute x2, starting transfers between devices, descend(): lax.ppermute(value, 'ctx', [(i, i - SQUAD) for i in range(2 * SQUAD, coun...  4.16 us
    ppermute x4, starting transfers between devices, turn(): lax.ppermute(value, 'tp', [(t, (t + r) % ranks) for t in range(ranks)])  3.18 us
    ppermute x1, starting transfers between devices, local(): lax.ppermute((tail_k * tail_v).astype(bf16), 'ctx', [(i, i + 1) for i in...  3.12 us
    ppermute x2, waiting for transfers between devices, descend(): lax.ppermute(value, 'ctx', [(i, i - SQUAD) for i in range(2 * SQUAD, coun...  1.97 us
  transfers between devices with their start and end apart: 17, of which 9 were waited for; matrix products, arithmetic and copies ran while one was open for 0% of the time, Pallas kernels for 23%

profile of v3, /device:TPU:17, one launch (start us, length us, event | category | flops | bytes accessed | tf_op | source)
XLA Modules:
  0.0 70.8 jit_solution(6757549931581204501)
XLA Ops:
  0.6 0.7 copy-done.2
  1.3 1.6 %deal.1 = (bf16[272,256]{1,0:T(8,128)(2,1)S(1)}, bf16[528,256]{1,0:T(8,128)(2,1)S(1)}, bf16[784,256]{1,0:T(8,128)(2,1)S(1)}, bf16[784,256]{1,0:T(8,128)(2,1)S(1)}, bf16[784,256]{1,0:T(8,128)(2,1)S(1)}) custom-call(bf16[256,1024]{1,0:T(8,128)(2,1)} %q_ref.2, bf16[256,1024]{1,0:T(8,128)(2,1)} %k_ref.2, bf16[256,1024]{1,0:T(8,128)(2,1)} %v_ref.2, ...), custom_call_target="tpu_custom_call" | custom-call | bytes 3145728 | tf_op jit(solution)/shard_map/deal/pallas_call | solution.py:134
  2.9 1.3 %collective-permute-start.1 = (bf16[784,256]{1,0:T(8,128)(2,1)S(1)}, bf16[784,256]{1,0:T(8,128)(2,1)S(1)}, u32[]{:S(2)}, u32[]{:S(2)}) collective-permute-start(bf16[784,256]{1,0:T(8,128)(2,1)S(1)} %get-tuple-element.25), channel_id=1, source_target_pairs={{0,2},{2,0},{4,6},{6,4},{8,10},{10,8},{12,14},{14,12},{16,18},{18,... | collective-permute-start | bytes 1204232 | tf_op jit(solution)/shard_map/ppermute | solution.py:312
  4.2 1.2 %collective-permute-start.2 = (bf16[784,256]{1,0:T(8,128)(2,1)S(1)}, bf16[784,256]{1,0:T(8,128)(2,1)S(1)}, u32[]{:S(2)}, u32[]{:S(2)}) collective-permute-start(bf16[784,256]{1,0:T(8,128)(2,1)S(1)} %get-tuple-element.27), channel_id=1, source_target_pairs={{0,4},{2,6},{4,0},{6,2},{8,12},{10,14},{12,8},{14,10},{16,20},{18,... | collective-permute-start | bytes 1204232 | tf_op jit(solution)/shard_map/ppermute | solution.py:312
  5.4 3.2 %collective-permute-start.3 = (bf16[528,256]{1,0:T(8,128)(2,1)S(1)}, bf16[528,256]{1,0:T(8,128)(2,1)S(1)}, u32[]{:S(2)}, u32[]{:S(2)}) collective-permute-start(bf16[528,256]{1,0:T(8,128)(2,1)S(1)} %get-tuple-element.23.refs_1_), channel_id=1, source_target_pairs={{0,8},{2,10},{4,12},{6,14},{8,16},{10,18},{12,20},{14,22},{16,24},... | collective-permute-start | bytes 811016 | tf_op jit(solution)/shard_map/ppermute | solution.py:315
  8.6 4.5 %collective-permute-done.1.refs_2_ = bf16[784,256]{1,0:T(8,128)(2,1)S(1)} collective-permute-done((bf16[784,256]{1,0:T(8,128)(2,1)S(1)}, bf16[784,256]{1,0:T(8,128)(2,1)S(1)}, u32[]{:S(2)}, u32[]{:S(2)}) %collective-permute-start.1) | collective-permute-done | bytes 401440 | tf_op jit(solution)/shard_map/ppermute | solution.py:312
  13.1 2.2 %collective-permute-start.4 = (bf16[784,256]{1,0:T(8,128)(2,1)S(1)}, bf16[784,256]{1,0:T(8,128)(2,1)S(1)}, u32[]{:S(2)}, u32[]{:S(2)}) collective-permute-start(bf16[784,256]{1,0:T(8,128)(2,1)S(1)} %get-tuple-element.29), channel_id=1, source_target_pairs={{0,6},{2,4},{4,2},{6,0},{8,14},{10,12},{12,10},{14,8},{16,22},{18,... | collective-permute-start | bytes 1204232 | tf_op jit(solution)/shard_map/ppermute | solution.py:312
  15.4 3.3 %collective-permute-start.5 = (bf16[1056,256]{1,0:T(8,128)(2,1)S(1)}, bf16[1056,256]{1,0:T(8,128)(2,1)S(1)}, u32[]{:S(2)}, u32[]{:S(2)}) collective-permute-start(bf16[1056,256]{1,0:T(8,128)(2,1)S(1)} %pad_maximum_fusion), channel_id=1, source_target_pairs={{0,8},{2,10},{4,12},{6,14},{8,16},{10,18},{12,20},{14,22},{16,24},... | collective-permute-start | bytes 1622024 | tf_op jit(solution)/shard_map/ppermute | solution.py:315
  18.8 2.1 %collective-permute-start.7 = (bf16[816,256]{1,0:T(8,128)(2,1)S(1)}, bf16[816,256]{1,0:T(8,128)(2,1)S(1)}, u32[]{:S(2)}, u32[]{:S(2)}) collective-permute-start(bf16[816,256]{1,0:T(8,128)(2,1)S(1)} %pad_maximum_fusion.1), channel_id=1, source_target_pairs={{16,8},{18,10},{20,12},{22,14},{24,16},{26,18},{28,20},{30,22},{17... | collective-permute-start | bytes 1253384 | tf_op jit(solution)/shard_map/ppermute | solution.py:318
  20.9 2.3 %collective-permute-done.4.refs_4_ = bf16[784,256]{1,0:T(8,128)(2,1)S(1)} collective-permute-done((bf16[784,256]{1,0:T(8,128)(2,1)S(1)}, bf16[784,256]{1,0:T(8,128)(2,1)S(1)}, u32[]{:S(2)}, u32[]{:S(2)}) %collective-permute-start.4) | collective-permute-done | bytes 401440 | tf_op jit(solution)/shard_map/ppermute | solution.py:312
  23.3 3.2 %collective-permute-start.6 = (bf16[528,256]{1,0:T(8,128)(2,1)S(1)}, bf16[528,256]{1,0:T(8,128)(2,1)S(1)}, u32[]{:S(2)}, u32[]{:S(2)}) collective-permute-start(bf16[528,256]{1,0:T(8,128)(2,1)S(1)} %slice.32), channel_id=1, source_target_pairs={{0,8},{2,10},{4,12},{6,14},{8,16},{10,18},{12,20},{14,22},{16,24},... | collective-permute-start | bytes 811016 | tf_op jit(solution)/shard_map/ppermute | solution.py:315
  26.5 2.1 %collective-permute-start.8 = (bf16[272,256]{1,0:T(8,128)(2,1)S(1)}, bf16[272,256]{1,0:T(8,128)(2,1)S(1)}, u32[]{:S(2)}, u32[]{:S(2)}) collective-permute-start(bf16[272,256]{1,0:T(8,128)(2,1)S(1)} %slice.33), channel_id=1, source_target_pairs={{16,8},{18,10},{20,12},{22,14},{24,16},{26,18},{28,20},{30,22},{17... | collective-permute-start | bytes 417800 | tf_op jit(solution)/shard_map/ppermute | solution.py:318
  28.8 3.1 %collective-permute-start = (bf16[128,2048]{1,0:T(8,128)(2,1)S(1)}, bf16[128,2048]{1,0:T(8,128)(2,1)S(1)}, u32[]{:S(2)}, u32[]{:S(2)}) collective-permute-start(bf16[128,2048]{1,0:T(8,128)(2,1)S(1)} %multiply_convert_fusion), channel_id=1, source_target_pairs={{0,2},{2,4},{4,6},{6,8},{8,10},{10,12},{12,14},{14,16},{16,18},{18... | collective-permute-start | bytes 1572872 | tf_op jit(solution)/shard_map/ppermute | solution.py:337
  31.9 2.0 %collective-permute-done.8.refs_1_ = bf16[272,256]{1,0:T(8,128)(2,1)S(1)} collective-permute-done((bf16[272,256]{1,0:T(8,128)(2,1)S(1)}, bf16[272,256]{1,0:T(8,128)(2,1)S(1)}, u32[]{:S(2)}, u32[]{:S(2)}) %collective-permute-start.8) | collective-permute-done | bytes 139296 | tf_op jit(solution)/shard_map/ppermute | solution.py:318
  33.9 1.3 %collective-permute-done.6.refs_7_.refs_4_ = bf16[528,256]{1,0:T(8,128)(2,1)S(1)} collective-permute-done((bf16[528,256]{1,0:T(8,128)(2,1)S(1)}, bf16[528,256]{1,0:T(8,128)(2,1)S(1)}, u32[]{:S(2)}, u32[]{:S(2)}) %collective-permute-start.6) | collective-permute-done | bytes 270368 | tf_op jit(solution)/shard_map/ppermute | solution.py:315
  35.2 2.6 %far.1 = bf16[272,768]{1,0:T(8,128)(2,1)S(1)} custom-call(bf16[816,256]{1,0:T(8,128)(2,1)S(1)} %collective-permute-done.7.refs_0_, bf16[272,256]{1,0:T(8,128)(2,1)S(1)} %collective-permute-done.8.refs_1_, bf16[528,256]{1,0:T(8,128)(2,1)S(1)} %collective-permute-done.3.refs_5_.refs_2_, bf16[1056,256]{1,0:T(8,128)(2,1)S(1)} %collective-permute-done.5.refs_6_.refs_3_, ...), custom_call_target="tpu_custom_call" | custom-call | flops 402653184 | bytes 2056192 | tf_op jit(solution)/shard_map/far/pallas_call | solution.py:26
  37.9 3.4 %collective-permute-start.9 = (bf16[272,768]{1,0:T(8,128)(2,1)S(1)}, bf16[272,768]{1,0:T(8,128)(2,1)S(1)}, u32[]{:S(2)}, u32[]{:S(2)}) collective-permute-start(bf16[272,768]{1,0:T(8,128)(2,1)S(1)} %far.1), channel_id=1, source_target_pairs={{8,16},{10,18},{12,20},{14,22},{16,24},{18,26},{20,28},{22,30},{9,... | collective-permute-start | bytes 1253384 | tf_op jit(solution)/shard_map/ppermute | solution.py:315
  41.3 8.0 %main.1.main_ref = f32[272,1024]{1,0:T(8,128)S(1)} custom-call(bf16[272,256]{1,0:T(8,128)(2,1)S(1)} %get-tuple-element.22.refs_0_, bf16[528,256]{1,0:T(8,128)(2,1)S(1)} %get-tuple-element.23.refs_1_, bf16[784,256]{1,0:T(8,128)(2,1)S(1)} %collective-permute-done.1.refs_2_, bf16[784,256]{1,0:T(8,128)(2,1)S(1)} %collective-permute-done.2.refs_3_, ...), custom_call_target="tpu_custom_call" | custom-call | flops 1744830464 | bytes 3809280 | tf_op jit(solution)/shard_map/main/pallas_call | solution.py:26
  50.1 6.8 %collective-permute-start.11 = (bf16[256,256]{1,0:T(8,128)(2,1)S(1)}, bf16[256,256]{1,0:T(8,128)(2,1)S(1)}, u32[]{:S(2)}, u32[]{:S(2)}) collective-permute-start(bf16[256,256]{1,0:T(8,128)(2,1)S(1)} %get-tuple-element.35), channel_id=1, source_target_pairs={{0,4},{2,6},{4,0},{6,2},{8,12},{10,14},{12,8},{14,10},{16,20},{18,... | collective-permute-start | bytes 393224 | tf_op jit(solution)/shard_map/ppermute | solution.py:312
  56.8 5.2 %hyena.1 = bf16[256,2048]{1,0:T(8,128)(2,1)} custom-call(bf16[256,2048]{1,0:T(8,128)(2,1)S(1)} %copy-done.3, bf16[256,2048]{1,0:T(8,128)(2,1)S(1)} %copy-done, bf16[256,2048]{1,0:T(8,128)(2,1)S(1)} %copy-done.1, bf16[128,2048]{1,0:T(8,128)(2,1)S(1)} %collective-permute-done.rim_ref, bf16[128,128]{1,0:T(8,128)(2,1)S(1)} %copy-done.4, ...), custom_call_target="tpu_custom_call" | custom-call | flops 4294967296 | bytes 4755456 | tf_op jit(solution)/shard_map/hyena/pallas_call | solution.py:26
  62.0 0.8 %collective-permute-done.12.refs_3_ = bf16[256,256]{1,0:T(8,128)(2,1)S(1)} collective-permute-done((bf16[256,256]{1,0:T(8,128)(2,1)S(1)}, bf16[256,256]{1,0:T(8,128)(2,1)S(1)}, u32[]{:S(2)}, u32[]{:S(2)}) %collective-permute-start.12) | collective-permute-done | bytes 131104 | tf_op jit(solution)/shard_map/ppermute | solution.py:312
  62.8 2.7 %collective-permute-start.13 = (bf16[256,256]{1,0:T(8,128)(2,1)S(1)}, bf16[256,256]{1,0:T(8,128)(2,1)S(1)}, u32[]{:S(2)}, u32[]{:S(2)}) collective-permute-start(bf16[256,256]{1,0:T(8,128)(2,1)S(1)} %get-tuple-element.38.refs_0_), channel_id=1, source_target_pairs={{0,1},{1,0},{2,3},{3,2},{4,5},{5,4},{6,7},{7,6},{8,9},{9,8},{10,11... | collective-permute-start | bytes 393224 | tf_op jit(solution)/shard_map/ppermute | solution.py:380
  65.5 0.5 collective-permute-start.15
  67.4 3.5 %project.1 = bf16[256,2048]{1,0:T(8,128)(2,1)} custom-call(bf16[256,256]{1,0:T(8,128)(2,1)S(1)} %get-tuple-element.38.refs_0_, bf16[256,256]{1,0:T(8,128)(2,1)S(1)} %collective-permute-done.10.refs_1_, bf16[256,256]{1,0:T(8,128)(2,1)S(1)} %collective-permute-done.11.refs_2_, bf16[256,256]{1,0:T(8,128)(2,1)S(1)} %collective-permute-done.12.refs_3_, ...), custom_call_target="tpu_custom_call" | custom-call | flops 2147483648 | bytes 10485760 | tf_op jit(solution)/shard_map/project/pallas_call | solution.py:26
  (43 shorter events, 2.4 us)
Async XLA Ops:
  2.9 10.2 %collective-permute-start.1 = (bf16[784,256]{1,0:T(8,128)(2,1)S(1)}, bf16[784,256]{1,0:T(8,128)(2,1)S(1)}, u32[]{:S(2)}, u32[]{:S(2)}) collective-permute-start(bf16[784,256]{1,0:T(8,128)(2,1)S(1)} %get-tuple-element.25), channel_id=1, source_target_pairs={{0,2},{2,0},{4,6},{6,4},{8,10},{10,8},{12,14},{14,12},{16,18},{18,... | collective-permute-start | bytes 1204232 | tf_op jit(solution)/shard_map/ppermute | solution.py:312
  4.2 11.1 %collective-permute-start.2 = (bf16[784,256]{1,0:T(8,128)(2,1)S(1)}, bf16[784,256]{1,0:T(8,128)(2,1)S(1)}, u32[]{:S(2)}, u32[]{:S(2)}) collective-permute-start(bf16[784,256]{1,0:T(8,128)(2,1)S(1)} %get-tuple-element.27), channel_id=1, source_target_pairs={{0,4},{2,6},{4,0},{6,2},{8,12},{10,14},{12,8},{14,10},{16,20},{18,... | collective-permute-start | bytes 1204232 | tf_op jit(solution)/shard_map/ppermute | solution.py:312
  5.4 9.9 %collective-permute-start.3 = (bf16[528,256]{1,0:T(8,128)(2,1)S(1)}, bf16[528,256]{1,0:T(8,128)(2,1)S(1)}, u32[]{:S(2)}, u32[]{:S(2)}) collective-permute-start(bf16[528,256]{1,0:T(8,128)(2,1)S(1)} %get-tuple-element.23.refs_1_), channel_id=1, source_target_pairs={{0,8},{2,10},{4,12},{6,14},{8,16},{10,18},{12,20},{14,22},{16,24},... | collective-permute-start | bytes 811016 | tf_op jit(solution)/shard_map/ppermute | solution.py:315
  13.1 10.1 %collective-permute-start.4 = (bf16[784,256]{1,0:T(8,128)(2,1)S(1)}, bf16[784,256]{1,0:T(8,128)(2,1)S(1)}, u32[]{:S(2)}, u32[]{:S(2)}) collective-permute-start(bf16[784,256]{1,0:T(8,128)(2,1)S(1)} %get-tuple-element.29), channel_id=1, source_target_pairs={{0,6},{2,4},{4,2},{6,0},{8,14},{10,12},{12,10},{14,8},{16,22},{18,... | collective-permute-start | bytes 1204232 | tf_op jit(solution)/shard_map/ppermute | solution.py:312
  15.4 13.2 %copy-start.1 = (bf16[256,2048]{1,0:T(8,128)(2,1)S(1)}, bf16[256,2048]{1,0:T(8,128)(2,1)}, u32[]{:S(2)}) copy-start(bf16[256,2048]{1,0:T(8,128)(2,1)} %v_ref.3) | copy-start | bytes 3145732
  15.4 13.2 %copy-start = (bf16[256,2048]{1,0:T(8,128)(2,1)S(1)}, bf16[256,2048]{1,0:T(8,128)(2,1)}, u32[]{:S(2)}) copy-start(bf16[256,2048]{1,0:T(8,128)(2,1)} %k_ref.3) | copy-start | bytes 3145732
  15.4 16.5 %collective-permute-start.5 = (bf16[1056,256]{1,0:T(8,128)(2,1)S(1)}, bf16[1056,256]{1,0:T(8,128)(2,1)S(1)}, u32[]{:S(2)}, u32[]{:S(2)}) collective-permute-start(bf16[1056,256]{1,0:T(8,128)(2,1)S(1)} %pad_maximum_fusion), channel_id=1, source_target_pairs={{0,8},{2,10},{4,12},{6,14},{8,16},{10,18},{12,20},{14,22},{16,24},... | collective-permute-start | bytes 1622024 | tf_op jit(solution)/shard_map/ppermute | solution.py:315
  18.8 13.1 %collective-permute-start.7 = (bf16[816,256]{1,0:T(8,128)(2,1)S(1)}, bf16[816,256]{1,0:T(8,128)(2,1)S(1)}, u32[]{:S(2)}, u32[]{:S(2)}) collective-permute-start(bf16[816,256]{1,0:T(8,128)(2,1)S(1)} %pad_maximum_fusion.1), channel_id=1, source_target_pairs={{16,8},{18,10},{20,12},{22,14},{24,16},{26,18},{28,20},{30,22},{17... | collective-permute-start | bytes 1253384 | tf_op jit(solution)/shard_map/ppermute | solution.py:318
  23.3 11.9 %collective-permute-start.6 = (bf16[528,256]{1,0:T(8,128)(2,1)S(1)}, bf16[528,256]{1,0:T(8,128)(2,1)S(1)}, u32[]{:S(2)}, u32[]{:S(2)}) collective-permute-start(bf16[528,256]{1,0:T(8,128)(2,1)S(1)} %slice.32), channel_id=1, source_target_pairs={{0,8},{2,10},{4,12},{6,14},{8,16},{10,18},{12,20},{14,22},{16,24},... | collective-permute-start | bytes 811016 | tf_op jit(solution)/shard_map/ppermute | solution.py:315
  26.5 7.4 %collective-permute-start.8 = (bf16[272,256]{1,0:T(8,128)(2,1)S(1)}, bf16[272,256]{1,0:T(8,128)(2,1)S(1)}, u32[]{:S(2)}, u32[]{:S(2)}) collective-permute-start(bf16[272,256]{1,0:T(8,128)(2,1)S(1)} %slice.33), channel_id=1, source_target_pairs={{16,8},{18,10},{20,12},{22,14},{24,16},{26,18},{28,20},{30,22},{17... | collective-permute-start | bytes 417800 | tf_op jit(solution)/shard_map/ppermute | solution.py:318
  28.7 12.5 %copy-start.5 = (bf16[2048]{0:T(1024)(128)(2,1)S(1)}, bf16[2048]{0:T(1024)(128)(2,1)}, u32[]{:S(2)}) copy-start(bf16[2048]{0:T(1024)(128)(2,1)} %param.14) | copy-start | bytes 12292
  28.8 21.0 %collective-permute-start = (bf16[128,2048]{1,0:T(8,128)(2,1)S(1)}, bf16[128,2048]{1,0:T(8,128)(2,1)S(1)}, u32[]{:S(2)}, u32[]{:S(2)}) collective-permute-start(bf16[128,2048]{1,0:T(8,128)(2,1)S(1)} %multiply_convert_fusion), channel_id=1, source_target_pairs={{0,2},{2,4},{4,6},{6,8},{8,10},{10,12},{12,14},{14,16},{16,18},{18... | collective-permute-start | bytes 1572872 | tf_op jit(solution)/shard_map/ppermute | solution.py:337
  37.9 11.5 %collective-permute-start.9 = (bf16[272,768]{1,0:T(8,128)(2,1)S(1)}, bf16[272,768]{1,0:T(8,128)(2,1)S(1)}, u32[]{:S(2)}, u32[]{:S(2)}) collective-permute-start(bf16[272,768]{1,0:T(8,128)(2,1)S(1)} %far.1), channel_id=1, source_target_pairs={{8,16},{10,18},{12,20},{14,22},{16,24},{18,26},{20,28},{22,30},{9,... | collective-permute-start | bytes 1253384 | tf_op jit(solution)/shard_map/ppermute | solution.py:315
  49.3 7.5 %copy-start.3 = (bf16[256,2048]{1,0:T(8,128)(2,1)S(1)}, bf16[256,2048]{1,0:T(8,128)(2,1)}, u32[]{:S(2)}) copy-start(bf16[256,2048]{1,0:T(8,128)(2,1)} %q_ref.3) | copy-start | bytes 3145732
  49.3 7.5 %copy-start.4 = (bf16[128,128]{1,0:T(8,128)(2,1)S(1)}, bf16[128,128]{1,0:T(8,128)(2,1)}, u32[]{:S(2)}) copy-start(bf16[128,128]{1,0:T(8,128)(2,1)} %taps_ref.1) | copy-start | bytes 98308
  49.7 12.3 %collective-permute-start.10 = (bf16[256,256]{1,0:T(8,128)(2,1)S(1)}, bf16[256,256]{1,0:T(8,128)(2,1)S(1)}, u32[]{:S(2)}, u32[]{:S(2)}) collective-permute-start(bf16[256,256]{1,0:T(8,128)(2,1)S(1)} %get-tuple-element.34), channel_id=1, source_target_pairs={{0,2},{2,0},{4,6},{6,4},{8,10},{10,8},{12,14},{14,12},{16,18},{18,... | collective-permute-start | bytes 393224 | tf_op jit(solution)/shard_map/ppermute | solution.py:312
  50.1 12.0 %collective-permute-start.11 = (bf16[256,256]{1,0:T(8,128)(2,1)S(1)}, bf16[256,256]{1,0:T(8,128)(2,1)S(1)}, u32[]{:S(2)}, u32[]{:S(2)}) collective-permute-start(bf16[256,256]{1,0:T(8,128)(2,1)S(1)} %get-tuple-element.35), channel_id=1, source_target_pairs={{0,4},{2,6},{4,0},{6,2},{8,12},{10,14},{12,8},{14,10},{16,20},{18,... | collective-permute-start | bytes 393224 | tf_op jit(solution)/shard_map/ppermute | solution.py:312
  56.8 10.5 %slice-start = ((s8[8388608]{0:T(1024)(128)(4,1)}), s8[4194304]{0:T(1024)(128)(4,1)S(1)}, s32[]{:S(2)}) async-start(s8[8388608]{0:T(1024)(128)(4,1)} %bitcast.1), calls=%async_computation | async-start | bytes 8388608
  56.8 10.5 %slice-start.1 = ((s8[8388608]{0:T(1024)(128)(4,1)}), s8[4194304]{0:T(1024)(128)(4,1)S(1)}, s32[]{:S(2)}) async-start(s8[8388608]{0:T(1024)(128)(4,1)} %bitcast.1), calls=%async_computation.1 | async-start | bytes 8388608
  56.8 6.0 %collective-permute-start.12 = (bf16[256,256]{1,0:T(8,128)(2,1)S(1)}, bf16[256,256]{1,0:T(8,128)(2,1)S(1)}, u32[]{:S(2)}, u32[]{:S(2)}) collective-permute-start(bf16[256,256]{1,0:T(8,128)(2,1)S(1)} %get-tuple-element.36), channel_id=1, source_target_pairs={{0,6},{2,4},{4,2},{6,0},{8,14},{10,12},{12,10},{14,8},{16,22},{18,... | collective-permute-start | bytes 393224 | tf_op jit(solution)/shard_map/ppermute | solution.py:312
  62.8 3.7 %collective-permute-start.13 = (bf16[256,256]{1,0:T(8,128)(2,1)S(1)}, bf16[256,256]{1,0:T(8,128)(2,1)S(1)}, u32[]{:S(2)}, u32[]{:S(2)}) collective-permute-start(bf16[256,256]{1,0:T(8,128)(2,1)S(1)} %get-tuple-element.38.refs_0_), channel_id=1, source_target_pairs={{0,1},{1,0},{2,3},{3,2},{4,5},{5,4},{6,7},{7,6},{8,9},{9,8},{10,11... | collective-permute-start | bytes 393224 | tf_op jit(solution)/shard_map/ppermute | solution.py:380
  65.5 1.3 %collective-permute-start.14 = (bf16[256,256]{1,0:T(8,128)(2,1)S(1)}, bf16[256,256]{1,0:T(8,128)(2,1)S(1)}, u32[]{:S(2)}, u32[]{:S(2)}) collective-permute-start(bf16[256,256]{1,0:T(8,128)(2,1)S(1)} %collective-permute-done.10.refs_1_), channel_id=1, source_target_pairs={{0,1},{1,0},{2,3},{3,2},{4,5},{5,4},{6,7},{7,6},{8,9},{9,8},{10,11... | collective-permute-start | bytes 393224 | tf_op jit(solution)/shard_map/ppermute | solution.py:380
  65.5 1.5 %collective-permute-start.15 = (bf16[256,256]{1,0:T(8,128)(2,1)S(1)}, bf16[256,256]{1,0:T(8,128)(2,1)S(1)}, u32[]{:S(2)}, u32[]{:S(2)}) collective-permute-start(bf16[256,256]{1,0:T(8,128)(2,1)S(1)} %collective-permute-done.11.refs_2_), channel_id=1, source_target_pairs={{0,1},{1,0},{2,3},{3,2},{4,5},{5,4},{6,7},{7,6},{8,9},{9,8},{10,11... | collective-permute-start | bytes 393224 | tf_op jit(solution)/shard_map/ppermute | solution.py:380
  66.0 1.3 %collective-permute-start.16 = (bf16[256,256]{1,0:T(8,128)(2,1)S(1)}, bf16[256,256]{1,0:T(8,128)(2,1)S(1)}, u32[]{:S(2)}, u32[]{:S(2)}) collective-permute-start(bf16[256,256]{1,0:T(8,128)(2,1)S(1)} %collective-permute-done.12.refs_3_), channel_id=1, source_target_pairs={{0,1},{1,0},{2,3},{3,2},{4,5},{5,4},{6,7},{7,6},{8,9},{9,8},{10,11... | collective-permute-start | bytes 393224 | tf_op jit(solution)/shard_map/ppermute | solution.py:380
  (1 other events, 0.7 us)

commit v4 on v3

--- a/solution.py
+++ b/solution.py
@@ -35,7 +35,7 @@
     )(*args))
 
 
-def hyena_kernel(q_ref, k_ref, v_ref, rim_ref, taps_ref, direct_ref, out_ref, taps):
+def hyena_kernel(q_ref, k_ref, v_ref, near_rim, ring_rim, far_rim, taps_ref, direct_ref, out_ref, taps, rim):
     rows, chans = q_ref.shape
     groups = taps_ref.shape[0]
     group = chans // groups
@@ -49,6 +49,14 @@
     taps[...] = jnp.dot(taps_ref[...], turn, preferred_element_type=jnp.float32)
     lane_group = lax.broadcasted_iota(jnp.int32, (LANES, windows * LANES), 1) % LANES // group
 
+    half = chans // 2
+    rim[:, :half] = near_rim[...]
+    rim[:, half:] = ring_rim[...]
+
+    @pl.when(corner_of() == 0)
+    def _():
+        rim[:, half:] = far_rim[...]
+
     @pl.loop(0, chans // LANES, unroll=2)
     def _(tile):
         cols = pl.ds(pl.multiple_of(tile * LANES, LANES), LANES)
@@ -56,7 +64,7 @@
         mixed = (k_ref[:, cols].astype(jnp.float32) * v_ref[:, cols].astype(jnp.float32)).astype(
             jnp.bfloat16
         )
-        full = jnp.concatenate([rim_ref[:, cols], mixed], axis=0)
+        full = jnp.concatenate([rim[:, cols], mixed], axis=0)
         stacked = jnp.concatenate(
             [full[w * LANES : (w + 2) * LANES] for w in range(windows)], axis=1
         )
@@ -77,23 +85,25 @@
         ).astype(jnp.bfloat16)
 
 
-def hyena(hyena_q, hyena_k, hyena_v, rim, filters, direct):
+def hyena(hyena_q, hyena_k, hyena_v, rims, filters, direct):
     rows, chans = hyena_q.shape
     groups, kernel = filters.shape
     taps = jnp.pad(filters, ((0, 0), (0, LANES - kernel)))
     (out,) = kernel_call(
         hyena_kernel,
-        (hyena_q, hyena_k, hyena_v, rim, taps, direct[None]),
+        (hyena_q, hyena_k, hyena_v, *rims, taps, direct[None]),
         [jax.ShapeDtypeStruct((rows, chans), jnp.bfloat16)],
         "hyena",
-        [pltpu.VMEM((groups, LANES), jnp.float32)],
+        [pltpu.VMEM((groups, LANES), jnp.float32), pltpu.VMEM((LANES, chans), jnp.bfloat16)],
         flops=4 * rows * chans * 2 * LANES * 8,
     )
     return out
 
 
 def deal_kernel(q_ref, k_ref, v_ref, id_ref, *refs):
-    outs, arrive = refs[:-1], refs[-1]
+    outs, (held, arrive, told) = refs[:-3], refs[-3:]
+    tell = pltpu.make_async_copy(id_ref, held, told)
+    tell.start()
     rows, feat = q_ref.shape
     width = feat // SQUAD
     corner = corner_of()
@@ -114,7 +124,8 @@
         ]
     for copy in copies:
         copy.start()
-    ids = (id_ref[...] + 1).astype(jnp.float32)
+    tell.wait()
+    ids = (held[...] + 1).astype(jnp.float32)
     spare = jnp.zeros((TAG - ids.shape[0], LANES), jnp.float32)
     ids = jnp.concatenate([ids, spare], axis=0)
     tag = jnp.concatenate([ids] * (width // LANES), axis=1).astype(jnp.bfloat16)
@@ -129,20 +140,24 @@
     rows, feat = queries.shape
     tall = [rows + TAG, 2 * rows + TAG] + [3 * rows + TAG] * (SQUAD - 1)
     shapes = [(x, feat // SQUAD) for x in tall]
-    held = [pltpu.with_memory_space_constraint(x, pltpu.HBM) for x in (queries, keys, values)]
+    held = [pltpu.with_memory_space_constraint(x, pltpu.HBM) for x in (queries, keys, values, ids)]
     return list(
         pl.pallas_call(
             deal_kernel,
-            in_specs=[pl.BlockSpec(memory_space=pl.ANY)] * 3 + [VMEM],
+            in_specs=[pl.BlockSpec(memory_space=pl.ANY)] * 4,
             out_specs=[VMEM] * len(tall),
             out_shape=[jax.ShapeDtypeStruct(x, jnp.bfloat16) for x in shapes],
-            scratch_shapes=[pltpu.SemaphoreType.DMA((SQUAD, 3))],
+            scratch_shapes=[
+                pltpu.VMEM(ids.shape, ids.dtype),
+                pltpu.SemaphoreType.DMA((SQUAD, 3)),
+                pltpu.SemaphoreType.DMA,
+            ],
             compiler_params=pltpu.CompilerParams(vmem_limit_bytes=VMEM_LIMIT),
             cost_estimate=pl.CostEstimate(
                 flops=0, bytes_accessed=12 * rows * feat, transcendentals=0
             ),
             name="deal",
-        )(*held, ids)
+        )(*held)
     )
 
 
@@ -331,14 +346,20 @@
     near.append(climb(jnp.concatenate([x[rows:] for x in beside], axis=0)))
     back = [descend(jnp.concatenate([asked] + [x[:tall] for x in beside], axis=0))]
     near.append(climb(across[rows:]))
-    back.append(descend(across[:tall]))
     tail_k = hyena_k[rows - LANES :].astype(f32)
     tail_v = hyena_v[rows - LANES :].astype(f32)
-    rim = lax.ppermute(
-        (tail_k * tail_v).astype(bf16),
-        "ctx",
-        [(i, i + 1) for i in range(count - 1)],
-    )
+    tail = (tail_k * tail_v).astype(bf16)
+    half = tail.shape[1] // 2
+    ring = lax.ppermute(
+        tail[:, half:], "ctx", [(i, i - i % SQUAD + (i + 1) % SQUAD) for i in range(count)]
+    )
+    across, ring = lax.optimization_barrier((across, ring))
+    back.append(descend(across[:tall]))
+    rims = [
+        lax.ppermute(tail[:, :half], "ctx", [(i, i + 1) for i in range(count - 1)]),
+        ring,
+        lax.ppermute(ring, "ctx", [(i, i + SQUAD) for i in range(0, count - SQUAD, SQUAD)]),
+    ]
     own = [asked, kept, *beside, across]
     def store(blocks):
         return [
@@ -357,6 +378,7 @@
         exps=6 * rows * rows * heads,
     )
     far = climb(far, SQUAD)
+    own[1], *rims = lax.optimization_barrier((own[1], *rims))
     (main,) = kernel_call(
         main_kernel,
         (*own, *near),
@@ -373,8 +395,8 @@
         "merge",
         [pltpu.VMEM((SQUAD, rows, width), bf16)],
     )
-    rim, done[0] = lax.optimization_barrier((rim, done[0]))
-    hyena_out = hyena(hyena_q, hyena_k, hyena_v, rim, filters, direct)
+    *rims, done[0] = lax.optimization_barrier((*rims, done[0]))
+    hyena_out = hyena(hyena_q, hyena_k, hyena_v, rims, filters, direct)
 
     def turn(value, r):
         return lax.ppermute(value, "tp", [(t, (t + r) % ranks) for t in range(ranks)])

time: 71.2 us -> 69.6 us (0.978)
  starting transfers between devices: 35.3 us -> 33.5 us
  other arithmetic: 0.19 us -> 1.24 us
  waiting for transfers between devices: 12.3 us -> 11.3 us
    ppermute x6, waiting for transfers between devices: 7.64 us -> 1.66 us  [swap(): return lax.ppermute(value, 'ctx', [(i, i ^ mask) for i in range(count)])]
    ppermute x6, starting transfers between devices: 11.8 us -> 6.46 us  [swap(): return lax.ppermute(value, 'ctx', [(i, i ^ mask) for i in range(count)])]
    ppermute x4, waiting for transfers between devices: 1.34 us -> 5.13 us  [climb(): lax.ppermute(value, 'ctx', [(i, i + SQUAD) for i in range(first, count -...]
    ppermute x1 -> x3, starting transfers between devices: 3.12 us -> 6.84 us  [the longest x1 3.37 us: local(): lax.ppermute(ring, 'ctx', [(i, i + SQUAD) for i in range(0, count - SQUAD...]
    ppermute x1 -> x3, waiting for transfers between devices: 0.01 us -> 3.21 us  [the longest x1 3.2 us: local(): lax.ppermute(tail[:, half:], 'ctx', [(i, i - i % SQUAD + (i + 1) % SQUAD)...]
    ppermute x2, waiting for transfers between devices: 1.97 us -> 0.01 us  [descend(): lax.ppermute(value, 'ctx', [(i, i - SQUAD) for i in range(2 * SQUAD, coun...]
    ppermute x4, starting transfers between devices: 13.1 us -> 11.5 us  [climb(): lax.ppermute(value, 'ctx', [(i, i + SQUAD) for i in range(first, count -...]
    ppermute x4, starting transfers between devices: 3.18 us -> 4.63 us  [turn(): lax.ppermute(value, 'tp', [(t, (t + r) % ranks) for t in range(ranks)])]
  transfers between devices with their start and end apart: 17 -> 19, of which waited for: 9 -> 8; matrix products, arithmetic and copies ran while one was open for 0% -> 2% of each run, Pallas kernels for 23% -> 23%
where the time goes in v4:
time: 69.6 us; the launch traced here: 68.6 us
  starting transfers between devices  33.5 us (48%)
  Pallas kernels  21.5 us (31%)
  waiting for transfers between devices  11.3 us (16%)
  other arithmetic  1.24 us (2%)
  between operations  0.95 us (1%)
    pallas_call x5, Pallas kernels, kernel_call(): pl.pallas_call(kernel, in_specs=[VMEM] * len(args), out_specs=[VMEM] * le...  19.8 us
    ppermute x4, starting transfers between devices, climb(): lax.ppermute(value, 'ctx', [(i, i + SQUAD) for i in range(first, count -...  11.5 us
    ppermute x6, starting transfers between devices, swap(): return lax.ppermute(value, 'ctx', [(i, i ^ mask) for i in range(count)])  6.46 us
    ppermute x4, waiting for transfers between devices, climb(): lax.ppermute(value, 'ctx', [(i, i + SQUAD) for i in range(first, count -...  5.13 us
    ppermute x4, starting transfers between devices, turn(): lax.ppermute(value, 'tp', [(t, (t + r) % ranks) for t in range(ranks)])  4.63 us
    ppermute x2, starting transfers between devices, descend(): lax.ppermute(value, 'ctx', [(i, i - SQUAD) for i in range(2 * SQUAD, coun...  4 us
    ppermute x1, starting transfers between devices, local(): lax.ppermute(ring, 'ctx', [(i, i + SQUAD) for i in range(0, count - SQUAD...  3.37 us
    ppermute x1, waiting for transfers between devices, local(): lax.ppermute(tail[:, half:], 'ctx', [(i, i - i % SQUAD + (i + 1) % SQUAD)...  3.2 us
  transfers between devices with their start and end apart: 19, of which 8 were waited for; matrix products, arithmetic and copies ran while one was open for 2% of the time, Pallas kernels for 23%

profile of v4, /device:TPU:17, one launch (start us, length us, event | category | flops | bytes accessed | tf_op | source)
XLA Modules:
  0.0 68.6 jit_solution(8114437849853589890)
XLA Ops:
  0.6 1.7 %deal.1 = (bf16[272,256]{1,0:T(8,128)(2,1)S(1)}, bf16[528,256]{1,0:T(8,128)(2,1)S(1)}, bf16[784,256]{1,0:T(8,128)(2,1)S(1)}, bf16[784,256]{1,0:T(8,128)(2,1)S(1)}, bf16[784,256]{1,0:T(8,128)(2,1)S(1)}) custom-call(bf16[256,1024]{1,0:T(8,128)(2,1)} %q_ref.2, bf16[256,1024]{1,0:T(8,128)(2,1)} %k_ref.2, bf16[256,1024]{1,0:T(8,128)(2,1)} %v_ref.2, s32[2,128]{1,0:T(2,128)} %bitcast.3), custom_call_target="tpu_custom_call" | custom-call | bytes 3145728 | tf_op jit(solution)/shard_map/deal/pallas_call | solution.py:145
  2.3 1.3 %collective-permute-start.1 = (bf16[784,256]{1,0:T(8,128)(2,1)S(1)}, bf16[784,256]{1,0:T(8,128)(2,1)S(1)}, u32[]{:S(2)}, u32[]{:S(2)}) collective-permute-start(bf16[784,256]{1,0:T(8,128)(2,1)S(1)} %get-tuple-element.32), channel_id=1, source_target_pairs={{0,2},{2,0},{4,6},{6,4},{8,10},{10,8},{12,14},{14,12},{16,18},{18,... | collective-permute-start | bytes 1204232 | tf_op jit(solution)/shard_map/ppermute | solution.py:327
  3.6 1.2 %collective-permute-start.5 = (bf16[784,256]{1,0:T(8,128)(2,1)S(1)}, bf16[784,256]{1,0:T(8,128)(2,1)S(1)}, u32[]{:S(2)}, u32[]{:S(2)}) collective-permute-start(bf16[784,256]{1,0:T(8,128)(2,1)S(1)} %get-tuple-element.41), channel_id=1, source_target_pairs={{0,4},{2,6},{4,0},{6,2},{8,12},{10,14},{12,8},{14,10},{16,20},{18,... | collective-permute-start | bytes 1204232 | tf_op jit(solution)/shard_map/ppermute | solution.py:327
  4.8 3.2 %collective-permute-start.6 = (bf16[528,256]{1,0:T(8,128)(2,1)S(1)}, bf16[528,256]{1,0:T(8,128)(2,1)S(1)}, u32[]{:S(2)}, u32[]{:S(2)}) collective-permute-start(bf16[528,256]{1,0:T(8,128)(2,1)S(1)} %get-tuple-element.39.refs_1_), channel_id=1, source_target_pairs={{0,8},{2,10},{4,12},{6,14},{8,16},{10,18},{12,20},{14,22},{16,24},... | collective-permute-start | bytes 811016 | tf_op jit(solution)/shard_map/ppermute | solution.py:330
  8.0 1.2 %multiply_convert_fusion = bf16[128,2048]{1,0:T(8,128)(2,1)S(1)} fusion(bf16[256,2048]{1,0:T(8,128)(2,1)} %v_ref.3, bf16[256,2048]{1,0:T(8,128)(2,1)S(1)} %copy-done), kind=kLoop, calls=%fused_computation | loop fusion | flops 1048576 | bytes 1572864 | tf_op jit(solution)/shard_map/convert_element_type | solution.py:351
  9.2 4.2 %collective-permute-done.6.refs_5_.refs_2_ = bf16[528,256]{1,0:T(8,128)(2,1)S(1)} collective-permute-done((bf16[528,256]{1,0:T(8,128)(2,1)S(1)}, bf16[528,256]{1,0:T(8,128)(2,1)S(1)}, u32[]{:S(2)}, u32[]{:S(2)}) %collective-permute-start.6) | collective-permute-done | bytes 270368 | tf_op jit(solution)/shard_map/ppermute | solution.py:330
  13.6 1.3 %collective-permute-start.2 = (bf16[784,256]{1,0:T(8,128)(2,1)S(1)}, bf16[784,256]{1,0:T(8,128)(2,1)S(1)}, u32[]{:S(2)}, u32[]{:S(2)}) collective-permute-start(bf16[784,256]{1,0:T(8,128)(2,1)S(1)} %get-tuple-element.33), channel_id=1, source_target_pairs={{0,6},{2,4},{4,2},{6,0},{8,14},{10,12},{12,10},{14,8},{16,22},{18,... | collective-permute-start | bytes 1204232 | tf_op jit(solution)/shard_map/ppermute | solution.py:327
  14.9 3.2 %collective-permute-start.7 = (bf16[1056,256]{1,0:T(8,128)(2,1)S(1)}, bf16[1056,256]{1,0:T(8,128)(2,1)S(1)}, u32[]{:S(2)}, u32[]{:S(2)}) collective-permute-start(bf16[1056,256]{1,0:T(8,128)(2,1)S(1)} %pad_maximum_fusion), channel_id=1, source_target_pairs={{0,8},{2,10},{4,12},{6,14},{8,16},{10,18},{12,20},{14,22},{16,24},... | collective-permute-start | bytes 1622024 | tf_op jit(solution)/shard_map/ppermute | solution.py:330
  18.1 2.1 %collective-permute-start.9 = (bf16[816,256]{1,0:T(8,128)(2,1)S(1)}, bf16[816,256]{1,0:T(8,128)(2,1)S(1)}, u32[]{:S(2)}, u32[]{:S(2)}) collective-permute-start(bf16[816,256]{1,0:T(8,128)(2,1)S(1)} %pad_maximum_fusion.1), channel_id=1, source_target_pairs={{16,8},{18,10},{20,12},{22,14},{24,16},{26,18},{28,20},{30,22},{17... | collective-permute-start | bytes 1253384 | tf_op jit(solution)/shard_map/ppermute | solution.py:333
  20.2 1.3 %collective-permute-start.3 = (bf16[128,1024]{1,0:T(8,128)(2,1)S(1)}, bf16[128,1024]{1,0:T(8,128)(2,1)S(1)}, u32[]{:S(2)}, u32[]{:S(2)}) collective-permute-start(bf16[128,1024]{1,0:T(8,128)(2,1)S(1)} %get-tuple-element.58), channel_id=1, source_target_pairs={{0,2},{2,4},{4,6},{6,0},{8,10},{10,12},{12,14},{14,8},{16,18},{18,... | collective-permute-start | bytes 786440 | tf_op jit(solution)/shard_map/ppermute | solution.py:353
  21.5 1.6 %collective-permute-done.2.refs_4_ = bf16[784,256]{1,0:T(8,128)(2,1)S(1)} collective-permute-done((bf16[784,256]{1,0:T(8,128)(2,1)S(1)}, bf16[784,256]{1,0:T(8,128)(2,1)S(1)}, u32[]{:S(2)}, u32[]{:S(2)}) %collective-permute-start.2) | collective-permute-done | bytes 401440 | tf_op jit(solution)/shard_map/ppermute | solution.py:327
  23.2 3.2 %collective-permute-start.8 = (bf16[528,256]{1,0:T(8,128)(2,1)S(1)}, bf16[528,256]{1,0:T(8,128)(2,1)S(1)}, u32[]{:S(2)}, u32[]{:S(2)}) collective-permute-start(bf16[528,256]{1,0:T(8,128)(2,1)S(1)} %slice.42), channel_id=1, source_target_pairs={{0,8},{2,10},{4,12},{6,14},{8,16},{10,18},{12,20},{14,22},{16,24},... | collective-permute-start | bytes 811016 | tf_op jit(solution)/shard_map/ppermute | solution.py:330
  26.4 3.2 %collective-permute-done.3.ring_rim = bf16[128,1024]{1,0:T(8,128)(2,1)S(1)} collective-permute-done((bf16[128,1024]{1,0:T(8,128)(2,1)S(1)}, bf16[128,1024]{1,0:T(8,128)(2,1)S(1)}, u32[]{:S(2)}, u32[]{:S(2)}) %collective-permute-start.3) | collective-permute-done | bytes 262176 | tf_op jit(solution)/shard_map/ppermute | solution.py:353
  29.6 1.9 %collective-permute-start.10 = (bf16[272,256]{1,0:T(8,128)(2,1)S(1)}, bf16[272,256]{1,0:T(8,128)(2,1)S(1)}, u32[]{:S(2)}, u32[]{:S(2)}) collective-permute-start(bf16[272,256]{1,0:T(8,128)(2,1)S(1)} %slice.39), channel_id=1, source_target_pairs={{16,8},{18,10},{20,12},{22,14},{24,16},{26,18},{28,20},{30,22},{17... | collective-permute-start | bytes 417800 | tf_op jit(solution)/shard_map/ppermute | solution.py:333
  31.5 2.2 %collective-permute-start = (bf16[128,1024]{1,0:T(8,128)(2,1)S(1)}, bf16[128,1024]{1,0:T(8,128)(2,1)S(1)}, u32[]{:S(2)}, u32[]{:S(2)}) collective-permute-start(bf16[128,1024]{1,0:T(8,128)(2,1)S(1)} %get-tuple-element.59), channel_id=1, source_target_pairs={{0,2},{2,4},{4,6},{6,8},{8,10},{10,12},{12,14},{14,16},{16,18},{18... | collective-permute-start | bytes 786440 | tf_op jit(solution)/shard_map/ppermute | solution.py:359
  33.8 3.4 %collective-permute-start.4 = (bf16[128,1024]{1,0:T(8,128)(2,1)S(1)}, bf16[128,1024]{1,0:T(8,128)(2,1)S(1)}, u32[]{:S(2)}, u32[]{:S(2)}) collective-permute-start(bf16[128,1024]{1,0:T(8,128)(2,1)S(1)} %collective-permute-done.3.ring_rim), channel_id=1, source_target_pairs={{0,8},{8,16},{16,24},{1,9},{9,17},{17,25}} | collective-permute-start | bytes 786440 | tf_op jit(solution)/shard_map/ppermute | solution.py:361
  37.2 2.6 %far.1 = bf16[272,768]{1,0:T(8,128)(2,1)S(1)} custom-call(bf16[816,256]{1,0:T(8,128)(2,1)S(1)} %collective-permute-done.9.refs_0_, bf16[272,256]{1,0:T(8,128)(2,1)S(1)} %collective-permute-done.10.refs_1_, bf16[528,256]{1,0:T(8,128)(2,1)S(1)} %collective-permute-done.6.refs_5_.refs_2_, bf16[1056,256]{1,0:T(8,128)(2,1)S(1)} %collective-permute-done.7.refs_6_.refs_3_, ...), custom_call_target="tpu_custom_call" | custom-call | flops 402653184 | bytes 2056192 | tf_op jit(solution)/shard_map/far/pallas_call | solution.py:26
  39.8 1.9 %collective-permute-start.11 = (bf16[272,768]{1,0:T(8,128)(2,1)S(1)}, bf16[272,768]{1,0:T(8,128)(2,1)S(1)}, u32[]{:S(2)}, u32[]{:S(2)}) collective-permute-start(bf16[272,768]{1,0:T(8,128)(2,1)S(1)} %far.1), channel_id=1, source_target_pairs={{8,16},{10,18},{12,20},{14,22},{16,24},{18,26},{20,28},{22,30},{9,... | collective-permute-start | bytes 1253384 | tf_op jit(solution)/shard_map/ppermute | solution.py:330
  41.8 8.1 %main.1.main_ref = f32[272,1024]{1,0:T(8,128)S(1)} custom-call(bf16[272,256]{1,0:T(8,128)(2,1)S(1)} %get-tuple-element.38.refs_0_, bf16[528,256]{1,0:T(8,128)(2,1)S(1)} %get-tuple-element.39.refs_1_, bf16[784,256]{1,0:T(8,128)(2,1)S(1)} %collective-permute-done.1.refs_2_, bf16[784,256]{1,0:T(8,128)(2,1)S(1)} %collective-permute-done.5.refs_3_, ...), custom_call_target="tpu_custom_call" | custom-call | flops 1744830464 | bytes 3809280 | tf_op jit(solution)/shard_map/main/pallas_call | solution.py:26
  49.9 0.9 %collective-permute-done.11.far_ref = bf16[272,768]{1,0:T(8,128)(2,1)S(1)} collective-permute-done((bf16[272,768]{1,0:T(8,128)(2,1)S(1)}, bf16[272,768]{1,0:T(8,128)(2,1)S(1)}, u32[]{:S(2)}, u32[]{:S(2)}) %collective-permute-start.11) | collective-permute-done | bytes 417824 | tf_op jit(solution)/shard_map/ppermute | solution.py:330
  51.3 2.5 %collective-permute-start.14 = (bf16[256,256]{1,0:T(8,128)(2,1)S(1)}, bf16[256,256]{1,0:T(8,128)(2,1)S(1)}, u32[]{:S(2)}, u32[]{:S(2)}) collective-permute-start(bf16[256,256]{1,0:T(8,128)(2,1)S(1)} %get-tuple-element.52), channel_id=1, source_target_pairs={{0,6},{2,4},{4,2},{6,0},{8,14},{10,12},{12,10},{14,8},{16,22},{18,... | collective-permute-start | bytes 393224 | tf_op jit(solution)/shard_map/ppermute | solution.py:327
  53.9 5.3 %hyena.1 = bf16[256,2048]{1,0:T(8,128)(2,1)} custom-call(bf16[256,2048]{1,0:T(8,128)(2,1)S(1)} %copy-done.2, bf16[256,2048]{1,0:T(8,128)(2,1)S(1)} %copy-done, bf16[256,2048]{1,0:T(8,128)(2,1)S(1)} %copy-done.1, bf16[128,1024]{1,0:T(8,128)(2,1)S(1)} %collective-permute-done.near_rim, bf16[128,1024]{1,0:T(8,128)(2,1)S(1)} %collective-permute-done.3.ring_rim, ...), custom_call_target="tpu_custom_call" | custom-call | flops 4294967296 | bytes 5017600 | tf_op jit(solution)/shard_map/hyena/pallas_call | solution.py:26
  59.2 4.0 %collective-permute-start.15 = (bf16[256,256]{1,0:T(8,128)(2,1)S(1)}, bf16[256,256]{1,0:T(8,128)(2,1)S(1)}, u32[]{:S(2)}, u32[]{:S(2)}) collective-permute-start(bf16[256,256]{1,0:T(8,128)(2,1)S(1)} %get-tuple-element.54.refs_0_), channel_id=1, source_target_pairs={{0,1},{1,0},{2,3},{3,2},{4,5},{5,4},{6,7},{7,6},{8,9},{9,8},{10,11... | collective-permute-start | bytes 393224 | tf_op jit(solution)/shard_map/ppermute | solution.py:402
  65.1 3.5 %project.1 = bf16[256,2048]{1,0:T(8,128)(2,1)} custom-call(bf16[256,256]{1,0:T(8,128)(2,1)S(1)} %get-tuple-element.54.refs_0_, bf16[256,256]{1,0:T(8,128)(2,1)S(1)} %collective-permute-done.12.refs_1_, bf16[256,256]{1,0:T(8,128)(2,1)S(1)} %collective-permute-done.13.refs_2_, bf16[256,256]{1,0:T(8,128)(2,1)S(1)} %collective-permute-done.14.refs_3_, ...), custom_call_target="tpu_custom_call" | custom-call | flops 2147483648 | bytes 10485760 | tf_op jit(solution)/shard_map/project/pallas_call | solution.py:26
  (46 shorter events, 2.6 us)
Async XLA Ops:
  0.6 7.4 %copy-start = (bf16[256,2048]{1,0:T(8,128)(2,1)S(1)}, bf16[256,2048]{1,0:T(8,128)(2,1)}, u32[]{:S(2)}) copy-start(bf16[256,2048]{1,0:T(8,128)(2,1)} %k_ref.3) | copy-start | bytes 3145732
  2.3 11.2 %collective-permute-start.1 = (bf16[784,256]{1,0:T(8,128)(2,1)S(1)}, bf16[784,256]{1,0:T(8,128)(2,1)S(1)}, u32[]{:S(2)}, u32[]{:S(2)}) collective-permute-start(bf16[784,256]{1,0:T(8,128)(2,1)S(1)} %get-tuple-element.32), channel_id=1, source_target_pairs={{0,2},{2,0},{4,6},{6,4},{8,10},{10,8},{12,14},{14,12},{16,18},{18,... | collective-permute-start | bytes 1204232 | tf_op jit(solution)/shard_map/ppermute | solution.py:327
  3.6 9.9 %collective-permute-start.5 = (bf16[784,256]{1,0:T(8,128)(2,1)S(1)}, bf16[784,256]{1,0:T(8,128)(2,1)S(1)}, u32[]{:S(2)}, u32[]{:S(2)}) collective-permute-start(bf16[784,256]{1,0:T(8,128)(2,1)S(1)} %get-tuple-element.41), channel_id=1, source_target_pairs={{0,4},{2,6},{4,0},{6,2},{8,12},{10,14},{12,8},{14,10},{16,20},{18,... | collective-permute-start | bytes 1204232 | tf_op jit(solution)/shard_map/ppermute | solution.py:327
  4.8 8.6 %collective-permute-start.6 = (bf16[528,256]{1,0:T(8,128)(2,1)S(1)}, bf16[528,256]{1,0:T(8,128)(2,1)S(1)}, u32[]{:S(2)}, u32[]{:S(2)}) collective-permute-start(bf16[528,256]{1,0:T(8,128)(2,1)S(1)} %get-tuple-element.39.refs_1_), channel_id=1, source_target_pairs={{0,8},{2,10},{4,12},{6,14},{8,16},{10,18},{12,20},{14,22},{16,24},... | collective-permute-start | bytes 811016 | tf_op jit(solution)/shard_map/ppermute | solution.py:330
  13.6 9.6 %collective-permute-start.2 = (bf16[784,256]{1,0:T(8,128)(2,1)S(1)}, bf16[784,256]{1,0:T(8,128)(2,1)S(1)}, u32[]{:S(2)}, u32[]{:S(2)}) collective-permute-start(bf16[784,256]{1,0:T(8,128)(2,1)S(1)} %get-tuple-element.33), channel_id=1, source_target_pairs={{0,6},{2,4},{4,2},{6,0},{8,14},{10,12},{12,10},{14,8},{16,22},{18,... | collective-permute-start | bytes 1204232 | tf_op jit(solution)/shard_map/ppermute | solution.py:327
  14.9 22.3 %collective-permute-start.7 = (bf16[1056,256]{1,0:T(8,128)(2,1)S(1)}, bf16[1056,256]{1,0:T(8,128)(2,1)S(1)}, u32[]{:S(2)}, u32[]{:S(2)}) collective-permute-start(bf16[1056,256]{1,0:T(8,128)(2,1)S(1)} %pad_maximum_fusion), channel_id=1, source_target_pairs={{0,8},{2,10},{4,12},{6,14},{8,16},{10,18},{12,20},{14,22},{16,24},... | collective-permute-start | bytes 1622024 | tf_op jit(solution)/shard_map/ppermute | solution.py:330
  18.1 15.7 %collective-permute-start.9 = (bf16[816,256]{1,0:T(8,128)(2,1)S(1)}, bf16[816,256]{1,0:T(8,128)(2,1)S(1)}, u32[]{:S(2)}, u32[]{:S(2)}) collective-permute-start(bf16[816,256]{1,0:T(8,128)(2,1)S(1)} %pad_maximum_fusion.1), channel_id=1, source_target_pairs={{16,8},{18,10},{20,12},{22,14},{24,16},{26,18},{28,20},{30,22},{17... | collective-permute-start | bytes 1253384 | tf_op jit(solution)/shard_map/ppermute | solution.py:333
  20.2 9.3 %collective-permute-start.3 = (bf16[128,1024]{1,0:T(8,128)(2,1)S(1)}, bf16[128,1024]{1,0:T(8,128)(2,1)S(1)}, u32[]{:S(2)}, u32[]{:S(2)}) collective-permute-start(bf16[128,1024]{1,0:T(8,128)(2,1)S(1)} %get-tuple-element.58), channel_id=1, source_target_pairs={{0,2},{2,4},{4,6},{6,0},{8,10},{10,12},{12,14},{14,8},{16,18},{18,... | collective-permute-start | bytes 786440 | tf_op jit(solution)/shard_map/ppermute | solution.py:353
  23.2 14.0 %collective-permute-start.8 = (bf16[528,256]{1,0:T(8,128)(2,1)S(1)}, bf16[528,256]{1,0:T(8,128)(2,1)S(1)}, u32[]{:S(2)}, u32[]{:S(2)}) collective-permute-start(bf16[528,256]{1,0:T(8,128)(2,1)S(1)} %slice.42), channel_id=1, source_target_pairs={{0,8},{2,10},{4,12},{6,14},{8,16},{10,18},{12,20},{14,22},{16,24},... | collective-permute-start | bytes 811016 | tf_op jit(solution)/shard_map/ppermute | solution.py:330
  29.6 12.2 %copy-start.4 = (bf16[2048]{0:T(1024)(128)(2,1)S(1)}, bf16[2048]{0:T(1024)(128)(2,1)}, u32[]{:S(2)}) copy-start(bf16[2048]{0:T(1024)(128)(2,1)} %param.14) | copy-start | bytes 12292
  29.6 7.6 %collective-permute-start.10 = (bf16[272,256]{1,0:T(8,128)(2,1)S(1)}, bf16[272,256]{1,0:T(8,128)(2,1)S(1)}, u32[]{:S(2)}, u32[]{:S(2)}) collective-permute-start(bf16[272,256]{1,0:T(8,128)(2,1)S(1)} %slice.39), channel_id=1, source_target_pairs={{16,8},{18,10},{20,12},{22,14},{24,16},{26,18},{28,20},{30,22},{17... | collective-permute-start | bytes 417800 | tf_op jit(solution)/shard_map/ppermute | solution.py:333
  31.5 10.3 %collective-permute-start = (bf16[128,1024]{1,0:T(8,128)(2,1)S(1)}, bf16[128,1024]{1,0:T(8,128)(2,1)S(1)}, u32[]{:S(2)}, u32[]{:S(2)}) collective-permute-start(bf16[128,1024]{1,0:T(8,128)(2,1)S(1)} %get-tuple-element.59), channel_id=1, source_target_pairs={{0,2},{2,4},{4,6},{6,8},{8,10},{10,12},{12,14},{14,16},{16,18},{18... | collective-permute-start | bytes 786440 | tf_op jit(solution)/shard_map/ppermute | solution.py:359
  33.8 8.0 %collective-permute-start.4 = (bf16[128,1024]{1,0:T(8,128)(2,1)S(1)}, bf16[128,1024]{1,0:T(8,128)(2,1)S(1)}, u32[]{:S(2)}, u32[]{:S(2)}) collective-permute-start(bf16[128,1024]{1,0:T(8,128)(2,1)S(1)} %collective-permute-done.3.ring_rim), channel_id=1, source_target_pairs={{0,8},{8,16},{16,24},{1,9},{9,17},{17,25}} | collective-permute-start | bytes 786440 | tf_op jit(solution)/shard_map/ppermute | solution.py:361
  39.8 11.0 %collective-permute-start.11 = (bf16[272,768]{1,0:T(8,128)(2,1)S(1)}, bf16[272,768]{1,0:T(8,128)(2,1)S(1)}, u32[]{:S(2)}, u32[]{:S(2)}) collective-permute-start(bf16[272,768]{1,0:T(8,128)(2,1)S(1)} %far.1), channel_id=1, source_target_pairs={{8,16},{10,18},{12,20},{14,22},{16,24},{18,26},{20,28},{22,30},{9,... | collective-permute-start | bytes 1253384 | tf_op jit(solution)/shard_map/ppermute | solution.py:330
  41.8 12.1 %copy-start.2 = (bf16[256,2048]{1,0:T(8,128)(2,1)S(1)}, bf16[256,2048]{1,0:T(8,128)(2,1)}, u32[]{:S(2)}) copy-start(bf16[256,2048]{1,0:T(8,128)(2,1)} %q_ref.3) | copy-start | bytes 3145732
  51.1 8.0 %collective-permute-start.12 = (bf16[256,256]{1,0:T(8,128)(2,1)S(1)}, bf16[256,256]{1,0:T(8,128)(2,1)S(1)}, u32[]{:S(2)}, u32[]{:S(2)}) collective-permute-start(bf16[256,256]{1,0:T(8,128)(2,1)S(1)} %get-tuple-element.50), channel_id=1, source_target_pairs={{0,2},{2,0},{4,6},{6,4},{8,10},{10,8},{12,14},{14,12},{16,18},{18,... | collective-permute-start | bytes 393224 | tf_op jit(solution)/shard_map/ppermute | solution.py:327
  51.2 8.0 %collective-permute-start.13 = (bf16[256,256]{1,0:T(8,128)(2,1)S(1)}, bf16[256,256]{1,0:T(8,128)(2,1)S(1)}, u32[]{:S(2)}, u32[]{:S(2)}) collective-permute-start(bf16[256,256]{1,0:T(8,128)(2,1)S(1)} %get-tuple-element.51), channel_id=1, source_target_pairs={{0,4},{2,6},{4,0},{6,2},{8,12},{10,14},{12,8},{14,10},{16,20},{18,... | collective-permute-start | bytes 393224 | tf_op jit(solution)/shard_map/ppermute | solution.py:327
  51.3 13.8 %slice-start = ((s8[8388608]{0:T(1024)(128)(4,1)}), s8[4194304]{0:T(1024)(128)(4,1)S(1)}, s32[]{:S(2)}) async-start(s8[8388608]{0:T(1024)(128)(4,1)} %bitcast.1), calls=%async_computation | async-start | bytes 8388608
  51.3 13.8 %slice-start.1 = ((s8[8388608]{0:T(1024)(128)(4,1)}), s8[4194304]{0:T(1024)(128)(4,1)S(1)}, s32[]{:S(2)}) async-start(s8[8388608]{0:T(1024)(128)(4,1)} %bitcast.1), calls=%async_computation.1 | async-start | bytes 8388608
  51.3 7.9 %collective-permute-start.14 = (bf16[256,256]{1,0:T(8,128)(2,1)S(1)}, bf16[256,256]{1,0:T(8,128)(2,1)S(1)}, u32[]{:S(2)}, u32[]{:S(2)}) collective-permute-start(bf16[256,256]{1,0:T(8,128)(2,1)S(1)} %get-tuple-element.52), channel_id=1, source_target_pairs={{0,6},{2,4},{4,2},{6,0},{8,14},{10,12},{12,10},{14,8},{16,22},{18,... | collective-permute-start | bytes 393224 | tf_op jit(solution)/shard_map/ppermute | solution.py:327
  59.2 5.0 %collective-permute-start.15 = (bf16[256,256]{1,0:T(8,128)(2,1)S(1)}, bf16[256,256]{1,0:T(8,128)(2,1)S(1)}, u32[]{:S(2)}, u32[]{:S(2)}) collective-permute-start(bf16[256,256]{1,0:T(8,128)(2,1)S(1)} %get-tuple-element.54.refs_0_), channel_id=1, source_target_pairs={{0,1},{1,0},{2,3},{3,2},{4,5},{5,4},{6,7},{7,6},{8,9},{9,8},{10,11... | collective-permute-start | bytes 393224 | tf_op jit(solution)/shard_map/ppermute | solution.py:402
  63.3 1.3 %collective-permute-start.16 = (bf16[256,256]{1,0:T(8,128)(2,1)S(1)}, bf16[256,256]{1,0:T(8,128)(2,1)S(1)}, u32[]{:S(2)}, u32[]{:S(2)}) collective-permute-start(bf16[256,256]{1,0:T(8,128)(2,1)S(1)} %collective-permute-done.12.refs_1_), channel_id=1, source_target_pairs={{0,1},{1,0},{2,3},{3,2},{4,5},{5,4},{6,7},{7,6},{8,9},{9,8},{10,11... | collective-permute-start | bytes 393224 | tf_op jit(solution)/shard_map/ppermute | solution.py:402
  63.3 1.5 %collective-permute-start.17 = (bf16[256,256]{1,0:T(8,128)(2,1)S(1)}, bf16[256,256]{1,0:T(8,128)(2,1)S(1)}, u32[]{:S(2)}, u32[]{:S(2)}) collective-permute-start(bf16[256,256]{1,0:T(8,128)(2,1)S(1)} %collective-permute-done.13.refs_2_), channel_id=1, source_target_pairs={{0,1},{1,0},{2,3},{3,2},{4,5},{5,4},{6,7},{7,6},{8,9},{9,8},{10,11... | collective-permute-start | bytes 393224 | tf_op jit(solution)/shard_map/ppermute | solution.py:402
  63.8 1.3 %collective-permute-start.18 = (bf16[256,256]{1,0:T(8,128)(2,1)S(1)}, bf16[256,256]{1,0:T(8,128)(2,1)S(1)}, u32[]{:S(2)}, u32[]{:S(2)}) collective-permute-start(bf16[256,256]{1,0:T(8,128)(2,1)S(1)} %collective-permute-done.14.refs_3_), channel_id=1, source_target_pairs={{0,1},{1,0},{2,3},{3,2},{4,5},{5,4},{6,7},{7,6},{8,9},{9,8},{10,11... | collective-permute-start | bytes 393224 | tf_op jit(solution)/shard_map/ppermute | solution.py:402
  (2 other events, 8.0 us)

commit v5 on v3

--- a/solution.py
+++ b/solution.py
@@ -93,7 +93,9 @@
 
 
 def deal_kernel(q_ref, k_ref, v_ref, id_ref, *refs):
-    outs, arrive = refs[:-1], refs[-1]
+    outs, (held, arrive, told) = refs[:-3], refs[-3:]
+    tell = pltpu.make_async_copy(id_ref, held, told)
+    tell.start()
     rows, feat = q_ref.shape
     width = feat // SQUAD
     corner = corner_of()
@@ -114,7 +116,8 @@
         ]
     for copy in copies:
         copy.start()
-    ids = (id_ref[...] + 1).astype(jnp.float32)
+    tell.wait()
+    ids = (held[...] + 1).astype(jnp.float32)
     spare = jnp.zeros((TAG - ids.shape[0], LANES), jnp.float32)
     ids = jnp.concatenate([ids, spare], axis=0)
     tag = jnp.concatenate([ids] * (width // LANES), axis=1).astype(jnp.bfloat16)
@@ -129,20 +132,24 @@
     rows, feat = queries.shape
     tall = [rows + TAG, 2 * rows + TAG] + [3 * rows + TAG] * (SQUAD - 1)
     shapes = [(x, feat // SQUAD) for x in tall]
-    held = [pltpu.with_memory_space_constraint(x, pltpu.HBM) for x in (queries, keys, values)]
+    held = [pltpu.with_memory_space_constraint(x, pltpu.HBM) for x in (queries, keys, values, ids)]
     return list(
         pl.pallas_call(
             deal_kernel,
-            in_specs=[pl.BlockSpec(memory_space=pl.ANY)] * 3 + [VMEM],
+            in_specs=[pl.BlockSpec(memory_space=pl.ANY)] * 4,
             out_specs=[VMEM] * len(tall),
             out_shape=[jax.ShapeDtypeStruct(x, jnp.bfloat16) for x in shapes],
-            scratch_shapes=[pltpu.SemaphoreType.DMA((SQUAD, 3))],
+            scratch_shapes=[
+                pltpu.VMEM(ids.shape, ids.dtype),
+                pltpu.SemaphoreType.DMA((SQUAD, 3)),
+                pltpu.SemaphoreType.DMA,
+            ],
             compiler_params=pltpu.CompilerParams(vmem_limit_bytes=VMEM_LIMIT),
             cost_estimate=pl.CostEstimate(
                 flops=0, bytes_accessed=12 * rows * feat, transcendentals=0
             ),
             name="deal",
-        )(*held, ids)
+        )(*held)
     )
 
 
@@ -231,15 +238,27 @@
         out[width + heads :, cols] = jnp.zeros((TAG - heads, rows), jnp.float32)
 
 
+def ask_kernel(*refs):
+    parts, out = refs[:-1], refs[-1]
+    tall = parts[0].shape[0]
+    corner = corner_of()
+    for k, part in enumerate(parts):
+        block = jnp.bitwise_xor(corner, k)
+
+        @pl.when(block < SQUAD - 1)
+        def _():
+            out[pl.ds(pl.multiple_of(block * tall, TAG), tall), :] = part[:tall]
+
+
 def far_kernel(*refs):
-    asked, near, out, (queries, keys, values) = refs[:2], refs[2:5], refs[5], refs[6:]
+    asked, near, out, (queries, keys, values) = refs[0], refs[1:4], refs[4], refs[5:]
     heads, span, _ = queries.shape
     rows = span // SQUAD
     width = heads * HD
     corner = corner_of()
     tall = rows + TAG
-    asked = [asked[0].at[k * tall : (k + 1) * tall] for k in range(SQUAD - 1)] + [asked[1]]
-    place_queries(asked, corner, rows, queries)
+    blocks = [asked.at[j * tall : (j + 1) * tall] for j in range(SQUAD - 1)]
+    place_queries(blocks, 0, rows, queries)
     place_keys(near_parts(near, rows), corner, 0, rows, keys, values)
     for j in range(SQUAD - 1):
         cols = slice(j * rows, (j + 1) * rows)
@@ -329,15 +348,18 @@
     across = swap(sent[2], 3)
     beside[1], near[0] = lax.optimization_barrier((beside[1], near[0]))
     near.append(climb(jnp.concatenate([x[rows:] for x in beside], axis=0)))
-    back = [descend(jnp.concatenate([asked] + [x[:tall] for x in beside], axis=0))]
+    (back,) = kernel_call(
+        ask_kernel,
+        (asked, *beside, across),
+        [jax.ShapeDtypeStruct(((SQUAD - 1) * tall, width), bf16)],
+        "ask",
+    )
+    back = descend(back)
     near.append(climb(across[rows:]))
-    back.append(descend(across[:tall]))
     tail_k = hyena_k[rows - LANES :].astype(f32)
     tail_v = hyena_v[rows - LANES :].astype(f32)
     rim = lax.ppermute(
-        (tail_k * tail_v).astype(bf16),
-        "ctx",
-        [(i, i + 1) for i in range(count - 1)],
+        (tail_k * tail_v).astype(bf16), "ctx", [(i, i + 1) for i in range(count - 1)]
     )
     own = [asked, kept, *beside, across]
     def store(blocks):
@@ -349,7 +371,7 @@
 
     (far,) = kernel_call(
         far_kernel,
-        (*back, *near),
+        (back, *near),
         [jax.ShapeDtypeStruct((width + TAG, (SQUAD - 1) * rows), bf16)],
         "far",
         store(SQUAD),

time: 71.2 us -> 71 us (level)
  waiting for transfers between devices: 12.3 us -> 13.9 us
  starting transfers between devices: 35.3 us -> 34 us
    ppermute x4, waiting for transfers between devices: 1.34 us -> 3.43 us  [climb(): lax.ppermute(value, 'ctx', [(i, i + SQUAD) for i in range(first, count -...]
    ppermute x2 -> x1, waiting for transfers between devices: 1.97 us -> 0.01 us  [descend(): lax.ppermute(value, 'ctx', [(i, i - SQUAD) for i in range(2 * SQUAD, coun...]
    ppermute x2 -> x1, starting transfers between devices: 4.16 us -> 2.21 us  [descend(): lax.ppermute(value, 'ctx', [(i, i - SQUAD) for i in range(2 * SQUAD, coun...]
    ppermute x6, waiting for transfers between devices: 7.64 us -> 9.17 us  [swap(): return lax.ppermute(value, 'ctx', [(i, i ^ mask) for i in range(count)])]
    ppermute x4, starting transfers between devices: 3.18 us -> 4.43 us  [turn(): lax.ppermute(value, 'tp', [(t, (t + r) % ranks) for t in range(ranks)])]
    pallas_call x5 -> x6, Pallas kernels: 19.7 us -> 19.7 us  [kernel_call(): pl.pallas_call(kernel, in_specs=[VMEM] * len(args), out_specs=[VMEM] * le...]
  transfers between devices with their start and end apart: 17 -> 16, of which waited for: 9 -> 7; matrix products, arithmetic and copies ran while one was open for 0% -> 0% of each run, Pallas kernels for 23% -> 23%
where the time goes in v5:
time: 71 us; the launch traced here: 70.3 us
  starting transfers between devices  34 us (48%)
  Pallas kernels  21.3 us (30%)
  waiting for transfers between devices  13.9 us (20%)
  between operations  0.86 us (1%)
    pallas_call x6, Pallas kernels, kernel_call(): pl.pallas_call(kernel, in_specs=[VMEM] * len(args), out_specs=[VMEM] * le...  19.7 us
    ppermute x4, starting transfers between devices, climb(): lax.ppermute(value, 'ctx', [(i, i + SQUAD) for i in range(first, count -...  13 us
    ppermute x6, starting transfers between devices, swap(): return lax.ppermute(value, 'ctx', [(i, i ^ mask) for i in range(count)])  11.3 us
    ppermute x6, waiting for transfers between devices, swap(): return lax.ppermute(value, 'ctx', [(i, i ^ mask) for i in range(count)])  9.17 us
    ppermute x4, starting transfers between devices, turn(): lax.ppermute(value, 'tp', [(t, (t + r) % ranks) for t in range(ranks)])  4.43 us
    ppermute x4, waiting for transfers between devices, climb(): lax.ppermute(value, 'ctx', [(i, i + SQUAD) for i in range(first, count -...  3.43 us
    ppermute x1, starting transfers between devices, local(): lax.ppermute((tail_k * tail_v).astype(bf16), 'ctx', [(i, i + 1) for i in...  3.12 us
    ppermute x1, starting transfers between devices, descend(): lax.ppermute(value, 'ctx', [(i, i - SQUAD) for i in range(2 * SQUAD, coun...  2.21 us
  transfers between devices with their start and end apart: 16, of which 7 were waited for; matrix products, arithmetic and copies ran while one was open for 0% of the time, Pallas kernels for 23%

profile of v5, /device:TPU:17, one launch (start us, length us, event | category | flops | bytes accessed | tf_op | source)
XLA Modules:
  0.0 70.3 jit_solution(8208467314179976737)
XLA Ops:
  0.6 1.6 %deal.1 = (bf16[272,256]{1,0:T(8,128)(2,1)S(1)}, bf16[528,256]{1,0:T(8,128)(2,1)S(1)}, bf16[784,256]{1,0:T(8,128)(2,1)S(1)}, bf16[784,256]{1,0:T(8,128)(2,1)S(1)}, bf16[784,256]{1,0:T(8,128)(2,1)S(1)}) custom-call(bf16[256,1024]{1,0:T(8,128)(2,1)} %q_ref.2, bf16[256,1024]{1,0:T(8,128)(2,1)} %k_ref.2, bf16[256,1024]{1,0:T(8,128)(2,1)} %v_ref.2, s32[2,128]{1,0:T(2,128)} %bitcast.3), custom_call_target="tpu_custom_call" | custom-call | bytes 3145728 | tf_op jit(solution)/shard_map/deal/pallas_call | solution.py:137
  2.2 1.3 %collective-permute-start.1 = (bf16[784,256]{1,0:T(8,128)(2,1)S(1)}, bf16[784,256]{1,0:T(8,128)(2,1)S(1)}, u32[]{:S(2)}, u32[]{:S(2)}) collective-permute-start(bf16[784,256]{1,0:T(8,128)(2,1)S(1)} %get-tuple-element.25), channel_id=1, source_target_pairs={{0,2},{2,0},{4,6},{6,4},{8,10},{10,8},{12,14},{14,12},{16,18},{18,... | collective-permute-start | bytes 1204232 | tf_op jit(solution)/shard_map/ppermute | solution.py:331
  3.5 1.2 %collective-permute-start.2 = (bf16[784,256]{1,0:T(8,128)(2,1)S(1)}, bf16[784,256]{1,0:T(8,128)(2,1)S(1)}, u32[]{:S(2)}, u32[]{:S(2)}) collective-permute-start(bf16[784,256]{1,0:T(8,128)(2,1)S(1)} %get-tuple-element.27), channel_id=1, source_target_pairs={{0,4},{2,6},{4,0},{6,2},{8,12},{10,14},{12,8},{14,10},{16,20},{18,... | collective-permute-start | bytes 1204232 | tf_op jit(solution)/shard_map/ppermute | solution.py:331
  4.8 3.2 %collective-permute-start.3 = (bf16[528,256]{1,0:T(8,128)(2,1)S(1)}, bf16[528,256]{1,0:T(8,128)(2,1)S(1)}, u32[]{:S(2)}, u32[]{:S(2)}) collective-permute-start(bf16[528,256]{1,0:T(8,128)(2,1)S(1)} %get-tuple-element.23.refs_1_), channel_id=1, source_target_pairs={{0,8},{2,10},{4,12},{6,14},{8,16},{10,18},{12,20},{14,22},{16,24},... | collective-permute-start | bytes 811016 | tf_op jit(solution)/shard_map/ppermute | solution.py:334
  8.0 4.5 %collective-permute-done.1.refs_2_.refs_1_ = bf16[784,256]{1,0:T(8,128)(2,1)S(1)} collective-permute-done((bf16[784,256]{1,0:T(8,128)(2,1)S(1)}, bf16[784,256]{1,0:T(8,128)(2,1)S(1)}, u32[]{:S(2)}, u32[]{:S(2)}) %collective-permute-start.1) | collective-permute-done | bytes 401440 | tf_op jit(solution)/shard_map/ppermute | solution.py:331
  12.5 2.2 %collective-permute-start.4 = (bf16[784,256]{1,0:T(8,128)(2,1)S(1)}, bf16[784,256]{1,0:T(8,128)(2,1)S(1)}, u32[]{:S(2)}, u32[]{:S(2)}) collective-permute-start(bf16[784,256]{1,0:T(8,128)(2,1)S(1)} %get-tuple-element.29), channel_id=1, source_target_pairs={{0,6},{2,4},{4,2},{6,0},{8,14},{10,12},{12,10},{14,8},{16,22},{18,... | collective-permute-start | bytes 1204232 | tf_op jit(solution)/shard_map/ppermute | solution.py:331
  14.7 3.2 %collective-permute-start.5 = (bf16[1056,256]{1,0:T(8,128)(2,1)S(1)}, bf16[1056,256]{1,0:T(8,128)(2,1)S(1)}, u32[]{:S(2)}, u32[]{:S(2)}) collective-permute-start(bf16[1056,256]{1,0:T(8,128)(2,1)S(1)} %pad_maximum_fusion), channel_id=1, source_target_pairs={{0,8},{2,10},{4,12},{6,14},{8,16},{10,18},{12,20},{14,22},{16,24},... | collective-permute-start | bytes 1622024 | tf_op jit(solution)/shard_map/ppermute | solution.py:334
  17.9 4.7 %collective-permute-done.4.refs_4_.refs_3_ = bf16[784,256]{1,0:T(8,128)(2,1)S(1)} collective-permute-done((bf16[784,256]{1,0:T(8,128)(2,1)S(1)}, bf16[784,256]{1,0:T(8,128)(2,1)S(1)}, u32[]{:S(2)}, u32[]{:S(2)}) %collective-permute-start.4) | collective-permute-done | bytes 401440 | tf_op jit(solution)/shard_map/ppermute | solution.py:331
  22.6 2.2 %collective-permute-start.7 = (bf16[816,256]{1,0:T(8,128)(2,1)S(1)}, bf16[816,256]{1,0:T(8,128)(2,1)S(1)}, u32[]{:S(2)}, u32[]{:S(2)}) collective-permute-start(bf16[816,256]{1,0:T(8,128)(2,1)S(1)} %ask.1), channel_id=1, source_target_pairs={{16,8},{18,10},{20,12},{22,14},{24,16},{26,18},{28,20},{30,22},{17... | collective-permute-start | bytes 1253384 | tf_op jit(solution)/shard_map/ppermute | solution.py:337
  24.9 3.2 %collective-permute-start.6 = (bf16[528,256]{1,0:T(8,128)(2,1)S(1)}, bf16[528,256]{1,0:T(8,128)(2,1)S(1)}, u32[]{:S(2)}, u32[]{:S(2)}) collective-permute-start(bf16[528,256]{1,0:T(8,128)(2,1)S(1)} %slice.20), channel_id=1, source_target_pairs={{0,8},{2,10},{4,12},{6,14},{8,16},{10,18},{12,20},{14,22},{16,24},... | collective-permute-start | bytes 811016 | tf_op jit(solution)/shard_map/ppermute | solution.py:334
  28.3 3.1 %collective-permute-start = (bf16[128,2048]{1,0:T(8,128)(2,1)S(1)}, bf16[128,2048]{1,0:T(8,128)(2,1)S(1)}, u32[]{:S(2)}, u32[]{:S(2)}) collective-permute-start(bf16[128,2048]{1,0:T(8,128)(2,1)S(1)} %multiply_convert_fusion), channel_id=1, source_target_pairs={{0,2},{2,4},{4,6},{6,8},{8,10},{10,12},{12,14},{14,16},{16,18},{18... | collective-permute-start | bytes 1572872 | tf_op jit(solution)/shard_map/ppermute | solution.py:361
  31.4 3.4 %collective-permute-done.6.refs_7_.refs_3_ = bf16[528,256]{1,0:T(8,128)(2,1)S(1)} collective-permute-done((bf16[528,256]{1,0:T(8,128)(2,1)S(1)}, bf16[528,256]{1,0:T(8,128)(2,1)S(1)}, u32[]{:S(2)}, u32[]{:S(2)}) %collective-permute-start.6) | collective-permute-done | bytes 270368 | tf_op jit(solution)/shard_map/ppermute | solution.py:334
  34.9 2.6 %far.1 = bf16[272,768]{1,0:T(8,128)(2,1)S(1)} custom-call(bf16[816,256]{1,0:T(8,128)(2,1)S(1)} %collective-permute-done.7.refs_0_, bf16[528,256]{1,0:T(8,128)(2,1)S(1)} %collective-permute-done.3.refs_5_.refs_1_, bf16[1056,256]{1,0:T(8,128)(2,1)S(1)} %collective-permute-done.5.refs_6_.refs_2_, bf16[528,256]{1,0:T(8,128)(2,1)S(1)} %collective-permute-done.6.refs_7_.refs_3_), custom_call_target="tpu_custom_call" | custom-call | flops 402653184 | bytes 1916928 | tf_op jit(solution)/shard_map/far/pallas_call | solution.py:26
  37.4 3.4 %collective-permute-start.8 = (bf16[272,768]{1,0:T(8,128)(2,1)S(1)}, bf16[272,768]{1,0:T(8,128)(2,1)S(1)}, u32[]{:S(2)}, u32[]{:S(2)}) collective-permute-start(bf16[272,768]{1,0:T(8,128)(2,1)S(1)} %far.1), channel_id=1, source_target_pairs={{8,16},{10,18},{12,20},{14,22},{16,24},{18,26},{20,28},{22,30},{9,... | collective-permute-start | bytes 1253384 | tf_op jit(solution)/shard_map/ppermute | solution.py:334
  40.8 8.0 %main.1.main_ref = f32[272,1024]{1,0:T(8,128)S(1)} custom-call(bf16[272,256]{1,0:T(8,128)(2,1)S(1)} %get-tuple-element.22.refs_0_, bf16[528,256]{1,0:T(8,128)(2,1)S(1)} %get-tuple-element.23.refs_1_, bf16[784,256]{1,0:T(8,128)(2,1)S(1)} %collective-permute-done.1.refs_2_.refs_1_, bf16[784,256]{1,0:T(8,128)(2,1)S(1)} %collective-permute-done.2.refs_3_.refs_2_, ...), custom_call_target="tpu_custom_call" | custom-call | flops 1744830464 | bytes 3809280 | tf_op jit(solution)/shard_map/main/pallas_call | solution.py:26
  48.9 0.4 merge.1
  49.4 6.3 %collective-permute-start.11 = (bf16[256,256]{1,0:T(8,128)(2,1)S(1)}, bf16[256,256]{1,0:T(8,128)(2,1)S(1)}, u32[]{:S(2)}, u32[]{:S(2)}) collective-permute-start(bf16[256,256]{1,0:T(8,128)(2,1)S(1)} %get-tuple-element.36), channel_id=1, source_target_pairs={{0,6},{2,4},{4,2},{6,0},{8,14},{10,12},{12,10},{14,8},{16,22},{18,... | collective-permute-start | bytes 393224 | tf_op jit(solution)/shard_map/ppermute | solution.py:331
  55.9 5.2 %hyena.1 = bf16[256,2048]{1,0:T(8,128)(2,1)} custom-call(bf16[256,2048]{1,0:T(8,128)(2,1)S(1)} %copy-done.2, bf16[256,2048]{1,0:T(8,128)(2,1)S(1)} %copy-done, bf16[256,2048]{1,0:T(8,128)(2,1)S(1)} %copy-done.1, bf16[128,2048]{1,0:T(8,128)(2,1)S(1)} %collective-permute-done.rim_ref, bf16[128,128]{1,0:T(8,128)(2,1)S(1)} %copy-done.3, ...), custom_call_target="tpu_custom_call" | custom-call | flops 4294967296 | bytes 4755456 | tf_op jit(solution)/shard_map/hyena/pallas_call | solution.py:26
  61.1 3.8 %collective-permute-start.12 = (bf16[256,256]{1,0:T(8,128)(2,1)S(1)}, bf16[256,256]{1,0:T(8,128)(2,1)S(1)}, u32[]{:S(2)}, u32[]{:S(2)}) collective-permute-start(bf16[256,256]{1,0:T(8,128)(2,1)S(1)} %get-tuple-element.38.refs_0_), channel_id=1, source_target_pairs={{0,1},{1,0},{2,3},{3,2},{4,5},{5,4},{6,7},{7,6},{8,9},{9,8},{10,11... | collective-permute-start | bytes 393224 | tf_op jit(solution)/shard_map/ppermute | solution.py:402
  65.0 0.4 collective-permute-start.14
  65.5 0.4 collective-permute-done.12.refs_4_
  65.9 0.4 collective-permute-done.13.refs_5_
  66.5 0.3 collective-permute-done.15.refs_7_
  66.8 3.5 %project.1 = bf16[256,2048]{1,0:T(8,128)(2,1)} custom-call(bf16[256,256]{1,0:T(8,128)(2,1)S(1)} %get-tuple-element.38.refs_0_, bf16[256,256]{1,0:T(8,128)(2,1)S(1)} %collective-permute-done.9.refs_1_, bf16[256,256]{1,0:T(8,128)(2,1)S(1)} %collective-permute-done.10.refs_2_, bf16[256,256]{1,0:T(8,128)(2,1)S(1)} %collective-permute-done.11.refs_3_, ...), custom_call_target="tpu_custom_call" | custom-call | flops 2147483648 | bytes 10485760 | tf_op jit(solution)/shard_map/project/pallas_call | solution.py:26
  (36 shorter events, 0.9 us)
Async XLA Ops:
  2.2 10.2 %collective-permute-start.1 = (bf16[784,256]{1,0:T(8,128)(2,1)S(1)}, bf16[784,256]{1,0:T(8,128)(2,1)S(1)}, u32[]{:S(2)}, u32[]{:S(2)}) collective-permute-start(bf16[784,256]{1,0:T(8,128)(2,1)S(1)} %get-tuple-element.25), channel_id=1, source_target_pairs={{0,2},{2,0},{4,6},{6,4},{8,10},{10,8},{12,14},{14,12},{16,18},{18,... | collective-permute-start | bytes 1204232 | tf_op jit(solution)/shard_map/ppermute | solution.py:331
  3.5 11.1 %collective-permute-start.2 = (bf16[784,256]{1,0:T(8,128)(2,1)S(1)}, bf16[784,256]{1,0:T(8,128)(2,1)S(1)}, u32[]{:S(2)}, u32[]{:S(2)}) collective-permute-start(bf16[784,256]{1,0:T(8,128)(2,1)S(1)} %get-tuple-element.27), channel_id=1, source_target_pairs={{0,4},{2,6},{4,0},{6,2},{8,12},{10,14},{12,8},{14,10},{16,20},{18,... | collective-permute-start | bytes 1204232 | tf_op jit(solution)/shard_map/ppermute | solution.py:331
  4.8 9.9 %collective-permute-start.3 = (bf16[528,256]{1,0:T(8,128)(2,1)S(1)}, bf16[528,256]{1,0:T(8,128)(2,1)S(1)}, u32[]{:S(2)}, u32[]{:S(2)}) collective-permute-start(bf16[528,256]{1,0:T(8,128)(2,1)S(1)} %get-tuple-element.23.refs_1_), channel_id=1, source_target_pairs={{0,8},{2,10},{4,12},{6,14},{8,16},{10,18},{12,20},{14,22},{16,24},... | collective-permute-start | bytes 811016 | tf_op jit(solution)/shard_map/ppermute | solution.py:334
  12.5 10.1 %collective-permute-start.4 = (bf16[784,256]{1,0:T(8,128)(2,1)S(1)}, bf16[784,256]{1,0:T(8,128)(2,1)S(1)}, u32[]{:S(2)}, u32[]{:S(2)}) collective-permute-start(bf16[784,256]{1,0:T(8,128)(2,1)S(1)} %get-tuple-element.29), channel_id=1, source_target_pairs={{0,6},{2,4},{4,2},{6,0},{8,14},{10,12},{12,10},{14,8},{16,22},{18,... | collective-permute-start | bytes 1204232 | tf_op jit(solution)/shard_map/ppermute | solution.py:331
  14.7 16.7 %collective-permute-start.5 = (bf16[1056,256]{1,0:T(8,128)(2,1)S(1)}, bf16[1056,256]{1,0:T(8,128)(2,1)S(1)}, u32[]{:S(2)}, u32[]{:S(2)}) collective-permute-start(bf16[1056,256]{1,0:T(8,128)(2,1)S(1)} %pad_maximum_fusion), channel_id=1, source_target_pairs={{0,8},{2,10},{4,12},{6,14},{8,16},{10,18},{12,20},{14,22},{16,24},... | collective-permute-start | bytes 1622024 | tf_op jit(solution)/shard_map/ppermute | solution.py:334
  22.6 5.5 %copy-start = (bf16[256,2048]{1,0:T(8,128)(2,1)S(1)}, bf16[256,2048]{1,0:T(8,128)(2,1)}, u32[]{:S(2)}) copy-start(bf16[256,2048]{1,0:T(8,128)(2,1)} %k_ref.3) | copy-start | bytes 3145732
  22.6 5.5 %copy-start.1 = (bf16[256,2048]{1,0:T(8,128)(2,1)S(1)}, bf16[256,2048]{1,0:T(8,128)(2,1)}, u32[]{:S(2)}) copy-start(bf16[256,2048]{1,0:T(8,128)(2,1)} %v_ref.3) | copy-start | bytes 3145732
  22.6 12.2 %collective-permute-start.7 = (bf16[816,256]{1,0:T(8,128)(2,1)S(1)}, bf16[816,256]{1,0:T(8,128)(2,1)S(1)}, u32[]{:S(2)}, u32[]{:S(2)}) collective-permute-start(bf16[816,256]{1,0:T(8,128)(2,1)S(1)} %ask.1), channel_id=1, source_target_pairs={{16,8},{18,10},{20,12},{22,14},{24,16},{26,18},{28,20},{30,22},{17... | collective-permute-start | bytes 1253384 | tf_op jit(solution)/shard_map/ppermute | solution.py:337
  24.9 10.0 %collective-permute-start.6 = (bf16[528,256]{1,0:T(8,128)(2,1)S(1)}, bf16[528,256]{1,0:T(8,128)(2,1)S(1)}, u32[]{:S(2)}, u32[]{:S(2)}) collective-permute-start(bf16[528,256]{1,0:T(8,128)(2,1)S(1)} %slice.20), channel_id=1, source_target_pairs={{0,8},{2,10},{4,12},{6,14},{8,16},{10,18},{12,20},{14,22},{16,24},... | collective-permute-start | bytes 811016 | tf_op jit(solution)/shard_map/ppermute | solution.py:334
  28.3 12.5 %copy-start.4 = (bf16[2048]{0:T(1024)(128)(2,1)S(1)}, bf16[2048]{0:T(1024)(128)(2,1)}, u32[]{:S(2)}) copy-start(bf16[2048]{0:T(1024)(128)(2,1)} %param.14) | copy-start | bytes 12292
  28.3 21.0 %collective-permute-start = (bf16[128,2048]{1,0:T(8,128)(2,1)S(1)}, bf16[128,2048]{1,0:T(8,128)(2,1)S(1)}, u32[]{:S(2)}, u32[]{:S(2)}) collective-permute-start(bf16[128,2048]{1,0:T(8,128)(2,1)S(1)} %multiply_convert_fusion), channel_id=1, source_target_pairs={{0,2},{2,4},{4,6},{6,8},{8,10},{10,12},{12,14},{14,16},{16,18},{18... | collective-permute-start | bytes 1572872 | tf_op jit(solution)/shard_map/ppermute | solution.py:361
  37.4 11.5 %collective-permute-start.8 = (bf16[272,768]{1,0:T(8,128)(2,1)S(1)}, bf16[272,768]{1,0:T(8,128)(2,1)S(1)}, u32[]{:S(2)}, u32[]{:S(2)}) collective-permute-start(bf16[272,768]{1,0:T(8,128)(2,1)S(1)} %far.1), channel_id=1, source_target_pairs={{8,16},{10,18},{12,20},{14,22},{16,24},{18,26},{20,28},{22,30},{9,... | collective-permute-start | bytes 1253384 | tf_op jit(solution)/shard_map/ppermute | solution.py:334
  48.9 7.0 %copy-start.2 = (bf16[256,2048]{1,0:T(8,128)(2,1)S(1)}, bf16[256,2048]{1,0:T(8,128)(2,1)}, u32[]{:S(2)}) copy-start(bf16[256,2048]{1,0:T(8,128)(2,1)} %q_ref.3) | copy-start | bytes 3145732
  48.9 7.0 %copy-start.3 = (bf16[128,128]{1,0:T(8,128)(2,1)S(1)}, bf16[128,128]{1,0:T(8,128)(2,1)}, u32[]{:S(2)}) copy-start(bf16[128,128]{1,0:T(8,128)(2,1)} %taps_ref.1) | copy-start | bytes 98308
  49.3 11.8 %collective-permute-start.10 = (bf16[256,256]{1,0:T(8,128)(2,1)S(1)}, bf16[256,256]{1,0:T(8,128)(2,1)S(1)}, u32[]{:S(2)}, u32[]{:S(2)}) collective-permute-start(bf16[256,256]{1,0:T(8,128)(2,1)S(1)} %get-tuple-element.35), channel_id=1, source_target_pairs={{0,4},{2,6},{4,0},{6,2},{8,12},{10,14},{12,8},{14,10},{16,20},{18,... | collective-permute-start | bytes 393224 | tf_op jit(solution)/shard_map/ppermute | solution.py:331
  49.4 11.8 %collective-permute-start.11 = (bf16[256,256]{1,0:T(8,128)(2,1)S(1)}, bf16[256,256]{1,0:T(8,128)(2,1)S(1)}, u32[]{:S(2)}, u32[]{:S(2)}) collective-permute-start(bf16[256,256]{1,0:T(8,128)(2,1)S(1)} %get-tuple-element.36), channel_id=1, source_target_pairs={{0,6},{2,4},{4,2},{6,0},{8,14},{10,12},{12,10},{14,8},{16,22},{18,... | collective-permute-start | bytes 393224 | tf_op jit(solution)/shard_map/ppermute | solution.py:331
  55.7 11.1 %slice-start = ((s8[8388608]{0:T(1024)(128)(4,1)}), s8[4194304]{0:T(1024)(128)(4,1)S(1)}, s32[]{:S(2)}) async-start(s8[8388608]{0:T(1024)(128)(4,1)} %bitcast.1), calls=%async_computation | async-start | bytes 8388608
  55.7 11.1 %slice-start.1 = ((s8[8388608]{0:T(1024)(128)(4,1)}), s8[4194304]{0:T(1024)(128)(4,1)S(1)}, s32[]{:S(2)}) async-start(s8[8388608]{0:T(1024)(128)(4,1)} %bitcast.1), calls=%async_computation.1 | async-start | bytes 8388608
  55.7 5.4 %collective-permute-start.9 = (bf16[256,256]{1,0:T(8,128)(2,1)S(1)}, bf16[256,256]{1,0:T(8,128)(2,1)S(1)}, u32[]{:S(2)}, u32[]{:S(2)}) collective-permute-start(bf16[256,256]{1,0:T(8,128)(2,1)S(1)} %get-tuple-element.34), channel_id=1, source_target_pairs={{0,2},{2,0},{4,6},{6,4},{8,10},{10,8},{12,14},{14,12},{16,18},{18,... | collective-permute-start | bytes 393224 | tf_op jit(solution)/shard_map/ppermute | solution.py:331
  61.1 4.8 %collective-permute-start.12 = (bf16[256,256]{1,0:T(8,128)(2,1)S(1)}, bf16[256,256]{1,0:T(8,128)(2,1)S(1)}, u32[]{:S(2)}, u32[]{:S(2)}) collective-permute-start(bf16[256,256]{1,0:T(8,128)(2,1)S(1)} %get-tuple-element.38.refs_0_), channel_id=1, source_target_pairs={{0,1},{1,0},{2,3},{3,2},{4,5},{5,4},{6,7},{7,6},{8,9},{9,8},{10,11... | collective-permute-start | bytes 393224 | tf_op jit(solution)/shard_map/ppermute | solution.py:402
  65.0 1.3 %collective-permute-start.13 = (bf16[256,256]{1,0:T(8,128)(2,1)S(1)}, bf16[256,256]{1,0:T(8,128)(2,1)S(1)}, u32[]{:S(2)}, u32[]{:S(2)}) collective-permute-start(bf16[256,256]{1,0:T(8,128)(2,1)S(1)} %collective-permute-done.9.refs_1_), channel_id=1, source_target_pairs={{0,1},{1,0},{2,3},{3,2},{4,5},{5,4},{6,7},{7,6},{8,9},{9,8},{10,11... | collective-permute-start | bytes 393224 | tf_op jit(solution)/shard_map/ppermute | solution.py:402
  65.0 1.5 %collective-permute-start.14 = (bf16[256,256]{1,0:T(8,128)(2,1)S(1)}, bf16[256,256]{1,0:T(8,128)(2,1)S(1)}, u32[]{:S(2)}, u32[]{:S(2)}) collective-permute-start(bf16[256,256]{1,0:T(8,128)(2,1)S(1)} %collective-permute-done.10.refs_2_), channel_id=1, source_target_pairs={{0,1},{1,0},{2,3},{3,2},{4,5},{5,4},{6,7},{7,6},{8,9},{9,8},{10,11... | collective-permute-start | bytes 393224 | tf_op jit(solution)/shard_map/ppermute | solution.py:402
  65.5 1.3 %collective-permute-start.15 = (bf16[256,256]{1,0:T(8,128)(2,1)S(1)}, bf16[256,256]{1,0:T(8,128)(2,1)S(1)}, u32[]{:S(2)}, u32[]{:S(2)}) collective-permute-start(bf16[256,256]{1,0:T(8,128)(2,1)S(1)} %collective-permute-done.11.refs_3_), channel_id=1, source_target_pairs={{0,1},{1,0},{2,3},{3,2},{4,5},{5,4},{6,7},{7,6},{8,9},{9,8},{10,11... | collective-permute-start | bytes 393224 | tf_op jit(solution)/shard_map/ppermute | solution.py:402

commit v6 on v5

--- a/solution.py
+++ b/solution.py
@@ -35,7 +35,7 @@
     )(*args))
 
 
-def hyena_kernel(q_ref, k_ref, v_ref, rim_ref, taps_ref, direct_ref, out_ref, taps):
+def hyena_kernel(q_ref, k_ref, v_ref, next_rim, far_rim, taps_ref, direct_ref, out_ref, taps, rim):
     rows, chans = q_ref.shape
     groups = taps_ref.shape[0]
     group = chans // groups
@@ -49,6 +49,16 @@
     taps[...] = jnp.dot(taps_ref[...], turn, preferred_element_type=jnp.float32)
     lane_group = lax.broadcasted_iota(jnp.int32, (LANES, windows * LANES), 1) % LANES // group
 
+    relayed = (corner_of() == 0) & (lax.axis_index("tp") % 2 == 1)
+
+    @pl.when(relayed)
+    def _():
+        rim[...] = far_rim[...]
+
+    @pl.when(jnp.logical_not(relayed))
+    def _():
+        rim[...] = next_rim[...]
+
     @pl.loop(0, chans // LANES, unroll=2)
     def _(tile):
         cols = pl.ds(pl.multiple_of(tile * LANES, LANES), LANES)
@@ -56,7 +66,7 @@
         mixed = (k_ref[:, cols].astype(jnp.float32) * v_ref[:, cols].astype(jnp.float32)).astype(
             jnp.bfloat16
         )
-        full = jnp.concatenate([rim_ref[:, cols], mixed], axis=0)
+        full = jnp.concatenate([rim[:, cols], mixed], axis=0)
         stacked = jnp.concatenate(
             [full[w * LANES : (w + 2) * LANES] for w in range(windows)], axis=1
         )
@@ -77,16 +87,16 @@
         ).astype(jnp.bfloat16)
 
 
-def hyena(hyena_q, hyena_k, hyena_v, rim, filters, direct):
+def hyena(hyena_q, hyena_k, hyena_v, rims, filters, direct):
     rows, chans = hyena_q.shape
     groups, kernel = filters.shape
     taps = jnp.pad(filters, ((0, 0), (0, LANES - kernel)))
     (out,) = kernel_call(
         hyena_kernel,
-        (hyena_q, hyena_k, hyena_v, rim, taps, direct[None]),
+        (hyena_q, hyena_k, hyena_v, *rims, taps, direct[None]),
         [jax.ShapeDtypeStruct((rows, chans), jnp.bfloat16)],
         "hyena",
-        [pltpu.VMEM((groups, LANES), jnp.float32)],
+        [pltpu.VMEM((groups, LANES), jnp.float32), pltpu.VMEM((LANES, chans), jnp.bfloat16)],
         flops=4 * rows * chans * 2 * LANES * 8,
     )
     return out
@@ -358,9 +368,25 @@
     near.append(climb(across[rows:]))
     tail_k = hyena_k[rows - LANES :].astype(f32)
     tail_v = hyena_v[rows - LANES :].astype(f32)
-    rim = lax.ppermute(
-        (tail_k * tail_v).astype(bf16), "ctx", [(i, i + 1) for i in range(count - 1)]
-    )
+    tail = (tail_k * tail_v).astype(bf16)
+
+    def hand(value, pairs):
+        ends = [(i * ranks + t, j * ranks + t) for i, j, t in pairs]
+        return lax.ppermute(value, ("ctx", "tp"), ends)
+
+    tail, beside[1] = lax.optimization_barrier((tail, beside[1]))
+    odd = range(1, ranks, 2)
+    ring = hand(
+        tail, [(i, i + 1 - SQUAD, t) for i in range(SQUAD - 1, count, SQUAD) for t in odd]
+    )
+    straight = [
+        (i, i + 1, t)
+        for i in range(count - 1)
+        for t in range(ranks)
+        if (i + 1) % SQUAD or t not in odd
+    ]
+    lifted = [(i, i + SQUAD, t) for i in range(0, count - SQUAD, SQUAD) for t in odd]
+    rims = [hand(tail, straight), hand(ring, lifted)]
     own = [asked, kept, *beside, across]
     def store(blocks):
         return [
@@ -379,6 +405,7 @@
         exps=6 * rows * rows * heads,
     )
     far = climb(far, SQUAD)
+    own[1], *rims = lax.optimization_barrier((own[1], *rims))
     (main,) = kernel_call(
         main_kernel,
         (*own, *near),
@@ -395,8 +422,8 @@
         "merge",
         [pltpu.VMEM((SQUAD, rows, width), bf16)],
     )
-    rim, done[0] = lax.optimization_barrier((rim, done[0]))
-    hyena_out = hyena(hyena_q, hyena_k, hyena_v, rim, filters, direct)
+    *rims, done[0] = lax.optimization_barrier((*rims, done[0]))
+    hyena_out = hyena(hyena_q, hyena_k, hyena_v, rims, filters, direct)
 
     def turn(value, r):
         return lax.ppermute(value, "tp", [(t, (t + r) % ranks) for t in range(ranks)])

time: 71 us -> 71.5 us (level)
  other arithmetic: 0.16 us -> 1.2 us
    ppermute x1 -> x3, starting transfers between devices: 3.12 us -> 6.46 us  [hand(): return lax.ppermute(value, ('ctx', 'tp'), ends)]
    ppermute x6, waiting for transfers between devices: 9.17 us -> 6.68 us  [swap(): return lax.ppermute(value, 'ctx', [(i, i ^ mask) for i in range(count)])]
    ppermute x4, starting transfers between devices: 4.43 us -> 2.34 us  [turn(): lax.ppermute(value, 'tp', [(t, (t + r) % ranks) for t in range(ranks)])]
    ppermute x6, starting transfers between devices: 11.3 us -> 9.56 us  [swap(): return lax.ppermute(value, 'ctx', [(i, i ^ mask) for i in range(count)])]
    ppermute x1 -> x3, waiting for transfers between devices: 0.01 us -> 1.57 us  [hand(): return lax.ppermute(value, ('ctx', 'tp'), ends)]
    convert_element_type x1, other arithmetic: 0.13 us -> 1.17 us  [local(): tail = (tail_k * tail_v).astype(bf16)]
    ppermute x4, waiting for transfers between devices: 3.43 us -> 4.25 us  [climb(): lax.ppermute(value, 'ctx', [(i, i + SQUAD) for i in range(first, count -...]
  transfers between devices with their start and end apart: 16 -> 18, of which waited for: 7 -> 8; matrix products, arithmetic and copies ran while one was open for 0% -> 2% of each run, Pallas kernels for 23% -> 23%
where the time goes in v6:
time: 71.5 us; the launch traced here: 70.8 us
  starting transfers between devices  33.3 us (47%)
  Pallas kernels  21.5 us (30%)
  waiting for transfers between devices  13.8 us (19%)
  other arithmetic  1.2 us (2%)
  between operations  0.91 us (1%)
    pallas_call x6, Pallas kernels, kernel_call(): pl.pallas_call(kernel, in_specs=[VMEM] * len(args), out_specs=[VMEM] * le...  19.9 us
    ppermute x4, starting transfers between devices, climb(): lax.ppermute(value, 'ctx', [(i, i + SQUAD) for i in range(first, count -...  12.8 us
    ppermute x6, starting transfers between devices, swap(): return lax.ppermute(value, 'ctx', [(i, i ^ mask) for i in range(count)])  9.56 us
    ppermute x6, waiting for transfers between devices, swap(): return lax.ppermute(value, 'ctx', [(i, i ^ mask) for i in range(count)])  6.68 us
    ppermute x3, starting transfers between devices, hand(): return lax.ppermute(value, ('ctx', 'tp'), ends)  6.46 us
    ppermute x4, waiting for transfers between devices, climb(): lax.ppermute(value, 'ctx', [(i, i + SQUAD) for i in range(first, count -...  4.25 us
    ppermute x4, starting transfers between devices, turn(): lax.ppermute(value, 'tp', [(t, (t + r) % ranks) for t in range(ranks)])  2.34 us
    ppermute x1, starting transfers between devices, descend(): lax.ppermute(value, 'ctx', [(i, i - SQUAD) for i in range(2 * SQUAD, coun...  2.08 us
  transfers between devices with their start and end apart: 18, of which 8 were waited for; matrix products, arithmetic and copies ran while one was open for 2% of the time, Pallas kernels for 23%

profile of v6, /device:TPU:17, one launch (start us, length us, event | category | flops | bytes accessed | tf_op | source)
XLA Modules:
  0.0 70.8 jit_solution(5346486948955867870)
XLA Ops:
  0.6 1.7 %deal.1 = (bf16[272,256]{1,0:T(8,128)(2,1)S(1)}, bf16[528,256]{1,0:T(8,128)(2,1)S(1)}, bf16[784,256]{1,0:T(8,128)(2,1)S(1)}, bf16[784,256]{1,0:T(8,128)(2,1)S(1)}, bf16[784,256]{1,0:T(8,128)(2,1)S(1)}) custom-call(bf16[256,1024]{1,0:T(8,128)(2,1)} %q_ref.2, bf16[256,1024]{1,0:T(8,128)(2,1)} %k_ref.2, bf16[256,1024]{1,0:T(8,128)(2,1)} %v_ref.2, s32[2,128]{1,0:T(2,128)} %bitcast.3), custom_call_target="tpu_custom_call" | custom-call | bytes 3145728 | tf_op jit(solution)/shard_map/deal/pallas_call | solution.py:147
  2.3 1.3 %collective-permute-start.5 = (bf16[784,256]{1,0:T(8,128)(2,1)S(1)}, bf16[784,256]{1,0:T(8,128)(2,1)S(1)}, u32[]{:S(2)}, u32[]{:S(2)}) collective-permute-start(bf16[784,256]{1,0:T(8,128)(2,1)S(1)} %get-tuple-element.37), channel_id=1, source_target_pairs={{0,2},{2,0},{4,6},{6,4},{8,10},{10,8},{12,14},{14,12},{16,18},{18,... | collective-permute-start | bytes 1204232 | tf_op jit(solution)/shard_map/ppermute | solution.py:341
  3.6 1.2 %collective-permute-start = (bf16[784,256]{1,0:T(8,128)(2,1)S(1)}, bf16[784,256]{1,0:T(8,128)(2,1)S(1)}, u32[]{:S(2)}, u32[]{:S(2)}) collective-permute-start(bf16[784,256]{1,0:T(8,128)(2,1)S(1)} %get-tuple-element.29), channel_id=1, source_target_pairs={{0,4},{2,6},{4,0},{6,2},{8,12},{10,14},{12,8},{14,10},{16,20},{18,... | collective-permute-start | bytes 1204232 | tf_op jit(solution)/shard_map/ppermute | solution.py:341
  4.8 3.2 %collective-permute-start.1 = (bf16[528,256]{1,0:T(8,128)(2,1)S(1)}, bf16[528,256]{1,0:T(8,128)(2,1)S(1)}, u32[]{:S(2)}, u32[]{:S(2)}) collective-permute-start(bf16[528,256]{1,0:T(8,128)(2,1)S(1)} %get-tuple-element.35.refs_1_), channel_id=1, source_target_pairs={{0,8},{2,10},{4,12},{6,14},{8,16},{10,18},{12,20},{14,22},{16,24},... | collective-permute-start | bytes 811016 | tf_op jit(solution)/shard_map/ppermute | solution.py:344
  8.0 4.5 %collective-permute-done.5.refs_2_.refs_1_ = bf16[784,256]{1,0:T(8,128)(2,1)S(1)} collective-permute-done((bf16[784,256]{1,0:T(8,128)(2,1)S(1)}, bf16[784,256]{1,0:T(8,128)(2,1)S(1)}, u32[]{:S(2)}, u32[]{:S(2)}) %collective-permute-start.5) | collective-permute-done | bytes 401440 | tf_op jit(solution)/shard_map/ppermute | solution.py:341
  12.5 2.2 %collective-permute-start.6 = (bf16[784,256]{1,0:T(8,128)(2,1)S(1)}, bf16[784,256]{1,0:T(8,128)(2,1)S(1)}, u32[]{:S(2)}, u32[]{:S(2)}) collective-permute-start(bf16[784,256]{1,0:T(8,128)(2,1)S(1)} %get-tuple-element.40), channel_id=1, source_target_pairs={{0,6},{2,4},{4,2},{6,0},{8,14},{10,12},{12,10},{14,8},{16,22},{18,... | collective-permute-start | bytes 1204232 | tf_op jit(solution)/shard_map/ppermute | solution.py:341
  14.7 1.2 %multiply_convert_fusion = bf16[128,2048]{1,0:T(8,128)(2,1)S(1)} fusion(bf16[256,2048]{1,0:T(8,128)(2,1)} %v_ref.3, bf16[256,2048]{1,0:T(8,128)(2,1)S(1)} %copy-done), kind=kLoop, calls=%fused_computation | loop fusion | flops 1048576 | bytes 1572864 | tf_op jit(solution)/shard_map/convert_element_type | solution.py:371
  15.9 1.3 %collective-permute-start.3 = (bf16[128,2048]{1,0:T(8,128)(2,1)S(1)}, bf16[128,2048]{1,0:T(8,128)(2,1)S(1)}, u32[]{:S(2)}, u32[]{:S(2)}) collective-permute-start(bf16[128,2048]{1,0:T(8,128)(2,1)S(1)} %multiply_convert_fusion), channel_id=1, source_target_pairs={{7,1},{15,9},{23,17},{31,25}} | collective-permute-start | bytes 1572872 | tf_op jit(solution)/shard_map/ppermute | solution.py:375
  17.3 3.2 %collective-permute-start.7 = (bf16[1056,256]{1,0:T(8,128)(2,1)S(1)}, bf16[1056,256]{1,0:T(8,128)(2,1)S(1)}, u32[]{:S(2)}, u32[]{:S(2)}) collective-permute-start(bf16[1056,256]{1,0:T(8,128)(2,1)S(1)} %pad_maximum_fusion), channel_id=1, source_target_pairs={{0,8},{2,10},{4,12},{6,14},{8,16},{10,18},{12,20},{14,22},{16,24},... | collective-permute-start | bytes 1622024 | tf_op jit(solution)/shard_map/ppermute | solution.py:344
  20.5 2.2 %collective-permute-done.6.refs_4_.refs_3_ = bf16[784,256]{1,0:T(8,128)(2,1)S(1)} collective-permute-done((bf16[784,256]{1,0:T(8,128)(2,1)S(1)}, bf16[784,256]{1,0:T(8,128)(2,1)S(1)}, u32[]{:S(2)}, u32[]{:S(2)}) %collective-permute-start.6) | collective-permute-done | bytes 401440 | tf_op jit(solution)/shard_map/ppermute | solution.py:341
  22.7 2.1 %collective-permute-start.9 = (bf16[816,256]{1,0:T(8,128)(2,1)S(1)}, bf16[816,256]{1,0:T(8,128)(2,1)S(1)}, u32[]{:S(2)}, u32[]{:S(2)}) collective-permute-start(bf16[816,256]{1,0:T(8,128)(2,1)S(1)} %ask.1), channel_id=1, source_target_pairs={{16,8},{18,10},{20,12},{22,14},{24,16},{26,18},{28,20},{30,22},{17... | collective-permute-start | bytes 1253384 | tf_op jit(solution)/shard_map/ppermute | solution.py:347
  24.9 3.2 %collective-permute-start.8 = (bf16[528,256]{1,0:T(8,128)(2,1)S(1)}, bf16[528,256]{1,0:T(8,128)(2,1)S(1)}, u32[]{:S(2)}, u32[]{:S(2)}) collective-permute-start(bf16[528,256]{1,0:T(8,128)(2,1)S(1)} %slice.20), channel_id=1, source_target_pairs={{0,8},{2,10},{4,12},{6,14},{8,16},{10,18},{12,20},{14,22},{16,24},... | collective-permute-start | bytes 811016 | tf_op jit(solution)/shard_map/ppermute | solution.py:344
  28.1 3.1 %collective-permute-start.2 = (bf16[128,2048]{1,0:T(8,128)(2,1)S(1)}, bf16[128,2048]{1,0:T(8,128)(2,1)S(1)}, u32[]{:S(2)}, u32[]{:S(2)}) collective-permute-start(bf16[128,2048]{1,0:T(8,128)(2,1)S(1)} %multiply_convert_fusion), channel_id=1, source_target_pairs={{0,2},{1,3},{2,4},{3,5},{4,6},{5,7},{6,8},{8,10},{9,11},{10,12},{1... | collective-permute-start | bytes 1572872 | tf_op jit(solution)/shard_map/ppermute | solution.py:375
  31.3 2.0 %collective-permute-start.4 = (bf16[128,2048]{1,0:T(8,128)(2,1)S(1)}, bf16[128,2048]{1,0:T(8,128)(2,1)S(1)}, u32[]{:S(2)}, u32[]{:S(2)}) collective-permute-start(bf16[128,2048]{1,0:T(8,128)(2,1)S(1)} %collective-permute-done.3), channel_id=1, source_target_pairs={{1,9},{9,17},{17,25}} | collective-permute-start | bytes 1572872 | tf_op jit(solution)/shard_map/ppermute | solution.py:375
  33.3 4.2 %collective-permute-done.8.refs_7_.refs_3_ = bf16[528,256]{1,0:T(8,128)(2,1)S(1)} collective-permute-done((bf16[528,256]{1,0:T(8,128)(2,1)S(1)}, bf16[528,256]{1,0:T(8,128)(2,1)S(1)}, u32[]{:S(2)}, u32[]{:S(2)}) %collective-permute-start.8) | collective-permute-done | bytes 270368 | tf_op jit(solution)/shard_map/ppermute | solution.py:344
  37.5 2.6 %far.1 = bf16[272,768]{1,0:T(8,128)(2,1)S(1)} custom-call(bf16[816,256]{1,0:T(8,128)(2,1)S(1)} %collective-permute-done.9.refs_0_, bf16[528,256]{1,0:T(8,128)(2,1)S(1)} %collective-permute-done.1.refs_5_.refs_1_, bf16[1056,256]{1,0:T(8,128)(2,1)S(1)} %collective-permute-done.7.refs_6_.refs_2_, bf16[528,256]{1,0:T(8,128)(2,1)S(1)} %collective-permute-done.8.refs_7_.refs_3_), custom_call_target="tpu_custom_call" | custom-call | flops 402653184 | bytes 1916928 | tf_op jit(solution)/shard_map/far/pallas_call | solution.py:26
  40.1 3.2 %collective-permute-start.10 = (bf16[272,768]{1,0:T(8,128)(2,1)S(1)}, bf16[272,768]{1,0:T(8,128)(2,1)S(1)}, u32[]{:S(2)}, u32[]{:S(2)}) collective-permute-start(bf16[272,768]{1,0:T(8,128)(2,1)S(1)} %far.1), channel_id=1, source_target_pairs={{8,16},{10,18},{12,20},{14,22},{16,24},{18,26},{20,28},{22,30},{9,... | collective-permute-start | bytes 1253384 | tf_op jit(solution)/shard_map/ppermute | solution.py:344
  43.3 1.6 %collective-permute-done.4.far_rim = bf16[128,2048]{1,0:T(8,128)(2,1)S(1)} collective-permute-done((bf16[128,2048]{1,0:T(8,128)(2,1)S(1)}, bf16[128,2048]{1,0:T(8,128)(2,1)S(1)}, u32[]{:S(2)}, u32[]{:S(2)}) %collective-permute-start.4) | collective-permute-done | bytes 524320 | tf_op jit(solution)/shard_map/ppermute | solution.py:375
  44.9 8.0 %main.1.main_ref = f32[272,1024]{1,0:T(8,128)S(1)} custom-call(bf16[272,256]{1,0:T(8,128)(2,1)S(1)} %get-tuple-element.34.refs_0_, bf16[528,256]{1,0:T(8,128)(2,1)S(1)} %get-tuple-element.35.refs_1_, bf16[784,256]{1,0:T(8,128)(2,1)S(1)} %collective-permute-done.5.refs_2_.refs_1_, bf16[784,256]{1,0:T(8,128)(2,1)S(1)} %collective-permute-done.refs_3_.refs_2_, ...), custom_call_target="tpu_custom_call" | custom-call | flops 1744830464 | bytes 3809280 | tf_op jit(solution)/shard_map/main/pallas_call | solution.py:26
  53.4 4.8 %collective-permute-start.12 = (bf16[256,256]{1,0:T(8,128)(2,1)S(1)}, bf16[256,256]{1,0:T(8,128)(2,1)S(1)}, u32[]{:S(2)}, u32[]{:S(2)}) collective-permute-start(bf16[256,256]{1,0:T(8,128)(2,1)S(1)} %get-tuple-element.47), channel_id=1, source_target_pairs={{0,4},{2,6},{4,0},{6,2},{8,12},{10,14},{12,8},{14,10},{16,20},{18,... | collective-permute-start | bytes 393224 | tf_op jit(solution)/shard_map/ppermute | solution.py:341
  58.3 5.4 %hyena.1 = bf16[256,2048]{1,0:T(8,128)(2,1)} custom-call(bf16[256,2048]{1,0:T(8,128)(2,1)S(1)} %copy-done.2, bf16[256,2048]{1,0:T(8,128)(2,1)S(1)} %copy-done, bf16[256,2048]{1,0:T(8,128)(2,1)S(1)} %copy-done.1, bf16[128,2048]{1,0:T(8,128)(2,1)S(1)} %collective-permute-done.2.next_rim, bf16[128,2048]{1,0:T(8,128)(2,1)S(1)} %collective-permute-done.4.far_rim, ...), custom_call_target="tpu_custom_call" | custom-call | flops 4294967296 | bytes 5279744 | tf_op jit(solution)/shard_map/hyena/pallas_call | solution.py:26
  63.7 1.8 %collective-permute-start.14 = (bf16[256,256]{1,0:T(8,128)(2,1)S(1)}, bf16[256,256]{1,0:T(8,128)(2,1)S(1)}, u32[]{:S(2)}, u32[]{:S(2)}) collective-permute-start(bf16[256,256]{1,0:T(8,128)(2,1)S(1)} %get-tuple-element.50.refs_0_), channel_id=1, source_target_pairs={{0,1},{1,0},{2,3},{3,2},{4,5},{5,4},{6,7},{7,6},{8,9},{9,8},{10,11... | collective-permute-start | bytes 393224 | tf_op jit(solution)/shard_map/ppermute | solution.py:429
  65.5 0.5 collective-permute-start.16
  67.4 3.5 %project.1 = bf16[256,2048]{1,0:T(8,128)(2,1)} custom-call(bf16[256,256]{1,0:T(8,128)(2,1)S(1)} %get-tuple-element.50.refs_0_, bf16[256,256]{1,0:T(8,128)(2,1)S(1)} %collective-permute-done.11.refs_1_, bf16[256,256]{1,0:T(8,128)(2,1)S(1)} %collective-permute-done.12.refs_2_, bf16[256,256]{1,0:T(8,128)(2,1)S(1)} %collective-permute-done.13.refs_3_, ...), custom_call_target="tpu_custom_call" | custom-call | flops 2147483648 | bytes 10485760 | tf_op jit(solution)/shard_map/project/pallas_call | solution.py:26
  (40 shorter events, 2.0 us)
Async XLA Ops:
  0.6 14.1 %copy-start = (bf16[256,2048]{1,0:T(8,128)(2,1)S(1)}, bf16[256,2048]{1,0:T(8,128)(2,1)}, u32[]{:S(2)}) copy-start(bf16[256,2048]{1,0:T(8,128)(2,1)} %k_ref.3) | copy-start | bytes 3145732
  2.3 10.2 %collective-permute-start.5 = (bf16[784,256]{1,0:T(8,128)(2,1)S(1)}, bf16[784,256]{1,0:T(8,128)(2,1)S(1)}, u32[]{:S(2)}, u32[]{:S(2)}) collective-permute-start(bf16[784,256]{1,0:T(8,128)(2,1)S(1)} %get-tuple-element.37), channel_id=1, source_target_pairs={{0,2},{2,0},{4,6},{6,4},{8,10},{10,8},{12,14},{14,12},{16,18},{18,... | collective-permute-start | bytes 1204232 | tf_op jit(solution)/shard_map/ppermute | solution.py:341
  3.6 12.3 %collective-permute-start = (bf16[784,256]{1,0:T(8,128)(2,1)S(1)}, bf16[784,256]{1,0:T(8,128)(2,1)S(1)}, u32[]{:S(2)}, u32[]{:S(2)}) collective-permute-start(bf16[784,256]{1,0:T(8,128)(2,1)S(1)} %get-tuple-element.29), channel_id=1, source_target_pairs={{0,4},{2,6},{4,0},{6,2},{8,12},{10,14},{12,8},{14,10},{16,20},{18,... | collective-permute-start | bytes 1204232 | tf_op jit(solution)/shard_map/ppermute | solution.py:341
  4.8 11.1 %collective-permute-start.1 = (bf16[528,256]{1,0:T(8,128)(2,1)S(1)}, bf16[528,256]{1,0:T(8,128)(2,1)S(1)}, u32[]{:S(2)}, u32[]{:S(2)}) collective-permute-start(bf16[528,256]{1,0:T(8,128)(2,1)S(1)} %get-tuple-element.35.refs_1_), channel_id=1, source_target_pairs={{0,8},{2,10},{4,12},{6,14},{8,16},{10,18},{12,20},{14,22},{16,24},... | collective-permute-start | bytes 811016 | tf_op jit(solution)/shard_map/ppermute | solution.py:344
  12.5 10.1 %collective-permute-start.6 = (bf16[784,256]{1,0:T(8,128)(2,1)S(1)}, bf16[784,256]{1,0:T(8,128)(2,1)S(1)}, u32[]{:S(2)}, u32[]{:S(2)}) collective-permute-start(bf16[784,256]{1,0:T(8,128)(2,1)S(1)} %get-tuple-element.40), channel_id=1, source_target_pairs={{0,6},{2,4},{4,2},{6,0},{8,14},{10,12},{12,10},{14,8},{16,22},{18,... | collective-permute-start | bytes 1204232 | tf_op jit(solution)/shard_map/ppermute | solution.py:341
  15.9 15.3 %collective-permute-start.3 = (bf16[128,2048]{1,0:T(8,128)(2,1)S(1)}, bf16[128,2048]{1,0:T(8,128)(2,1)S(1)}, u32[]{:S(2)}, u32[]{:S(2)}) collective-permute-start(bf16[128,2048]{1,0:T(8,128)(2,1)S(1)} %multiply_convert_fusion), channel_id=1, source_target_pairs={{7,1},{15,9},{23,17},{31,25}} | collective-permute-start | bytes 1572872 | tf_op jit(solution)/shard_map/ppermute | solution.py:375
  17.3 16.0 %collective-permute-start.7 = (bf16[1056,256]{1,0:T(8,128)(2,1)S(1)}, bf16[1056,256]{1,0:T(8,128)(2,1)S(1)}, u32[]{:S(2)}, u32[]{:S(2)}) collective-permute-start(bf16[1056,256]{1,0:T(8,128)(2,1)S(1)} %pad_maximum_fusion), channel_id=1, source_target_pairs={{0,8},{2,10},{4,12},{6,14},{8,16},{10,18},{12,20},{14,22},{16,24},... | collective-permute-start | bytes 1622024 | tf_op jit(solution)/shard_map/ppermute | solution.py:344
  22.7 14.8 %collective-permute-start.9 = (bf16[816,256]{1,0:T(8,128)(2,1)S(1)}, bf16[816,256]{1,0:T(8,128)(2,1)S(1)}, u32[]{:S(2)}, u32[]{:S(2)}) collective-permute-start(bf16[816,256]{1,0:T(8,128)(2,1)S(1)} %ask.1), channel_id=1, source_target_pairs={{16,8},{18,10},{20,12},{22,14},{24,16},{26,18},{28,20},{30,22},{17... | collective-permute-start | bytes 1253384 | tf_op jit(solution)/shard_map/ppermute | solution.py:347
  24.8 18.5 %copy-start.4 = (bf16[2048]{0:T(1024)(128)(2,1)S(1)}, bf16[2048]{0:T(1024)(128)(2,1)}, u32[]{:S(2)}) copy-start(bf16[2048]{0:T(1024)(128)(2,1)} %param.14) | copy-start | bytes 12292
  24.9 12.7 %collective-permute-start.8 = (bf16[528,256]{1,0:T(8,128)(2,1)S(1)}, bf16[528,256]{1,0:T(8,128)(2,1)S(1)}, u32[]{:S(2)}, u32[]{:S(2)}) collective-permute-start(bf16[528,256]{1,0:T(8,128)(2,1)S(1)} %slice.20), channel_id=1, source_target_pairs={{0,8},{2,10},{4,12},{6,14},{8,16},{10,18},{12,20},{14,22},{16,24},... | collective-permute-start | bytes 811016 | tf_op jit(solution)/shard_map/ppermute | solution.py:344
  28.1 15.2 %collective-permute-start.2 = (bf16[128,2048]{1,0:T(8,128)(2,1)S(1)}, bf16[128,2048]{1,0:T(8,128)(2,1)S(1)}, u32[]{:S(2)}, u32[]{:S(2)}) collective-permute-start(bf16[128,2048]{1,0:T(8,128)(2,1)S(1)} %multiply_convert_fusion), channel_id=1, source_target_pairs={{0,2},{1,3},{2,4},{3,5},{4,6},{5,7},{6,8},{8,10},{9,11},{10,12},{1... | collective-permute-start | bytes 1572872 | tf_op jit(solution)/shard_map/ppermute | solution.py:375
  31.3 13.7 %collective-permute-start.4 = (bf16[128,2048]{1,0:T(8,128)(2,1)S(1)}, bf16[128,2048]{1,0:T(8,128)(2,1)S(1)}, u32[]{:S(2)}, u32[]{:S(2)}) collective-permute-start(bf16[128,2048]{1,0:T(8,128)(2,1)S(1)} %collective-permute-done.3), channel_id=1, source_target_pairs={{1,9},{9,17},{17,25}} | collective-permute-start | bytes 1572872 | tf_op jit(solution)/shard_map/ppermute | solution.py:375
  40.1 12.9 %collective-permute-start.10 = (bf16[272,768]{1,0:T(8,128)(2,1)S(1)}, bf16[272,768]{1,0:T(8,128)(2,1)S(1)}, u32[]{:S(2)}, u32[]{:S(2)}) collective-permute-start(bf16[272,768]{1,0:T(8,128)(2,1)S(1)} %far.1), channel_id=1, source_target_pairs={{8,16},{10,18},{12,20},{14,22},{16,24},{18,26},{20,28},{22,30},{9,... | collective-permute-start | bytes 1253384 | tf_op jit(solution)/shard_map/ppermute | solution.py:344
  44.9 13.3 %copy-start.2 = (bf16[256,2048]{1,0:T(8,128)(2,1)S(1)}, bf16[256,2048]{1,0:T(8,128)(2,1)}, u32[]{:S(2)}) copy-start(bf16[256,2048]{1,0:T(8,128)(2,1)} %q_ref.3) | copy-start | bytes 3145732
  53.0 5.3 %copy-start.1 = (bf16[256,2048]{1,0:T(8,128)(2,1)S(1)}, bf16[256,2048]{1,0:T(8,128)(2,1)}, u32[]{:S(2)}) copy-start(bf16[256,2048]{1,0:T(8,128)(2,1)} %v_ref.3) | copy-start | bytes 3145732
  53.4 10.3 %collective-permute-start.11 = (bf16[256,256]{1,0:T(8,128)(2,1)S(1)}, bf16[256,256]{1,0:T(8,128)(2,1)S(1)}, u32[]{:S(2)}, u32[]{:S(2)}) collective-permute-start(bf16[256,256]{1,0:T(8,128)(2,1)S(1)} %get-tuple-element.46), channel_id=1, source_target_pairs={{0,2},{2,0},{4,6},{6,4},{8,10},{10,8},{12,14},{14,12},{16,18},{18,... | collective-permute-start | bytes 393224 | tf_op jit(solution)/shard_map/ppermute | solution.py:341
  53.4 10.2 %collective-permute-start.12 = (bf16[256,256]{1,0:T(8,128)(2,1)S(1)}, bf16[256,256]{1,0:T(8,128)(2,1)S(1)}, u32[]{:S(2)}, u32[]{:S(2)}) collective-permute-start(bf16[256,256]{1,0:T(8,128)(2,1)S(1)} %get-tuple-element.47), channel_id=1, source_target_pairs={{0,4},{2,6},{4,0},{6,2},{8,12},{10,14},{12,8},{14,10},{16,20},{18,... | collective-permute-start | bytes 393224 | tf_op jit(solution)/shard_map/ppermute | solution.py:341
  58.2 9.1 %slice-start = ((s8[8388608]{0:T(1024)(128)(4,1)}), s8[4194304]{0:T(1024)(128)(4,1)S(1)}, s32[]{:S(2)}) async-start(s8[8388608]{0:T(1024)(128)(4,1)} %bitcast.1), calls=%async_computation | async-start | bytes 8388608
  58.2 9.1 %slice-start.1 = ((s8[8388608]{0:T(1024)(128)(4,1)}), s8[4194304]{0:T(1024)(128)(4,1)S(1)}, s32[]{:S(2)}) async-start(s8[8388608]{0:T(1024)(128)(4,1)} %bitcast.1), calls=%async_computation.1 | async-start | bytes 8388608
  58.2 5.4 %collective-permute-start.13 = (bf16[256,256]{1,0:T(8,128)(2,1)S(1)}, bf16[256,256]{1,0:T(8,128)(2,1)S(1)}, u32[]{:S(2)}, u32[]{:S(2)}) collective-permute-start(bf16[256,256]{1,0:T(8,128)(2,1)S(1)} %get-tuple-element.48), channel_id=1, source_target_pairs={{0,6},{2,4},{4,2},{6,0},{8,14},{10,12},{12,10},{14,8},{16,22},{18,... | collective-permute-start | bytes 393224 | tf_op jit(solution)/shard_map/ppermute | solution.py:341
  63.7 2.8 %collective-permute-start.14 = (bf16[256,256]{1,0:T(8,128)(2,1)S(1)}, bf16[256,256]{1,0:T(8,128)(2,1)S(1)}, u32[]{:S(2)}, u32[]{:S(2)}) collective-permute-start(bf16[256,256]{1,0:T(8,128)(2,1)S(1)} %get-tuple-element.50.refs_0_), channel_id=1, source_target_pairs={{0,1},{1,0},{2,3},{3,2},{4,5},{5,4},{6,7},{7,6},{8,9},{9,8},{10,11... | collective-permute-start | bytes 393224 | tf_op jit(solution)/shard_map/ppermute | solution.py:429
  65.5 1.3 %collective-permute-start.15 = (bf16[256,256]{1,0:T(8,128)(2,1)S(1)}, bf16[256,256]{1,0:T(8,128)(2,1)S(1)}, u32[]{:S(2)}, u32[]{:S(2)}) collective-permute-start(bf16[256,256]{1,0:T(8,128)(2,1)S(1)} %collective-permute-done.11.refs_1_), channel_id=1, source_target_pairs={{0,1},{1,0},{2,3},{3,2},{4,5},{5,4},{6,7},{7,6},{8,9},{9,8},{10,11... | collective-permute-start | bytes 393224 | tf_op jit(solution)/shard_map/ppermute | solution.py:429
  65.5 1.5 %collective-permute-start.16 = (bf16[256,256]{1,0:T(8,128)(2,1)S(1)}, bf16[256,256]{1,0:T(8,128)(2,1)S(1)}, u32[]{:S(2)}, u32[]{:S(2)}) collective-permute-start(bf16[256,256]{1,0:T(8,128)(2,1)S(1)} %collective-permute-done.12.refs_2_), channel_id=1, source_target_pairs={{0,1},{1,0},{2,3},{3,2},{4,5},{5,4},{6,7},{7,6},{8,9},{9,8},{10,11... | collective-permute-start | bytes 393224 | tf_op jit(solution)/shard_map/ppermute | solution.py:429
  66.0 1.3 %collective-permute-start.17 = (bf16[256,256]{1,0:T(8,128)(2,1)S(1)}, bf16[256,256]{1,0:T(8,128)(2,1)S(1)}, u32[]{:S(2)}, u32[]{:S(2)}) collective-permute-start(bf16[256,256]{1,0:T(8,128)(2,1)S(1)} %collective-permute-done.13.refs_3_), channel_id=1, source_target_pairs={{0,1},{1,0},{2,3},{3,2},{4,5},{5,4},{6,7},{7,6},{8,9},{9,8},{10,11... | collective-permute-start | bytes 393224 | tf_op jit(solution)/shard_map/ppermute | solution.py:429
  (1 other events, 5.3 us)

commit v7 on v4

--- a/solution.py
+++ b/solution.py
@@ -35,20 +35,69 @@
     )(*args))
 
 
-def hyena_kernel(q_ref, k_ref, v_ref, near_rim, ring_rim, far_rim, taps_ref, direct_ref, out_ref, taps, rim):
-    rows, chans = q_ref.shape
-    groups = taps_ref.shape[0]
-    group = chans // groups
-    per_tile = LANES // group
-    windows = rows // LANES
-    shape = (LANES, LANES)
-    down, along = (lax.broadcasted_iota(jnp.int32, shape, i) for i in range(2))
-    turn = jnp.where((down + along) % LANES == 0, 1.0, 0.0).astype(jnp.bfloat16)
+def filtered(tables, stacked, per_tile):
+    lanes = stacked.shape[1]
+    lane_group = lax.broadcasted_iota(jnp.int32, (LANES, lanes), 1) % LANES // (LANES // per_tile)
+    conv = jnp.zeros((LANES, lanes), jnp.float32)
+    for g, table in enumerate(tables):
+        part = jnp.dot(table, stacked, preferred_element_type=jnp.float32)
+        conv = jnp.where(lane_group == g, part, conv)
+    return conv
+
+
+def halves():
+    down, along = (lax.broadcasted_iota(jnp.int32, (LANES, LANES), i) for i in range(2))
     before = jnp.where(along > down, 1.0, 0.0).astype(jnp.bfloat16)
     within = jnp.where(along > down, 0.0, 1.0).astype(jnp.bfloat16)
+    return before, within
+
+
+def gate(q, conv, direct, mixed):
+    return (
+        q.astype(jnp.float32) * (conv + direct.astype(jnp.float32) * mixed.astype(jnp.float32))
+    ).astype(jnp.bfloat16)
+
+
+def later_kernel(q_ref, k_ref, v_ref, taps_ref, direct_ref, out_ref, rings, taps):
+    rows, chans = q_ref.shape
+    per_tile = taps_ref.shape[0] * LANES // chans
+    windows = rows // LANES
+    down, along = (lax.broadcasted_iota(jnp.int32, (LANES, LANES), i) for i in range(2))
+    turn = jnp.where((down + along) % LANES == 0, 1.0, 0.0).astype(jnp.bfloat16)
     taps[...] = jnp.dot(taps_ref[...], turn, preferred_element_type=jnp.float32)
-    lane_group = lax.broadcasted_iota(jnp.int32, (LANES, windows * LANES), 1) % LANES // group
-
+    before, within = halves()
+
+    @pl.loop(0, chans // LANES, unroll=2)
+    def _(tile):
+        cols = pl.ds(pl.multiple_of(tile * LANES, LANES), LANES)
+        first = pl.multiple_of(tile * per_tile, per_tile)
+        lines = taps[pl.ds(first, per_tile), :]
+        mixed = (k_ref[:, cols].astype(jnp.float32) * v_ref[:, cols].astype(jnp.float32)).astype(
+            jnp.bfloat16
+        )
+        stacked = jnp.concatenate(
+            [mixed[w * LANES : (w + 2) * LANES] for w in range(windows - 1)], axis=1
+        )
+        tables = []
+        for g in range(per_tile):
+            ring = pltpu.roll(
+                jnp.broadcast_to(lines[g : g + 1], (LANES, LANES)), 0, 1, stride=1, stride_axis=0
+            ).astype(jnp.bfloat16)
+            rings[first + g] = ring
+            tables.append(jnp.concatenate([ring * before, ring * within], axis=1))
+        conv = filtered(tables, stacked, per_tile)
+        conv = jnp.concatenate(
+            [conv[:, w * LANES : (w + 1) * LANES] for w in range(windows - 1)], axis=0
+        )
+        out_ref[LANES:, cols] = gate(q_ref[LANES:, cols], conv, direct_ref[:, cols], mixed[LANES:])
+
+
+def first_kernel(
+    q_ref, k_ref, v_ref, near_rim, ring_rim, far_rim, direct_ref, rings, _, out_ref, rim
+):
+    chans = q_ref.shape[1]
+    per_tile = rings.shape[0] * LANES // chans
+    before, within = halves()
     half = chans // 2
     rim[:, :half] = near_rim[...]
     rim[:, half:] = ring_rim[...]
@@ -60,44 +109,53 @@
     @pl.loop(0, chans // LANES, unroll=2)
     def _(tile):
         cols = pl.ds(pl.multiple_of(tile * LANES, LANES), LANES)
-        rings = taps[pl.ds(pl.multiple_of(tile * per_tile, per_tile), per_tile), :]
+        first = pl.multiple_of(tile * per_tile, per_tile)
         mixed = (k_ref[:, cols].astype(jnp.float32) * v_ref[:, cols].astype(jnp.float32)).astype(
             jnp.bfloat16
         )
-        full = jnp.concatenate([rim[:, cols], mixed], axis=0)
-        stacked = jnp.concatenate(
-            [full[w * LANES : (w + 2) * LANES] for w in range(windows)], axis=1
-        )
-        conv = jnp.zeros((LANES, windows * LANES), jnp.float32)
+        stacked = jnp.concatenate([rim[:, cols], mixed], axis=0)
+        tables = []
         for g in range(per_tile):
-            ring = pltpu.roll(
-                jnp.broadcast_to(rings[g : g + 1], shape), 0, 1, stride=1, stride_axis=0
-            ).astype(jnp.bfloat16)
-            table = jnp.concatenate([ring * before, ring * within], axis=1)
-            part = jnp.dot(table, stacked, preferred_element_type=jnp.float32)
-            conv = jnp.where(lane_group == g, part, conv)
-        conv = jnp.concatenate(
-            [conv[:, w * LANES : (w + 1) * LANES] for w in range(windows)], axis=0
-        )
-        out_ref[:, cols] = (
-            q_ref[:, cols].astype(jnp.float32)
-            * (conv + direct_ref[:, cols].astype(jnp.float32) * mixed.astype(jnp.float32))
-        ).astype(jnp.bfloat16)
-
-
-def hyena(hyena_q, hyena_k, hyena_v, rims, filters, direct):
+            ring = rings[first + g]
+            tables.append(jnp.concatenate([ring * before, ring * within], axis=1))
+        conv = filtered(tables, stacked, per_tile)
+        out_ref[:, cols] = gate(q_ref[:, cols], conv, direct_ref[:, cols], mixed)
+
+
+def hyena_later(hyena_q, hyena_k, hyena_v, filters, direct):
     rows, chans = hyena_q.shape
     groups, kernel = filters.shape
     taps = jnp.pad(filters, ((0, 0), (0, LANES - kernel)))
-    (out,) = kernel_call(
-        hyena_kernel,
-        (hyena_q, hyena_k, hyena_v, *rims, taps, direct[None]),
-        [jax.ShapeDtypeStruct((rows, chans), jnp.bfloat16)],
-        "hyena",
-        [pltpu.VMEM((groups, LANES), jnp.float32), pltpu.VMEM((LANES, chans), jnp.bfloat16)],
-        flops=4 * rows * chans * 2 * LANES * 8,
-    )
-    return out
+    return kernel_call(
+        later_kernel,
+        (hyena_q, hyena_k, hyena_v, taps, direct[None]),
+        [
+            jax.ShapeDtypeStruct((rows, chans), jnp.bfloat16),
+            jax.ShapeDtypeStruct((groups, LANES, LANES), jnp.bfloat16),
+        ],
+        "hyena_later",
+        [pltpu.VMEM((groups, LANES), jnp.float32)],
+        flops=4 * rows * chans * LANES * 8,
+    )
+
+
+def hyena_first(hyena_q, hyena_k, hyena_v, rims, direct, rings, later):
+    rows, chans = hyena_q.shape
+    top = pl.BlockSpec((LANES, chans), lambda i: (0, 0))
+    return pl.pallas_call(
+        first_kernel,
+        grid=(1,),
+        in_specs=[top] * 3 + [VMEM] * 5 + [pl.BlockSpec(memory_space=pl.ANY)],
+        out_specs=top,
+        out_shape=jax.ShapeDtypeStruct((rows, chans), jnp.bfloat16),
+        scratch_shapes=[pltpu.VMEM((LANES, chans), jnp.bfloat16)],
+        input_output_aliases={8: 0},
+        compiler_params=pltpu.CompilerParams(vmem_limit_bytes=VMEM_LIMIT),
+        cost_estimate=pl.CostEstimate(
+            flops=4 * LANES * chans * LANES * 8, bytes_accessed=16 * LANES * chans, transcendentals=0
+        ),
+        name="hyena_first",
+    )(hyena_q, hyena_k, hyena_v, *rims, direct[None], rings, later)
 
 
 def deal_kernel(q_ref, k_ref, v_ref, id_ref, *refs):
@@ -200,19 +258,20 @@
             queries[h, span, HD:] = mask
 
 
-def attend(query, keys, values, diagonal):
+def score_of(query, keys):
+    return lax.dot_general(
+        keys, query, (((1,), (1,)), ((), ())), preferred_element_type=jnp.float32
+    )
+
+
+def attend(score, values, diagonal):
     factor = math.log2(math.e) / math.sqrt(HD)
-    rows = query.shape[0]
-    score = lax.dot_general(
-        keys, query, (((1,), (1,)), ((), ())), preferred_element_type=jnp.float32
-    )
+    rows = score.shape[1]
     if diagonal:
         older = lax.broadcasted_iota(jnp.int32, (rows, rows), 0) <= lax.broadcasted_iota(
             jnp.int32, (rows, rows), 1
         )
-        score = jnp.concatenate(
-            [score[:-rows], jnp.where(older, score[-rows:], NEG)], axis=0
-        )
+        score = jnp.concatenate([score[:-rows], jnp.where(older, score[-rows:], NEG)], axis=0)
     high = jnp.max(score, axis=0, keepdims=True)
     expo = jnp.exp2((score - high) * factor)
     total = jnp.sum(expo, axis=0, keepdims=True)
@@ -223,6 +282,13 @@
         preferred_element_type=jnp.float32,
     )
     return summed / total, high * factor + jnp.log2(total)
+
+
+def ahead(steps, product):
+    late = product(*steps[0])
+    for step, following in zip(steps, steps[1:] + [None]):
+        now, late = late, product(*following) if following else None
+        yield step, now
 
 
 def main_kernel(*refs):
@@ -236,14 +302,16 @@
     place_queries(asked, corner, rows, queries)
     place_keys(held, corner, SQUAD, rows, keys, values)
     place_keys(near_parts(near, rows), corner, 0, rows, keys, values)
-    for j in range(SQUAD):
-        cols = slice(j * rows, (j + 1) * rows)
-        reach = (SQUAD + 1 + j) * rows
-        for h in range(heads):
-            mixed, lse = attend(queries[h, cols], keys[h, :reach], values[h, :reach], True)
-            out[h * HD : (h + 1) * HD, cols] = mixed
-            out[width + h : width + h + 1, cols] = lse
-        out[width + heads :, cols] = jnp.zeros((TAG - heads, rows), jnp.float32)
+    span = [slice(j * rows, (j + 1) * rows) for j in range(SQUAD)]
+    reach = [(SQUAD + 1 + j) * rows for j in range(SQUAD)]
+    steps = [(j, h) for j in range(SQUAD) for h in range(heads)]
+    for (j, h), score in ahead(
+        steps, lambda j, h: score_of(queries[h, span[j]], keys[h, : reach[j]])
+    ):
+        mixed, lse = attend(score, values[h, : reach[j]], True)
+        out[h * HD : (h + 1) * HD, span[j]] = mixed
+        out[width + h : width + h + 1, span[j]] = lse
+    out[width + heads :, :] = jnp.zeros((TAG - heads, SQUAD * rows), jnp.float32)
 
 
 def far_kernel(*refs):
@@ -256,19 +324,20 @@
     asked = [asked[0].at[k * tall : (k + 1) * tall] for k in range(SQUAD - 1)] + [asked[1]]
     place_queries(asked, corner, rows, queries)
     place_keys(near_parts(near, rows), corner, 0, rows, keys, values)
-    for j in range(SQUAD - 1):
-        cols = slice(j * rows, (j + 1) * rows)
-        stats = []
-        for h in range(heads):
-            mixed, lse = attend(
-                queries[h, cols], keys[h, cols.stop :], values[h, cols.stop :], False
-            )
-            out[h * HD : (h + 1) * HD, cols] = mixed.astype(out.dtype)
-            top = lse.astype(jnp.bfloat16).astype(jnp.float32)
-            mid = (lse - top).astype(jnp.bfloat16).astype(jnp.float32)
-            stats += [top, mid, lse - top - mid]
-        stats.append(jnp.zeros((TAG - len(stats), rows), jnp.float32))
-        out[width:, cols] = jnp.concatenate(stats, axis=0).astype(out.dtype)
+    span = [slice(j * rows, (j + 1) * rows) for j in range(SQUAD)]
+    stats = [[] for _ in range(SQUAD - 1)]
+    steps = [(j, h) for j in range(SQUAD - 1) for h in range(heads)]
+    for (j, h), score in ahead(
+        steps, lambda j, h: score_of(queries[h, span[j]], keys[h, span[j].stop :])
+    ):
+        mixed, lse = attend(score, values[h, span[j].stop :], False)
+        out[h * HD : (h + 1) * HD, span[j]] = mixed.astype(out.dtype)
+        top = lse.astype(jnp.bfloat16).astype(jnp.float32)
+        mid = (lse - top).astype(jnp.bfloat16).astype(jnp.float32)
+        stats[j] += [top, mid, lse - top - mid]
+    for j, stat in enumerate(stats):
+        stat.append(jnp.zeros((TAG - len(stat), rows), jnp.float32))
+        out[width:, span[j]] = jnp.concatenate(stat, axis=0).astype(out.dtype)
 
 
 def merge_kernel(main_ref, far_ref, *refs):
@@ -340,6 +409,8 @@
     tall = rows + TAG
     near = [climb(kept)]
     beside = [swap(sent[0], 1), swap(sent[1], 2)]
+    later, rings = hyena_later(hyena_q, hyena_k, hyena_v, filters, direct)
+    beside[0], rings = lax.optimization_barrier((beside[0], rings))
     sent[2], beside[0] = lax.optimization_barrier((sent[2], beside[0]))
     across = swap(sent[2], 3)
     beside[1], near[0] = lax.optimization_barrier((beside[1], near[0]))
@@ -396,7 +467,7 @@
         [pltpu.VMEM((SQUAD, rows, width), bf16)],
     )
     *rims, done[0] = lax.optimization_barrier((*rims, done[0]))
-    hyena_out = hyena(hyena_q, hyena_k, hyena_v, rims, filters, direct)
+    hyena_out = hyena_first(hyena_q, hyena_k, hyena_v, rims, direct, rings, later)
 
     def turn(value, r):
         return lax.ppermute(value, "tp", [(t, (t + r) % ranks) for t in range(ranks)])

time: 69.6 us -> 69.8 us (level)
  starting transfers between devices: 33.5 us -> 30.4 us
  Pallas kernels: 21.5 us -> 23.1 us
  waiting for transfers between devices: 11.3 us -> 12.7 us
  local copies, waits for them, and re-layouts: 0.17 us -> 0.91 us
    pallas_call x0 -> x1, Pallas kernels: none -> 4.65 us  [hyena_first(): pl.pallas_call(first_kernel, grid=(1,), in_specs=[top] * 3 + [VMEM] * 5 +...]
    pallas_call x5, Pallas kernels: 19.8 us -> 16.8 us  [kernel_call(): pl.pallas_call(kernel, in_specs=[VMEM] * len(args), out_specs=[VMEM] * le...]
    ppermute x4, starting transfers between devices: 11.5 us -> 9.5 us  [climb(): lax.ppermute(value, 'ctx', [(i, i + SQUAD) for i in range(first, count -...]
    ppermute x6, waiting for transfers between devices: 1.66 us -> 3.33 us  [swap(): return lax.ppermute(value, 'ctx', [(i, i ^ mask) for i in range(count)])]
    ppermute x6, starting transfers between devices: 6.46 us -> 5.48 us  [swap(): return lax.ppermute(value, 'ctx', [(i, i ^ mask) for i in range(count)])]
    ppermute x2, starting transfers between devices: 4 us -> 4.84 us  [descend(): lax.ppermute(value, 'ctx', [(i, i - SQUAD) for i in range(2 * SQUAD, coun...]
    ppermute x4, waiting for transfers between devices: 5.13 us -> 4.34 us  [climb(): lax.ppermute(value, 'ctx', [(i, i + SQUAD) for i in range(first, count -...]
    unnamed x14, local copies, waits for them, and re-layouts: 0.04 us -> 0.78 us
  transfers between devices with their start and end apart: 19 -> 19, of which waited for: 8 -> 8; matrix products, arithmetic and copies ran while one was open for 2% -> 2% of each run, Pallas kernels for 23% -> 25%
where the time goes in v7:
time: 69.8 us; the launch traced here: 69.4 us
  starting transfers between devices  30.4 us (44%)
  Pallas kernels  23.1 us (33%)
  waiting for transfers between devices  12.7 us (18%)
  other arithmetic  1.24 us (2%)
  between operations  0.94 us (1%)
  local copies, waits for them, and re-layouts  0.91 us (1%)
    pallas_call x5, Pallas kernels, kernel_call(): pl.pallas_call(kernel, in_specs=[VMEM] * len(args), out_specs=[VMEM] * le...  16.8 us
    ppermute x4, starting transfers between devices, climb(): lax.ppermute(value, 'ctx', [(i, i + SQUAD) for i in range(first, count -...  9.5 us
    ppermute x6, starting transfers between devices, swap(): return lax.ppermute(value, 'ctx', [(i, i ^ mask) for i in range(count)])  5.48 us
    ppermute x2, starting transfers between devices, descend(): lax.ppermute(value, 'ctx', [(i, i - SQUAD) for i in range(2 * SQUAD, coun...  4.84 us
    pallas_call x1, Pallas kernels, hyena_first(): pl.pallas_call(first_kernel, grid=(1,), in_specs=[top] * 3 + [VMEM] * 5 +...  4.65 us
    ppermute x4, waiting for transfers between devices, climb(): lax.ppermute(value, 'ctx', [(i, i + SQUAD) for i in range(first, count -...  4.34 us
    ppermute x4, starting transfers between devices, turn(): lax.ppermute(value, 'tp', [(t, (t + r) % ranks) for t in range(ranks)])  4.19 us
    ppermute x1, waiting for transfers between devices, local(): lax.ppermute(tail[:, half:], 'ctx', [(i, i - i % SQUAD + (i + 1) % SQUAD)...  3.67 us
  transfers between devices with their start and end apart: 19, of which 8 were waited for; matrix products, arithmetic and copies ran while one was open for 2% of the time, Pallas kernels for 25%

profile of v7, /device:TPU:17, one launch (start us, length us, event | category | flops | bytes accessed | tf_op | source)
XLA Modules:
  0.0 69.4 jit_solution(480473900338547280)
XLA Ops:
  0.7 1.7 %deal.1 = (bf16[272,256]{1,0:T(8,128)(2,1)S(1)}, bf16[528,256]{1,0:T(8,128)(2,1)S(1)}, bf16[784,256]{1,0:T(8,128)(2,1)S(1)}, bf16[784,256]{1,0:T(8,128)(2,1)S(1)}, bf16[784,256]{1,0:T(8,128)(2,1)S(1)}) custom-call(bf16[256,1024]{1,0:T(8,128)(2,1)} %q_ref.3, bf16[256,1024]{1,0:T(8,128)(2,1)} %k_ref.3, bf16[256,1024]{1,0:T(8,128)(2,1)} %v_ref.3, s32[2,128]{1,0:T(2,128)} %bitcast.3), custom_call_target="tpu_custom_call" | custom-call | bytes 3145728 | tf_op jit(solution)/shard_map/deal/pallas_call | solution.py:203
  2.4 1.3 %collective-permute-start.1 = (bf16[784,256]{1,0:T(8,128)(2,1)S(1)}, bf16[784,256]{1,0:T(8,128)(2,1)S(1)}, u32[]{:S(2)}, u32[]{:S(2)}) collective-permute-start(bf16[784,256]{1,0:T(8,128)(2,1)S(1)} %get-tuple-element.36), channel_id=1, source_target_pairs={{0,2},{2,0},{4,6},{6,4},{8,10},{10,8},{12,14},{14,12},{16,18},{18,... | collective-permute-start | bytes 1204232 | tf_op jit(solution)/shard_map/ppermute | solution.py:396
  3.7 1.2 %collective-permute-start.5 = (bf16[784,256]{1,0:T(8,128)(2,1)S(1)}, bf16[784,256]{1,0:T(8,128)(2,1)S(1)}, u32[]{:S(2)}, u32[]{:S(2)}) collective-permute-start(bf16[784,256]{1,0:T(8,128)(2,1)S(1)} %get-tuple-element.47), channel_id=1, source_target_pairs={{0,4},{2,6},{4,0},{6,2},{8,12},{10,14},{12,8},{14,10},{16,20},{18,... | collective-permute-start | bytes 1204232 | tf_op jit(solution)/shard_map/ppermute | solution.py:396
  4.9 3.2 %collective-permute-start.6 = (bf16[528,256]{1,0:T(8,128)(2,1)S(1)}, bf16[528,256]{1,0:T(8,128)(2,1)S(1)}, u32[]{:S(2)}, u32[]{:S(2)}) collective-permute-start(bf16[528,256]{1,0:T(8,128)(2,1)S(1)} %get-tuple-element.45.refs_1_), channel_id=1, source_target_pairs={{0,8},{2,10},{4,12},{6,14},{8,16},{10,18},{12,20},{14,22},{16,24},... | collective-permute-start | bytes 811016 | tf_op jit(solution)/shard_map/ppermute | solution.py:399
  8.1 1.2 %multiply_convert_fusion = bf16[128,2048]{1,0:T(8,128)(2,1)S(1)} fusion(bf16[256,2048]{1,0:T(8,128)(2,1)} %v_ref.5, bf16[256,2048]{1,0:T(8,128)(2,1)S(1)} %copy-done), kind=kLoop, calls=%fused_computation | loop fusion | flops 1048576 | bytes 1572864 | tf_op jit(solution)/shard_map/convert_element_type | solution.py:422
  9.4 0.7 %copy-done.3 = bf16[128,128]{1,0:T(8,128)(2,1)S(1)} copy-done((bf16[128,128]{1,0:T(8,128)(2,1)S(1)}, bf16[128,128]{1,0:T(8,128)(2,1)}, u32[]{:S(2)}) %copy-start.3) | copy-done | bytes 32792
  10.1 5.2 %hyena_later.1 = (bf16[256,2048]{1,0:T(8,128)(2,1)}, bf16[128,128,128]{2,1,0:T(8,128)(2,1)S(1)}) custom-call(bf16[256,2048]{1,0:T(8,128)(2,1)S(1)} %copy-done.2, bf16[256,2048]{1,0:T(8,128)(2,1)S(1)} %copy-done, bf16[256,2048]{1,0:T(8,128)(2,1)S(1)} %copy-done.1, bf16[128,128]{1,0:T(8,128)(2,1)S(1)} %copy-done.3, bf16[1,2048]{1,0:T(2,128)(2,1)S(1)} %broadcast_in_dim.4.direct_ref), custom_call_target="tpu_custom_call" | custom-call | flops 2147483648 | bytes 8425472 | tf_op jit(solution)/shard_map/hyena_later/pallas_call | solution.py:26
  15.7 2.5 %collective-permute-start.7 = (bf16[1056,256]{1,0:T(8,128)(2,1)S(1)}, bf16[1056,256]{1,0:T(8,128)(2,1)S(1)}, u32[]{:S(2)}, u32[]{:S(2)}) collective-permute-start(bf16[1056,256]{1,0:T(8,128)(2,1)S(1)} %pad_maximum_fusion), channel_id=1, source_target_pairs={{0,8},{2,10},{4,12},{6,14},{8,16},{10,18},{12,20},{14,22},{16,24},... | collective-permute-start | bytes 1622024 | tf_op jit(solution)/shard_map/ppermute | solution.py:399
  18.2 2.8 %collective-permute-start.9 = (bf16[816,256]{1,0:T(8,128)(2,1)S(1)}, bf16[816,256]{1,0:T(8,128)(2,1)S(1)}, u32[]{:S(2)}, u32[]{:S(2)}) collective-permute-start(bf16[816,256]{1,0:T(8,128)(2,1)S(1)} %pad_maximum_fusion.1), channel_id=1, source_target_pairs={{16,8},{18,10},{20,12},{22,14},{24,16},{26,18},{28,20},{30,22},{17... | collective-permute-start | bytes 1253384 | tf_op jit(solution)/shard_map/ppermute | solution.py:402
  21.1 1.3 %collective-permute-start.3 = (bf16[128,1024]{1,0:T(8,128)(2,1)S(1)}, bf16[128,1024]{1,0:T(8,128)(2,1)S(1)}, u32[]{:S(2)}, u32[]{:S(2)}) collective-permute-start(bf16[128,1024]{1,0:T(8,128)(2,1)S(1)} %get-tuple-element.66), channel_id=1, source_target_pairs={{0,2},{2,4},{4,6},{6,0},{8,10},{10,12},{12,14},{14,8},{16,18},{18,... | collective-permute-start | bytes 786440 | tf_op jit(solution)/shard_map/ppermute | solution.py:424
  22.3 3.3 %collective-permute-done.2.refs_4_ = bf16[784,256]{1,0:T(8,128)(2,1)S(1)} collective-permute-done((bf16[784,256]{1,0:T(8,128)(2,1)S(1)}, bf16[784,256]{1,0:T(8,128)(2,1)S(1)}, u32[]{:S(2)}, u32[]{:S(2)}) %collective-permute-start.2) | collective-permute-done | bytes 401440 | tf_op jit(solution)/shard_map/ppermute | solution.py:396
  25.7 1.9 %collective-permute-start.8 = (bf16[528,256]{1,0:T(8,128)(2,1)S(1)}, bf16[528,256]{1,0:T(8,128)(2,1)S(1)}, u32[]{:S(2)}, u32[]{:S(2)}) collective-permute-start(bf16[528,256]{1,0:T(8,128)(2,1)S(1)} %slice.42), channel_id=1, source_target_pairs={{0,8},{2,10},{4,12},{6,14},{8,16},{10,18},{12,20},{14,22},{16,24},... | collective-permute-start | bytes 811016 | tf_op jit(solution)/shard_map/ppermute | solution.py:399
  27.6 3.7 %collective-permute-done.3.ring_rim = bf16[128,1024]{1,0:T(8,128)(2,1)S(1)} collective-permute-done((bf16[128,1024]{1,0:T(8,128)(2,1)S(1)}, bf16[128,1024]{1,0:T(8,128)(2,1)S(1)}, u32[]{:S(2)}, u32[]{:S(2)}) %collective-permute-start.3) | collective-permute-done | bytes 262176 | tf_op jit(solution)/shard_map/ppermute | solution.py:424
  31.3 2.0 %collective-permute-start.10 = (bf16[272,256]{1,0:T(8,128)(2,1)S(1)}, bf16[272,256]{1,0:T(8,128)(2,1)S(1)}, u32[]{:S(2)}, u32[]{:S(2)}) collective-permute-start(bf16[272,256]{1,0:T(8,128)(2,1)S(1)} %slice.39), channel_id=1, source_target_pairs={{16,8},{18,10},{20,12},{22,14},{24,16},{26,18},{28,20},{30,22},{17... | collective-permute-start | bytes 417800 | tf_op jit(solution)/shard_map/ppermute | solution.py:402
  33.3 1.9 %collective-permute-start = (bf16[128,1024]{1,0:T(8,128)(2,1)S(1)}, bf16[128,1024]{1,0:T(8,128)(2,1)S(1)}, u32[]{:S(2)}, u32[]{:S(2)}) collective-permute-start(bf16[128,1024]{1,0:T(8,128)(2,1)S(1)} %get-tuple-element.67), channel_id=1, source_target_pairs={{0,2},{2,4},{4,6},{6,8},{8,10},{10,12},{12,14},{14,16},{16,18},{18... | collective-permute-start | bytes 786440 | tf_op jit(solution)/shard_map/ppermute | solution.py:430
  35.2 3.3 %collective-permute-start.4 = (bf16[128,1024]{1,0:T(8,128)(2,1)S(1)}, bf16[128,1024]{1,0:T(8,128)(2,1)S(1)}, u32[]{:S(2)}, u32[]{:S(2)}) collective-permute-start(bf16[128,1024]{1,0:T(8,128)(2,1)S(1)} %collective-permute-done.3.ring_rim), channel_id=1, source_target_pairs={{0,8},{8,16},{16,24},{1,9},{9,17},{17,25}} | collective-permute-start | bytes 786440 | tf_op jit(solution)/shard_map/ppermute | solution.py:432
  38.5 1.8 %far.1 = bf16[272,768]{1,0:T(8,128)(2,1)S(1)} custom-call(bf16[816,256]{1,0:T(8,128)(2,1)S(1)} %collective-permute-done.9.refs_0_, bf16[272,256]{1,0:T(8,128)(2,1)S(1)} %collective-permute-done.10.refs_1_, bf16[528,256]{1,0:T(8,128)(2,1)S(1)} %collective-permute-done.6.refs_5_.refs_2_, bf16[1056,256]{1,0:T(8,128)(2,1)S(1)} %collective-permute-done.7.refs_6_.refs_3_, ...), custom_call_target="tpu_custom_call" | custom-call | flops 402653184 | bytes 2056192 | tf_op jit(solution)/shard_map/far/pallas_call | solution.py:26
  40.3 1.9 %collective-permute-start.11 = (bf16[272,768]{1,0:T(8,128)(2,1)S(1)}, bf16[272,768]{1,0:T(8,128)(2,1)S(1)}, u32[]{:S(2)}, u32[]{:S(2)}) collective-permute-start(bf16[272,768]{1,0:T(8,128)(2,1)S(1)} %far.1), channel_id=1, source_target_pairs={{8,16},{10,18},{12,20},{14,22},{16,24},{18,26},{20,28},{22,30},{9,... | collective-permute-start | bytes 1253384 | tf_op jit(solution)/shard_map/ppermute | solution.py:399
  42.4 6.0 %main.1.main_ref = f32[272,1024]{1,0:T(8,128)S(1)} custom-call(bf16[272,256]{1,0:T(8,128)(2,1)S(1)} %get-tuple-element.44.refs_0_, bf16[528,256]{1,0:T(8,128)(2,1)S(1)} %get-tuple-element.45.refs_1_, bf16[784,256]{1,0:T(8,128)(2,1)S(1)} %collective-permute-done.1.refs_2_, bf16[784,256]{1,0:T(8,128)(2,1)S(1)} %collective-permute-done.5.refs_3_, ...), custom_call_target="tpu_custom_call" | custom-call | flops 1744830464 | bytes 3809280 | tf_op jit(solution)/shard_map/main/pallas_call | solution.py:26
  48.4 4.3 %collective-permute-done.11.far_ref = bf16[272,768]{1,0:T(8,128)(2,1)S(1)} collective-permute-done((bf16[272,768]{1,0:T(8,128)(2,1)S(1)}, bf16[272,768]{1,0:T(8,128)(2,1)S(1)}, u32[]{:S(2)}, u32[]{:S(2)}) %collective-permute-start.11) | collective-permute-done | bytes 417824 | tf_op jit(solution)/shard_map/ppermute | solution.py:399
  53.3 2.6 %collective-permute-start.14 = (bf16[256,256]{1,0:T(8,128)(2,1)S(1)}, bf16[256,256]{1,0:T(8,128)(2,1)S(1)}, u32[]{:S(2)}, u32[]{:S(2)}) collective-permute-start(bf16[256,256]{1,0:T(8,128)(2,1)S(1)} %get-tuple-element.60), channel_id=1, source_target_pairs={{0,6},{2,4},{4,2},{6,0},{8,14},{10,12},{12,10},{14,8},{16,22},{18,... | collective-permute-start | bytes 393224 | tf_op jit(solution)/shard_map/ppermute | solution.py:396
  55.8 4.6 %hyena_first.1 = bf16[256,2048]{1,0:T(8,128)(2,1)} custom-call(bf16[256,2048]{1,0:T(8,128)(2,1)S(1)} %copy-done.2, bf16[256,2048]{1,0:T(8,128)(2,1)S(1)} %copy-done, bf16[256,2048]{1,0:T(8,128)(2,1)S(1)} %copy-done.1, bf16[128,1024]{1,0:T(8,128)(2,1)S(1)} %collective-permute-done.near_rim, ...), custom_call_target="tpu_custom_call", output_to_operand_aliasing={{}: (8, {})} | custom-call | flops 1073741824 | bytes 4194304 | tf_op jit(solution)/shard_map/hyena_first/pallas_call | solution.py:145
  60.5 3.6 %collective-permute-start.15 = (bf16[256,256]{1,0:T(8,128)(2,1)S(1)}, bf16[256,256]{1,0:T(8,128)(2,1)S(1)}, u32[]{:S(2)}, u32[]{:S(2)}) collective-permute-start(bf16[256,256]{1,0:T(8,128)(2,1)S(1)} %get-tuple-element.62.refs_0_), channel_id=1, source_target_pairs={{0,1},{1,0},{2,3},{3,2},{4,5},{5,4},{6,7},{7,6},{8,9},{9,8},{10,11... | collective-permute-start | bytes 393224 | tf_op jit(solution)/shard_map/ppermute | solution.py:473
  66.0 3.5 %project.1 = bf16[256,2048]{1,0:T(8,128)(2,1)} custom-call(bf16[256,256]{1,0:T(8,128)(2,1)S(1)} %get-tuple-element.62.refs_0_, bf16[256,256]{1,0:T(8,128)(2,1)S(1)} %collective-permute-done.12.refs_1_, bf16[256,256]{1,0:T(8,128)(2,1)S(1)} %collective-permute-done.13.refs_2_, bf16[256,256]{1,0:T(8,128)(2,1)S(1)} %collective-permute-done.14.refs_3_, ...), custom_call_target="tpu_custom_call" | custom-call | flops 2147483648 | bytes 10485760 | tf_op jit(solution)/shard_map/project/pallas_call | solution.py:26
  (47 shorter events, 3.0 us)
Async XLA Ops:
  0.6 7.5 %copy-start = (bf16[256,2048]{1,0:T(8,128)(2,1)S(1)}, bf16[256,2048]{1,0:T(8,128)(2,1)}, u32[]{:S(2)}) copy-start(bf16[256,2048]{1,0:T(8,128)(2,1)} %k_ref.5) | copy-start | bytes 3145732
  0.6 8.7 %copy-start.2 = (bf16[256,2048]{1,0:T(8,128)(2,1)S(1)}, bf16[256,2048]{1,0:T(8,128)(2,1)}, u32[]{:S(2)}) copy-start(bf16[256,2048]{1,0:T(8,128)(2,1)} %q_ref.5) | copy-start | bytes 3145732
  2.4 7.0 %copy-start.1 = (bf16[256,2048]{1,0:T(8,128)(2,1)S(1)}, bf16[256,2048]{1,0:T(8,128)(2,1)}, u32[]{:S(2)}) copy-start(bf16[256,2048]{1,0:T(8,128)(2,1)} %v_ref.5) | copy-start | bytes 3145732
  2.4 12.9 %collective-permute-start.1 = (bf16[784,256]{1,0:T(8,128)(2,1)S(1)}, bf16[784,256]{1,0:T(8,128)(2,1)S(1)}, u32[]{:S(2)}, u32[]{:S(2)}) collective-permute-start(bf16[784,256]{1,0:T(8,128)(2,1)S(1)} %get-tuple-element.36), channel_id=1, source_target_pairs={{0,2},{2,0},{4,6},{6,4},{8,10},{10,8},{12,14},{14,12},{16,18},{18,... | collective-permute-start | bytes 1204232 | tf_op jit(solution)/shard_map/ppermute | solution.py:396
  3.7 11.6 %collective-permute-start.5 = (bf16[784,256]{1,0:T(8,128)(2,1)S(1)}, bf16[784,256]{1,0:T(8,128)(2,1)S(1)}, u32[]{:S(2)}, u32[]{:S(2)}) collective-permute-start(bf16[784,256]{1,0:T(8,128)(2,1)S(1)} %get-tuple-element.47), channel_id=1, source_target_pairs={{0,4},{2,6},{4,0},{6,2},{8,12},{10,14},{12,8},{14,10},{16,20},{18,... | collective-permute-start | bytes 1204232 | tf_op jit(solution)/shard_map/ppermute | solution.py:396
  4.9 10.3 %collective-permute-start.6 = (bf16[528,256]{1,0:T(8,128)(2,1)S(1)}, bf16[528,256]{1,0:T(8,128)(2,1)S(1)}, u32[]{:S(2)}, u32[]{:S(2)}) collective-permute-start(bf16[528,256]{1,0:T(8,128)(2,1)S(1)} %get-tuple-element.45.refs_1_), channel_id=1, source_target_pairs={{0,8},{2,10},{4,12},{6,14},{8,16},{10,18},{12,20},{14,22},{16,24},... | collective-permute-start | bytes 811016 | tf_op jit(solution)/shard_map/ppermute | solution.py:399
  15.4 10.3 %collective-permute-start.2 = (bf16[784,256]{1,0:T(8,128)(2,1)S(1)}, bf16[784,256]{1,0:T(8,128)(2,1)S(1)}, u32[]{:S(2)}, u32[]{:S(2)}) collective-permute-start(bf16[784,256]{1,0:T(8,128)(2,1)S(1)} %get-tuple-element.39), channel_id=1, source_target_pairs={{0,6},{2,4},{4,2},{6,0},{8,14},{10,12},{12,10},{14,8},{16,22},{18,... | collective-permute-start | bytes 1204232 | tf_op jit(solution)/shard_map/ppermute | solution.py:396
  15.7 22.8 %collective-permute-start.7 = (bf16[1056,256]{1,0:T(8,128)(2,1)S(1)}, bf16[1056,256]{1,0:T(8,128)(2,1)S(1)}, u32[]{:S(2)}, u32[]{:S(2)}) collective-permute-start(bf16[1056,256]{1,0:T(8,128)(2,1)S(1)} %pad_maximum_fusion), channel_id=1, source_target_pairs={{0,8},{2,10},{4,12},{6,14},{8,16},{10,18},{12,20},{14,22},{16,24},... | collective-permute-start | bytes 1622024 | tf_op jit(solution)/shard_map/ppermute | solution.py:399
  18.2 17.0 %collective-permute-start.9 = (bf16[816,256]{1,0:T(8,128)(2,1)S(1)}, bf16[816,256]{1,0:T(8,128)(2,1)S(1)}, u32[]{:S(2)}, u32[]{:S(2)}) collective-permute-start(bf16[816,256]{1,0:T(8,128)(2,1)S(1)} %pad_maximum_fusion.1), channel_id=1, source_target_pairs={{16,8},{18,10},{20,12},{22,14},{24,16},{26,18},{28,20},{30,22},{17... | collective-permute-start | bytes 1253384 | tf_op jit(solution)/shard_map/ppermute | solution.py:402
  21.1 10.2 %collective-permute-start.3 = (bf16[128,1024]{1,0:T(8,128)(2,1)S(1)}, bf16[128,1024]{1,0:T(8,128)(2,1)S(1)}, u32[]{:S(2)}, u32[]{:S(2)}) collective-permute-start(bf16[128,1024]{1,0:T(8,128)(2,1)S(1)} %get-tuple-element.66), channel_id=1, source_target_pairs={{0,2},{2,4},{4,6},{6,0},{8,10},{10,12},{12,14},{14,8},{16,18},{18,... | collective-permute-start | bytes 786440 | tf_op jit(solution)/shard_map/ppermute | solution.py:424
  25.7 12.9 %collective-permute-start.8 = (bf16[528,256]{1,0:T(8,128)(2,1)S(1)}, bf16[528,256]{1,0:T(8,128)(2,1)S(1)}, u32[]{:S(2)}, u32[]{:S(2)}) collective-permute-start(bf16[528,256]{1,0:T(8,128)(2,1)S(1)} %slice.42), channel_id=1, source_target_pairs={{0,8},{2,10},{4,12},{6,14},{8,16},{10,18},{12,20},{14,22},{16,24},... | collective-permute-start | bytes 811016 | tf_op jit(solution)/shard_map/ppermute | solution.py:399
  31.3 7.3 %collective-permute-start.10 = (bf16[272,256]{1,0:T(8,128)(2,1)S(1)}, bf16[272,256]{1,0:T(8,128)(2,1)S(1)}, u32[]{:S(2)}, u32[]{:S(2)}) collective-permute-start(bf16[272,256]{1,0:T(8,128)(2,1)S(1)} %slice.39), channel_id=1, source_target_pairs={{16,8},{18,10},{20,12},{22,14},{24,16},{26,18},{28,20},{30,22},{17... | collective-permute-start | bytes 417800 | tf_op jit(solution)/shard_map/ppermute | solution.py:402
  33.3 8.9 %collective-permute-start = (bf16[128,1024]{1,0:T(8,128)(2,1)S(1)}, bf16[128,1024]{1,0:T(8,128)(2,1)S(1)}, u32[]{:S(2)}, u32[]{:S(2)}) collective-permute-start(bf16[128,1024]{1,0:T(8,128)(2,1)S(1)} %get-tuple-element.67), channel_id=1, source_target_pairs={{0,2},{2,4},{4,6},{6,8},{8,10},{10,12},{12,14},{14,16},{16,18},{18... | collective-permute-start | bytes 786440 | tf_op jit(solution)/shard_map/ppermute | solution.py:430
  35.2 7.1 %collective-permute-start.4 = (bf16[128,1024]{1,0:T(8,128)(2,1)S(1)}, bf16[128,1024]{1,0:T(8,128)(2,1)S(1)}, u32[]{:S(2)}, u32[]{:S(2)}) collective-permute-start(bf16[128,1024]{1,0:T(8,128)(2,1)S(1)} %collective-permute-done.3.ring_rim), channel_id=1, source_target_pairs={{0,8},{8,16},{16,24},{1,9},{9,17},{17,25}} | collective-permute-start | bytes 786440 | tf_op jit(solution)/shard_map/ppermute | solution.py:432
  40.3 12.4 %collective-permute-start.11 = (bf16[272,768]{1,0:T(8,128)(2,1)S(1)}, bf16[272,768]{1,0:T(8,128)(2,1)S(1)}, u32[]{:S(2)}, u32[]{:S(2)}) collective-permute-start(bf16[272,768]{1,0:T(8,128)(2,1)S(1)} %far.1), channel_id=1, source_target_pairs={{8,16},{10,18},{12,20},{14,22},{16,24},{18,26},{20,28},{22,30},{9,... | collective-permute-start | bytes 1253384 | tf_op jit(solution)/shard_map/ppermute | solution.py:399
  42.4 23.6 %slice-start = ((s8[8388608]{0:T(1024)(128)(4,1)}), s8[4194304]{0:T(1024)(128)(4,1)S(1)}, s32[]{:S(2)}) async-start(s8[8388608]{0:T(1024)(128)(4,1)} %bitcast.1), calls=%async_computation | async-start | bytes 8388608
  53.1 7.4 %collective-permute-start.12 = (bf16[256,256]{1,0:T(8,128)(2,1)S(1)}, bf16[256,256]{1,0:T(8,128)(2,1)S(1)}, u32[]{:S(2)}, u32[]{:S(2)}) collective-permute-start(bf16[256,256]{1,0:T(8,128)(2,1)S(1)} %get-tuple-element.58), channel_id=1, source_target_pairs={{0,2},{2,0},{4,6},{6,4},{8,10},{10,8},{12,14},{14,12},{16,18},{18,... | collective-permute-start | bytes 393224 | tf_op jit(solution)/shard_map/ppermute | solution.py:396
  53.2 7.3 %collective-permute-start.13 = (bf16[256,256]{1,0:T(8,128)(2,1)S(1)}, bf16[256,256]{1,0:T(8,128)(2,1)S(1)}, u32[]{:S(2)}, u32[]{:S(2)}) collective-permute-start(bf16[256,256]{1,0:T(8,128)(2,1)S(1)} %get-tuple-element.59), channel_id=1, source_target_pairs={{0,4},{2,6},{4,0},{6,2},{8,12},{10,14},{12,8},{14,10},{16,20},{18,... | collective-permute-start | bytes 393224 | tf_op jit(solution)/shard_map/ppermute | solution.py:396
  53.3 7.2 %collective-permute-start.14 = (bf16[256,256]{1,0:T(8,128)(2,1)S(1)}, bf16[256,256]{1,0:T(8,128)(2,1)S(1)}, u32[]{:S(2)}, u32[]{:S(2)}) collective-permute-start(bf16[256,256]{1,0:T(8,128)(2,1)S(1)} %get-tuple-element.60), channel_id=1, source_target_pairs={{0,6},{2,4},{4,2},{6,0},{8,14},{10,12},{12,10},{14,8},{16,22},{18,... | collective-permute-start | bytes 393224 | tf_op jit(solution)/shard_map/ppermute | solution.py:396
  55.8 10.1 %slice-start.1 = ((s8[8388608]{0:T(1024)(128)(4,1)}), s8[4194304]{0:T(1024)(128)(4,1)S(1)}, s32[]{:S(2)}) async-start(s8[8388608]{0:T(1024)(128)(4,1)} %bitcast.1), calls=%async_computation.1 | async-start | bytes 8388608
  60.5 4.6 %collective-permute-start.15 = (bf16[256,256]{1,0:T(8,128)(2,1)S(1)}, bf16[256,256]{1,0:T(8,128)(2,1)S(1)}, u32[]{:S(2)}, u32[]{:S(2)}) collective-permute-start(bf16[256,256]{1,0:T(8,128)(2,1)S(1)} %get-tuple-element.62.refs_0_), channel_id=1, source_target_pairs={{0,1},{1,0},{2,3},{3,2},{4,5},{5,4},{6,7},{7,6},{8,9},{9,8},{10,11... | collective-permute-start | bytes 393224 | tf_op jit(solution)/shard_map/ppermute | solution.py:473
  64.1 1.3 %collective-permute-start.16 = (bf16[256,256]{1,0:T(8,128)(2,1)S(1)}, bf16[256,256]{1,0:T(8,128)(2,1)S(1)}, u32[]{:S(2)}, u32[]{:S(2)}) collective-permute-start(bf16[256,256]{1,0:T(8,128)(2,1)S(1)} %collective-permute-done.12.refs_1_), channel_id=1, source_target_pairs={{0,1},{1,0},{2,3},{3,2},{4,5},{5,4},{6,7},{7,6},{8,9},{9,8},{10,11... | collective-permute-start | bytes 393224 | tf_op jit(solution)/shard_map/ppermute | solution.py:473
  64.2 1.5 %collective-permute-start.17 = (bf16[256,256]{1,0:T(8,128)(2,1)S(1)}, bf16[256,256]{1,0:T(8,128)(2,1)S(1)}, u32[]{:S(2)}, u32[]{:S(2)}) collective-permute-start(bf16[256,256]{1,0:T(8,128)(2,1)S(1)} %collective-permute-done.13.refs_2_), channel_id=1, source_target_pairs={{0,1},{1,0},{2,3},{3,2},{4,5},{5,4},{6,7},{7,6},{8,9},{9,8},{10,11... | collective-permute-start | bytes 393224 | tf_op jit(solution)/shard_map/ppermute | solution.py:473
  64.6 1.3 %collective-permute-start.18 = (bf16[256,256]{1,0:T(8,128)(2,1)S(1)}, bf16[256,256]{1,0:T(8,128)(2,1)S(1)}, u32[]{:S(2)}, u32[]{:S(2)}) collective-permute-start(bf16[256,256]{1,0:T(8,128)(2,1)S(1)} %collective-permute-done.14.refs_3_), channel_id=1, source_target_pairs={{0,1},{1,0},{2,3},{3,2},{4,5},{5,4},{6,7},{7,6},{8,9},{9,8},{10,11... | collective-permute-start | bytes 393224 | tf_op jit(solution)/shard_map/ppermute | solution.py:473
  (2 other events, 7.7 us)

commit v8 on v4

--- a/solution.py
+++ b/solution.py
@@ -49,7 +49,7 @@
     taps[...] = jnp.dot(taps_ref[...], turn, preferred_element_type=jnp.float32)
     lane_group = lax.broadcasted_iota(jnp.int32, (LANES, windows * LANES), 1) % LANES // group
 
-    half = chans // 2
+    half = near_rim.shape[1]
     rim[:, :half] = near_rim[...]
     rim[:, half:] = ring_rim[...]
 
@@ -57,32 +57,53 @@
     def _():
         rim[:, half:] = far_rim[...]
 
-    @pl.loop(0, chans // LANES, unroll=2)
-    def _(tile):
-        cols = pl.ds(pl.multiple_of(tile * LANES, LANES), LANES)
-        rings = taps[pl.ds(pl.multiple_of(tile * per_tile, per_tile), per_tile), :]
-        mixed = (k_ref[:, cols].astype(jnp.float32) * v_ref[:, cols].astype(jnp.float32)).astype(
-            jnp.bfloat16
-        )
-        full = jnp.concatenate([rim[:, cols], mixed], axis=0)
-        stacked = jnp.concatenate(
-            [full[w * LANES : (w + 2) * LANES] for w in range(windows)], axis=1
-        )
-        conv = jnp.zeros((LANES, windows * LANES), jnp.float32)
-        for g in range(per_tile):
-            ring = pltpu.roll(
-                jnp.broadcast_to(rings[g : g + 1], shape), 0, 1, stride=1, stride_axis=0
-            ).astype(jnp.bfloat16)
-            table = jnp.concatenate([ring * before, ring * within], axis=1)
-            part = jnp.dot(table, stacked, preferred_element_type=jnp.float32)
-            conv = jnp.where(lane_group == g, part, conv)
-        conv = jnp.concatenate(
-            [conv[:, w * LANES : (w + 1) * LANES] for w in range(windows)], axis=0
-        )
-        out_ref[:, cols] = (
-            q_ref[:, cols].astype(jnp.float32)
-            * (conv + direct_ref[:, cols].astype(jnp.float32) * mixed.astype(jnp.float32))
+    def table(at):
+        ring = pltpu.roll(
+            jnp.broadcast_to(taps[pl.ds(at, 1), :], shape), 0, 1, stride=1, stride_axis=0
         ).astype(jnp.bfloat16)
+        return jnp.concatenate([ring * before, ring * within], axis=1)
+
+    pair = 2
+
+    @pl.loop(0, chans // LANES, step=pair)
+    def _(begin):
+        tiles = [
+            pl.ds(pl.multiple_of((begin + t) * LANES, LANES), LANES) for t in range(pair)
+        ]
+        mixed, stacked = [], []
+        for cols in tiles:
+            product = k_ref[:, cols].astype(jnp.float32) * v_ref[:, cols].astype(jnp.float32)
+            mixed.append(product.astype(jnp.bfloat16))
+            full = jnp.concatenate([rim[:, cols], mixed[-1]], axis=0)
+            stacked.append(
+                jnp.concatenate(
+                    [full[w * LANES : (w + 2) * LANES] for w in range(windows)], axis=1
+                )
+            )
+        steps = [(t, g) for t in range(pair) for g in range(per_tile)]
+        tables = [table((begin + t) * per_tile + g) for t, g in steps[:2]]
+        parts = [jnp.dot(tables[0], stacked[0], preferred_element_type=jnp.float32)]
+        conv = None
+        for i, (t, g) in enumerate(steps):
+            if i + 2 < len(steps):
+                t2, g2 = steps[i + 2]
+                tables.append(table((begin + t2) * per_tile + g2))
+            if i + 1 < len(steps):
+                parts.append(
+                    jnp.dot(
+                        tables[i + 1], stacked[steps[i + 1][0]], preferred_element_type=jnp.float32
+                    )
+                )
+            conv = parts[i] if g == 0 else jnp.where(lane_group == g, parts[i], conv)
+            if g == per_tile - 1:
+                cols = tiles[t]
+                joined = jnp.concatenate(
+                    [conv[:, w * LANES : (w + 1) * LANES] for w in range(windows)], axis=0
+                )
+                passed = direct_ref[:, cols].astype(jnp.float32) * mixed[t].astype(jnp.float32)
+                out_ref[:, cols] = (
+                    q_ref[:, cols].astype(jnp.float32) * (joined + passed)
+                ).astype(jnp.bfloat16)
 
 
 def hyena(hyena_q, hyena_k, hyena_v, rims, filters, direct):
@@ -200,19 +221,20 @@
             queries[h, span, HD:] = mask
 
 
-def attend(query, keys, values, diagonal):
+def score_of(query, keys):
+    return lax.dot_general(
+        keys, query, (((1,), (1,)), ((), ())), preferred_element_type=jnp.float32
+    )
+
+
+def attend(score, values, diagonal):
     factor = math.log2(math.e) / math.sqrt(HD)
-    rows = query.shape[0]
-    score = lax.dot_general(
-        keys, query, (((1,), (1,)), ((), ())), preferred_element_type=jnp.float32
-    )
+    rows = score.shape[1]
     if diagonal:
         older = lax.broadcasted_iota(jnp.int32, (rows, rows), 0) <= lax.broadcasted_iota(
             jnp.int32, (rows, rows), 1
         )
-        score = jnp.concatenate(
-            [score[:-rows], jnp.where(older, score[-rows:], NEG)], axis=0
-        )
+        score = jnp.concatenate([score[:-rows], jnp.where(older, score[-rows:], NEG)], axis=0)
     high = jnp.max(score, axis=0, keepdims=True)
     expo = jnp.exp2((score - high) * factor)
     total = jnp.sum(expo, axis=0, keepdims=True)
@@ -223,6 +245,13 @@
         preferred_element_type=jnp.float32,
     )
     return summed / total, high * factor + jnp.log2(total)
+
+
+def ahead(steps, product):
+    late = product(*steps[0])
+    for step, following in zip(steps, steps[1:] + [None]):
+        now, late = late, product(*following) if following else None
+        yield step, now
 
 
 def main_kernel(*refs):
@@ -236,14 +265,16 @@
     place_queries(asked, corner, rows, queries)
     place_keys(held, corner, SQUAD, rows, keys, values)
     place_keys(near_parts(near, rows), corner, 0, rows, keys, values)
-    for j in range(SQUAD):
-        cols = slice(j * rows, (j + 1) * rows)
-        reach = (SQUAD + 1 + j) * rows
-        for h in range(heads):
-            mixed, lse = attend(queries[h, cols], keys[h, :reach], values[h, :reach], True)
-            out[h * HD : (h + 1) * HD, cols] = mixed
-            out[width + h : width + h + 1, cols] = lse
-        out[width + heads :, cols] = jnp.zeros((TAG - heads, rows), jnp.float32)
+    span = [slice(j * rows, (j + 1) * rows) for j in range(SQUAD)]
+    reach = [(SQUAD + 1 + j) * rows for j in range(SQUAD)]
+    steps = [(j, h) for j in range(SQUAD) for h in range(heads)]
+    for (j, h), score in ahead(
+        steps, lambda j, h: score_of(queries[h, span[j]], keys[h, : reach[j]])
+    ):
+        mixed, lse = attend(score, values[h, : reach[j]], True)
+        out[h * HD : (h + 1) * HD, span[j]] = mixed
+        out[width + h : width + h + 1, span[j]] = lse
+    out[width + heads :, :] = jnp.zeros((TAG - heads, SQUAD * rows), jnp.float32)
 
 
 def far_kernel(*refs):
@@ -256,19 +287,20 @@
     asked = [asked[0].at[k * tall : (k + 1) * tall] for k in range(SQUAD - 1)] + [asked[1]]
     place_queries(asked, corner, rows, queries)
     place_keys(near_parts(near, rows), corner, 0, rows, keys, values)
-    for j in range(SQUAD - 1):
-        cols = slice(j * rows, (j + 1) * rows)
-        stats = []
-        for h in range(heads):
-            mixed, lse = attend(
-                queries[h, cols], keys[h, cols.stop :], values[h, cols.stop :], False
-            )
-            out[h * HD : (h + 1) * HD, cols] = mixed.astype(out.dtype)
-            top = lse.astype(jnp.bfloat16).astype(jnp.float32)
-            mid = (lse - top).astype(jnp.bfloat16).astype(jnp.float32)
-            stats += [top, mid, lse - top - mid]
-        stats.append(jnp.zeros((TAG - len(stats), rows), jnp.float32))
-        out[width:, cols] = jnp.concatenate(stats, axis=0).astype(out.dtype)
+    span = [slice(j * rows, (j + 1) * rows) for j in range(SQUAD)]
+    stats = [[] for _ in range(SQUAD - 1)]
+    steps = [(j, h) for j in range(SQUAD - 1) for h in range(heads)]
+    for (j, h), score in ahead(
+        steps, lambda j, h: score_of(queries[h, span[j]], keys[h, span[j].stop :])
+    ):
+        mixed, lse = attend(score, values[h, span[j].stop :], False)
+        out[h * HD : (h + 1) * HD, span[j]] = mixed.astype(out.dtype)
+        top = lse.astype(jnp.bfloat16).astype(jnp.float32)
+        mid = (lse - top).astype(jnp.bfloat16).astype(jnp.float32)
+        stats[j] += [top, mid, lse - top - mid]
+    for j, stat in enumerate(stats):
+        stat.append(jnp.zeros((TAG - len(stat), rows), jnp.float32))
+        out[width:, span[j]] = jnp.concatenate(stat, axis=0).astype(out.dtype)
 
 
 def merge_kernel(main_ref, far_ref, *refs):
@@ -349,17 +381,13 @@
     tail_k = hyena_k[rows - LANES :].astype(f32)
     tail_v = hyena_v[rows - LANES :].astype(f32)
     tail = (tail_k * tail_v).astype(bf16)
-    half = tail.shape[1] // 2
+    half = tail.shape[1] * 12 // 16
     ring = lax.ppermute(
         tail[:, half:], "ctx", [(i, i - i % SQUAD + (i + 1) % SQUAD) for i in range(count)]
     )
     across, ring = lax.optimization_barrier((across, ring))
     back.append(descend(across[:tall]))
-    rims = [
-        lax.ppermute(tail[:, :half], "ctx", [(i, i + 1) for i in range(count - 1)]),
-        ring,
-        lax.ppermute(ring, "ctx", [(i, i + SQUAD) for i in range(0, count - SQUAD, SQUAD)]),
-    ]
+    rims = [lax.ppermute(tail[:, :half], "ctx", [(i, i + 1) for i in range(count - 1)]), ring]
     own = [asked, kept, *beside, across]
     def store(blocks):
         return [
@@ -378,7 +406,7 @@
         exps=6 * rows * rows * heads,
     )
     far = climb(far, SQUAD)
-    own[1], *rims = lax.optimization_barrier((own[1], *rims))
+    own[1], rims[0] = lax.optimization_barrier((own[1], rims[0]))
     (main,) = kernel_call(
         main_kernel,
         (*own, *near),
@@ -387,6 +415,10 @@
         store(2 * SQUAD),
         flops=26 * 4 * rows * rows * width,
         exps=26 * rows * rows * heads,
+    )
+    main, rims[1] = lax.optimization_barrier((main, rims[1]))
+    rims.append(
+        lax.ppermute(rims[1], "ctx", [(i, i + SQUAD) for i in range(0, count - SQUAD, SQUAD)])
     )
     done = kernel_call(
         merge_kernel,

time: 69.6 us -> 76.8 us (1.10)
  waiting for transfers between devices: 11.3 us -> 18.9 us
  starting transfers between devices: 33.5 us -> 37.7 us
  Pallas kernels: 21.5 us -> 18.5 us
  other arithmetic: 1.24 us -> 0.19 us
    ppermute x2, waiting for transfers between devices: 0.01 us -> 3.99 us  [descend(): lax.ppermute(value, 'ctx', [(i, i - SQUAD) for i in range(2 * SQUAD, coun...]
    ppermute x1, waiting for transfers between devices: 0.01 us -> 3.86 us  [local(): lax.ppermute(tail[:, :half], 'ctx', [(i, i + 1) for i in range(count - 1)])]
    ppermute x4, starting transfers between devices: 4.63 us -> 8.41 us  [turn(): lax.ppermute(value, 'tp', [(t, (t + r) % ranks) for t in range(ranks)])]
    ppermute x1, waiting for transfers between devices: 3.2 us -> 0.01 us  [local(): lax.ppermute(tail[:, half:], 'ctx', [(i, i - i % SQUAD + (i + 1) % SQUAD)...]
    pallas_call x5, Pallas kernels: 19.8 us -> 16.9 us  [kernel_call(): pl.pallas_call(kernel, in_specs=[VMEM] * len(args), out_specs=[VMEM] * le...]
    ppermute x1, waiting for transfers between devices: 0.01 us -> 2.1 us  [local(): lax.ppermute(rims[1], 'ctx', [(i, i + SQUAD) for i in range(0, count - SQ...]
    ppermute x1, starting transfers between devices: 2.22 us -> 3.37 us  [local(): lax.ppermute(tail[:, :half], 'ctx', [(i, i + 1) for i in range(count - 1)])]
    convert_element_type x1, other arithmetic: 1.17 us -> 0.13 us  [local(): tail = (tail_k * tail_v).astype(bf16)]
  transfers between devices with their start and end apart: 19 -> 19, of which waited for: 8 -> 9; matrix products, arithmetic and copies ran while one was open for 2% -> 0% of each run, Pallas kernels for 23% -> 18%
where the time goes in v8:
time: 76.8 us; the launch traced here: 76.4 us
  starting transfers between devices  37.7 us (49%)
  waiting for transfers between devices  18.9 us (25%)
  Pallas kernels  18.5 us (24%)
  between operations  0.94 us (1%)
    pallas_call x5, Pallas kernels, kernel_call(): pl.pallas_call(kernel, in_specs=[VMEM] * len(args), out_specs=[VMEM] * le...  16.9 us
    ppermute x4, starting transfers between devices, climb(): lax.ppermute(value, 'ctx', [(i, i + SQUAD) for i in range(first, count -...  11.5 us
    ppermute x4, starting transfers between devices, turn(): lax.ppermute(value, 'tp', [(t, (t + r) % ranks) for t in range(ranks)])  8.41 us
    ppermute x6, starting transfers between devices, swap(): return lax.ppermute(value, 'ctx', [(i, i ^ mask) for i in range(count)])  6.47 us
    ppermute x4, waiting for transfers between devices, climb(): lax.ppermute(value, 'ctx', [(i, i + SQUAD) for i in range(first, count -...  5.42 us
    ppermute x2, starting transfers between devices, descend(): lax.ppermute(value, 'ctx', [(i, i - SQUAD) for i in range(2 * SQUAD, coun...  4.16 us
    ppermute x2, waiting for transfers between devices, descend(): lax.ppermute(value, 'ctx', [(i, i - SQUAD) for i in range(2 * SQUAD, coun...  3.99 us
    ppermute x1, waiting for transfers between devices, local(): lax.ppermute(tail[:, :half], 'ctx', [(i, i + 1) for i in range(count - 1)])  3.86 us
  transfers between devices with their start and end apart: 19, of which 9 were waited for; matrix products, arithmetic and copies ran while one was open for 0% of the time, Pallas kernels for 18%

profile of v8, /device:TPU:17, one launch (start us, length us, event | category | flops | bytes accessed | tf_op | source)
XLA Modules:
  0.0 76.4 jit_solution(14676474568481022620)
XLA Ops:
  0.6 1.6 %deal.1 = (bf16[272,256]{1,0:T(8,128)(2,1)S(1)}, bf16[528,256]{1,0:T(8,128)(2,1)S(1)}, bf16[784,256]{1,0:T(8,128)(2,1)S(1)}, bf16[784,256]{1,0:T(8,128)(2,1)S(1)}, bf16[784,256]{1,0:T(8,128)(2,1)S(1)}) custom-call(bf16[256,1024]{1,0:T(8,128)(2,1)} %q_ref.2, bf16[256,1024]{1,0:T(8,128)(2,1)} %k_ref.2, bf16[256,1024]{1,0:T(8,128)(2,1)} %v_ref.2, s32[2,128]{1,0:T(2,128)} %bitcast.3), custom_call_target="tpu_custom_call" | custom-call | bytes 3145728 | tf_op jit(solution)/shard_map/deal/pallas_call | solution.py:166
  2.2 1.3 %collective-permute-start.2 = (bf16[784,256]{1,0:T(8,128)(2,1)S(1)}, bf16[784,256]{1,0:T(8,128)(2,1)S(1)}, u32[]{:S(2)}, u32[]{:S(2)}) collective-permute-start(bf16[784,256]{1,0:T(8,128)(2,1)S(1)} %get-tuple-element.37), channel_id=1, source_target_pairs={{0,4},{2,6},{4,0},{6,2},{8,12},{10,14},{12,8},{14,10},{16,20},{18,... | collective-permute-start | bytes 1204232 | tf_op jit(solution)/shard_map/ppermute | solution.py:359
  3.5 1.2 %collective-permute-start.1 = (bf16[784,256]{1,0:T(8,128)(2,1)S(1)}, bf16[784,256]{1,0:T(8,128)(2,1)S(1)}, u32[]{:S(2)}, u32[]{:S(2)}) collective-permute-start(bf16[784,256]{1,0:T(8,128)(2,1)S(1)} %get-tuple-element.35), channel_id=1, source_target_pairs={{0,2},{2,0},{4,6},{6,4},{8,10},{10,8},{12,14},{14,12},{16,18},{18,... | collective-permute-start | bytes 1204232 | tf_op jit(solution)/shard_map/ppermute | solution.py:359
  4.8 3.2 %collective-permute-start.3 = (bf16[528,256]{1,0:T(8,128)(2,1)S(1)}, bf16[528,256]{1,0:T(8,128)(2,1)S(1)}, u32[]{:S(2)}, u32[]{:S(2)}) collective-permute-start(bf16[528,256]{1,0:T(8,128)(2,1)S(1)} %get-tuple-element.33.refs_1_), channel_id=1, source_target_pairs={{0,8},{2,10},{4,12},{6,14},{8,16},{10,18},{12,20},{14,22},{16,24},... | collective-permute-start | bytes 811016 | tf_op jit(solution)/shard_map/ppermute | solution.py:362
  8.0 5.4 %collective-permute-done.3.refs_5_.refs_2_ = bf16[528,256]{1,0:T(8,128)(2,1)S(1)} collective-permute-done((bf16[528,256]{1,0:T(8,128)(2,1)S(1)}, bf16[528,256]{1,0:T(8,128)(2,1)S(1)}, u32[]{:S(2)}, u32[]{:S(2)}) %collective-permute-start.3) | collective-permute-done | bytes 270368 | tf_op jit(solution)/shard_map/ppermute | solution.py:362
  13.5 1.3 %collective-permute-start.4 = (bf16[784,256]{1,0:T(8,128)(2,1)S(1)}, bf16[784,256]{1,0:T(8,128)(2,1)S(1)}, u32[]{:S(2)}, u32[]{:S(2)}) collective-permute-start(bf16[784,256]{1,0:T(8,128)(2,1)S(1)} %get-tuple-element.39), channel_id=1, source_target_pairs={{0,6},{2,4},{4,2},{6,0},{8,14},{10,12},{12,10},{14,8},{16,22},{18,... | collective-permute-start | bytes 1204232 | tf_op jit(solution)/shard_map/ppermute | solution.py:359
  14.9 3.2 %collective-permute-start.6 = (bf16[1056,256]{1,0:T(8,128)(2,1)S(1)}, bf16[1056,256]{1,0:T(8,128)(2,1)S(1)}, u32[]{:S(2)}, u32[]{:S(2)}) collective-permute-start(bf16[1056,256]{1,0:T(8,128)(2,1)S(1)} %pad_maximum_fusion), channel_id=1, source_target_pairs={{0,8},{2,10},{4,12},{6,14},{8,16},{10,18},{12,20},{14,22},{16,24},... | collective-permute-start | bytes 1622024 | tf_op jit(solution)/shard_map/ppermute | solution.py:362
  18.1 2.1 %collective-permute-start.9 = (bf16[816,256]{1,0:T(8,128)(2,1)S(1)}, bf16[816,256]{1,0:T(8,128)(2,1)S(1)}, u32[]{:S(2)}, u32[]{:S(2)}) collective-permute-start(bf16[816,256]{1,0:T(8,128)(2,1)S(1)} %pad_maximum_fusion.1), channel_id=1, source_target_pairs={{16,8},{18,10},{20,12},{22,14},{24,16},{26,18},{28,20},{30,22},{17... | collective-permute-start | bytes 1253384 | tf_op jit(solution)/shard_map/ppermute | solution.py:365
  20.4 0.4 collective-permute-start.5
  20.8 2.3 %collective-permute-done.4.refs_4_ = bf16[784,256]{1,0:T(8,128)(2,1)S(1)} collective-permute-done((bf16[784,256]{1,0:T(8,128)(2,1)S(1)}, bf16[784,256]{1,0:T(8,128)(2,1)S(1)}, u32[]{:S(2)}, u32[]{:S(2)}) %collective-permute-start.4) | collective-permute-done | bytes 401440 | tf_op jit(solution)/shard_map/ppermute | solution.py:359
  23.1 3.2 %collective-permute-start.7 = (bf16[528,256]{1,0:T(8,128)(2,1)S(1)}, bf16[528,256]{1,0:T(8,128)(2,1)S(1)}, u32[]{:S(2)}, u32[]{:S(2)}) collective-permute-start(bf16[528,256]{1,0:T(8,128)(2,1)S(1)} %slice.42), channel_id=1, source_target_pairs={{0,8},{2,10},{4,12},{6,14},{8,16},{10,18},{12,20},{14,22},{16,24},... | collective-permute-start | bytes 811016 | tf_op jit(solution)/shard_map/ppermute | solution.py:362
  26.4 3.4 %collective-permute-start = (bf16[128,1536]{1,0:T(8,128)(2,1)S(1)}, bf16[128,1536]{1,0:T(8,128)(2,1)S(1)}, u32[]{:S(2)}, u32[]{:S(2)}) collective-permute-start(bf16[128,1536]{1,0:T(8,128)(2,1)S(1)} %slice.40), channel_id=1, source_target_pairs={{0,2},{2,4},{4,6},{6,8},{8,10},{10,12},{12,14},{14,16},{16,18},{18... | collective-permute-start | bytes 1179656 | tf_op jit(solution)/shard_map/ppermute | solution.py:390
  29.8 2.1 %collective-permute-start.10 = (bf16[272,256]{1,0:T(8,128)(2,1)S(1)}, bf16[272,256]{1,0:T(8,128)(2,1)S(1)}, u32[]{:S(2)}, u32[]{:S(2)}) collective-permute-start(bf16[272,256]{1,0:T(8,128)(2,1)S(1)} %slice.39), channel_id=1, source_target_pairs={{16,8},{18,10},{20,12},{22,14},{24,16},{26,18},{28,20},{30,22},{17... | collective-permute-start | bytes 417800 | tf_op jit(solution)/shard_map/ppermute | solution.py:365
  31.9 4.0 %collective-permute-done.10.refs_1_ = bf16[272,256]{1,0:T(8,128)(2,1)S(1)} collective-permute-done((bf16[272,256]{1,0:T(8,128)(2,1)S(1)}, bf16[272,256]{1,0:T(8,128)(2,1)S(1)}, u32[]{:S(2)}, u32[]{:S(2)}) %collective-permute-start.10) | collective-permute-done | bytes 139296 | tf_op jit(solution)/shard_map/ppermute | solution.py:365
  35.9 1.7 %far.1 = bf16[272,768]{1,0:T(8,128)(2,1)S(1)} custom-call(bf16[816,256]{1,0:T(8,128)(2,1)S(1)} %collective-permute-done.9.refs_0_, bf16[272,256]{1,0:T(8,128)(2,1)S(1)} %collective-permute-done.10.refs_1_, bf16[528,256]{1,0:T(8,128)(2,1)S(1)} %collective-permute-done.3.refs_5_.refs_2_, bf16[1056,256]{1,0:T(8,128)(2,1)S(1)} %collective-permute-done.6.refs_6_.refs_3_, ...), custom_call_target="tpu_custom_call" | custom-call | flops 402653184 | bytes 2056192 | tf_op jit(solution)/shard_map/far/pallas_call | solution.py:26
  37.6 1.9 %collective-permute-start.11 = (bf16[272,768]{1,0:T(8,128)(2,1)S(1)}, bf16[272,768]{1,0:T(8,128)(2,1)S(1)}, u32[]{:S(2)}, u32[]{:S(2)}) collective-permute-start(bf16[272,768]{1,0:T(8,128)(2,1)S(1)} %far.1), channel_id=1, source_target_pairs={{8,16},{10,18},{12,20},{14,22},{16,24},{18,26},{20,28},{22,30},{9,... | collective-permute-start | bytes 1253384 | tf_op jit(solution)/shard_map/ppermute | solution.py:362
  39.5 3.9 %collective-permute-done.near_rim = bf16[128,1536]{1,0:T(8,128)(2,1)S(1)} collective-permute-done((bf16[128,1536]{1,0:T(8,128)(2,1)S(1)}, bf16[128,1536]{1,0:T(8,128)(2,1)S(1)}, u32[]{:S(2)}, u32[]{:S(2)}) %collective-permute-start) | collective-permute-done | bytes 393248 | tf_op jit(solution)/shard_map/ppermute | solution.py:390
  43.4 6.0 %main.1.main_ref = f32[272,1024]{1,0:T(8,128)S(1)} custom-call(bf16[272,256]{1,0:T(8,128)(2,1)S(1)} %get-tuple-element.32.refs_0_, bf16[528,256]{1,0:T(8,128)(2,1)S(1)} %get-tuple-element.33.refs_1_, bf16[784,256]{1,0:T(8,128)(2,1)S(1)} %collective-permute-done.1.refs_2_, bf16[784,256]{1,0:T(8,128)(2,1)S(1)} %collective-permute-done.2.refs_3_, ...), custom_call_target="tpu_custom_call" | custom-call | flops 1744830464 | bytes 3809280 | tf_op jit(solution)/shard_map/main/pallas_call | solution.py:26
  49.5 3.3 %collective-permute-start.8 = (bf16[128,512]{1,0:T(8,128)(2,1)S(1)}, bf16[128,512]{1,0:T(8,128)(2,1)S(1)}, u32[]{:S(2)}, u32[]{:S(2)}) collective-permute-start(bf16[128,512]{1,0:T(8,128)(2,1)S(1)} %collective-permute-done.5.ring_rim), channel_id=1, source_target_pairs={{0,8},{8,16},{16,24},{1,9},{9,17},{17,25}} | collective-permute-start | bytes 393224 | tf_op jit(solution)/shard_map/ppermute | solution.py:421
  53.2 2.1 %collective-permute-done.8.far_rim = bf16[128,512]{1,0:T(8,128)(2,1)S(1)} collective-permute-done((bf16[128,512]{1,0:T(8,128)(2,1)S(1)}, bf16[128,512]{1,0:T(8,128)(2,1)S(1)}, u32[]{:S(2)}, u32[]{:S(2)}) %collective-permute-start.8) | collective-permute-done | bytes 131104 | tf_op jit(solution)/shard_map/ppermute | solution.py:421
  55.3 2.6 %collective-permute-start.14 = (bf16[256,256]{1,0:T(8,128)(2,1)S(1)}, bf16[256,256]{1,0:T(8,128)(2,1)S(1)}, u32[]{:S(2)}, u32[]{:S(2)}) collective-permute-start(bf16[256,256]{1,0:T(8,128)(2,1)S(1)} %get-tuple-element.52), channel_id=1, source_target_pairs={{0,6},{2,4},{4,2},{6,0},{8,14},{10,12},{12,10},{14,8},{16,22},{18,... | collective-permute-start | bytes 393224 | tf_op jit(solution)/shard_map/ppermute | solution.py:359
  58.0 5.3 %hyena.1 = bf16[256,2048]{1,0:T(8,128)(2,1)} custom-call(bf16[256,2048]{1,0:T(8,128)(2,1)S(1)} %copy-done.2, bf16[256,2048]{1,0:T(8,128)(2,1)S(1)} %copy-done, bf16[256,2048]{1,0:T(8,128)(2,1)S(1)} %copy-done.1, bf16[128,1536]{1,0:T(8,128)(2,1)S(1)} %collective-permute-done.near_rim, bf16[128,512]{1,0:T(8,128)(2,1)S(1)} %collective-permute-done.5.ring_rim, ...), custom_call_target="tpu_custom_call" | custom-call | flops 4294967296 | bytes 4886528 | tf_op jit(solution)/shard_map/hyena/pallas_call | solution.py:26
  63.3 7.8 %collective-permute-start.15 = (bf16[256,256]{1,0:T(8,128)(2,1)S(1)}, bf16[256,256]{1,0:T(8,128)(2,1)S(1)}, u32[]{:S(2)}, u32[]{:S(2)}) collective-permute-start(bf16[256,256]{1,0:T(8,128)(2,1)S(1)} %get-tuple-element.54.refs_0_), channel_id=1, source_target_pairs={{0,1},{1,0},{2,3},{3,2},{4,5},{5,4},{6,7},{7,6},{8,9},{9,8},{10,11... | collective-permute-start | bytes 393224 | tf_op jit(solution)/shard_map/ppermute | solution.py:434
  73.0 3.5 %project.1 = bf16[256,2048]{1,0:T(8,128)(2,1)} custom-call(bf16[256,256]{1,0:T(8,128)(2,1)S(1)} %get-tuple-element.54.refs_0_, bf16[256,256]{1,0:T(8,128)(2,1)S(1)} %collective-permute-done.12.refs_1_, bf16[256,256]{1,0:T(8,128)(2,1)S(1)} %collective-permute-done.13.refs_2_, bf16[256,256]{1,0:T(8,128)(2,1)S(1)} %collective-permute-done.14.refs_3_, ...), custom_call_target="tpu_custom_call" | custom-call | flops 2147483648 | bytes 10485760 | tf_op jit(solution)/shard_map/project/pallas_call | solution.py:26
  (47 shorter events, 2.6 us)
Async XLA Ops:
  2.2 11.1 %collective-permute-start.2 = (bf16[784,256]{1,0:T(8,128)(2,1)S(1)}, bf16[784,256]{1,0:T(8,128)(2,1)S(1)}, u32[]{:S(2)}, u32[]{:S(2)}) collective-permute-start(bf16[784,256]{1,0:T(8,128)(2,1)S(1)} %get-tuple-element.37), channel_id=1, source_target_pairs={{0,4},{2,6},{4,0},{6,2},{8,12},{10,14},{12,8},{14,10},{16,20},{18,... | collective-permute-start | bytes 1204232 | tf_op jit(solution)/shard_map/ppermute | solution.py:359
  3.5 9.9 %collective-permute-start.1 = (bf16[784,256]{1,0:T(8,128)(2,1)S(1)}, bf16[784,256]{1,0:T(8,128)(2,1)S(1)}, u32[]{:S(2)}, u32[]{:S(2)}) collective-permute-start(bf16[784,256]{1,0:T(8,128)(2,1)S(1)} %get-tuple-element.35), channel_id=1, source_target_pairs={{0,2},{2,0},{4,6},{6,4},{8,10},{10,8},{12,14},{14,12},{16,18},{18,... | collective-permute-start | bytes 1204232 | tf_op jit(solution)/shard_map/ppermute | solution.py:359
  4.8 8.6 %collective-permute-start.3 = (bf16[528,256]{1,0:T(8,128)(2,1)S(1)}, bf16[528,256]{1,0:T(8,128)(2,1)S(1)}, u32[]{:S(2)}, u32[]{:S(2)}) collective-permute-start(bf16[528,256]{1,0:T(8,128)(2,1)S(1)} %get-tuple-element.33.refs_1_), channel_id=1, source_target_pairs={{0,8},{2,10},{4,12},{6,14},{8,16},{10,18},{12,20},{14,22},{16,24},... | collective-permute-start | bytes 811016 | tf_op jit(solution)/shard_map/ppermute | solution.py:362
  13.5 9.6 %collective-permute-start.4 = (bf16[784,256]{1,0:T(8,128)(2,1)S(1)}, bf16[784,256]{1,0:T(8,128)(2,1)S(1)}, u32[]{:S(2)}, u32[]{:S(2)}) collective-permute-start(bf16[784,256]{1,0:T(8,128)(2,1)S(1)} %get-tuple-element.39), channel_id=1, source_target_pairs={{0,6},{2,4},{4,2},{6,0},{8,14},{10,12},{12,10},{14,8},{16,22},{18,... | collective-permute-start | bytes 1204232 | tf_op jit(solution)/shard_map/ppermute | solution.py:359
  14.9 17.0 %collective-permute-start.6 = (bf16[1056,256]{1,0:T(8,128)(2,1)S(1)}, bf16[1056,256]{1,0:T(8,128)(2,1)S(1)}, u32[]{:S(2)}, u32[]{:S(2)}) collective-permute-start(bf16[1056,256]{1,0:T(8,128)(2,1)S(1)} %pad_maximum_fusion), channel_id=1, source_target_pairs={{0,8},{2,10},{4,12},{6,14},{8,16},{10,18},{12,20},{14,22},{16,24},... | collective-permute-start | bytes 1622024 | tf_op jit(solution)/shard_map/ppermute | solution.py:362
  18.1 13.7 %collective-permute-start.9 = (bf16[816,256]{1,0:T(8,128)(2,1)S(1)}, bf16[816,256]{1,0:T(8,128)(2,1)S(1)}, u32[]{:S(2)}, u32[]{:S(2)}) collective-permute-start(bf16[816,256]{1,0:T(8,128)(2,1)S(1)} %pad_maximum_fusion.1), channel_id=1, source_target_pairs={{16,8},{18,10},{20,12},{22,14},{24,16},{26,18},{28,20},{30,22},{17... | collective-permute-start | bytes 1253384 | tf_op jit(solution)/shard_map/ppermute | solution.py:365
  20.4 9.4 %collective-permute-start.5 = (bf16[128,512]{1,0:T(8,128)(2,1)S(1)}, bf16[128,512]{1,0:T(8,128)(2,1)S(1)}, u32[]{:S(2)}, u32[]{:S(2)}) collective-permute-start(bf16[128,512]{1,0:T(8,128)(2,1)S(1)} %slice.41), channel_id=1, source_target_pairs={{0,2},{2,4},{4,6},{6,0},{8,10},{10,12},{12,14},{14,8},{16,18},{18,... | collective-permute-start | bytes 393224 | tf_op jit(solution)/shard_map/ppermute | solution.py:385
  23.1 12.8 %collective-permute-start.7 = (bf16[528,256]{1,0:T(8,128)(2,1)S(1)}, bf16[528,256]{1,0:T(8,128)(2,1)S(1)}, u32[]{:S(2)}, u32[]{:S(2)}) collective-permute-start(bf16[528,256]{1,0:T(8,128)(2,1)S(1)} %slice.42), channel_id=1, source_target_pairs={{0,8},{2,10},{4,12},{6,14},{8,16},{10,18},{12,20},{14,22},{16,24},... | collective-permute-start | bytes 811016 | tf_op jit(solution)/shard_map/ppermute | solution.py:362
  26.4 17.0 %collective-permute-start = (bf16[128,1536]{1,0:T(8,128)(2,1)S(1)}, bf16[128,1536]{1,0:T(8,128)(2,1)S(1)}, u32[]{:S(2)}, u32[]{:S(2)}) collective-permute-start(bf16[128,1536]{1,0:T(8,128)(2,1)S(1)} %slice.40), channel_id=1, source_target_pairs={{0,2},{2,4},{4,6},{6,8},{8,10},{10,12},{12,14},{14,16},{16,18},{18... | collective-permute-start | bytes 1179656 | tf_op jit(solution)/shard_map/ppermute | solution.py:390
  29.8 6.1 %collective-permute-start.10 = (bf16[272,256]{1,0:T(8,128)(2,1)S(1)}, bf16[272,256]{1,0:T(8,128)(2,1)S(1)}, u32[]{:S(2)}, u32[]{:S(2)}) collective-permute-start(bf16[272,256]{1,0:T(8,128)(2,1)S(1)} %slice.39), channel_id=1, source_target_pairs={{16,8},{18,10},{20,12},{22,14},{24,16},{26,18},{28,20},{30,22},{17... | collective-permute-start | bytes 417800 | tf_op jit(solution)/shard_map/ppermute | solution.py:365
  37.6 15.2 %copy-start.4 = (bf16[2048]{0:T(1024)(128)(2,1)S(1)}, bf16[2048]{0:T(1024)(128)(2,1)}, u32[]{:S(2)}) copy-start(bf16[2048]{0:T(1024)(128)(2,1)} %param.14) | copy-start | bytes 12292
  37.6 15.2 %collective-permute-start.11 = (bf16[272,768]{1,0:T(8,128)(2,1)S(1)}, bf16[272,768]{1,0:T(8,128)(2,1)S(1)}, u32[]{:S(2)}, u32[]{:S(2)}) collective-permute-start(bf16[272,768]{1,0:T(8,128)(2,1)S(1)} %far.1), channel_id=1, source_target_pairs={{8,16},{10,18},{12,20},{14,22},{16,24},{18,26},{20,28},{22,30},{9,... | collective-permute-start | bytes 1253384 | tf_op jit(solution)/shard_map/ppermute | solution.py:362
  49.4 8.5 %copy-start.2 = (bf16[256,2048]{1,0:T(8,128)(2,1)S(1)}, bf16[256,2048]{1,0:T(8,128)(2,1)}, u32[]{:S(2)}) copy-start(bf16[256,2048]{1,0:T(8,128)(2,1)} %q_ref.3) | copy-start | bytes 3145732
  49.5 8.5 %copy-start.3 = (bf16[128,128]{1,0:T(8,128)(2,1)S(1)}, bf16[128,128]{1,0:T(8,128)(2,1)}, u32[]{:S(2)}) copy-start(bf16[128,128]{1,0:T(8,128)(2,1)} %taps_ref.1) | copy-start | bytes 98308
  49.5 5.8 %collective-permute-start.8 = (bf16[128,512]{1,0:T(8,128)(2,1)S(1)}, bf16[128,512]{1,0:T(8,128)(2,1)S(1)}, u32[]{:S(2)}, u32[]{:S(2)}) collective-permute-start(bf16[128,512]{1,0:T(8,128)(2,1)S(1)} %collective-permute-done.5.ring_rim), channel_id=1, source_target_pairs={{0,8},{8,16},{16,24},{1,9},{9,17},{17,25}} | collective-permute-start | bytes 393224 | tf_op jit(solution)/shard_map/ppermute | solution.py:421
  55.3 8.0 %collective-permute-start.12 = (bf16[256,256]{1,0:T(8,128)(2,1)S(1)}, bf16[256,256]{1,0:T(8,128)(2,1)S(1)}, u32[]{:S(2)}, u32[]{:S(2)}) collective-permute-start(bf16[256,256]{1,0:T(8,128)(2,1)S(1)} %get-tuple-element.50), channel_id=1, source_target_pairs={{0,2},{2,0},{4,6},{6,4},{8,10},{10,8},{12,14},{14,12},{16,18},{18,... | collective-permute-start | bytes 393224 | tf_op jit(solution)/shard_map/ppermute | solution.py:359
  55.3 8.0 %collective-permute-start.13 = (bf16[256,256]{1,0:T(8,128)(2,1)S(1)}, bf16[256,256]{1,0:T(8,128)(2,1)S(1)}, u32[]{:S(2)}, u32[]{:S(2)}) collective-permute-start(bf16[256,256]{1,0:T(8,128)(2,1)S(1)} %get-tuple-element.51), channel_id=1, source_target_pairs={{0,4},{2,6},{4,0},{6,2},{8,12},{10,14},{12,8},{14,10},{16,20},{18,... | collective-permute-start | bytes 393224 | tf_op jit(solution)/shard_map/ppermute | solution.py:359
  55.3 17.6 %slice-start = ((s8[8388608]{0:T(1024)(128)(4,1)}), s8[4194304]{0:T(1024)(128)(4,1)S(1)}, s32[]{:S(2)}) async-start(s8[8388608]{0:T(1024)(128)(4,1)} %bitcast.1), calls=%async_computation | async-start | bytes 8388608
  55.3 17.6 %slice-start.1 = ((s8[8388608]{0:T(1024)(128)(4,1)}), s8[4194304]{0:T(1024)(128)(4,1)S(1)}, s32[]{:S(2)}) async-start(s8[8388608]{0:T(1024)(128)(4,1)} %bitcast.1), calls=%async_computation.1 | async-start | bytes 8388608
  55.3 7.9 %collective-permute-start.14 = (bf16[256,256]{1,0:T(8,128)(2,1)S(1)}, bf16[256,256]{1,0:T(8,128)(2,1)S(1)}, u32[]{:S(2)}, u32[]{:S(2)}) collective-permute-start(bf16[256,256]{1,0:T(8,128)(2,1)S(1)} %get-tuple-element.52), channel_id=1, source_target_pairs={{0,6},{2,4},{4,2},{6,0},{8,14},{10,12},{12,10},{14,8},{16,22},{18,... | collective-permute-start | bytes 393224 | tf_op jit(solution)/shard_map/ppermute | solution.py:359
  63.3 8.8 %collective-permute-start.15 = (bf16[256,256]{1,0:T(8,128)(2,1)S(1)}, bf16[256,256]{1,0:T(8,128)(2,1)S(1)}, u32[]{:S(2)}, u32[]{:S(2)}) collective-permute-start(bf16[256,256]{1,0:T(8,128)(2,1)S(1)} %get-tuple-element.54.refs_0_), channel_id=1, source_target_pairs={{0,1},{1,0},{2,3},{3,2},{4,5},{5,4},{6,7},{7,6},{8,9},{9,8},{10,11... | collective-permute-start | bytes 393224 | tf_op jit(solution)/shard_map/ppermute | solution.py:434
  71.1 1.3 %collective-permute-start.16 = (bf16[256,256]{1,0:T(8,128)(2,1)S(1)}, bf16[256,256]{1,0:T(8,128)(2,1)S(1)}, u32[]{:S(2)}, u32[]{:S(2)}) collective-permute-start(bf16[256,256]{1,0:T(8,128)(2,1)S(1)} %collective-permute-done.12.refs_1_), channel_id=1, source_target_pairs={{0,1},{1,0},{2,3},{3,2},{4,5},{5,4},{6,7},{7,6},{8,9},{9,8},{10,11... | collective-permute-start | bytes 393224 | tf_op jit(solution)/shard_map/ppermute | solution.py:434
  71.2 1.5 %collective-permute-start.17 = (bf16[256,256]{1,0:T(8,128)(2,1)S(1)}, bf16[256,256]{1,0:T(8,128)(2,1)S(1)}, u32[]{:S(2)}, u32[]{:S(2)}) collective-permute-start(bf16[256,256]{1,0:T(8,128)(2,1)S(1)} %collective-permute-done.13.refs_2_), channel_id=1, source_target_pairs={{0,1},{1,0},{2,3},{3,2},{4,5},{5,4},{6,7},{7,6},{8,9},{9,8},{10,11... | collective-permute-start | bytes 393224 | tf_op jit(solution)/shard_map/ppermute | solution.py:434
  71.6 1.3 %collective-permute-start.18 = (bf16[256,256]{1,0:T(8,128)(2,1)S(1)}, bf16[256,256]{1,0:T(8,128)(2,1)S(1)}, u32[]{:S(2)}, u32[]{:S(2)}) collective-permute-start(bf16[256,256]{1,0:T(8,128)(2,1)S(1)} %collective-permute-done.14.refs_3_), channel_id=1, source_target_pairs={{0,1},{1,0},{2,3},{3,2},{4,5},{5,4},{6,7},{7,6},{8,9},{9,8},{10,11... | collective-permute-start | bytes 393224 | tf_op jit(solution)/shard_map/ppermute | solution.py:434
  (2 other events, 13.5 us)

commit v9 on v4

--- a/solution.py
+++ b/solution.py
@@ -200,19 +200,20 @@
             queries[h, span, HD:] = mask
 
 
-def attend(query, keys, values, diagonal):
+def score_of(query, keys):
+    return lax.dot_general(
+        keys, query, (((1,), (1,)), ((), ())), preferred_element_type=jnp.float32
+    )
+
+
+def attend(score, values, diagonal):
     factor = math.log2(math.e) / math.sqrt(HD)
-    rows = query.shape[0]
-    score = lax.dot_general(
-        keys, query, (((1,), (1,)), ((), ())), preferred_element_type=jnp.float32
-    )
+    rows = score.shape[1]
     if diagonal:
         older = lax.broadcasted_iota(jnp.int32, (rows, rows), 0) <= lax.broadcasted_iota(
             jnp.int32, (rows, rows), 1
         )
-        score = jnp.concatenate(
-            [score[:-rows], jnp.where(older, score[-rows:], NEG)], axis=0
-        )
+        score = jnp.concatenate([score[:-rows], jnp.where(older, score[-rows:], NEG)], axis=0)
     high = jnp.max(score, axis=0, keepdims=True)
     expo = jnp.exp2((score - high) * factor)
     total = jnp.sum(expo, axis=0, keepdims=True)
@@ -223,6 +224,13 @@
         preferred_element_type=jnp.float32,
     )
     return summed / total, high * factor + jnp.log2(total)
+
+
+def ahead(steps, product):
+    late = product(*steps[0])
+    for step, following in zip(steps, steps[1:] + [None]):
+        now, late = late, product(*following) if following else None
+        yield step, now
 
 
 def main_kernel(*refs):
@@ -236,14 +244,16 @@
     place_queries(asked, corner, rows, queries)
     place_keys(held, corner, SQUAD, rows, keys, values)
     place_keys(near_parts(near, rows), corner, 0, rows, keys, values)
-    for j in range(SQUAD):
-        cols = slice(j * rows, (j + 1) * rows)
-        reach = (SQUAD + 1 + j) * rows
-        for h in range(heads):
-            mixed, lse = attend(queries[h, cols], keys[h, :reach], values[h, :reach], True)
-            out[h * HD : (h + 1) * HD, cols] = mixed
-            out[width + h : width + h + 1, cols] = lse
-        out[width + heads :, cols] = jnp.zeros((TAG - heads, rows), jnp.float32)
+    span = [slice(j * rows, (j + 1) * rows) for j in range(SQUAD)]
+    reach = [(SQUAD + 1 + j) * rows for j in range(SQUAD)]
+    steps = [(j, h) for j in range(SQUAD) for h in range(heads)]
+    for (j, h), score in ahead(
+        steps, lambda j, h: score_of(queries[h, span[j]], keys[h, : reach[j]])
+    ):
+        mixed, lse = attend(score, values[h, : reach[j]], True)
+        out[h * HD : (h + 1) * HD, span[j]] = mixed
+        out[width + h : width + h + 1, span[j]] = lse
+    out[width + heads :, :] = jnp.zeros((TAG - heads, SQUAD * rows), jnp.float32)
 
 
 def far_kernel(*refs):
@@ -256,19 +266,20 @@
     asked = [asked[0].at[k * tall : (k + 1) * tall] for k in range(SQUAD - 1)] + [asked[1]]
     place_queries(asked, corner, rows, queries)
     place_keys(near_parts(near, rows), corner, 0, rows, keys, values)
-    for j in range(SQUAD - 1):
-        cols = slice(j * rows, (j + 1) * rows)
-        stats = []
-        for h in range(heads):
-            mixed, lse = attend(
-                queries[h, cols], keys[h, cols.stop :], values[h, cols.stop :], False
-            )
-            out[h * HD : (h + 1) * HD, cols] = mixed.astype(out.dtype)
-            top = lse.astype(jnp.bfloat16).astype(jnp.float32)
-            mid = (lse - top).astype(jnp.bfloat16).astype(jnp.float32)
-            stats += [top, mid, lse - top - mid]
-        stats.append(jnp.zeros((TAG - len(stats), rows), jnp.float32))
-        out[width:, cols] = jnp.concatenate(stats, axis=0).astype(out.dtype)
+    span = [slice(j * rows, (j + 1) * rows) for j in range(SQUAD)]
+    stats = [[] for _ in range(SQUAD - 1)]
+    steps = [(j, h) for j in range(SQUAD - 1) for h in range(heads)]
+    for (j, h), score in ahead(
+        steps, lambda j, h: score_of(queries[h, span[j]], keys[h, span[j].stop :])
+    ):
+        mixed, lse = attend(score, values[h, span[j].stop :], False)
+        out[h * HD : (h + 1) * HD, span[j]] = mixed.astype(out.dtype)
+        top = lse.astype(jnp.bfloat16).astype(jnp.float32)
+        mid = (lse - top).astype(jnp.bfloat16).astype(jnp.float32)
+        stats[j] += [top, mid, lse - top - mid]
+    for j, stat in enumerate(stats):
+        stat.append(jnp.zeros((TAG - len(stat), rows), jnp.float32))
+        out[width:, span[j]] = jnp.concatenate(stat, axis=0).astype(out.dtype)
 
 
 def merge_kernel(main_ref, far_ref, *refs):

time: 69.6 us -> 69 us (level)
  waiting for transfers between devices: 11.3 us -> 14.4 us
  Pallas kernels: 21.5 us -> 18.6 us
    pallas_call x5, Pallas kernels: 19.8 us -> 16.9 us  [kernel_call(): pl.pallas_call(kernel, in_specs=[VMEM] * len(args), out_specs=[VMEM] * le...]
    ppermute x4, waiting for transfers between devices: 5.13 us -> 8.01 us  [climb(): lax.ppermute(value, 'ctx', [(i, i + SQUAD) for i in range(first, count -...]
  transfers between devices with their start and end apart: 19 -> 19, of which waited for: 8 -> 9; matrix products, arithmetic and copies ran while one was open for 2% -> 2% of each run, Pallas kernels for 23% -> 19%
where the time goes in v9:
time: 69 us; the launch traced here: 68.6 us
  starting transfers between devices  33.2 us (48%)
  Pallas kernels  18.6 us (27%)
  waiting for transfers between devices  14.4 us (21%)
  other arithmetic  1.24 us (2%)
  between operations  0.94 us (1%)
    pallas_call x5, Pallas kernels, kernel_call(): pl.pallas_call(kernel, in_specs=[VMEM] * len(args), out_specs=[VMEM] * le...  16.9 us
    ppermute x4, starting transfers between devices, climb(): lax.ppermute(value, 'ctx', [(i, i + SQUAD) for i in range(first, count -...  11.5 us
    ppermute x4, waiting for transfers between devices, climb(): lax.ppermute(value, 'ctx', [(i, i + SQUAD) for i in range(first, count -...  8.01 us
    ppermute x6, starting transfers between devices, swap(): return lax.ppermute(value, 'ctx', [(i, i ^ mask) for i in range(count)])  6.46 us
    ppermute x4, starting transfers between devices, turn(): lax.ppermute(value, 'tp', [(t, (t + r) % ranks) for t in range(ranks)])  4.39 us
    ppermute x2, starting transfers between devices, descend(): lax.ppermute(value, 'ctx', [(i, i - SQUAD) for i in range(2 * SQUAD, coun...  4 us
    ppermute x1, starting transfers between devices, local(): lax.ppermute(ring, 'ctx', [(i, i + SQUAD) for i in range(0, count - SQUAD...  3.37 us
    ppermute x1, waiting for transfers between devices, local(): lax.ppermute(tail[:, half:], 'ctx', [(i, i - i % SQUAD + (i + 1) % SQUAD)...  3.2 us
  transfers between devices with their start and end apart: 19, of which 9 were waited for; matrix products, arithmetic and copies ran while one was open for 2% of the time, Pallas kernels for 19%

profile of v9, /device:TPU:17, one launch (start us, length us, event | category | flops | bytes accessed | tf_op | source)
XLA Modules:
  0.0 68.6 jit_solution(11487938764891530750)
XLA Ops:
  0.6 1.7 %deal.1 = (bf16[272,256]{1,0:T(8,128)(2,1)S(1)}, bf16[528,256]{1,0:T(8,128)(2,1)S(1)}, bf16[784,256]{1,0:T(8,128)(2,1)S(1)}, bf16[784,256]{1,0:T(8,128)(2,1)S(1)}, bf16[784,256]{1,0:T(8,128)(2,1)S(1)}) custom-call(bf16[256,1024]{1,0:T(8,128)(2,1)} %q_ref.2, bf16[256,1024]{1,0:T(8,128)(2,1)} %k_ref.2, bf16[256,1024]{1,0:T(8,128)(2,1)} %v_ref.2, s32[2,128]{1,0:T(2,128)} %bitcast.3), custom_call_target="tpu_custom_call" | custom-call | bytes 3145728 | tf_op jit(solution)/shard_map/deal/pallas_call | solution.py:145
  2.3 1.3 %collective-permute-start.1 = (bf16[784,256]{1,0:T(8,128)(2,1)S(1)}, bf16[784,256]{1,0:T(8,128)(2,1)S(1)}, u32[]{:S(2)}, u32[]{:S(2)}) collective-permute-start(bf16[784,256]{1,0:T(8,128)(2,1)S(1)} %get-tuple-element.32), channel_id=1, source_target_pairs={{0,2},{2,0},{4,6},{6,4},{8,10},{10,8},{12,14},{14,12},{16,18},{18,... | collective-permute-start | bytes 1204232 | tf_op jit(solution)/shard_map/ppermute | solution.py:338
  3.6 1.2 %collective-permute-start.5 = (bf16[784,256]{1,0:T(8,128)(2,1)S(1)}, bf16[784,256]{1,0:T(8,128)(2,1)S(1)}, u32[]{:S(2)}, u32[]{:S(2)}) collective-permute-start(bf16[784,256]{1,0:T(8,128)(2,1)S(1)} %get-tuple-element.41), channel_id=1, source_target_pairs={{0,4},{2,6},{4,0},{6,2},{8,12},{10,14},{12,8},{14,10},{16,20},{18,... | collective-permute-start | bytes 1204232 | tf_op jit(solution)/shard_map/ppermute | solution.py:338
  4.8 3.2 %collective-permute-start.6 = (bf16[528,256]{1,0:T(8,128)(2,1)S(1)}, bf16[528,256]{1,0:T(8,128)(2,1)S(1)}, u32[]{:S(2)}, u32[]{:S(2)}) collective-permute-start(bf16[528,256]{1,0:T(8,128)(2,1)S(1)} %get-tuple-element.39.refs_1_), channel_id=1, source_target_pairs={{0,8},{2,10},{4,12},{6,14},{8,16},{10,18},{12,20},{14,22},{16,24},... | collective-permute-start | bytes 811016 | tf_op jit(solution)/shard_map/ppermute | solution.py:341
  8.0 1.2 %multiply_convert_fusion = bf16[128,2048]{1,0:T(8,128)(2,1)S(1)} fusion(bf16[256,2048]{1,0:T(8,128)(2,1)} %v_ref.3, bf16[256,2048]{1,0:T(8,128)(2,1)S(1)} %copy-done), kind=kLoop, calls=%fused_computation | loop fusion | flops 1048576 | bytes 1572864 | tf_op jit(solution)/shard_map/convert_element_type | solution.py:362
  9.2 4.2 %collective-permute-done.6.refs_5_.refs_2_ = bf16[528,256]{1,0:T(8,128)(2,1)S(1)} collective-permute-done((bf16[528,256]{1,0:T(8,128)(2,1)S(1)}, bf16[528,256]{1,0:T(8,128)(2,1)S(1)}, u32[]{:S(2)}, u32[]{:S(2)}) %collective-permute-start.6) | collective-permute-done | bytes 270368 | tf_op jit(solution)/shard_map/ppermute | solution.py:341
  13.6 1.3 %collective-permute-start.2 = (bf16[784,256]{1,0:T(8,128)(2,1)S(1)}, bf16[784,256]{1,0:T(8,128)(2,1)S(1)}, u32[]{:S(2)}, u32[]{:S(2)}) collective-permute-start(bf16[784,256]{1,0:T(8,128)(2,1)S(1)} %get-tuple-element.33), channel_id=1, source_target_pairs={{0,6},{2,4},{4,2},{6,0},{8,14},{10,12},{12,10},{14,8},{16,22},{18,... | collective-permute-start | bytes 1204232 | tf_op jit(solution)/shard_map/ppermute | solution.py:338
  14.9 3.2 %collective-permute-start.7 = (bf16[1056,256]{1,0:T(8,128)(2,1)S(1)}, bf16[1056,256]{1,0:T(8,128)(2,1)S(1)}, u32[]{:S(2)}, u32[]{:S(2)}) collective-permute-start(bf16[1056,256]{1,0:T(8,128)(2,1)S(1)} %pad_maximum_fusion), channel_id=1, source_target_pairs={{0,8},{2,10},{4,12},{6,14},{8,16},{10,18},{12,20},{14,22},{16,24},... | collective-permute-start | bytes 1622024 | tf_op jit(solution)/shard_map/ppermute | solution.py:341
  18.1 2.1 %collective-permute-start.9 = (bf16[816,256]{1,0:T(8,128)(2,1)S(1)}, bf16[816,256]{1,0:T(8,128)(2,1)S(1)}, u32[]{:S(2)}, u32[]{:S(2)}) collective-permute-start(bf16[816,256]{1,0:T(8,128)(2,1)S(1)} %pad_maximum_fusion.1), channel_id=1, source_target_pairs={{16,8},{18,10},{20,12},{22,14},{24,16},{26,18},{28,20},{30,22},{17... | collective-permute-start | bytes 1253384 | tf_op jit(solution)/shard_map/ppermute | solution.py:344
  20.2 1.3 %collective-permute-start.3 = (bf16[128,1024]{1,0:T(8,128)(2,1)S(1)}, bf16[128,1024]{1,0:T(8,128)(2,1)S(1)}, u32[]{:S(2)}, u32[]{:S(2)}) collective-permute-start(bf16[128,1024]{1,0:T(8,128)(2,1)S(1)} %get-tuple-element.58), channel_id=1, source_target_pairs={{0,2},{2,4},{4,6},{6,0},{8,10},{10,12},{12,14},{14,8},{16,18},{18,... | collective-permute-start | bytes 786440 | tf_op jit(solution)/shard_map/ppermute | solution.py:364
  21.5 1.6 %collective-permute-done.2.refs_4_ = bf16[784,256]{1,0:T(8,128)(2,1)S(1)} collective-permute-done((bf16[784,256]{1,0:T(8,128)(2,1)S(1)}, bf16[784,256]{1,0:T(8,128)(2,1)S(1)}, u32[]{:S(2)}, u32[]{:S(2)}) %collective-permute-start.2) | collective-permute-done | bytes 401440 | tf_op jit(solution)/shard_map/ppermute | solution.py:338
  23.2 3.2 %collective-permute-start.8 = (bf16[528,256]{1,0:T(8,128)(2,1)S(1)}, bf16[528,256]{1,0:T(8,128)(2,1)S(1)}, u32[]{:S(2)}, u32[]{:S(2)}) collective-permute-start(bf16[528,256]{1,0:T(8,128)(2,1)S(1)} %slice.42), channel_id=1, source_target_pairs={{0,8},{2,10},{4,12},{6,14},{8,16},{10,18},{12,20},{14,22},{16,24},... | collective-permute-start | bytes 811016 | tf_op jit(solution)/shard_map/ppermute | solution.py:341
  26.4 3.2 %collective-permute-done.3.ring_rim = bf16[128,1024]{1,0:T(8,128)(2,1)S(1)} collective-permute-done((bf16[128,1024]{1,0:T(8,128)(2,1)S(1)}, bf16[128,1024]{1,0:T(8,128)(2,1)S(1)}, u32[]{:S(2)}, u32[]{:S(2)}) %collective-permute-start.3) | collective-permute-done | bytes 262176 | tf_op jit(solution)/shard_map/ppermute | solution.py:364
  29.6 1.9 %collective-permute-start.10 = (bf16[272,256]{1,0:T(8,128)(2,1)S(1)}, bf16[272,256]{1,0:T(8,128)(2,1)S(1)}, u32[]{:S(2)}, u32[]{:S(2)}) collective-permute-start(bf16[272,256]{1,0:T(8,128)(2,1)S(1)} %slice.39), channel_id=1, source_target_pairs={{16,8},{18,10},{20,12},{22,14},{24,16},{26,18},{28,20},{30,22},{17... | collective-permute-start | bytes 417800 | tf_op jit(solution)/shard_map/ppermute | solution.py:344
  31.5 2.2 %collective-permute-start = (bf16[128,1024]{1,0:T(8,128)(2,1)S(1)}, bf16[128,1024]{1,0:T(8,128)(2,1)S(1)}, u32[]{:S(2)}, u32[]{:S(2)}) collective-permute-start(bf16[128,1024]{1,0:T(8,128)(2,1)S(1)} %get-tuple-element.59), channel_id=1, source_target_pairs={{0,2},{2,4},{4,6},{6,8},{8,10},{10,12},{12,14},{14,16},{16,18},{18... | collective-permute-start | bytes 786440 | tf_op jit(solution)/shard_map/ppermute | solution.py:370
  33.8 3.4 %collective-permute-start.4 = (bf16[128,1024]{1,0:T(8,128)(2,1)S(1)}, bf16[128,1024]{1,0:T(8,128)(2,1)S(1)}, u32[]{:S(2)}, u32[]{:S(2)}) collective-permute-start(bf16[128,1024]{1,0:T(8,128)(2,1)S(1)} %collective-permute-done.3.ring_rim), channel_id=1, source_target_pairs={{0,8},{8,16},{16,24},{1,9},{9,17},{17,25}} | collective-permute-start | bytes 786440 | tf_op jit(solution)/shard_map/ppermute | solution.py:372
  37.2 1.8 %far.1 = bf16[272,768]{1,0:T(8,128)(2,1)S(1)} custom-call(bf16[816,256]{1,0:T(8,128)(2,1)S(1)} %collective-permute-done.9.refs_0_, bf16[272,256]{1,0:T(8,128)(2,1)S(1)} %collective-permute-done.10.refs_1_, bf16[528,256]{1,0:T(8,128)(2,1)S(1)} %collective-permute-done.6.refs_5_.refs_2_, bf16[1056,256]{1,0:T(8,128)(2,1)S(1)} %collective-permute-done.7.refs_6_.refs_3_, ...), custom_call_target="tpu_custom_call" | custom-call | flops 402653184 | bytes 2056192 | tf_op jit(solution)/shard_map/far/pallas_call | solution.py:26
  38.9 1.9 %collective-permute-start.11 = (bf16[272,768]{1,0:T(8,128)(2,1)S(1)}, bf16[272,768]{1,0:T(8,128)(2,1)S(1)}, u32[]{:S(2)}, u32[]{:S(2)}) collective-permute-start(bf16[272,768]{1,0:T(8,128)(2,1)S(1)} %far.1), channel_id=1, source_target_pairs={{8,16},{10,18},{12,20},{14,22},{16,24},{18,26},{20,28},{22,30},{9,... | collective-permute-start | bytes 1253384 | tf_op jit(solution)/shard_map/ppermute | solution.py:341
  41.2 6.0 %main.1.main_ref = f32[272,1024]{1,0:T(8,128)S(1)} custom-call(bf16[272,256]{1,0:T(8,128)(2,1)S(1)} %get-tuple-element.38.refs_0_, bf16[528,256]{1,0:T(8,128)(2,1)S(1)} %get-tuple-element.39.refs_1_, bf16[784,256]{1,0:T(8,128)(2,1)S(1)} %collective-permute-done.1.refs_2_, bf16[784,256]{1,0:T(8,128)(2,1)S(1)} %collective-permute-done.5.refs_3_, ...), custom_call_target="tpu_custom_call" | custom-call | flops 1744830464 | bytes 3809280 | tf_op jit(solution)/shard_map/main/pallas_call | solution.py:26
  47.2 3.8 %collective-permute-done.11.far_ref = bf16[272,768]{1,0:T(8,128)(2,1)S(1)} collective-permute-done((bf16[272,768]{1,0:T(8,128)(2,1)S(1)}, bf16[272,768]{1,0:T(8,128)(2,1)S(1)}, u32[]{:S(2)}, u32[]{:S(2)}) %collective-permute-start.11) | collective-permute-done | bytes 417824 | tf_op jit(solution)/shard_map/ppermute | solution.py:341
  51.6 2.5 %collective-permute-start.14 = (bf16[256,256]{1,0:T(8,128)(2,1)S(1)}, bf16[256,256]{1,0:T(8,128)(2,1)S(1)}, u32[]{:S(2)}, u32[]{:S(2)}) collective-permute-start(bf16[256,256]{1,0:T(8,128)(2,1)S(1)} %get-tuple-element.52), channel_id=1, source_target_pairs={{0,6},{2,4},{4,2},{6,0},{8,14},{10,12},{12,10},{14,8},{16,22},{18,... | collective-permute-start | bytes 393224 | tf_op jit(solution)/shard_map/ppermute | solution.py:338
  54.1 5.3 %hyena.1 = bf16[256,2048]{1,0:T(8,128)(2,1)} custom-call(bf16[256,2048]{1,0:T(8,128)(2,1)S(1)} %copy-done.2, bf16[256,2048]{1,0:T(8,128)(2,1)S(1)} %copy-done, bf16[256,2048]{1,0:T(8,128)(2,1)S(1)} %copy-done.1, bf16[128,1024]{1,0:T(8,128)(2,1)S(1)} %collective-permute-done.near_rim, bf16[128,1024]{1,0:T(8,128)(2,1)S(1)} %collective-permute-done.3.ring_rim, ...), custom_call_target="tpu_custom_call" | custom-call | flops 4294967296 | bytes 5017600 | tf_op jit(solution)/shard_map/hyena/pallas_call | solution.py:26
  59.5 3.8 %collective-permute-start.15 = (bf16[256,256]{1,0:T(8,128)(2,1)S(1)}, bf16[256,256]{1,0:T(8,128)(2,1)S(1)}, u32[]{:S(2)}, u32[]{:S(2)}) collective-permute-start(bf16[256,256]{1,0:T(8,128)(2,1)S(1)} %get-tuple-element.54.refs_0_), channel_id=1, source_target_pairs={{0,1},{1,0},{2,3},{3,2},{4,5},{5,4},{6,7},{7,6},{8,9},{9,8},{10,11... | collective-permute-start | bytes 393224 | tf_op jit(solution)/shard_map/ppermute | solution.py:413
  65.1 3.5 %project.1 = bf16[256,2048]{1,0:T(8,128)(2,1)} custom-call(bf16[256,256]{1,0:T(8,128)(2,1)S(1)} %get-tuple-element.54.refs_0_, bf16[256,256]{1,0:T(8,128)(2,1)S(1)} %collective-permute-done.12.refs_1_, bf16[256,256]{1,0:T(8,128)(2,1)S(1)} %collective-permute-done.13.refs_2_, bf16[256,256]{1,0:T(8,128)(2,1)S(1)} %collective-permute-done.14.refs_3_, ...), custom_call_target="tpu_custom_call" | custom-call | flops 2147483648 | bytes 10485760 | tf_op jit(solution)/shard_map/project/pallas_call | solution.py:26
  (46 shorter events, 2.9 us)
Async XLA Ops:
  0.6 7.4 %copy-start = (bf16[256,2048]{1,0:T(8,128)(2,1)S(1)}, bf16[256,2048]{1,0:T(8,128)(2,1)}, u32[]{:S(2)}) copy-start(bf16[256,2048]{1,0:T(8,128)(2,1)} %k_ref.3) | copy-start | bytes 3145732
  2.3 11.2 %collective-permute-start.1 = (bf16[784,256]{1,0:T(8,128)(2,1)S(1)}, bf16[784,256]{1,0:T(8,128)(2,1)S(1)}, u32[]{:S(2)}, u32[]{:S(2)}) collective-permute-start(bf16[784,256]{1,0:T(8,128)(2,1)S(1)} %get-tuple-element.32), channel_id=1, source_target_pairs={{0,2},{2,0},{4,6},{6,4},{8,10},{10,8},{12,14},{14,12},{16,18},{18,... | collective-permute-start | bytes 1204232 | tf_op jit(solution)/shard_map/ppermute | solution.py:338
  3.6 9.9 %collective-permute-start.5 = (bf16[784,256]{1,0:T(8,128)(2,1)S(1)}, bf16[784,256]{1,0:T(8,128)(2,1)S(1)}, u32[]{:S(2)}, u32[]{:S(2)}) collective-permute-start(bf16[784,256]{1,0:T(8,128)(2,1)S(1)} %get-tuple-element.41), channel_id=1, source_target_pairs={{0,4},{2,6},{4,0},{6,2},{8,12},{10,14},{12,8},{14,10},{16,20},{18,... | collective-permute-start | bytes 1204232 | tf_op jit(solution)/shard_map/ppermute | solution.py:338
  4.8 8.6 %collective-permute-start.6 = (bf16[528,256]{1,0:T(8,128)(2,1)S(1)}, bf16[528,256]{1,0:T(8,128)(2,1)S(1)}, u32[]{:S(2)}, u32[]{:S(2)}) collective-permute-start(bf16[528,256]{1,0:T(8,128)(2,1)S(1)} %get-tuple-element.39.refs_1_), channel_id=1, source_target_pairs={{0,8},{2,10},{4,12},{6,14},{8,16},{10,18},{12,20},{14,22},{16,24},... | collective-permute-start | bytes 811016 | tf_op jit(solution)/shard_map/ppermute | solution.py:341
  13.6 9.6 %collective-permute-start.2 = (bf16[784,256]{1,0:T(8,128)(2,1)S(1)}, bf16[784,256]{1,0:T(8,128)(2,1)S(1)}, u32[]{:S(2)}, u32[]{:S(2)}) collective-permute-start(bf16[784,256]{1,0:T(8,128)(2,1)S(1)} %get-tuple-element.33), channel_id=1, source_target_pairs={{0,6},{2,4},{4,2},{6,0},{8,14},{10,12},{12,10},{14,8},{16,22},{18,... | collective-permute-start | bytes 1204232 | tf_op jit(solution)/shard_map/ppermute | solution.py:338
  14.9 22.3 %collective-permute-start.7 = (bf16[1056,256]{1,0:T(8,128)(2,1)S(1)}, bf16[1056,256]{1,0:T(8,128)(2,1)S(1)}, u32[]{:S(2)}, u32[]{:S(2)}) collective-permute-start(bf16[1056,256]{1,0:T(8,128)(2,1)S(1)} %pad_maximum_fusion), channel_id=1, source_target_pairs={{0,8},{2,10},{4,12},{6,14},{8,16},{10,18},{12,20},{14,22},{16,24},... | collective-permute-start | bytes 1622024 | tf_op jit(solution)/shard_map/ppermute | solution.py:341
  18.1 15.7 %collective-permute-start.9 = (bf16[816,256]{1,0:T(8,128)(2,1)S(1)}, bf16[816,256]{1,0:T(8,128)(2,1)S(1)}, u32[]{:S(2)}, u32[]{:S(2)}) collective-permute-start(bf16[816,256]{1,0:T(8,128)(2,1)S(1)} %pad_maximum_fusion.1), channel_id=1, source_target_pairs={{16,8},{18,10},{20,12},{22,14},{24,16},{26,18},{28,20},{30,22},{17... | collective-permute-start | bytes 1253384 | tf_op jit(solution)/shard_map/ppermute | solution.py:344
  20.2 9.3 %collective-permute-start.3 = (bf16[128,1024]{1,0:T(8,128)(2,1)S(1)}, bf16[128,1024]{1,0:T(8,128)(2,1)S(1)}, u32[]{:S(2)}, u32[]{:S(2)}) collective-permute-start(bf16[128,1024]{1,0:T(8,128)(2,1)S(1)} %get-tuple-element.58), channel_id=1, source_target_pairs={{0,2},{2,4},{4,6},{6,0},{8,10},{10,12},{12,14},{14,8},{16,18},{18,... | collective-permute-start | bytes 786440 | tf_op jit(solution)/shard_map/ppermute | solution.py:364
  23.2 14.0 %collective-permute-start.8 = (bf16[528,256]{1,0:T(8,128)(2,1)S(1)}, bf16[528,256]{1,0:T(8,128)(2,1)S(1)}, u32[]{:S(2)}, u32[]{:S(2)}) collective-permute-start(bf16[528,256]{1,0:T(8,128)(2,1)S(1)} %slice.42), channel_id=1, source_target_pairs={{0,8},{2,10},{4,12},{6,14},{8,16},{10,18},{12,20},{14,22},{16,24},... | collective-permute-start | bytes 811016 | tf_op jit(solution)/shard_map/ppermute | solution.py:341
  29.6 11.3 %copy-start.4 = (bf16[2048]{0:T(1024)(128)(2,1)S(1)}, bf16[2048]{0:T(1024)(128)(2,1)}, u32[]{:S(2)}) copy-start(bf16[2048]{0:T(1024)(128)(2,1)} %param.14) | copy-start | bytes 12292
  29.6 7.6 %collective-permute-start.10 = (bf16[272,256]{1,0:T(8,128)(2,1)S(1)}, bf16[272,256]{1,0:T(8,128)(2,1)S(1)}, u32[]{:S(2)}, u32[]{:S(2)}) collective-permute-start(bf16[272,256]{1,0:T(8,128)(2,1)S(1)} %slice.39), channel_id=1, source_target_pairs={{16,8},{18,10},{20,12},{22,14},{24,16},{26,18},{28,20},{30,22},{17... | collective-permute-start | bytes 417800 | tf_op jit(solution)/shard_map/ppermute | solution.py:344
  31.5 9.4 %collective-permute-start = (bf16[128,1024]{1,0:T(8,128)(2,1)S(1)}, bf16[128,1024]{1,0:T(8,128)(2,1)S(1)}, u32[]{:S(2)}, u32[]{:S(2)}) collective-permute-start(bf16[128,1024]{1,0:T(8,128)(2,1)S(1)} %get-tuple-element.59), channel_id=1, source_target_pairs={{0,2},{2,4},{4,6},{6,8},{8,10},{10,12},{12,14},{14,16},{16,18},{18... | collective-permute-start | bytes 786440 | tf_op jit(solution)/shard_map/ppermute | solution.py:370
  33.8 7.4 %collective-permute-start.4 = (bf16[128,1024]{1,0:T(8,128)(2,1)S(1)}, bf16[128,1024]{1,0:T(8,128)(2,1)S(1)}, u32[]{:S(2)}, u32[]{:S(2)}) collective-permute-start(bf16[128,1024]{1,0:T(8,128)(2,1)S(1)} %collective-permute-done.3.ring_rim), channel_id=1, source_target_pairs={{0,8},{8,16},{16,24},{1,9},{9,17},{17,25}} | collective-permute-start | bytes 786440 | tf_op jit(solution)/shard_map/ppermute | solution.py:372
  38.9 12.1 %collective-permute-start.11 = (bf16[272,768]{1,0:T(8,128)(2,1)S(1)}, bf16[272,768]{1,0:T(8,128)(2,1)S(1)}, u32[]{:S(2)}, u32[]{:S(2)}) collective-permute-start(bf16[272,768]{1,0:T(8,128)(2,1)S(1)} %far.1), channel_id=1, source_target_pairs={{8,16},{10,18},{12,20},{14,22},{16,24},{18,26},{20,28},{22,30},{9,... | collective-permute-start | bytes 1253384 | tf_op jit(solution)/shard_map/ppermute | solution.py:341
  41.2 12.9 %copy-start.2 = (bf16[256,2048]{1,0:T(8,128)(2,1)S(1)}, bf16[256,2048]{1,0:T(8,128)(2,1)}, u32[]{:S(2)}) copy-start(bf16[256,2048]{1,0:T(8,128)(2,1)} %q_ref.3) | copy-start | bytes 3145732
  51.4 8.1 %collective-permute-start.12 = (bf16[256,256]{1,0:T(8,128)(2,1)S(1)}, bf16[256,256]{1,0:T(8,128)(2,1)S(1)}, u32[]{:S(2)}, u32[]{:S(2)}) collective-permute-start(bf16[256,256]{1,0:T(8,128)(2,1)S(1)} %get-tuple-element.50), channel_id=1, source_target_pairs={{0,2},{2,0},{4,6},{6,4},{8,10},{10,8},{12,14},{14,12},{16,18},{18,... | collective-permute-start | bytes 393224 | tf_op jit(solution)/shard_map/ppermute | solution.py:338
  51.5 8.0 %collective-permute-start.13 = (bf16[256,256]{1,0:T(8,128)(2,1)S(1)}, bf16[256,256]{1,0:T(8,128)(2,1)S(1)}, u32[]{:S(2)}, u32[]{:S(2)}) collective-permute-start(bf16[256,256]{1,0:T(8,128)(2,1)S(1)} %get-tuple-element.51), channel_id=1, source_target_pairs={{0,4},{2,6},{4,0},{6,2},{8,12},{10,14},{12,8},{14,10},{16,20},{18,... | collective-permute-start | bytes 393224 | tf_op jit(solution)/shard_map/ppermute | solution.py:338
  51.5 13.6 %slice-start = ((s8[8388608]{0:T(1024)(128)(4,1)}), s8[4194304]{0:T(1024)(128)(4,1)S(1)}, s32[]{:S(2)}) async-start(s8[8388608]{0:T(1024)(128)(4,1)} %bitcast.1), calls=%async_computation | async-start | bytes 8388608
  51.5 13.6 %slice-start.1 = ((s8[8388608]{0:T(1024)(128)(4,1)}), s8[4194304]{0:T(1024)(128)(4,1)S(1)}, s32[]{:S(2)}) async-start(s8[8388608]{0:T(1024)(128)(4,1)} %bitcast.1), calls=%async_computation.1 | async-start | bytes 8388608
  51.6 7.9 %collective-permute-start.14 = (bf16[256,256]{1,0:T(8,128)(2,1)S(1)}, bf16[256,256]{1,0:T(8,128)(2,1)S(1)}, u32[]{:S(2)}, u32[]{:S(2)}) collective-permute-start(bf16[256,256]{1,0:T(8,128)(2,1)S(1)} %get-tuple-element.52), channel_id=1, source_target_pairs={{0,6},{2,4},{4,2},{6,0},{8,14},{10,12},{12,10},{14,8},{16,22},{18,... | collective-permute-start | bytes 393224 | tf_op jit(solution)/shard_map/ppermute | solution.py:338
  59.5 4.8 %collective-permute-start.15 = (bf16[256,256]{1,0:T(8,128)(2,1)S(1)}, bf16[256,256]{1,0:T(8,128)(2,1)S(1)}, u32[]{:S(2)}, u32[]{:S(2)}) collective-permute-start(bf16[256,256]{1,0:T(8,128)(2,1)S(1)} %get-tuple-element.54.refs_0_), channel_id=1, source_target_pairs={{0,1},{1,0},{2,3},{3,2},{4,5},{5,4},{6,7},{7,6},{8,9},{9,8},{10,11... | collective-permute-start | bytes 393224 | tf_op jit(solution)/shard_map/ppermute | solution.py:413
  63.3 1.3 %collective-permute-start.16 = (bf16[256,256]{1,0:T(8,128)(2,1)S(1)}, bf16[256,256]{1,0:T(8,128)(2,1)S(1)}, u32[]{:S(2)}, u32[]{:S(2)}) collective-permute-start(bf16[256,256]{1,0:T(8,128)(2,1)S(1)} %collective-permute-done.12.refs_1_), channel_id=1, source_target_pairs={{0,1},{1,0},{2,3},{3,2},{4,5},{5,4},{6,7},{7,6},{8,9},{9,8},{10,11... | collective-permute-start | bytes 393224 | tf_op jit(solution)/shard_map/ppermute | solution.py:413
  63.3 1.5 %collective-permute-start.17 = (bf16[256,256]{1,0:T(8,128)(2,1)S(1)}, bf16[256,256]{1,0:T(8,128)(2,1)S(1)}, u32[]{:S(2)}, u32[]{:S(2)}) collective-permute-start(bf16[256,256]{1,0:T(8,128)(2,1)S(1)} %collective-permute-done.13.refs_2_), channel_id=1, source_target_pairs={{0,1},{1,0},{2,3},{3,2},{4,5},{5,4},{6,7},{7,6},{8,9},{9,8},{10,11... | collective-permute-start | bytes 393224 | tf_op jit(solution)/shard_map/ppermute | solution.py:413
  63.8 1.3 %collective-permute-start.18 = (bf16[256,256]{1,0:T(8,128)(2,1)S(1)}, bf16[256,256]{1,0:T(8,128)(2,1)S(1)}, u32[]{:S(2)}, u32[]{:S(2)}) collective-permute-start(bf16[256,256]{1,0:T(8,128)(2,1)S(1)} %collective-permute-done.14.refs_3_), channel_id=1, source_target_pairs={{0,1},{1,0},{2,3},{3,2},{4,5},{5,4},{6,7},{7,6},{8,9},{9,8},{10,11... | collective-permute-start | bytes 393224 | tf_op jit(solution)/shard_map/ppermute | solution.py:413
  (2 other events, 13.7 us)

commit v10 on v9

--- a/solution.py
+++ b/solution.py
@@ -107,14 +107,16 @@
     rows, feat = q_ref.shape
     width = feat // SQUAD
     corner = corner_of()
+    homes = {0: (outs[0], outs[1]), 1: (outs[2], outs[2]), 2: (outs[3], outs[3]), 3: outs[4:]}
     copies = []
-    for k in (*range(1, SQUAD), 0):
+    for k in (1, 2, 0, 3):
         cols = pl.ds(pl.multiple_of(jnp.bitwise_xor(corner, k) * width, width), width)
-        base = rows if k else 0
+        asking, keeping = homes[k]
+        base = TAG if asking is not keeping else rows + TAG
         places = (
-            (q_ref, outs[k + 1] if k else outs[0], 0),
-            (k_ref, outs[k + 1], base + TAG),
-            (v_ref, outs[k + 1], base + TAG + rows),
+            (q_ref, asking, 0),
+            (k_ref, keeping, base),
+            (v_ref, keeping, base + rows),
         )
         copies += [
             pltpu.make_async_copy(
@@ -130,7 +132,7 @@
     ids = jnp.concatenate([ids, spare], axis=0)
     tag = jnp.concatenate([ids] * (width // LANES), axis=1).astype(jnp.bfloat16)
     for i, target in enumerate(outs):
-        begin = 0 if i == 1 else rows
+        begin = 0 if i in (1, 5) else rows
         target[begin : begin + TAG, :] = tag
     for copy in copies:
         copy.wait()
@@ -138,7 +140,8 @@
 
 def deal(queries, keys, values, ids):
     rows, feat = queries.shape
-    tall = [rows + TAG, 2 * rows + TAG] + [3 * rows + TAG] * (SQUAD - 1)
+    asking, keeping = rows + TAG, 2 * rows + TAG
+    tall = [asking, keeping, asking + 2 * rows, asking + 2 * rows, asking, keeping]
     shapes = [(x, feat // SQUAD) for x in tall]
     held = [pltpu.with_memory_space_constraint(x, pltpu.HBM) for x in (queries, keys, values, ids)]
     return list(
@@ -234,13 +237,13 @@
 
 
 def main_kernel(*refs):
-    own, near, out, (queries, keys, values) = refs[:5], refs[5:8], refs[8], refs[9:]
+    own, near, out, (queries, keys, values) = refs[:6], refs[6:9], refs[9], refs[10:]
     heads, span, _ = queries.shape
     rows = span // SQUAD
     width = heads * HD
     corner = corner_of()
-    asked = [own[0]] + [p.at[: rows + TAG] for p in own[2:]]
-    held = [own[1]] + [p.at[rows:] for p in own[2:]]
+    asked = [own[0]] + [p.at[: rows + TAG] for p in own[2:4]] + [own[4]]
+    held = [own[1]] + [p.at[rows:] for p in own[2:4]] + [own[5]]
     place_queries(asked, corner, rows, queries)
     place_keys(held, corner, SQUAD, rows, keys, values)
     place_keys(near_parts(near, rows), corner, 0, rows, keys, values)
@@ -351,12 +354,14 @@
     tall = rows + TAG
     near = [climb(kept)]
     beside = [swap(sent[0], 1), swap(sent[1], 2)]
-    sent[2], beside[0] = lax.optimization_barrier((sent[2], beside[0]))
-    across = swap(sent[2], 3)
+    sent[3], beside[0] = lax.optimization_barrier((sent[3], beside[0]))
+    across = swap(sent[3], 3)
+    sent[2], beside[1] = lax.optimization_barrier((sent[2], beside[1]))
+    across_asked = swap(sent[2], 3)
     beside[1], near[0] = lax.optimization_barrier((beside[1], near[0]))
     near.append(climb(jnp.concatenate([x[rows:] for x in beside], axis=0)))
     back = [descend(jnp.concatenate([asked] + [x[:tall] for x in beside], axis=0))]
-    near.append(climb(across[rows:]))
+    near.append(climb(across))
     tail_k = hyena_k[rows - LANES :].astype(f32)
     tail_v = hyena_v[rows - LANES :].astype(f32)
     tail = (tail_k * tail_v).astype(bf16)
@@ -364,14 +369,14 @@
     ring = lax.ppermute(
         tail[:, half:], "ctx", [(i, i - i % SQUAD + (i + 1) % SQUAD) for i in range(count)]
     )
-    across, ring = lax.optimization_barrier((across, ring))
-    back.append(descend(across[:tall]))
+    across_asked, ring = lax.optimization_barrier((across_asked, ring))
+    back.append(descend(across_asked))
     rims = [
         lax.ppermute(tail[:, :half], "ctx", [(i, i + 1) for i in range(count - 1)]),
         ring,
         lax.ppermute(ring, "ctx", [(i, i + SQUAD) for i in range(0, count - SQUAD, SQUAD)]),
     ]
-    own = [asked, kept, *beside, across]
+    own = [asked, kept, *beside, across_asked, across]
     def store(blocks):
         return [
             pltpu.VMEM((heads, SQUAD * rows, 2 * HD), bf16),

time: 69 us -> 72.1 us (1.045)
  starting transfers between devices: 33.2 us -> 35.8 us
    ppermute x6 -> x7, waiting for transfers between devices: 1.66 us -> 6.34 us  [swap(): return lax.ppermute(value, 'ctx', [(i, i ^ mask) for i in range(count)])]
    ppermute x4, waiting for transfers between devices: 8.01 us -> 3.6 us  [climb(): lax.ppermute(value, 'ctx', [(i, i + SQUAD) for i in range(first, count -...]
    ppermute x1, waiting for transfers between devices: 3.2 us -> 0.53 us  [local(): lax.ppermute(tail[:, half:], 'ctx', [(i, i - i % SQUAD + (i + 1) % SQUAD)...]
    ppermute x4, starting transfers between devices: 4.39 us -> 6.83 us  [turn(): lax.ppermute(value, 'tp', [(t, (t + r) % ranks) for t in range(ranks)])]
    ppermute x6 -> x7, starting transfers between devices: 6.46 us -> 8.63 us  [swap(): return lax.ppermute(value, 'ctx', [(i, i ^ mask) for i in range(count)])]
    ppermute x2, waiting for transfers between devices: 0.01 us -> 1.55 us  [descend(): lax.ppermute(value, 'ctx', [(i, i - SQUAD) for i in range(2 * SQUAD, coun...]
    ppermute x1, starting transfers between devices: 3.37 us -> 1.91 us  [local(): lax.ppermute(ring, 'ctx', [(i, i + SQUAD) for i in range(0, count - SQUAD...]
    ppermute x1, waiting for transfers between devices: 0.29 us -> 1.74 us  [local(): lax.ppermute(ring, 'ctx', [(i, i + SQUAD) for i in range(0, count - SQUAD...]
  transfers between devices with their start and end apart: 19 -> 20, of which waited for: 9 -> 11; matrix products, arithmetic and copies ran while one was open for 2% -> 2% of each run, Pallas kernels for 19% -> 18%
where the time goes in v10:
time: 72.1 us; the launch traced here: 71.7 us
  starting transfers between devices  35.8 us (50%)
  Pallas kernels  18.6 us (26%)
  waiting for transfers between devices  15 us (21%)
  other arithmetic  1.24 us (2%)
  between operations  0.92 us (1%)
    pallas_call x5, Pallas kernels, kernel_call(): pl.pallas_call(kernel, in_specs=[VMEM] * len(args), out_specs=[VMEM] * le...  16.9 us
    ppermute x4, starting transfers between devices, climb(): lax.ppermute(value, 'ctx', [(i, i + SQUAD) for i in range(first, count -...  11.5 us
    ppermute x7, starting transfers between devices, swap(): return lax.ppermute(value, 'ctx', [(i, i ^ mask) for i in range(count)])  8.63 us
    ppermute x4, starting transfers between devices, turn(): lax.ppermute(value, 'tp', [(t, (t + r) % ranks) for t in range(ranks)])  6.83 us
    ppermute x7, waiting for transfers between devices, swap(): return lax.ppermute(value, 'ctx', [(i, i ^ mask) for i in range(count)])  6.34 us
    ppermute x2, starting transfers between devices, descend(): lax.ppermute(value, 'ctx', [(i, i - SQUAD) for i in range(2 * SQUAD, coun...  3.99 us
    ppermute x4, waiting for transfers between devices, climb(): lax.ppermute(value, 'ctx', [(i, i + SQUAD) for i in range(first, count -...  3.6 us
    ppermute x1, starting transfers between devices, local(): lax.ppermute(tail[:, :half], 'ctx', [(i, i + 1) for i in range(count - 1)])  2.62 us
  transfers between devices with their start and end apart: 20, of which 11 were waited for; matrix products, arithmetic and copies ran while one was open for 2% of the time, Pallas kernels for 18%

profile of v10, /device:TPU:17, one launch (start us, length us, event | category | flops | bytes accessed | tf_op | source)
XLA Modules:
  0.0 71.7 jit_solution(6858910523277167491)
XLA Ops:
  0.6 1.7 %deal.1 = (bf16[272,256]{1,0:T(8,128)(2,1)S(1)}, bf16[528,256]{1,0:T(8,128)(2,1)S(1)}, bf16[784,256]{1,0:T(8,128)(2,1)S(1)}, bf16[784,256]{1,0:T(8,128)(2,1)S(1)...) custom-call(bf16[256,1024]{1,0:T(8,128)(2,1)} %q_ref.2, bf16[256,1024]{1,0:T(8,128)(2,1)} %k_ref.2, ...), custom_call_target="tpu_custom_call" | custom-call | bytes 3145728 | tf_op jit(solution)/shard_map/deal/pallas_call | solution.py:148
  2.3 1.3 %collective-permute-start.1 = (bf16[784,256]{1,0:T(8,128)(2,1)S(1)}, bf16[784,256]{1,0:T(8,128)(2,1)S(1)}, u32[]{:S(2)}, u32[]{:S(2)}) collective-permute-start(bf16[784,256]{1,0:T(8,128)(2,1)S(1)} %get-tuple-element.35), channel_id=1, source_target_pairs={{0,4},{2,6},{4,0},{6,2},{8,12},{10,14},{12,8},{14,10},{16,20},{18,... | collective-permute-start | bytes 1204232 | tf_op jit(solution)/shard_map/ppermute | solution.py:341
  3.6 1.2 %collective-permute-start.5 = (bf16[784,256]{1,0:T(8,128)(2,1)S(1)}, bf16[784,256]{1,0:T(8,128)(2,1)S(1)}, u32[]{:S(2)}, u32[]{:S(2)}) collective-permute-start(bf16[784,256]{1,0:T(8,128)(2,1)S(1)} %get-tuple-element.44), channel_id=1, source_target_pairs={{0,2},{2,0},{4,6},{6,4},{8,10},{10,8},{12,14},{14,12},{16,18},{18,... | collective-permute-start | bytes 1204232 | tf_op jit(solution)/shard_map/ppermute | solution.py:341
  4.8 3.2 %collective-permute-start.6 = (bf16[528,256]{1,0:T(8,128)(2,1)S(1)}, bf16[528,256]{1,0:T(8,128)(2,1)S(1)}, u32[]{:S(2)}, u32[]{:S(2)}) collective-permute-start(bf16[528,256]{1,0:T(8,128)(2,1)S(1)} %get-tuple-element.42.refs_1_), channel_id=1, source_target_pairs={{0,8},{2,10},{4,12},{6,14},{8,16},{10,18},{12,20},{14,22},{16,24},... | collective-permute-start | bytes 811016 | tf_op jit(solution)/shard_map/ppermute | solution.py:344
  9.2 3.3 %collective-permute-done.1.refs_3_ = bf16[784,256]{1,0:T(8,128)(2,1)S(1)} collective-permute-done((bf16[784,256]{1,0:T(8,128)(2,1)S(1)}, bf16[784,256]{1,0:T(8,128)(2,1)S(1)}, u32[]{:S(2)}, u32[]{:S(2)}) %collective-permute-start.1) | collective-permute-done | bytes 401440 | tf_op jit(solution)/shard_map/ppermute | solution.py:341
  13.6 1.3 %collective-permute-start.7 = (bf16[528,256]{1,0:T(8,128)(2,1)S(1)}, bf16[528,256]{1,0:T(8,128)(2,1)S(1)}, u32[]{:S(2)}, u32[]{:S(2)}) collective-permute-start(bf16[528,256]{1,0:T(8,128)(2,1)S(1)} %get-tuple-element.49), channel_id=1, source_target_pairs={{0,6},{2,4},{4,2},{6,0},{8,14},{10,12},{12,10},{14,8},{16,22},{18,... | collective-permute-start | bytes 811016 | tf_op jit(solution)/shard_map/ppermute | solution.py:341
  14.9 3.2 %collective-permute-start.8 = (bf16[1056,256]{1,0:T(8,128)(2,1)S(1)}, bf16[1056,256]{1,0:T(8,128)(2,1)S(1)}, u32[]{:S(2)}, u32[]{:S(2)}) collective-permute-start(bf16[1056,256]{1,0:T(8,128)(2,1)S(1)} %pad_maximum_fusion), channel_id=1, source_target_pairs={{0,8},{2,10},{4,12},{6,14},{8,16},{10,18},{12,20},{14,22},{16,24},... | collective-permute-start | bytes 1622024 | tf_op jit(solution)/shard_map/ppermute | solution.py:344
  18.2 2.1 %collective-permute-start.10 = (bf16[816,256]{1,0:T(8,128)(2,1)S(1)}, bf16[816,256]{1,0:T(8,128)(2,1)S(1)}, u32[]{:S(2)}, u32[]{:S(2)}) collective-permute-start(bf16[816,256]{1,0:T(8,128)(2,1)S(1)} %pad_maximum_fusion.1), channel_id=1, source_target_pairs={{16,8},{18,10},{20,12},{22,14},{24,16},{26,18},{28,20},{30,22},{17... | collective-permute-start | bytes 1253384 | tf_op jit(solution)/shard_map/ppermute | solution.py:347
  20.6 2.1 %collective-permute-start.2 = (bf16[272,256]{1,0:T(8,128)(2,1)S(1)}, bf16[272,256]{1,0:T(8,128)(2,1)S(1)}, u32[]{:S(2)}, u32[]{:S(2)}) collective-permute-start(bf16[272,256]{1,0:T(8,128)(2,1)S(1)} %get-tuple-element.36), channel_id=1, source_target_pairs={{0,6},{2,4},{4,2},{6,0},{8,14},{10,12},{12,10},{14,8},{16,22},{18,... | collective-permute-start | bytes 417800 | tf_op jit(solution)/shard_map/ppermute | solution.py:341
  22.7 3.2 %collective-permute-start.9 = (bf16[528,256]{1,0:T(8,128)(2,1)S(1)}, bf16[528,256]{1,0:T(8,128)(2,1)S(1)}, u32[]{:S(2)}, u32[]{:S(2)}) collective-permute-start(bf16[528,256]{1,0:T(8,128)(2,1)S(1)} %collective-permute-done.7.refs_5_), channel_id=1, source_target_pairs={{0,8},{2,10},{4,12},{6,14},{8,16},{10,18},{12,20},{14,22},{16,24},... | collective-permute-start | bytes 811016 | tf_op jit(solution)/shard_map/ppermute | solution.py:344
  26.5 3.0 %collective-permute-done.2.refs_4_ = bf16[272,256]{1,0:T(8,128)(2,1)S(1)} collective-permute-done((bf16[272,256]{1,0:T(8,128)(2,1)S(1)}, bf16[272,256]{1,0:T(8,128)(2,1)S(1)}, u32[]{:S(2)}, u32[]{:S(2)}) %collective-permute-start.2) | collective-permute-done | bytes 139296 | tf_op jit(solution)/shard_map/ppermute | solution.py:341
  29.5 1.9 %collective-permute-start.11 = (bf16[272,256]{1,0:T(8,128)(2,1)S(1)}, bf16[272,256]{1,0:T(8,128)(2,1)S(1)}, u32[]{:S(2)}, u32[]{:S(2)}) collective-permute-start(bf16[272,256]{1,0:T(8,128)(2,1)S(1)} %collective-permute-done.2.refs_4_), channel_id=1, source_target_pairs={{16,8},{18,10},{20,12},{22,14},{24,16},{26,18},{28,20},{30,22},{17... | collective-permute-start | bytes 417800 | tf_op jit(solution)/shard_map/ppermute | solution.py:347
  31.4 2.6 %collective-permute-start = (bf16[128,1024]{1,0:T(8,128)(2,1)S(1)}, bf16[128,1024]{1,0:T(8,128)(2,1)S(1)}, u32[]{:S(2)}, u32[]{:S(2)}) collective-permute-start(bf16[128,1024]{1,0:T(8,128)(2,1)S(1)} %get-tuple-element.65), channel_id=1, source_target_pairs={{0,2},{2,4},{4,6},{6,8},{8,10},{10,12},{12,14},{14,16},{16,18},{18... | collective-permute-start | bytes 786440 | tf_op jit(solution)/shard_map/ppermute | solution.py:375
  34.0 1.5 %collective-permute-done.11.refs_1_ = bf16[272,256]{1,0:T(8,128)(2,1)S(1)} collective-permute-done((bf16[272,256]{1,0:T(8,128)(2,1)S(1)}, bf16[272,256]{1,0:T(8,128)(2,1)S(1)}, u32[]{:S(2)}, u32[]{:S(2)}) %collective-permute-start.11) | collective-permute-done | bytes 139296 | tf_op jit(solution)/shard_map/ppermute | solution.py:347
  35.6 1.9 %collective-permute-start.4 = (bf16[128,1024]{1,0:T(8,128)(2,1)S(1)}, bf16[128,1024]{1,0:T(8,128)(2,1)S(1)}, u32[]{:S(2)}, u32[]{:S(2)}) collective-permute-start(bf16[128,1024]{1,0:T(8,128)(2,1)S(1)} %collective-permute-done.3.ring_rim), channel_id=1, source_target_pairs={{0,8},{8,16},{16,24},{1,9},{9,17},{17,25}} | collective-permute-start | bytes 786440 | tf_op jit(solution)/shard_map/ppermute | solution.py:377
  37.5 1.7 %far.1 = bf16[272,768]{1,0:T(8,128)(2,1)S(1)} custom-call(bf16[816,256]{1,0:T(8,128)(2,1)S(1)} %collective-permute-done.10.refs_0_, bf16[272,256]{1,0:T(8,128)(2,1)S(1)} %collective-permute-done.11.refs_1_, bf16[528,256]{1,0:T(8,128)(2,1)S(1)} %collective-permute-done.6.refs_6_.refs_2_, bf16[1056,256]{1,0:T(8,128)(2,1)S(1)} %collective-permute-done.8.refs_7_.refs_3_, ...), custom_call_target="tpu_custom_call" | custom-call | flops 402653184 | bytes 2056192 | tf_op jit(solution)/shard_map/far/pallas_call | solution.py:26
  39.3 1.9 %collective-permute-start.12 = (bf16[272,768]{1,0:T(8,128)(2,1)S(1)}, bf16[272,768]{1,0:T(8,128)(2,1)S(1)}, u32[]{:S(2)}, u32[]{:S(2)}) collective-permute-start(bf16[272,768]{1,0:T(8,128)(2,1)S(1)} %far.1), channel_id=1, source_target_pairs={{8,16},{10,18},{12,20},{14,22},{16,24},{18,26},{20,28},{22,30},{9,... | collective-permute-start | bytes 1253384 | tf_op jit(solution)/shard_map/ppermute | solution.py:344
  41.2 1.7 %collective-permute-done.4.far_rim = bf16[128,1024]{1,0:T(8,128)(2,1)S(1)} collective-permute-done((bf16[128,1024]{1,0:T(8,128)(2,1)S(1)}, bf16[128,1024]{1,0:T(8,128)(2,1)S(1)}, u32[]{:S(2)}, u32[]{:S(2)}) %collective-permute-start.4) | collective-permute-done | bytes 262176 | tf_op jit(solution)/shard_map/ppermute | solution.py:377
  43.0 6.0 %main.1.main_ref = f32[272,1024]{1,0:T(8,128)S(1)} custom-call(bf16[272,256]{1,0:T(8,128)(2,1)S(1)} %get-tuple-element.41.refs_0_, bf16[528,256]{1,0:T(8,128)(2,1)S(1)} %get-tuple-element.42.refs_1_, bf16[784,256]{1,0:T(8,128)(2,1)S(1)} %collective-permute-done.5.refs_2_, bf16[784,256]{1,0:T(8,128)(2,1)S(1)} %collective-permute-done.1.refs_3_, ...), custom_call_target="tpu_custom_call" | custom-call | flops 1744830464 | bytes 3817472 | tf_op jit(solution)/shard_map/main/pallas_call | solution.py:26
  49.0 2.7 %collective-permute-done.12.far_ref = bf16[272,768]{1,0:T(8,128)(2,1)S(1)} collective-permute-done((bf16[272,768]{1,0:T(8,128)(2,1)S(1)}, bf16[272,768]{1,0:T(8,128)(2,1)S(1)}, u32[]{:S(2)}, u32[]{:S(2)}) %collective-permute-start.12) | collective-permute-done | bytes 417824 | tf_op jit(solution)/shard_map/ppermute | solution.py:344
  52.3 2.5 %collective-permute-start.15 = (bf16[256,256]{1,0:T(8,128)(2,1)S(1)}, bf16[256,256]{1,0:T(8,128)(2,1)S(1)}, u32[]{:S(2)}, u32[]{:S(2)}) collective-permute-start(bf16[256,256]{1,0:T(8,128)(2,1)S(1)} %get-tuple-element.58), channel_id=1, source_target_pairs={{0,6},{2,4},{4,2},{6,0},{8,14},{10,12},{12,10},{14,8},{16,22},{18,... | collective-permute-start | bytes 393224 | tf_op jit(solution)/shard_map/ppermute | solution.py:341
  54.8 5.3 %hyena.1 = bf16[256,2048]{1,0:T(8,128)(2,1)} custom-call(bf16[256,2048]{1,0:T(8,128)(2,1)S(1)} %copy-done.2, bf16[256,2048]{1,0:T(8,128)(2,1)S(1)} %copy-done, bf16[256,2048]{1,0:T(8,128)(2,1)S(1)} %copy-done.1, bf16[128,1024]{1,0:T(8,128)(2,1)S(1)} %collective-permute-done.near_rim, bf16[128,1024]{1,0:T(8,128)(2,1)S(1)} %collective-permute-done.3.ring_rim, ...), custom_call_target="tpu_custom_call" | custom-call | flops 4294967296 | bytes 5017600 | tf_op jit(solution)/shard_map/hyena/pallas_call | solution.py:26
  60.1 6.2 %collective-permute-start.16 = (bf16[256,256]{1,0:T(8,128)(2,1)S(1)}, bf16[256,256]{1,0:T(8,128)(2,1)S(1)}, u32[]{:S(2)}, u32[]{:S(2)}) collective-permute-start(bf16[256,256]{1,0:T(8,128)(2,1)S(1)} %get-tuple-element.60.refs_0_), channel_id=1, source_target_pairs={{0,1},{1,0},{2,3},{3,2},{4,5},{5,4},{6,7},{7,6},{8,9},{9,8},{10,11... | collective-permute-start | bytes 393224 | tf_op jit(solution)/shard_map/ppermute | solution.py:418
  68.2 3.5 %project.1 = bf16[256,2048]{1,0:T(8,128)(2,1)} custom-call(bf16[256,256]{1,0:T(8,128)(2,1)S(1)} %get-tuple-element.60.refs_0_, bf16[256,256]{1,0:T(8,128)(2,1)S(1)} %collective-permute-done.13.refs_1_, bf16[256,256]{1,0:T(8,128)(2,1)S(1)} %collective-permute-done.14.refs_2_, bf16[256,256]{1,0:T(8,128)(2,1)S(1)} %collective-permute-done.15.refs_3_, ...), custom_call_target="tpu_custom_call" | custom-call | flops 2147483648 | bytes 10485760 | tf_op jit(solution)/shard_map/project/pallas_call | solution.py:26
  (46 shorter events, 5.5 us)
Async XLA Ops:
  2.3 10.2 %collective-permute-start.1 = (bf16[784,256]{1,0:T(8,128)(2,1)S(1)}, bf16[784,256]{1,0:T(8,128)(2,1)S(1)}, u32[]{:S(2)}, u32[]{:S(2)}) collective-permute-start(bf16[784,256]{1,0:T(8,128)(2,1)S(1)} %get-tuple-element.35), channel_id=1, source_target_pairs={{0,4},{2,6},{4,0},{6,2},{8,12},{10,14},{12,8},{14,10},{16,20},{18,... | collective-permute-start | bytes 1204232 | tf_op jit(solution)/shard_map/ppermute | solution.py:341
  3.6 9.9 %collective-permute-start.5 = (bf16[784,256]{1,0:T(8,128)(2,1)S(1)}, bf16[784,256]{1,0:T(8,128)(2,1)S(1)}, u32[]{:S(2)}, u32[]{:S(2)}) collective-permute-start(bf16[784,256]{1,0:T(8,128)(2,1)S(1)} %get-tuple-element.44), channel_id=1, source_target_pairs={{0,2},{2,0},{4,6},{6,4},{8,10},{10,8},{12,14},{14,12},{16,18},{18,... | collective-permute-start | bytes 1204232 | tf_op jit(solution)/shard_map/ppermute | solution.py:341
  4.8 8.6 %collective-permute-start.6 = (bf16[528,256]{1,0:T(8,128)(2,1)S(1)}, bf16[528,256]{1,0:T(8,128)(2,1)S(1)}, u32[]{:S(2)}, u32[]{:S(2)}) collective-permute-start(bf16[528,256]{1,0:T(8,128)(2,1)S(1)} %get-tuple-element.42.refs_1_), channel_id=1, source_target_pairs={{0,8},{2,10},{4,12},{6,14},{8,16},{10,18},{12,20},{14,22},{16,24},... | collective-permute-start | bytes 811016 | tf_op jit(solution)/shard_map/ppermute | solution.py:344
  13.6 9.2 %collective-permute-start.7 = (bf16[528,256]{1,0:T(8,128)(2,1)S(1)}, bf16[528,256]{1,0:T(8,128)(2,1)S(1)}, u32[]{:S(2)}, u32[]{:S(2)}) collective-permute-start(bf16[528,256]{1,0:T(8,128)(2,1)S(1)} %get-tuple-element.49), channel_id=1, source_target_pairs={{0,6},{2,4},{4,2},{6,0},{8,14},{10,12},{12,10},{14,8},{16,22},{18,... | collective-permute-start | bytes 811016 | tf_op jit(solution)/shard_map/ppermute | solution.py:341
  14.9 22.6 %collective-permute-start.8 = (bf16[1056,256]{1,0:T(8,128)(2,1)S(1)}, bf16[1056,256]{1,0:T(8,128)(2,1)S(1)}, u32[]{:S(2)}, u32[]{:S(2)}) collective-permute-start(bf16[1056,256]{1,0:T(8,128)(2,1)S(1)} %pad_maximum_fusion), channel_id=1, source_target_pairs={{0,8},{2,10},{4,12},{6,14},{8,16},{10,18},{12,20},{14,22},{16,24},... | collective-permute-start | bytes 1622024 | tf_op jit(solution)/shard_map/ppermute | solution.py:344
  18.2 19.3 %collective-permute-start.10 = (bf16[816,256]{1,0:T(8,128)(2,1)S(1)}, bf16[816,256]{1,0:T(8,128)(2,1)S(1)}, u32[]{:S(2)}, u32[]{:S(2)}) collective-permute-start(bf16[816,256]{1,0:T(8,128)(2,1)S(1)} %pad_maximum_fusion.1), channel_id=1, source_target_pairs={{16,8},{18,10},{20,12},{22,14},{24,16},{26,18},{28,20},{30,22},{17... | collective-permute-start | bytes 1253384 | tf_op jit(solution)/shard_map/ppermute | solution.py:347
  20.3 20.9 %copy-start.4 = (bf16[2048]{0:T(1024)(128)(2,1)S(1)}, bf16[2048]{0:T(1024)(128)(2,1)}, u32[]{:S(2)}) copy-start(bf16[2048]{0:T(1024)(128)(2,1)} %param.14) | copy-start | bytes 12292
  20.3 6.2 %collective-permute-start.3 = (bf16[128,1024]{1,0:T(8,128)(2,1)S(1)}, bf16[128,1024]{1,0:T(8,128)(2,1)S(1)}, u32[]{:S(2)}, u32[]{:S(2)}) collective-permute-start(bf16[128,1024]{1,0:T(8,128)(2,1)S(1)} %get-tuple-element.64), channel_id=1, source_target_pairs={{0,2},{2,4},{4,6},{6,0},{8,10},{10,12},{12,14},{14,8},{16,18},{18,... | collective-permute-start | bytes 786440 | tf_op jit(solution)/shard_map/ppermute | solution.py:369
  20.6 8.9 %collective-permute-start.2 = (bf16[272,256]{1,0:T(8,128)(2,1)S(1)}, bf16[272,256]{1,0:T(8,128)(2,1)S(1)}, u32[]{:S(2)}, u32[]{:S(2)}) collective-permute-start(bf16[272,256]{1,0:T(8,128)(2,1)S(1)} %get-tuple-element.36), channel_id=1, source_target_pairs={{0,6},{2,4},{4,2},{6,0},{8,14},{10,12},{12,10},{14,8},{16,22},{18,... | collective-permute-start | bytes 417800 | tf_op jit(solution)/shard_map/ppermute | solution.py:341
  22.7 14.8 %collective-permute-start.9 = (bf16[528,256]{1,0:T(8,128)(2,1)S(1)}, bf16[528,256]{1,0:T(8,128)(2,1)S(1)}, u32[]{:S(2)}, u32[]{:S(2)}) collective-permute-start(bf16[528,256]{1,0:T(8,128)(2,1)S(1)} %collective-permute-done.7.refs_5_), channel_id=1, source_target_pairs={{0,8},{2,10},{4,12},{6,14},{8,16},{10,18},{12,20},{14,22},{16,24},... | collective-permute-start | bytes 811016 | tf_op jit(solution)/shard_map/ppermute | solution.py:344
  29.5 6.1 %collective-permute-start.11 = (bf16[272,256]{1,0:T(8,128)(2,1)S(1)}, bf16[272,256]{1,0:T(8,128)(2,1)S(1)}, u32[]{:S(2)}, u32[]{:S(2)}) collective-permute-start(bf16[272,256]{1,0:T(8,128)(2,1)S(1)} %collective-permute-done.2.refs_4_), channel_id=1, source_target_pairs={{16,8},{18,10},{20,12},{22,14},{24,16},{26,18},{28,20},{30,22},{17... | collective-permute-start | bytes 417800 | tf_op jit(solution)/shard_map/ppermute | solution.py:347
  31.4 9.8 %collective-permute-start = (bf16[128,1024]{1,0:T(8,128)(2,1)S(1)}, bf16[128,1024]{1,0:T(8,128)(2,1)S(1)}, u32[]{:S(2)}, u32[]{:S(2)}) collective-permute-start(bf16[128,1024]{1,0:T(8,128)(2,1)S(1)} %get-tuple-element.65), channel_id=1, source_target_pairs={{0,2},{2,4},{4,6},{6,8},{8,10},{10,12},{12,14},{14,16},{16,18},{18... | collective-permute-start | bytes 786440 | tf_op jit(solution)/shard_map/ppermute | solution.py:375
  35.6 7.4 %collective-permute-start.4 = (bf16[128,1024]{1,0:T(8,128)(2,1)S(1)}, bf16[128,1024]{1,0:T(8,128)(2,1)S(1)}, u32[]{:S(2)}, u32[]{:S(2)}) collective-permute-start(bf16[128,1024]{1,0:T(8,128)(2,1)S(1)} %collective-permute-done.3.ring_rim), channel_id=1, source_target_pairs={{0,8},{8,16},{16,24},{1,9},{9,17},{17,25}} | collective-permute-start | bytes 786440 | tf_op jit(solution)/shard_map/ppermute | solution.py:377
  39.3 12.5 %collective-permute-start.12 = (bf16[272,768]{1,0:T(8,128)(2,1)S(1)}, bf16[272,768]{1,0:T(8,128)(2,1)S(1)}, u32[]{:S(2)}, u32[]{:S(2)}) collective-permute-start(bf16[272,768]{1,0:T(8,128)(2,1)S(1)} %far.1), channel_id=1, source_target_pairs={{8,16},{10,18},{12,20},{14,22},{16,24},{18,26},{20,28},{22,30},{9,... | collective-permute-start | bytes 1253384 | tf_op jit(solution)/shard_map/ppermute | solution.py:344
  43.0 11.8 %copy-start.2 = (bf16[256,2048]{1,0:T(8,128)(2,1)S(1)}, bf16[256,2048]{1,0:T(8,128)(2,1)}, u32[]{:S(2)}) copy-start(bf16[256,2048]{1,0:T(8,128)(2,1)} %q_ref.3) | copy-start | bytes 3145732
  52.1 8.0 %collective-permute-start.13 = (bf16[256,256]{1,0:T(8,128)(2,1)S(1)}, bf16[256,256]{1,0:T(8,128)(2,1)S(1)}, u32[]{:S(2)}, u32[]{:S(2)}) collective-permute-start(bf16[256,256]{1,0:T(8,128)(2,1)S(1)} %get-tuple-element.56), channel_id=1, source_target_pairs={{0,2},{2,0},{4,6},{6,4},{8,10},{10,8},{12,14},{14,12},{16,18},{18,... | collective-permute-start | bytes 393224 | tf_op jit(solution)/shard_map/ppermute | solution.py:341
  52.2 7.9 %collective-permute-start.14 = (bf16[256,256]{1,0:T(8,128)(2,1)S(1)}, bf16[256,256]{1,0:T(8,128)(2,1)S(1)}, u32[]{:S(2)}, u32[]{:S(2)}) collective-permute-start(bf16[256,256]{1,0:T(8,128)(2,1)S(1)} %get-tuple-element.57), channel_id=1, source_target_pairs={{0,4},{2,6},{4,0},{6,2},{8,12},{10,14},{12,8},{14,10},{16,20},{18,... | collective-permute-start | bytes 393224 | tf_op jit(solution)/shard_map/ppermute | solution.py:341
  52.2 16.0 %slice-start = ((s8[8388608]{0:T(1024)(128)(4,1)}), s8[4194304]{0:T(1024)(128)(4,1)S(1)}, s32[]{:S(2)}) async-start(s8[8388608]{0:T(1024)(128)(4,1)} %bitcast.1), calls=%async_computation | async-start | bytes 8388608
  52.3 16.0 %slice-start.1 = ((s8[8388608]{0:T(1024)(128)(4,1)}), s8[4194304]{0:T(1024)(128)(4,1)S(1)}, s32[]{:S(2)}) async-start(s8[8388608]{0:T(1024)(128)(4,1)} %bitcast.1), calls=%async_computation.1 | async-start | bytes 8388608
  52.3 7.8 %collective-permute-start.15 = (bf16[256,256]{1,0:T(8,128)(2,1)S(1)}, bf16[256,256]{1,0:T(8,128)(2,1)S(1)}, u32[]{:S(2)}, u32[]{:S(2)}) collective-permute-start(bf16[256,256]{1,0:T(8,128)(2,1)S(1)} %get-tuple-element.58), channel_id=1, source_target_pairs={{0,6},{2,4},{4,2},{6,0},{8,14},{10,12},{12,10},{14,8},{16,22},{18,... | collective-permute-start | bytes 393224 | tf_op jit(solution)/shard_map/ppermute | solution.py:341
  60.1 7.2 %collective-permute-start.16 = (bf16[256,256]{1,0:T(8,128)(2,1)S(1)}, bf16[256,256]{1,0:T(8,128)(2,1)S(1)}, u32[]{:S(2)}, u32[]{:S(2)}) collective-permute-start(bf16[256,256]{1,0:T(8,128)(2,1)S(1)} %get-tuple-element.60.refs_0_), channel_id=1, source_target_pairs={{0,1},{1,0},{2,3},{3,2},{4,5},{5,4},{6,7},{7,6},{8,9},{9,8},{10,11... | collective-permute-start | bytes 393224 | tf_op jit(solution)/shard_map/ppermute | solution.py:418
  66.4 1.3 %collective-permute-start.17 = (bf16[256,256]{1,0:T(8,128)(2,1)S(1)}, bf16[256,256]{1,0:T(8,128)(2,1)S(1)}, u32[]{:S(2)}, u32[]{:S(2)}) collective-permute-start(bf16[256,256]{1,0:T(8,128)(2,1)S(1)} %collective-permute-done.13.refs_1_), channel_id=1, source_target_pairs={{0,1},{1,0},{2,3},{3,2},{4,5},{5,4},{6,7},{7,6},{8,9},{9,8},{10,11... | collective-permute-start | bytes 393224 | tf_op jit(solution)/shard_map/ppermute | solution.py:418
  66.4 1.5 %collective-permute-start.18 = (bf16[256,256]{1,0:T(8,128)(2,1)S(1)}, bf16[256,256]{1,0:T(8,128)(2,1)S(1)}, u32[]{:S(2)}, u32[]{:S(2)}) collective-permute-start(bf16[256,256]{1,0:T(8,128)(2,1)S(1)} %collective-permute-done.14.refs_2_), channel_id=1, source_target_pairs={{0,1},{1,0},{2,3},{3,2},{4,5},{5,4},{6,7},{7,6},{8,9},{9,8},{10,11... | collective-permute-start | bytes 393224 | tf_op jit(solution)/shard_map/ppermute | solution.py:418
  66.9 1.3 %collective-permute-start.19 = (bf16[256,256]{1,0:T(8,128)(2,1)S(1)}, bf16[256,256]{1,0:T(8,128)(2,1)S(1)}, u32[]{:S(2)}, u32[]{:S(2)}) collective-permute-start(bf16[256,256]{1,0:T(8,128)(2,1)S(1)} %collective-permute-done.15.refs_3_), channel_id=1, source_target_pairs={{0,1},{1,0},{2,3},{3,2},{4,5},{5,4},{6,7},{7,6},{8,9},{9,8},{10,11... | collective-permute-start | bytes 393224 | tf_op jit(solution)/shard_map/ppermute | solution.py:418
  (3 other events, 19.0 us)

commit v11 on v9

--- a/solution.py
+++ b/solution.py
@@ -21,12 +21,12 @@
     return lax.rem(lax.axis_index("ctx"), SQUAD)
 
 
-def kernel_call(kernel, args, shapes, name, scratch=(), flops=0, exps=0):
+def kernel_call(kernel, args, shapes, name, scratch=(), flops=0, exps=0, out=VMEM):
     total = sum(math.prod(x.shape) * x.dtype.itemsize for x in (*args, *shapes))
     return list(pl.pallas_call(
         kernel,
         in_specs=[VMEM] * len(args),
-        out_specs=[VMEM] * len(shapes),
+        out_specs=[out] * len(shapes),
         out_shape=shapes,
         scratch_shapes=scratch,
         compiler_params=pltpu.CompilerParams(vmem_limit_bytes=VMEM_LIMIT),
@@ -35,7 +35,7 @@
     )(*args))
 
 
-def hyena_kernel(q_ref, k_ref, v_ref, near_rim, ring_rim, far_rim, taps_ref, direct_ref, out_ref, taps, rim):
+def hyena_kernel(q_ref, k_ref, v_ref, near_rim, ring_rim, far_rim, taps_ref, direct_ref, out_ref, taps, rim, made, sent):
     rows, chans = q_ref.shape
     groups = taps_ref.shape[0]
     group = chans // groups
@@ -57,6 +57,11 @@
     def _():
         rim[:, half:] = far_rim[...]
 
+    def leave(tile):
+        begin = tile * LANES if isinstance(tile, int) else pl.multiple_of(tile * LANES, LANES)
+        cols = pl.ds(begin, LANES)
+        return pltpu.make_async_copy(made.at[:, cols], out_ref.at[:, cols], sent.at[tile])
+
     @pl.loop(0, chans // LANES, unroll=2)
     def _(tile):
         cols = pl.ds(pl.multiple_of(tile * LANES, LANES), LANES)
@@ -79,10 +84,14 @@
         conv = jnp.concatenate(
             [conv[:, w * LANES : (w + 1) * LANES] for w in range(windows)], axis=0
         )
-        out_ref[:, cols] = (
+        made[:, cols] = (
             q_ref[:, cols].astype(jnp.float32)
             * (conv + direct_ref[:, cols].astype(jnp.float32) * mixed.astype(jnp.float32))
         ).astype(jnp.bfloat16)
+        leave(tile).start()
+
+    for tile in range(chans // LANES):
+        leave(tile).wait()
 
 
 def hyena(hyena_q, hyena_k, hyena_v, rims, filters, direct):
@@ -94,8 +103,14 @@
         (hyena_q, hyena_k, hyena_v, *rims, taps, direct[None]),
         [jax.ShapeDtypeStruct((rows, chans), jnp.bfloat16)],
         "hyena",
-        [pltpu.VMEM((groups, LANES), jnp.float32), pltpu.VMEM((LANES, chans), jnp.bfloat16)],
+        [
+            pltpu.VMEM((groups, LANES), jnp.float32),
+            pltpu.VMEM((LANES, chans), jnp.bfloat16),
+            pltpu.VMEM((rows, chans), jnp.bfloat16),
+            pltpu.SemaphoreType.DMA((chans // LANES,)),
+        ],
         flops=4 * rows * chans * 2 * LANES * 8,
+        out=pl.BlockSpec(memory_space=pl.ANY),
     )
     return out
 
@@ -309,7 +324,7 @@
 
 
 def project_kernel(ranks, *refs):
-    parts, weight_ref, out_ref, whole = refs[:-3], refs[-3], refs[-2], refs[-1]
+    parts, (weight_ref, out_ref, whole, made, sent) = refs[:-5], refs[-5:]
     mine, corner = lax.axis_index("tp"), corner_of()
     width = parts[0].shape[1]
     for r in range(ranks):
@@ -318,11 +333,19 @@
             begin = (source * SQUAD + jnp.bitwise_xor(corner, k)) * width
             whole[:, pl.ds(pl.multiple_of(begin, width), width)] = parts[r * SQUAD + k][...]
     block = 2 * LANES
+    copies = []
     for c in range(out_ref.shape[1] // block):
         cols = slice(c * block, (c + 1) * block)
-        out_ref[:, cols] = jnp.dot(
+        made[:, cols] = jnp.dot(
             whole[...], weight_ref[:, cols], preferred_element_type=jnp.float32
-        ).astype(out_ref.dtype)
+        ).astype(made.dtype)
+        span = pl.ds(c * block, block)
+        copies.append(
+            pltpu.make_async_copy(made.at[:, span], out_ref.at[:, span], sent.at[c])
+        )
+        copies[-1].start()
+    for copy in copies:
+        copy.wait()
 
 
 def local(
@@ -420,8 +443,13 @@
         (*pieces, out_weight),
         [jax.ShapeDtypeStruct((rows, out_weight.shape[1]), bf16)],
         "project",
-        [pltpu.VMEM((rows, ranks * feat), bf16)],
+        [
+            pltpu.VMEM((rows, ranks * feat), bf16),
+            pltpu.VMEM((rows, out_weight.shape[1]), bf16),
+            pltpu.SemaphoreType.DMA((out_weight.shape[1] // (2 * LANES),)),
+        ],
         flops=2 * rows * math.prod(out_weight.shape),
+        out=pl.BlockSpec(memory_space=pl.ANY),
     )
     return (hyena_out, attn_out)
 

time: 69 us -> 68.9 us (level)
  no operation moved by 1% of the time
where the time goes in v11:
time: 68.9 us; the launch traced here: 68.5 us
  starting transfers between devices  33.3 us (48%)
  Pallas kernels  18.3 us (27%)
  waiting for transfers between devices  14.4 us (21%)
  other arithmetic  1.24 us (2%)
  between operations  1.12 us (2%)
    pallas_call x5, Pallas kernels, kernel_call(): pl.pallas_call(kernel, in_specs=[VMEM] * len(args), out_specs=[out] * len...  16.6 us
    ppermute x4, starting transfers between devices, climb(): lax.ppermute(value, 'ctx', [(i, i + SQUAD) for i in range(first, count -...  11.5 us
    ppermute x4, waiting for transfers between devices, climb(): lax.ppermute(value, 'ctx', [(i, i + SQUAD) for i in range(first, count -...  8.01 us
    ppermute x6, starting transfers between devices, swap(): return lax.ppermute(value, 'ctx', [(i, i ^ mask) for i in range(count)])  6.46 us
    ppermute x4, starting transfers between devices, turn(): lax.ppermute(value, 'tp', [(t, (t + r) % ranks) for t in range(ranks)])  4.44 us
    ppermute x2, starting transfers between devices, descend(): lax.ppermute(value, 'ctx', [(i, i - SQUAD) for i in range(2 * SQUAD, coun...  4 us
    ppermute x1, starting transfers between devices, local(): lax.ppermute(ring, 'ctx', [(i, i + SQUAD) for i in range(0, count - SQUAD...  3.37 us
    ppermute x1, waiting for transfers between devices, local(): lax.ppermute(tail[:, half:], 'ctx', [(i, i - i % SQUAD + (i + 1) % SQUAD)...  3.2 us
  transfers between devices with their start and end apart: 19, of which 9 were waited for; matrix products, arithmetic and copies ran while one was open for 2% of the time, Pallas kernels for 19%

profile of v11, /device:TPU:17, one launch (start us, length us, event | category | flops | bytes accessed | tf_op | source)
XLA Modules:
  0.0 68.5 jit_solution(6845892704772040041)
XLA Ops:
  0.6 1.7 %deal.1 = (bf16[272,256]{1,0:T(8,128)(2,1)S(1)}, bf16[528,256]{1,0:T(8,128)(2,1)S(1)}, bf16[784,256]{1,0:T(8,128)(2,1)S(1)}, bf16[784,256]{1,0:T(8,128)(2,1)S(1)}, bf16[784,256]{1,0:T(8,128)(2,1)S(1)}) custom-call(bf16[256,1024]{1,0:T(8,128)(2,1)} %q_ref.2, bf16[256,1024]{1,0:T(8,128)(2,1)} %k_ref.2, bf16[256,1024]{1,0:T(8,128)(2,1)} %v_ref.2, s32[2,128]{1,0:T(2,128)} %bitcast.3), custom_call_target="tpu_custom_call" | custom-call | bytes 3145728 | tf_op jit(solution)/shard_map/deal/pallas_call | solution.py:160
  2.3 1.3 %collective-permute-start.1 = (bf16[784,256]{1,0:T(8,128)(2,1)S(1)}, bf16[784,256]{1,0:T(8,128)(2,1)S(1)}, u32[]{:S(2)}, u32[]{:S(2)}) collective-permute-start(bf16[784,256]{1,0:T(8,128)(2,1)S(1)} %get-tuple-element.32), channel_id=1, source_target_pairs={{0,2},{2,0},{4,6},{6,4},{8,10},{10,8},{12,14},{14,12},{16,18},{18,... | collective-permute-start | bytes 1204232 | tf_op jit(solution)/shard_map/ppermute | solution.py:361
  3.6 1.2 %collective-permute-start.5 = (bf16[784,256]{1,0:T(8,128)(2,1)S(1)}, bf16[784,256]{1,0:T(8,128)(2,1)S(1)}, u32[]{:S(2)}, u32[]{:S(2)}) collective-permute-start(bf16[784,256]{1,0:T(8,128)(2,1)S(1)} %get-tuple-element.41), channel_id=1, source_target_pairs={{0,4},{2,6},{4,0},{6,2},{8,12},{10,14},{12,8},{14,10},{16,20},{18,... | collective-permute-start | bytes 1204232 | tf_op jit(solution)/shard_map/ppermute | solution.py:361
  4.8 3.2 %collective-permute-start.6 = (bf16[528,256]{1,0:T(8,128)(2,1)S(1)}, bf16[528,256]{1,0:T(8,128)(2,1)S(1)}, u32[]{:S(2)}, u32[]{:S(2)}) collective-permute-start(bf16[528,256]{1,0:T(8,128)(2,1)S(1)} %get-tuple-element.39.refs_1_), channel_id=1, source_target_pairs={{0,8},{2,10},{4,12},{6,14},{8,16},{10,18},{12,20},{14,22},{16,24},... | collective-permute-start | bytes 811016 | tf_op jit(solution)/shard_map/ppermute | solution.py:364
  8.0 1.2 %multiply_convert_fusion = bf16[128,2048]{1,0:T(8,128)(2,1)S(1)} fusion(bf16[256,2048]{1,0:T(8,128)(2,1)} %v_ref.3, bf16[256,2048]{1,0:T(8,128)(2,1)S(1)} %copy-done), kind=kLoop, calls=%fused_computation | loop fusion | flops 1048576 | bytes 1572864 | tf_op jit(solution)/shard_map/convert_element_type | solution.py:385
  9.2 4.2 %collective-permute-done.6.refs_5_.refs_2_ = bf16[528,256]{1,0:T(8,128)(2,1)S(1)} collective-permute-done((bf16[528,256]{1,0:T(8,128)(2,1)S(1)}, bf16[528,256]{1,0:T(8,128)(2,1)S(1)}, u32[]{:S(2)}, u32[]{:S(2)}) %collective-permute-start.6) | collective-permute-done | bytes 270368 | tf_op jit(solution)/shard_map/ppermute | solution.py:364
  13.6 1.3 %collective-permute-start.2 = (bf16[784,256]{1,0:T(8,128)(2,1)S(1)}, bf16[784,256]{1,0:T(8,128)(2,1)S(1)}, u32[]{:S(2)}, u32[]{:S(2)}) collective-permute-start(bf16[784,256]{1,0:T(8,128)(2,1)S(1)} %get-tuple-element.33), channel_id=1, source_target_pairs={{0,6},{2,4},{4,2},{6,0},{8,14},{10,12},{12,10},{14,8},{16,22},{18,... | collective-permute-start | bytes 1204232 | tf_op jit(solution)/shard_map/ppermute | solution.py:361
  14.9 3.2 %collective-permute-start.7 = (bf16[1056,256]{1,0:T(8,128)(2,1)S(1)}, bf16[1056,256]{1,0:T(8,128)(2,1)S(1)}, u32[]{:S(2)}, u32[]{:S(2)}) collective-permute-start(bf16[1056,256]{1,0:T(8,128)(2,1)S(1)} %pad_maximum_fusion), channel_id=1, source_target_pairs={{0,8},{2,10},{4,12},{6,14},{8,16},{10,18},{12,20},{14,22},{16,24},... | collective-permute-start | bytes 1622024 | tf_op jit(solution)/shard_map/ppermute | solution.py:364
  18.1 2.1 %collective-permute-start.9 = (bf16[816,256]{1,0:T(8,128)(2,1)S(1)}, bf16[816,256]{1,0:T(8,128)(2,1)S(1)}, u32[]{:S(2)}, u32[]{:S(2)}) collective-permute-start(bf16[816,256]{1,0:T(8,128)(2,1)S(1)} %pad_maximum_fusion.1), channel_id=1, source_target_pairs={{16,8},{18,10},{20,12},{22,14},{24,16},{26,18},{28,20},{30,22},{17... | collective-permute-start | bytes 1253384 | tf_op jit(solution)/shard_map/ppermute | solution.py:367
  20.2 1.3 %collective-permute-start.3 = (bf16[128,1024]{1,0:T(8,128)(2,1)S(1)}, bf16[128,1024]{1,0:T(8,128)(2,1)S(1)}, u32[]{:S(2)}, u32[]{:S(2)}) collective-permute-start(bf16[128,1024]{1,0:T(8,128)(2,1)S(1)} %get-tuple-element.58), channel_id=1, source_target_pairs={{0,2},{2,4},{4,6},{6,0},{8,10},{10,12},{12,14},{14,8},{16,18},{18,... | collective-permute-start | bytes 786440 | tf_op jit(solution)/shard_map/ppermute | solution.py:387
  21.5 1.6 %collective-permute-done.2.refs_4_ = bf16[784,256]{1,0:T(8,128)(2,1)S(1)} collective-permute-done((bf16[784,256]{1,0:T(8,128)(2,1)S(1)}, bf16[784,256]{1,0:T(8,128)(2,1)S(1)}, u32[]{:S(2)}, u32[]{:S(2)}) %collective-permute-start.2) | collective-permute-done | bytes 401440 | tf_op jit(solution)/shard_map/ppermute | solution.py:361
  23.2 3.2 %collective-permute-start.8 = (bf16[528,256]{1,0:T(8,128)(2,1)S(1)}, bf16[528,256]{1,0:T(8,128)(2,1)S(1)}, u32[]{:S(2)}, u32[]{:S(2)}) collective-permute-start(bf16[528,256]{1,0:T(8,128)(2,1)S(1)} %slice.42), channel_id=1, source_target_pairs={{0,8},{2,10},{4,12},{6,14},{8,16},{10,18},{12,20},{14,22},{16,24},... | collective-permute-start | bytes 811016 | tf_op jit(solution)/shard_map/ppermute | solution.py:364
  26.4 3.2 %collective-permute-done.3.ring_rim = bf16[128,1024]{1,0:T(8,128)(2,1)S(1)} collective-permute-done((bf16[128,1024]{1,0:T(8,128)(2,1)S(1)}, bf16[128,1024]{1,0:T(8,128)(2,1)S(1)}, u32[]{:S(2)}, u32[]{:S(2)}) %collective-permute-start.3) | collective-permute-done | bytes 262176 | tf_op jit(solution)/shard_map/ppermute | solution.py:387
  29.6 1.9 %collective-permute-start.10 = (bf16[272,256]{1,0:T(8,128)(2,1)S(1)}, bf16[272,256]{1,0:T(8,128)(2,1)S(1)}, u32[]{:S(2)}, u32[]{:S(2)}) collective-permute-start(bf16[272,256]{1,0:T(8,128)(2,1)S(1)} %slice.39), channel_id=1, source_target_pairs={{16,8},{18,10},{20,12},{22,14},{24,16},{26,18},{28,20},{30,22},{17... | collective-permute-start | bytes 417800 | tf_op jit(solution)/shard_map/ppermute | solution.py:367
  31.5 2.2 %collective-permute-start = (bf16[128,1024]{1,0:T(8,128)(2,1)S(1)}, bf16[128,1024]{1,0:T(8,128)(2,1)S(1)}, u32[]{:S(2)}, u32[]{:S(2)}) collective-permute-start(bf16[128,1024]{1,0:T(8,128)(2,1)S(1)} %get-tuple-element.59), channel_id=1, source_target_pairs={{0,2},{2,4},{4,6},{6,8},{8,10},{10,12},{12,14},{14,16},{16,18},{18... | collective-permute-start | bytes 786440 | tf_op jit(solution)/shard_map/ppermute | solution.py:393
  33.8 3.4 %collective-permute-start.4 = (bf16[128,1024]{1,0:T(8,128)(2,1)S(1)}, bf16[128,1024]{1,0:T(8,128)(2,1)S(1)}, u32[]{:S(2)}, u32[]{:S(2)}) collective-permute-start(bf16[128,1024]{1,0:T(8,128)(2,1)S(1)} %collective-permute-done.3.ring_rim), channel_id=1, source_target_pairs={{0,8},{8,16},{16,24},{1,9},{9,17},{17,25}} | collective-permute-start | bytes 786440 | tf_op jit(solution)/shard_map/ppermute | solution.py:395
  37.2 1.8 %far.1 = bf16[272,768]{1,0:T(8,128)(2,1)S(1)} custom-call(bf16[816,256]{1,0:T(8,128)(2,1)S(1)} %collective-permute-done.9.refs_0_, bf16[272,256]{1,0:T(8,128)(2,1)S(1)} %collective-permute-done.10.refs_1_, bf16[528,256]{1,0:T(8,128)(2,1)S(1)} %collective-permute-done.6.refs_5_.refs_2_, bf16[1056,256]{1,0:T(8,128)(2,1)S(1)} %collective-permute-done.7.refs_6_.refs_3_, ...), custom_call_target="tpu_custom_call" | custom-call | flops 402653184 | bytes 2056192 | tf_op jit(solution)/shard_map/far/pallas_call | solution.py:26
  38.9 1.9 %collective-permute-start.11 = (bf16[272,768]{1,0:T(8,128)(2,1)S(1)}, bf16[272,768]{1,0:T(8,128)(2,1)S(1)}, u32[]{:S(2)}, u32[]{:S(2)}) collective-permute-start(bf16[272,768]{1,0:T(8,128)(2,1)S(1)} %far.1), channel_id=1, source_target_pairs={{8,16},{10,18},{12,20},{14,22},{16,24},{18,26},{20,28},{22,30},{9,... | collective-permute-start | bytes 1253384 | tf_op jit(solution)/shard_map/ppermute | solution.py:364
  41.2 6.0 %main.1.main_ref = f32[272,1024]{1,0:T(8,128)S(1)} custom-call(bf16[272,256]{1,0:T(8,128)(2,1)S(1)} %get-tuple-element.38.refs_0_, bf16[528,256]{1,0:T(8,128)(2,1)S(1)} %get-tuple-element.39.refs_1_, bf16[784,256]{1,0:T(8,128)(2,1)S(1)} %collective-permute-done.1.refs_2_, bf16[784,256]{1,0:T(8,128)(2,1)S(1)} %collective-permute-done.5.refs_3_, ...), custom_call_target="tpu_custom_call" | custom-call | flops 1744830464 | bytes 3809280 | tf_op jit(solution)/shard_map/main/pallas_call | solution.py:26
  47.2 3.8 %collective-permute-done.11.far_ref = bf16[272,768]{1,0:T(8,128)(2,1)S(1)} collective-permute-done((bf16[272,768]{1,0:T(8,128)(2,1)S(1)}, bf16[272,768]{1,0:T(8,128)(2,1)S(1)}, u32[]{:S(2)}, u32[]{:S(2)}) %collective-permute-start.11) | collective-permute-done | bytes 417824 | tf_op jit(solution)/shard_map/ppermute | solution.py:364
  51.6 2.5 %collective-permute-start.14 = (bf16[256,256]{1,0:T(8,128)(2,1)S(1)}, bf16[256,256]{1,0:T(8,128)(2,1)S(1)}, u32[]{:S(2)}, u32[]{:S(2)}) collective-permute-start(bf16[256,256]{1,0:T(8,128)(2,1)S(1)} %get-tuple-element.52), channel_id=1, source_target_pairs={{0,6},{2,4},{4,2},{6,0},{8,14},{10,12},{12,10},{14,8},{16,22},{18,... | collective-permute-start | bytes 393224 | tf_op jit(solution)/shard_map/ppermute | solution.py:361
  54.1 5.1 %hyena.1 = bf16[256,2048]{1,0:T(8,128)(2,1)} custom-call(bf16[256,2048]{1,0:T(8,128)(2,1)S(1)} %copy-done.2, bf16[256,2048]{1,0:T(8,128)(2,1)S(1)} %copy-done, bf16[256,2048]{1,0:T(8,128)(2,1)S(1)} %copy-done.1, bf16[128,1024]{1,0:T(8,128)(2,1)S(1)} %collective-permute-done.near_rim, bf16[128,1024]{1,0:T(8,128)(2,1)S(1)} %collective-permute-done.3.ring_rim, ...), custom_call_target="tpu_custom_call" | custom-call | flops 4294967296 | bytes 5017600 | tf_op jit(solution)/shard_map/hyena/pallas_call | solution.py:26
  59.3 3.9 %collective-permute-start.15 = (bf16[256,256]{1,0:T(8,128)(2,1)S(1)}, bf16[256,256]{1,0:T(8,128)(2,1)S(1)}, u32[]{:S(2)}, u32[]{:S(2)}) collective-permute-start(bf16[256,256]{1,0:T(8,128)(2,1)S(1)} %get-tuple-element.54.refs_0_), channel_id=1, source_target_pairs={{0,1},{1,0},{2,3},{3,2},{4,5},{5,4},{6,7},{7,6},{8,9},{9,8},{10,11... | collective-permute-start | bytes 393224 | tf_op jit(solution)/shard_map/ppermute | solution.py:436
  65.0 3.3 %project.1 = bf16[256,2048]{1,0:T(8,128)(2,1)} custom-call(bf16[256,256]{1,0:T(8,128)(2,1)S(1)} %get-tuple-element.54.refs_0_, bf16[256,256]{1,0:T(8,128)(2,1)S(1)} %collective-permute-done.12.refs_1_, bf16[256,256]{1,0:T(8,128)(2,1)S(1)} %collective-permute-done.13.refs_2_, bf16[256,256]{1,0:T(8,128)(2,1)S(1)} %collective-permute-done.14.refs_3_, ...), custom_call_target="tpu_custom_call" | custom-call | flops 2147483648 | bytes 10485760 | tf_op jit(solution)/shard_map/project/pallas_call | solution.py:26
  (46 shorter events, 2.9 us)
Async XLA Ops:
  0.6 7.4 %copy-start = (bf16[256,2048]{1,0:T(8,128)(2,1)S(1)}, bf16[256,2048]{1,0:T(8,128)(2,1)}, u32[]{:S(2)}) copy-start(bf16[256,2048]{1,0:T(8,128)(2,1)} %k_ref.3) | copy-start | bytes 3145732
  2.3 11.2 %collective-permute-start.1 = (bf16[784,256]{1,0:T(8,128)(2,1)S(1)}, bf16[784,256]{1,0:T(8,128)(2,1)S(1)}, u32[]{:S(2)}, u32[]{:S(2)}) collective-permute-start(bf16[784,256]{1,0:T(8,128)(2,1)S(1)} %get-tuple-element.32), channel_id=1, source_target_pairs={{0,2},{2,0},{4,6},{6,4},{8,10},{10,8},{12,14},{14,12},{16,18},{18,... | collective-permute-start | bytes 1204232 | tf_op jit(solution)/shard_map/ppermute | solution.py:361
  3.6 9.9 %collective-permute-start.5 = (bf16[784,256]{1,0:T(8,128)(2,1)S(1)}, bf16[784,256]{1,0:T(8,128)(2,1)S(1)}, u32[]{:S(2)}, u32[]{:S(2)}) collective-permute-start(bf16[784,256]{1,0:T(8,128)(2,1)S(1)} %get-tuple-element.41), channel_id=1, source_target_pairs={{0,4},{2,6},{4,0},{6,2},{8,12},{10,14},{12,8},{14,10},{16,20},{18,... | collective-permute-start | bytes 1204232 | tf_op jit(solution)/shard_map/ppermute | solution.py:361
  4.8 8.6 %collective-permute-start.6 = (bf16[528,256]{1,0:T(8,128)(2,1)S(1)}, bf16[528,256]{1,0:T(8,128)(2,1)S(1)}, u32[]{:S(2)}, u32[]{:S(2)}) collective-permute-start(bf16[528,256]{1,0:T(8,128)(2,1)S(1)} %get-tuple-element.39.refs_1_), channel_id=1, source_target_pairs={{0,8},{2,10},{4,12},{6,14},{8,16},{10,18},{12,20},{14,22},{16,24},... | collective-permute-start | bytes 811016 | tf_op jit(solution)/shard_map/ppermute | solution.py:364
  13.6 9.6 %collective-permute-start.2 = (bf16[784,256]{1,0:T(8,128)(2,1)S(1)}, bf16[784,256]{1,0:T(8,128)(2,1)S(1)}, u32[]{:S(2)}, u32[]{:S(2)}) collective-permute-start(bf16[784,256]{1,0:T(8,128)(2,1)S(1)} %get-tuple-element.33), channel_id=1, source_target_pairs={{0,6},{2,4},{4,2},{6,0},{8,14},{10,12},{12,10},{14,8},{16,22},{18,... | collective-permute-start | bytes 1204232 | tf_op jit(solution)/shard_map/ppermute | solution.py:361
  14.9 22.3 %collective-permute-start.7 = (bf16[1056,256]{1,0:T(8,128)(2,1)S(1)}, bf16[1056,256]{1,0:T(8,128)(2,1)S(1)}, u32[]{:S(2)}, u32[]{:S(2)}) collective-permute-start(bf16[1056,256]{1,0:T(8,128)(2,1)S(1)} %pad_maximum_fusion), channel_id=1, source_target_pairs={{0,8},{2,10},{4,12},{6,14},{8,16},{10,18},{12,20},{14,22},{16,24},... | collective-permute-start | bytes 1622024 | tf_op jit(solution)/shard_map/ppermute | solution.py:364
  18.1 15.7 %collective-permute-start.9 = (bf16[816,256]{1,0:T(8,128)(2,1)S(1)}, bf16[816,256]{1,0:T(8,128)(2,1)S(1)}, u32[]{:S(2)}, u32[]{:S(2)}) collective-permute-start(bf16[816,256]{1,0:T(8,128)(2,1)S(1)} %pad_maximum_fusion.1), channel_id=1, source_target_pairs={{16,8},{18,10},{20,12},{22,14},{24,16},{26,18},{28,20},{30,22},{17... | collective-permute-start | bytes 1253384 | tf_op jit(solution)/shard_map/ppermute | solution.py:367
  20.2 9.3 %collective-permute-start.3 = (bf16[128,1024]{1,0:T(8,128)(2,1)S(1)}, bf16[128,1024]{1,0:T(8,128)(2,1)S(1)}, u32[]{:S(2)}, u32[]{:S(2)}) collective-permute-start(bf16[128,1024]{1,0:T(8,128)(2,1)S(1)} %get-tuple-element.58), channel_id=1, source_target_pairs={{0,2},{2,4},{4,6},{6,0},{8,10},{10,12},{12,14},{14,8},{16,18},{18,... | collective-permute-start | bytes 786440 | tf_op jit(solution)/shard_map/ppermute | solution.py:387
  23.2 14.0 %collective-permute-start.8 = (bf16[528,256]{1,0:T(8,128)(2,1)S(1)}, bf16[528,256]{1,0:T(8,128)(2,1)S(1)}, u32[]{:S(2)}, u32[]{:S(2)}) collective-permute-start(bf16[528,256]{1,0:T(8,128)(2,1)S(1)} %slice.42), channel_id=1, source_target_pairs={{0,8},{2,10},{4,12},{6,14},{8,16},{10,18},{12,20},{14,22},{16,24},... | collective-permute-start | bytes 811016 | tf_op jit(solution)/shard_map/ppermute | solution.py:364
  29.6 11.3 %copy-start.4 = (bf16[2048]{0:T(1024)(128)(2,1)S(1)}, bf16[2048]{0:T(1024)(128)(2,1)}, u32[]{:S(2)}) copy-start(bf16[2048]{0:T(1024)(128)(2,1)} %param.14) | copy-start | bytes 12292
  29.6 7.6 %collective-permute-start.10 = (bf16[272,256]{1,0:T(8,128)(2,1)S(1)}, bf16[272,256]{1,0:T(8,128)(2,1)S(1)}, u32[]{:S(2)}, u32[]{:S(2)}) collective-permute-start(bf16[272,256]{1,0:T(8,128)(2,1)S(1)} %slice.39), channel_id=1, source_target_pairs={{16,8},{18,10},{20,12},{22,14},{24,16},{26,18},{28,20},{30,22},{17... | collective-permute-start | bytes 417800 | tf_op jit(solution)/shard_map/ppermute | solution.py:367
  31.5 9.4 %collective-permute-start = (bf16[128,1024]{1,0:T(8,128)(2,1)S(1)}, bf16[128,1024]{1,0:T(8,128)(2,1)S(1)}, u32[]{:S(2)}, u32[]{:S(2)}) collective-permute-start(bf16[128,1024]{1,0:T(8,128)(2,1)S(1)} %get-tuple-element.59), channel_id=1, source_target_pairs={{0,2},{2,4},{4,6},{6,8},{8,10},{10,12},{12,14},{14,16},{16,18},{18... | collective-permute-start | bytes 786440 | tf_op jit(solution)/shard_map/ppermute | solution.py:393
  33.8 7.4 %collective-permute-start.4 = (bf16[128,1024]{1,0:T(8,128)(2,1)S(1)}, bf16[128,1024]{1,0:T(8,128)(2,1)S(1)}, u32[]{:S(2)}, u32[]{:S(2)}) collective-permute-start(bf16[128,1024]{1,0:T(8,128)(2,1)S(1)} %collective-permute-done.3.ring_rim), channel_id=1, source_target_pairs={{0,8},{8,16},{16,24},{1,9},{9,17},{17,25}} | collective-permute-start | bytes 786440 | tf_op jit(solution)/shard_map/ppermute | solution.py:395
  38.9 12.1 %collective-permute-start.11 = (bf16[272,768]{1,0:T(8,128)(2,1)S(1)}, bf16[272,768]{1,0:T(8,128)(2,1)S(1)}, u32[]{:S(2)}, u32[]{:S(2)}) collective-permute-start(bf16[272,768]{1,0:T(8,128)(2,1)S(1)} %far.1), channel_id=1, source_target_pairs={{8,16},{10,18},{12,20},{14,22},{16,24},{18,26},{20,28},{22,30},{9,... | collective-permute-start | bytes 1253384 | tf_op jit(solution)/shard_map/ppermute | solution.py:364
  41.2 12.9 %copy-start.2 = (bf16[256,2048]{1,0:T(8,128)(2,1)S(1)}, bf16[256,2048]{1,0:T(8,128)(2,1)}, u32[]{:S(2)}) copy-start(bf16[256,2048]{1,0:T(8,128)(2,1)} %q_ref.3) | copy-start | bytes 3145732
  51.4 7.9 %collective-permute-start.12 = (bf16[256,256]{1,0:T(8,128)(2,1)S(1)}, bf16[256,256]{1,0:T(8,128)(2,1)S(1)}, u32[]{:S(2)}, u32[]{:S(2)}) collective-permute-start(bf16[256,256]{1,0:T(8,128)(2,1)S(1)} %get-tuple-element.50), channel_id=1, source_target_pairs={{0,2},{2,0},{4,6},{6,4},{8,10},{10,8},{12,14},{14,12},{16,18},{18,... | collective-permute-start | bytes 393224 | tf_op jit(solution)/shard_map/ppermute | solution.py:361
  51.5 7.8 %collective-permute-start.13 = (bf16[256,256]{1,0:T(8,128)(2,1)S(1)}, bf16[256,256]{1,0:T(8,128)(2,1)S(1)}, u32[]{:S(2)}, u32[]{:S(2)}) collective-permute-start(bf16[256,256]{1,0:T(8,128)(2,1)S(1)} %get-tuple-element.51), channel_id=1, source_target_pairs={{0,4},{2,6},{4,0},{6,2},{8,12},{10,14},{12,8},{14,10},{16,20},{18,... | collective-permute-start | bytes 393224 | tf_op jit(solution)/shard_map/ppermute | solution.py:361
  51.5 13.5 %slice-start = ((s8[8388608]{0:T(1024)(128)(4,1)}), s8[4194304]{0:T(1024)(128)(4,1)S(1)}, s32[]{:S(2)}) async-start(s8[8388608]{0:T(1024)(128)(4,1)} %bitcast.1), calls=%async_computation | async-start | bytes 8388608
  51.5 13.5 %slice-start.1 = ((s8[8388608]{0:T(1024)(128)(4,1)}), s8[4194304]{0:T(1024)(128)(4,1)S(1)}, s32[]{:S(2)}) async-start(s8[8388608]{0:T(1024)(128)(4,1)} %bitcast.1), calls=%async_computation.1 | async-start | bytes 8388608
  51.6 7.7 %collective-permute-start.14 = (bf16[256,256]{1,0:T(8,128)(2,1)S(1)}, bf16[256,256]{1,0:T(8,128)(2,1)S(1)}, u32[]{:S(2)}, u32[]{:S(2)}) collective-permute-start(bf16[256,256]{1,0:T(8,128)(2,1)S(1)} %get-tuple-element.52), channel_id=1, source_target_pairs={{0,6},{2,4},{4,2},{6,0},{8,14},{10,12},{12,10},{14,8},{16,22},{18,... | collective-permute-start | bytes 393224 | tf_op jit(solution)/shard_map/ppermute | solution.py:361
  59.3 4.8 %collective-permute-start.15 = (bf16[256,256]{1,0:T(8,128)(2,1)S(1)}, bf16[256,256]{1,0:T(8,128)(2,1)S(1)}, u32[]{:S(2)}, u32[]{:S(2)}) collective-permute-start(bf16[256,256]{1,0:T(8,128)(2,1)S(1)} %get-tuple-element.54.refs_0_), channel_id=1, source_target_pairs={{0,1},{1,0},{2,3},{3,2},{4,5},{5,4},{6,7},{7,6},{8,9},{9,8},{10,11... | collective-permute-start | bytes 393224 | tf_op jit(solution)/shard_map/ppermute | solution.py:436
  63.1 1.3 %collective-permute-start.16 = (bf16[256,256]{1,0:T(8,128)(2,1)S(1)}, bf16[256,256]{1,0:T(8,128)(2,1)S(1)}, u32[]{:S(2)}, u32[]{:S(2)}) collective-permute-start(bf16[256,256]{1,0:T(8,128)(2,1)S(1)} %collective-permute-done.12.refs_1_), channel_id=1, source_target_pairs={{0,1},{1,0},{2,3},{3,2},{4,5},{5,4},{6,7},{7,6},{8,9},{9,8},{10,11... | collective-permute-start | bytes 393224 | tf_op jit(solution)/shard_map/ppermute | solution.py:436
  63.2 1.5 %collective-permute-start.17 = (bf16[256,256]{1,0:T(8,128)(2,1)S(1)}, bf16[256,256]{1,0:T(8,128)(2,1)S(1)}, u32[]{:S(2)}, u32[]{:S(2)}) collective-permute-start(bf16[256,256]{1,0:T(8,128)(2,1)S(1)} %collective-permute-done.13.refs_2_), channel_id=1, source_target_pairs={{0,1},{1,0},{2,3},{3,2},{4,5},{5,4},{6,7},{7,6},{8,9},{9,8},{10,11... | collective-permute-start | bytes 393224 | tf_op jit(solution)/shard_map/ppermute | solution.py:436
  63.7 1.3 %collective-permute-start.18 = (bf16[256,256]{1,0:T(8,128)(2,1)S(1)}, bf16[256,256]{1,0:T(8,128)(2,1)S(1)}, u32[]{:S(2)}, u32[]{:S(2)}) collective-permute-start(bf16[256,256]{1,0:T(8,128)(2,1)S(1)} %collective-permute-done.14.refs_3_), channel_id=1, source_target_pairs={{0,1},{1,0},{2,3},{3,2},{4,5},{5,4},{6,7},{7,6},{8,9},{9,8},{10,11... | collective-permute-start | bytes 393224 | tf_op jit(solution)/shard_map/ppermute | solution.py:436
  (2 other events, 13.7 us)

commit v12 on v11

--- a/solution.py
+++ b/solution.py
@@ -323,15 +323,23 @@
         out[...] = ready[jnp.bitwise_xor(corner, k)]
 
 
+def join_kernel(*refs):
+    parts, out = refs[:-1], refs[-1]
+    width = parts[0].shape[1]
+    for i, part in enumerate(parts):
+        out[:, i * width : (i + 1) * width] = part[...]
+
+
 def project_kernel(ranks, *refs):
     parts, (weight_ref, out_ref, whole, made, sent) = refs[:-5], refs[-5:]
     mine, corner = lax.axis_index("tp"), corner_of()
-    width = parts[0].shape[1]
-    for r in range(ranks):
+    width = parts[0].shape[1] // SQUAD
+    for r, part in enumerate(parts):
         source = lax.rem(mine + ranks - r, ranks)
         for k in range(SQUAD):
             begin = (source * SQUAD + jnp.bitwise_xor(corner, k)) * width
-            whole[:, pl.ds(pl.multiple_of(begin, width), width)] = parts[r * SQUAD + k][...]
+            cols = pl.ds(pl.multiple_of(begin, width), width)
+            whole[:, cols] = part[:, k * width : (k + 1) * width]
     block = 2 * LANES
     copies = []
     for c in range(out_ref.shape[1] // block):
@@ -437,7 +445,13 @@
 
     pieces = [swap(done[k], k) for k in range(1, SQUAD)]
     hyena_out, *pieces = lax.optimization_barrier((hyena_out, done[0], *pieces))
-    pieces += [turn(piece, r) for r in range(1, ranks) for piece in pieces]
+    (joined,) = kernel_call(
+        join_kernel,
+        pieces,
+        [jax.ShapeDtypeStruct((rows, feat), bf16)],
+        "join",
+    )
+    pieces = [joined] + [turn(joined, r) for r in range(1, ranks)]
     (attn_out,) = kernel_call(
         functools.partial(project_kernel, ranks),
         (*pieces, out_weight),

time: 68.9 us -> 68.3 us (level)
    ppermute x4 -> x1, starting transfers between devices: 4.44 us -> 3.85 us  [turn(): lax.ppermute(value, 'tp', [(t, (t + r) % ranks) for t in range(ranks)])]
    ppermute x4 -> x1, waiting for transfers between devices: 1.27 us -> 1.54 us  [turn(): lax.ppermute(value, 'tp', [(t, (t + r) % ranks) for t in range(ranks)])]
    pallas_call x5 -> x6, Pallas kernels: 16.6 us -> 16.5 us  [kernel_call(): pl.pallas_call(kernel, in_specs=[VMEM] * len(args), out_specs=[out] * len...]
  transfers between devices with their start and end apart: 19 -> 16, of which waited for: 9 -> 6; matrix products, arithmetic and copies ran while one was open for 2% -> 2% of each run, Pallas kernels for 19% -> 19%
where the time goes in v12:
time: 68.3 us; the launch traced here: 67.9 us
  starting transfers between devices  32.7 us (48%)
  Pallas kernels  18.2 us (27%)
  waiting for transfers between devices  14.7 us (22%)
  other arithmetic  1.24 us (2%)
  between operations  0.97 us (1%)
    pallas_call x6, Pallas kernels, kernel_call(): pl.pallas_call(kernel, in_specs=[VMEM] * len(args), out_specs=[out] * len...  16.5 us
    ppermute x4, starting transfers between devices, climb(): lax.ppermute(value, 'ctx', [(i, i + SQUAD) for i in range(first, count -...  11.5 us
    ppermute x4, waiting for transfers between devices, climb(): lax.ppermute(value, 'ctx', [(i, i + SQUAD) for i in range(first, count -...  8.01 us
    ppermute x6, starting transfers between devices, swap(): return lax.ppermute(value, 'ctx', [(i, i ^ mask) for i in range(count)])  6.46 us
    ppermute x2, starting transfers between devices, descend(): lax.ppermute(value, 'ctx', [(i, i - SQUAD) for i in range(2 * SQUAD, coun...  4 us
    ppermute x1, starting transfers between devices, turn(): lax.ppermute(value, 'tp', [(t, (t + r) % ranks) for t in range(ranks)])  3.85 us
    ppermute x1, starting transfers between devices, local(): lax.ppermute(ring, 'ctx', [(i, i + SQUAD) for i in range(0, count - SQUAD...  3.37 us
    ppermute x1, waiting for transfers between devices, local(): lax.ppermute(tail[:, half:], 'ctx', [(i, i - i % SQUAD + (i + 1) % SQUAD)...  3.2 us
  transfers between devices with their start and end apart: 16, of which 6 were waited for; matrix products, arithmetic and copies ran while one was open for 2% of the time, Pallas kernels for 19%

profile of v12, /device:TPU:17, one launch (start us, length us, event | category | flops | bytes accessed | tf_op | source)
XLA Modules:
  0.0 67.9 jit_solution(5191228177246682222)
XLA Ops:
  0.6 1.7 %deal.1 = (bf16[272,256]{1,0:T(8,128)(2,1)S(1)}, bf16[528,256]{1,0:T(8,128)(2,1)S(1)}, bf16[784,256]{1,0:T(8,128)(2,1)S(1)}, bf16[784,256]{1,0:T(8,128)(2,1)S(1)}, bf16[784,256]{1,0:T(8,128)(2,1)S(1)}) custom-call(bf16[256,1024]{1,0:T(8,128)(2,1)} %q_ref.2, bf16[256,1024]{1,0:T(8,128)(2,1)} %k_ref.2, bf16[256,1024]{1,0:T(8,128)(2,1)} %v_ref.2, s32[2,128]{1,0:T(2,128)} %bitcast.3), custom_call_target="tpu_custom_call" | custom-call | bytes 3145728 | tf_op jit(solution)/shard_map/deal/pallas_call | solution.py:160
  2.3 1.3 %collective-permute-start.1 = (bf16[784,256]{1,0:T(8,128)(2,1)S(1)}, bf16[784,256]{1,0:T(8,128)(2,1)S(1)}, u32[]{:S(2)}, u32[]{:S(2)}) collective-permute-start(bf16[784,256]{1,0:T(8,128)(2,1)S(1)} %get-tuple-element.32), channel_id=1, source_target_pairs={{0,2},{2,0},{4,6},{6,4},{8,10},{10,8},{12,14},{14,12},{16,18},{18,... | collective-permute-start | bytes 1204232 | tf_op jit(solution)/shard_map/ppermute | solution.py:369
  3.6 1.2 %collective-permute-start.5 = (bf16[784,256]{1,0:T(8,128)(2,1)S(1)}, bf16[784,256]{1,0:T(8,128)(2,1)S(1)}, u32[]{:S(2)}, u32[]{:S(2)}) collective-permute-start(bf16[784,256]{1,0:T(8,128)(2,1)S(1)} %get-tuple-element.41), channel_id=1, source_target_pairs={{0,4},{2,6},{4,0},{6,2},{8,12},{10,14},{12,8},{14,10},{16,20},{18,... | collective-permute-start | bytes 1204232 | tf_op jit(solution)/shard_map/ppermute | solution.py:369
  4.8 3.2 %collective-permute-start.6 = (bf16[528,256]{1,0:T(8,128)(2,1)S(1)}, bf16[528,256]{1,0:T(8,128)(2,1)S(1)}, u32[]{:S(2)}, u32[]{:S(2)}) collective-permute-start(bf16[528,256]{1,0:T(8,128)(2,1)S(1)} %get-tuple-element.39.refs_1_), channel_id=1, source_target_pairs={{0,8},{2,10},{4,12},{6,14},{8,16},{10,18},{12,20},{14,22},{16,24},... | collective-permute-start | bytes 811016 | tf_op jit(solution)/shard_map/ppermute | solution.py:372
  9.2 4.2 %collective-permute-done.6.refs_5_.refs_2_ = bf16[528,256]{1,0:T(8,128)(2,1)S(1)} collective-permute-done((bf16[528,256]{1,0:T(8,128)(2,1)S(1)}, bf16[528,256]{1,0:T(8,128)(2,1)S(1)}, u32[]{:S(2)}, u32[]{:S(2)}) %collective-permute-start.6) | collective-permute-done | bytes 270368 | tf_op jit(solution)/shard_map/ppermute | solution.py:372
  13.6 1.3 %collective-permute-start.2 = (bf16[784,256]{1,0:T(8,128)(2,1)S(1)}, bf16[784,256]{1,0:T(8,128)(2,1)S(1)}, u32[]{:S(2)}, u32[]{:S(2)}) collective-permute-start(bf16[784,256]{1,0:T(8,128)(2,1)S(1)} %get-tuple-element.33), channel_id=1, source_target_pairs={{0,6},{2,4},{4,2},{6,0},{8,14},{10,12},{12,10},{14,8},{16,22},{18,... | collective-permute-start | bytes 1204232 | tf_op jit(solution)/shard_map/ppermute | solution.py:369
  14.9 3.2 %collective-permute-start.7 = (bf16[1056,256]{1,0:T(8,128)(2,1)S(1)}, bf16[1056,256]{1,0:T(8,128)(2,1)S(1)}, u32[]{:S(2)}, u32[]{:S(2)}) collective-permute-start(bf16[1056,256]{1,0:T(8,128)(2,1)S(1)} %pad_maximum_fusion), channel_id=1, source_target_pairs={{0,8},{2,10},{4,12},{6,14},{8,16},{10,18},{12,20},{14,22},{16,24},... | collective-permute-start | bytes 1622024 | tf_op jit(solution)/shard_map/ppermute | solution.py:372
  18.1 2.1 %collective-permute-start.9 = (bf16[816,256]{1,0:T(8,128)(2,1)S(1)}, bf16[816,256]{1,0:T(8,128)(2,1)S(1)}, u32[]{:S(2)}, u32[]{:S(2)}) collective-permute-start(bf16[816,256]{1,0:T(8,128)(2,1)S(1)} %pad_maximum_fusion.1), channel_id=1, source_target_pairs={{16,8},{18,10},{20,12},{22,14},{24,16},{26,18},{28,20},{30,22},{17... | collective-permute-start | bytes 1253384 | tf_op jit(solution)/shard_map/ppermute | solution.py:375
  20.2 1.3 %collective-permute-start.3 = (bf16[128,1024]{1,0:T(8,128)(2,1)S(1)}, bf16[128,1024]{1,0:T(8,128)(2,1)S(1)}, u32[]{:S(2)}, u32[]{:S(2)}) collective-permute-start(bf16[128,1024]{1,0:T(8,128)(2,1)S(1)} %get-tuple-element.58), channel_id=1, source_target_pairs={{0,2},{2,4},{4,6},{6,0},{8,10},{10,12},{12,14},{14,8},{16,18},{18,... | collective-permute-start | bytes 786440 | tf_op jit(solution)/shard_map/ppermute | solution.py:395
  21.5 1.6 %collective-permute-done.2.refs_4_ = bf16[784,256]{1,0:T(8,128)(2,1)S(1)} collective-permute-done((bf16[784,256]{1,0:T(8,128)(2,1)S(1)}, bf16[784,256]{1,0:T(8,128)(2,1)S(1)}, u32[]{:S(2)}, u32[]{:S(2)}) %collective-permute-start.2) | collective-permute-done | bytes 401440 | tf_op jit(solution)/shard_map/ppermute | solution.py:369
  23.2 3.2 %collective-permute-start.8 = (bf16[528,256]{1,0:T(8,128)(2,1)S(1)}, bf16[528,256]{1,0:T(8,128)(2,1)S(1)}, u32[]{:S(2)}, u32[]{:S(2)}) collective-permute-start(bf16[528,256]{1,0:T(8,128)(2,1)S(1)} %slice.42), channel_id=1, source_target_pairs={{0,8},{2,10},{4,12},{6,14},{8,16},{10,18},{12,20},{14,22},{16,24},... | collective-permute-start | bytes 811016 | tf_op jit(solution)/shard_map/ppermute | solution.py:372
  26.4 3.2 %collective-permute-done.3.ring_rim = bf16[128,1024]{1,0:T(8,128)(2,1)S(1)} collective-permute-done((bf16[128,1024]{1,0:T(8,128)(2,1)S(1)}, bf16[128,1024]{1,0:T(8,128)(2,1)S(1)}, u32[]{:S(2)}, u32[]{:S(2)}) %collective-permute-start.3) | collective-permute-done | bytes 262176 | tf_op jit(solution)/shard_map/ppermute | solution.py:395
  29.6 1.9 %collective-permute-start.10 = (bf16[272,256]{1,0:T(8,128)(2,1)S(1)}, bf16[272,256]{1,0:T(8,128)(2,1)S(1)}, u32[]{:S(2)}, u32[]{:S(2)}) collective-permute-start(bf16[272,256]{1,0:T(8,128)(2,1)S(1)} %slice.39), channel_id=1, source_target_pairs={{16,8},{18,10},{20,12},{22,14},{24,16},{26,18},{28,20},{30,22},{17... | collective-permute-start | bytes 417800 | tf_op jit(solution)/shard_map/ppermute | solution.py:375
  31.5 2.2 %collective-permute-start = (bf16[128,1024]{1,0:T(8,128)(2,1)S(1)}, bf16[128,1024]{1,0:T(8,128)(2,1)S(1)}, u32[]{:S(2)}, u32[]{:S(2)}) collective-permute-start(bf16[128,1024]{1,0:T(8,128)(2,1)S(1)} %get-tuple-element.59), channel_id=1, source_target_pairs={{0,2},{2,4},{4,6},{6,8},{8,10},{10,12},{12,14},{14,16},{16,18},{18... | collective-permute-start | bytes 786440 | tf_op jit(solution)/shard_map/ppermute | solution.py:401
  33.8 3.4 %collective-permute-start.4 = (bf16[128,1024]{1,0:T(8,128)(2,1)S(1)}, bf16[128,1024]{1,0:T(8,128)(2,1)S(1)}, u32[]{:S(2)}, u32[]{:S(2)}) collective-permute-start(bf16[128,1024]{1,0:T(8,128)(2,1)S(1)} %collective-permute-done.3.ring_rim), channel_id=1, source_target_pairs={{0,8},{8,16},{16,24},{1,9},{9,17},{17,25}} | collective-permute-start | bytes 786440 | tf_op jit(solution)/shard_map/ppermute | solution.py:403
  37.2 1.8 %far.1 = bf16[272,768]{1,0:T(8,128)(2,1)S(1)} custom-call(bf16[816,256]{1,0:T(8,128)(2,1)S(1)} %collective-permute-done.9.refs_0_, bf16[272,256]{1,0:T(8,128)(2,1)S(1)} %collective-permute-done.10.refs_1_, bf16[528,256]{1,0:T(8,128)(2,1)S(1)} %collective-permute-done.6.refs_5_.refs_2_, bf16[1056,256]{1,0:T(8,128)(2,1)S(1)} %collective-permute-done.7.refs_6_.refs_3_, ...), custom_call_target="tpu_custom_call" | custom-call | flops 402653184 | bytes 2056192 | tf_op jit(solution)/shard_map/far/pallas_call | solution.py:26
  38.9 1.9 %collective-permute-start.11 = (bf16[272,768]{1,0:T(8,128)(2,1)S(1)}, bf16[272,768]{1,0:T(8,128)(2,1)S(1)}, u32[]{:S(2)}, u32[]{:S(2)}) collective-permute-start(bf16[272,768]{1,0:T(8,128)(2,1)S(1)} %far.1), channel_id=1, source_target_pairs={{8,16},{10,18},{12,20},{14,22},{16,24},{18,26},{20,28},{22,30},{9,... | collective-permute-start | bytes 1253384 | tf_op jit(solution)/shard_map/ppermute | solution.py:372
  41.2 6.0 %main.1.main_ref = f32[272,1024]{1,0:T(8,128)S(1)} custom-call(bf16[272,256]{1,0:T(8,128)(2,1)S(1)} %get-tuple-element.38.refs_0_, bf16[528,256]{1,0:T(8,128)(2,1)S(1)} %get-tuple-element.39.refs_1_, bf16[784,256]{1,0:T(8,128)(2,1)S(1)} %collective-permute-done.1.refs_2_, bf16[784,256]{1,0:T(8,128)(2,1)S(1)} %collective-permute-done.5.refs_3_, ...), custom_call_target="tpu_custom_call" | custom-call | flops 1744830464 | bytes 3809280 | tf_op jit(solution)/shard_map/main/pallas_call | solution.py:26
  47.3 3.8 %collective-permute-done.11.far_ref = bf16[272,768]{1,0:T(8,128)(2,1)S(1)} collective-permute-done((bf16[272,768]{1,0:T(8,128)(2,1)S(1)}, bf16[272,768]{1,0:T(8,128)(2,1)S(1)}, u32[]{:S(2)}, u32[]{:S(2)}) %collective-permute-start.11) | collective-permute-done | bytes 417824 | tf_op jit(solution)/shard_map/ppermute | solution.py:372
  51.6 2.5 %collective-permute-start.14 = (bf16[256,256]{1,0:T(8,128)(2,1)S(1)}, bf16[256,256]{1,0:T(8,128)(2,1)S(1)}, u32[]{:S(2)}, u32[]{:S(2)}) collective-permute-start(bf16[256,256]{1,0:T(8,128)(2,1)S(1)} %get-tuple-element.52), channel_id=1, source_target_pairs={{0,6},{2,4},{4,2},{6,0},{8,14},{10,12},{12,10},{14,8},{16,22},{18,... | collective-permute-start | bytes 393224 | tf_op jit(solution)/shard_map/ppermute | solution.py:369
  54.1 5.0 %hyena.1 = bf16[256,2048]{1,0:T(8,128)(2,1)} custom-call(bf16[256,2048]{1,0:T(8,128)(2,1)S(1)} %copy-done.2, bf16[256,2048]{1,0:T(8,128)(2,1)S(1)} %copy-done, bf16[256,2048]{1,0:T(8,128)(2,1)S(1)} %copy-done.1, bf16[128,1024]{1,0:T(8,128)(2,1)S(1)} %collective-permute-done.near_rim, bf16[128,1024]{1,0:T(8,128)(2,1)S(1)} %collective-permute-done.3.ring_rim, ...), custom_call_target="tpu_custom_call" | custom-call | flops 4294967296 | bytes 5017600 | tf_op jit(solution)/shard_map/hyena/pallas_call | solution.py:26
  59.2 3.8 %collective-permute-start.15 = (bf16[256,1024]{1,0:T(8,128)(2,1)S(1)}, bf16[256,1024]{1,0:T(8,128)(2,1)S(1)}, u32[]{:S(2)}, u32[]{:S(2)}) collective-permute-start(bf16[256,1024]{1,0:T(8,128)(2,1)S(1)} %join.1.refs_0_), channel_id=1, source_target_pairs={{0,1},{1,0},{2,3},{3,2},{4,5},{5,4},{6,7},{7,6},{8,9},{9,8},{10,11... | collective-permute-start | bytes 1572872 | tf_op jit(solution)/shard_map/ppermute | solution.py:444
  63.1 1.5 %collective-permute-done.15.refs_1_ = bf16[256,1024]{1,0:T(8,128)(2,1)S(1)} collective-permute-done((bf16[256,1024]{1,0:T(8,128)(2,1)S(1)}, bf16[256,1024]{1,0:T(8,128)(2,1)S(1)}, u32[]{:S(2)}, u32[]{:S(2)}) %collective-permute-start.15) | collective-permute-done | bytes 524320 | tf_op jit(solution)/shard_map/ppermute | solution.py:444
  64.6 3.3 %project.1 = bf16[256,2048]{1,0:T(8,128)(2,1)} custom-call(bf16[256,1024]{1,0:T(8,128)(2,1)S(1)} %join.1.refs_0_, bf16[256,1024]{1,0:T(8,128)(2,1)S(1)} %collective-permute-done.15.refs_1_, bf16[2048,2048]{1,0:T(8,128)(2,1)S(1)} %bitcast.2), custom_call_target="tpu_custom_call" | custom-call | flops 2147483648 | bytes 10485760 | tf_op jit(solution)/shard_map/project/pallas_call | solution.py:26
  (41 shorter events, 2.3 us)
Async XLA Ops:
  0.6 7.4 %copy-start = (bf16[256,2048]{1,0:T(8,128)(2,1)S(1)}, bf16[256,2048]{1,0:T(8,128)(2,1)}, u32[]{:S(2)}) copy-start(bf16[256,2048]{1,0:T(8,128)(2,1)} %k_ref.3) | copy-start | bytes 3145732
  2.3 11.2 %collective-permute-start.1 = (bf16[784,256]{1,0:T(8,128)(2,1)S(1)}, bf16[784,256]{1,0:T(8,128)(2,1)S(1)}, u32[]{:S(2)}, u32[]{:S(2)}) collective-permute-start(bf16[784,256]{1,0:T(8,128)(2,1)S(1)} %get-tuple-element.32), channel_id=1, source_target_pairs={{0,2},{2,0},{4,6},{6,4},{8,10},{10,8},{12,14},{14,12},{16,18},{18,... | collective-permute-start | bytes 1204232 | tf_op jit(solution)/shard_map/ppermute | solution.py:369
  3.6 9.9 %collective-permute-start.5 = (bf16[784,256]{1,0:T(8,128)(2,1)S(1)}, bf16[784,256]{1,0:T(8,128)(2,1)S(1)}, u32[]{:S(2)}, u32[]{:S(2)}) collective-permute-start(bf16[784,256]{1,0:T(8,128)(2,1)S(1)} %get-tuple-element.41), channel_id=1, source_target_pairs={{0,4},{2,6},{4,0},{6,2},{8,12},{10,14},{12,8},{14,10},{16,20},{18,... | collective-permute-start | bytes 1204232 | tf_op jit(solution)/shard_map/ppermute | solution.py:369
  4.8 8.6 %collective-permute-start.6 = (bf16[528,256]{1,0:T(8,128)(2,1)S(1)}, bf16[528,256]{1,0:T(8,128)(2,1)S(1)}, u32[]{:S(2)}, u32[]{:S(2)}) collective-permute-start(bf16[528,256]{1,0:T(8,128)(2,1)S(1)} %get-tuple-element.39.refs_1_), channel_id=1, source_target_pairs={{0,8},{2,10},{4,12},{6,14},{8,16},{10,18},{12,20},{14,22},{16,24},... | collective-permute-start | bytes 811016 | tf_op jit(solution)/shard_map/ppermute | solution.py:372
  13.6 9.6 %collective-permute-start.2 = (bf16[784,256]{1,0:T(8,128)(2,1)S(1)}, bf16[784,256]{1,0:T(8,128)(2,1)S(1)}, u32[]{:S(2)}, u32[]{:S(2)}) collective-permute-start(bf16[784,256]{1,0:T(8,128)(2,1)S(1)} %get-tuple-element.33), channel_id=1, source_target_pairs={{0,6},{2,4},{4,2},{6,0},{8,14},{10,12},{12,10},{14,8},{16,22},{18,... | collective-permute-start | bytes 1204232 | tf_op jit(solution)/shard_map/ppermute | solution.py:369
  14.9 22.3 %collective-permute-start.7 = (bf16[1056,256]{1,0:T(8,128)(2,1)S(1)}, bf16[1056,256]{1,0:T(8,128)(2,1)S(1)}, u32[]{:S(2)}, u32[]{:S(2)}) collective-permute-start(bf16[1056,256]{1,0:T(8,128)(2,1)S(1)} %pad_maximum_fusion), channel_id=1, source_target_pairs={{0,8},{2,10},{4,12},{6,14},{8,16},{10,18},{12,20},{14,22},{16,24},... | collective-permute-start | bytes 1622024 | tf_op jit(solution)/shard_map/ppermute | solution.py:372
  18.1 15.7 %collective-permute-start.9 = (bf16[816,256]{1,0:T(8,128)(2,1)S(1)}, bf16[816,256]{1,0:T(8,128)(2,1)S(1)}, u32[]{:S(2)}, u32[]{:S(2)}) collective-permute-start(bf16[816,256]{1,0:T(8,128)(2,1)S(1)} %pad_maximum_fusion.1), channel_id=1, source_target_pairs={{16,8},{18,10},{20,12},{22,14},{24,16},{26,18},{28,20},{30,22},{17... | collective-permute-start | bytes 1253384 | tf_op jit(solution)/shard_map/ppermute | solution.py:375
  20.2 9.3 %collective-permute-start.3 = (bf16[128,1024]{1,0:T(8,128)(2,1)S(1)}, bf16[128,1024]{1,0:T(8,128)(2,1)S(1)}, u32[]{:S(2)}, u32[]{:S(2)}) collective-permute-start(bf16[128,1024]{1,0:T(8,128)(2,1)S(1)} %get-tuple-element.58), channel_id=1, source_target_pairs={{0,2},{2,4},{4,6},{6,0},{8,10},{10,12},{12,14},{14,8},{16,18},{18,... | collective-permute-start | bytes 786440 | tf_op jit(solution)/shard_map/ppermute | solution.py:395
  23.2 14.0 %collective-permute-start.8 = (bf16[528,256]{1,0:T(8,128)(2,1)S(1)}, bf16[528,256]{1,0:T(8,128)(2,1)S(1)}, u32[]{:S(2)}, u32[]{:S(2)}) collective-permute-start(bf16[528,256]{1,0:T(8,128)(2,1)S(1)} %slice.42), channel_id=1, source_target_pairs={{0,8},{2,10},{4,12},{6,14},{8,16},{10,18},{12,20},{14,22},{16,24},... | collective-permute-start | bytes 811016 | tf_op jit(solution)/shard_map/ppermute | solution.py:372
  29.6 11.3 %copy-start.4 = (bf16[2048]{0:T(1024)(128)(2,1)S(1)}, bf16[2048]{0:T(1024)(128)(2,1)}, u32[]{:S(2)}) copy-start(bf16[2048]{0:T(1024)(128)(2,1)} %param.14) | copy-start | bytes 12292
  29.6 7.6 %collective-permute-start.10 = (bf16[272,256]{1,0:T(8,128)(2,1)S(1)}, bf16[272,256]{1,0:T(8,128)(2,1)S(1)}, u32[]{:S(2)}, u32[]{:S(2)}) collective-permute-start(bf16[272,256]{1,0:T(8,128)(2,1)S(1)} %slice.39), channel_id=1, source_target_pairs={{16,8},{18,10},{20,12},{22,14},{24,16},{26,18},{28,20},{30,22},{17... | collective-permute-start | bytes 417800 | tf_op jit(solution)/shard_map/ppermute | solution.py:375
  31.5 9.4 %collective-permute-start = (bf16[128,1024]{1,0:T(8,128)(2,1)S(1)}, bf16[128,1024]{1,0:T(8,128)(2,1)S(1)}, u32[]{:S(2)}, u32[]{:S(2)}) collective-permute-start(bf16[128,1024]{1,0:T(8,128)(2,1)S(1)} %get-tuple-element.59), channel_id=1, source_target_pairs={{0,2},{2,4},{4,6},{6,8},{8,10},{10,12},{12,14},{14,16},{16,18},{18... | collective-permute-start | bytes 786440 | tf_op jit(solution)/shard_map/ppermute | solution.py:401
  33.8 7.4 %collective-permute-start.4 = (bf16[128,1024]{1,0:T(8,128)(2,1)S(1)}, bf16[128,1024]{1,0:T(8,128)(2,1)S(1)}, u32[]{:S(2)}, u32[]{:S(2)}) collective-permute-start(bf16[128,1024]{1,0:T(8,128)(2,1)S(1)} %collective-permute-done.3.ring_rim), channel_id=1, source_target_pairs={{0,8},{8,16},{16,24},{1,9},{9,17},{17,25}} | collective-permute-start | bytes 786440 | tf_op jit(solution)/shard_map/ppermute | solution.py:403
  38.9 12.1 %collective-permute-start.11 = (bf16[272,768]{1,0:T(8,128)(2,1)S(1)}, bf16[272,768]{1,0:T(8,128)(2,1)S(1)}, u32[]{:S(2)}, u32[]{:S(2)}) collective-permute-start(bf16[272,768]{1,0:T(8,128)(2,1)S(1)} %far.1), channel_id=1, source_target_pairs={{8,16},{10,18},{12,20},{14,22},{16,24},{18,26},{20,28},{22,30},{9,... | collective-permute-start | bytes 1253384 | tf_op jit(solution)/shard_map/ppermute | solution.py:372
  41.2 12.9 %copy-start.2 = (bf16[256,2048]{1,0:T(8,128)(2,1)S(1)}, bf16[256,2048]{1,0:T(8,128)(2,1)}, u32[]{:S(2)}) copy-start(bf16[256,2048]{1,0:T(8,128)(2,1)} %q_ref.3) | copy-start | bytes 3145732
  47.2 6.9 %copy-start.1 = (bf16[256,2048]{1,0:T(8,128)(2,1)S(1)}, bf16[256,2048]{1,0:T(8,128)(2,1)}, u32[]{:S(2)}) copy-start(bf16[256,2048]{1,0:T(8,128)(2,1)} %v_ref.3) | copy-start | bytes 3145732
  47.2 6.9 %copy-start.3 = (bf16[128,128]{1,0:T(8,128)(2,1)S(1)}, bf16[128,128]{1,0:T(8,128)(2,1)}, u32[]{:S(2)}) copy-start(bf16[128,128]{1,0:T(8,128)(2,1)} %taps_ref.1) | copy-start | bytes 98308
  51.4 7.8 %collective-permute-start.12 = (bf16[256,256]{1,0:T(8,128)(2,1)S(1)}, bf16[256,256]{1,0:T(8,128)(2,1)S(1)}, u32[]{:S(2)}, u32[]{:S(2)}) collective-permute-start(bf16[256,256]{1,0:T(8,128)(2,1)S(1)} %get-tuple-element.50), channel_id=1, source_target_pairs={{0,2},{2,0},{4,6},{6,4},{8,10},{10,8},{12,14},{14,12},{16,18},{18,... | collective-permute-start | bytes 393224 | tf_op jit(solution)/shard_map/ppermute | solution.py:369
  51.5 7.7 %collective-permute-start.13 = (bf16[256,256]{1,0:T(8,128)(2,1)S(1)}, bf16[256,256]{1,0:T(8,128)(2,1)S(1)}, u32[]{:S(2)}, u32[]{:S(2)}) collective-permute-start(bf16[256,256]{1,0:T(8,128)(2,1)S(1)} %get-tuple-element.51), channel_id=1, source_target_pairs={{0,4},{2,6},{4,0},{6,2},{8,12},{10,14},{12,8},{14,10},{16,20},{18,... | collective-permute-start | bytes 393224 | tf_op jit(solution)/shard_map/ppermute | solution.py:369
  51.5 13.1 %slice-start = ((s8[8388608]{0:T(1024)(128)(4,1)}), s8[4194304]{0:T(1024)(128)(4,1)S(1)}, s32[]{:S(2)}) async-start(s8[8388608]{0:T(1024)(128)(4,1)} %bitcast.1), calls=%async_computation | async-start | bytes 8388608
  51.5 13.1 %slice-start.1 = ((s8[8388608]{0:T(1024)(128)(4,1)}), s8[4194304]{0:T(1024)(128)(4,1)S(1)}, s32[]{:S(2)}) async-start(s8[8388608]{0:T(1024)(128)(4,1)} %bitcast.1), calls=%async_computation.1 | async-start | bytes 8388608
  51.6 7.6 %collective-permute-start.14 = (bf16[256,256]{1,0:T(8,128)(2,1)S(1)}, bf16[256,256]{1,0:T(8,128)(2,1)S(1)}, u32[]{:S(2)}, u32[]{:S(2)}) collective-permute-start(bf16[256,256]{1,0:T(8,128)(2,1)S(1)} %get-tuple-element.52), channel_id=1, source_target_pairs={{0,6},{2,4},{4,2},{6,0},{8,14},{10,12},{12,10},{14,8},{16,22},{18,... | collective-permute-start | bytes 393224 | tf_op jit(solution)/shard_map/ppermute | solution.py:369
  59.2 5.4 %collective-permute-start.15 = (bf16[256,1024]{1,0:T(8,128)(2,1)S(1)}, bf16[256,1024]{1,0:T(8,128)(2,1)S(1)}, u32[]{:S(2)}, u32[]{:S(2)}) collective-permute-start(bf16[256,1024]{1,0:T(8,128)(2,1)S(1)} %join.1.refs_0_), channel_id=1, source_target_pairs={{0,1},{1,0},{2,3},{3,2},{4,5},{5,4},{6,7},{7,6},{8,9},{9,8},{10,11... | collective-permute-start | bytes 1572872 | tf_op jit(solution)/shard_map/ppermute | solution.py:444

commit v13 on v12

--- a/solution.py
+++ b/solution.py
@@ -62,7 +62,7 @@
         cols = pl.ds(begin, LANES)
         return pltpu.make_async_copy(made.at[:, cols], out_ref.at[:, cols], sent.at[tile])
 
-    @pl.loop(0, chans // LANES, unroll=2)
+    @pl.loop(0, chans // LANES, unroll=4)
     def _(tile):
         cols = pl.ds(pl.multiple_of(tile * LANES, LANES), LANES)
         rings = taps[pl.ds(pl.multiple_of(tile * per_tile, per_tile), per_tile), :]
@@ -341,15 +341,19 @@
             cols = pl.ds(pl.multiple_of(begin, width), width)
             whole[:, cols] = part[:, k * width : (k + 1) * width]
     block = 2 * LANES
+    spans = [slice(c, c + block) for c in range(0, out_ref.shape[1], block)]
+
+    def product(cols):
+        return jnp.dot(whole[...], weight_ref[:, cols], preferred_element_type=jnp.float32)
+
     copies = []
-    for c in range(out_ref.shape[1] // block):
-        cols = slice(c * block, (c + 1) * block)
-        made[:, cols] = jnp.dot(
-            whole[...], weight_ref[:, cols], preferred_element_type=jnp.float32
-        ).astype(made.dtype)
-        span = pl.ds(c * block, block)
+    for (cols,), total in ahead([(x,) for x in spans], product):
+        made[:, cols] = total.astype(made.dtype)
+        span = pl.ds(cols.start, block)
         copies.append(
-            pltpu.make_async_copy(made.at[:, span], out_ref.at[:, span], sent.at[c])
+            pltpu.make_async_copy(
+                made.at[:, span], out_ref.at[:, span], sent.at[cols.start // block]
+            )
         )
         copies[-1].start()
     for copy in copies:

time: 68.3 us -> 67.8 us (level)
  Pallas kernels: 18.2 us -> 17.5 us
  transfers between devices with their start and end apart: 16 -> 16, of which waited for: 6 -> 6; matrix products, arithmetic and copies ran while one was open for 2% -> 2% of each run, Pallas kernels for 19% -> 18%
where the time goes in v13:
time: 67.8 us; the launch traced here: 67.4 us
  starting transfers between devices  32.7 us (48%)
  Pallas kernels  17.5 us (26%)
  waiting for transfers between devices  14.7 us (22%)
  other arithmetic  1.24 us (2%)
  between operations  1.13 us (2%)
    pallas_call x6, Pallas kernels, kernel_call(): pl.pallas_call(kernel, in_specs=[VMEM] * len(args), out_specs=[out] * len...  15.9 us
    ppermute x4, starting transfers between devices, climb(): lax.ppermute(value, 'ctx', [(i, i + SQUAD) for i in range(first, count -...  11.5 us
    ppermute x4, waiting for transfers between devices, climb(): lax.ppermute(value, 'ctx', [(i, i + SQUAD) for i in range(first, count -...  8.01 us
    ppermute x6, starting transfers between devices, swap(): return lax.ppermute(value, 'ctx', [(i, i ^ mask) for i in range(count)])  6.46 us
    ppermute x2, starting transfers between devices, descend(): lax.ppermute(value, 'ctx', [(i, i - SQUAD) for i in range(2 * SQUAD, coun...  4 us
    ppermute x1, starting transfers between devices, turn(): lax.ppermute(value, 'tp', [(t, (t + r) % ranks) for t in range(ranks)])  3.84 us
    ppermute x1, starting transfers between devices, local(): lax.ppermute(ring, 'ctx', [(i, i + SQUAD) for i in range(0, count - SQUAD...  3.37 us
    ppermute x1, waiting for transfers between devices, local(): lax.ppermute(tail[:, half:], 'ctx', [(i, i - i % SQUAD + (i + 1) % SQUAD)...  3.2 us
  transfers between devices with their start and end apart: 16, of which 6 were waited for; matrix products, arithmetic and copies ran while one was open for 2% of the time, Pallas kernels for 18%

profile of v13, /device:TPU:17, one launch (start us, length us, event | category | flops | bytes accessed | tf_op | source)
XLA Modules:
  0.0 67.4 jit_solution(12143158158964589471)
XLA Ops:
  0.6 1.7 %deal.1 = (bf16[272,256]{1,0:T(8,128)(2,1)S(1)}, bf16[528,256]{1,0:T(8,128)(2,1)S(1)}, bf16[784,256]{1,0:T(8,128)(2,1)S(1)}, bf16[784,256]{1,0:T(8,128)(2,1)S(1)}, bf16[784,256]{1,0:T(8,128)(2,1)S(1)}) custom-call(bf16[256,1024]{1,0:T(8,128)(2,1)} %q_ref.2, bf16[256,1024]{1,0:T(8,128)(2,1)} %k_ref.2, bf16[256,1024]{1,0:T(8,128)(2,1)} %v_ref.2, s32[2,128]{1,0:T(2,128)} %bitcast.3), custom_call_target="tpu_custom_call" | custom-call | bytes 3145728 | tf_op jit(solution)/shard_map/deal/pallas_call | solution.py:160
  2.3 1.3 %collective-permute-start.1 = (bf16[784,256]{1,0:T(8,128)(2,1)S(1)}, bf16[784,256]{1,0:T(8,128)(2,1)S(1)}, u32[]{:S(2)}, u32[]{:S(2)}) collective-permute-start(bf16[784,256]{1,0:T(8,128)(2,1)S(1)} %get-tuple-element.32), channel_id=1, source_target_pairs={{0,2},{2,0},{4,6},{6,4},{8,10},{10,8},{12,14},{14,12},{16,18},{18,... | collective-permute-start | bytes 1204232 | tf_op jit(solution)/shard_map/ppermute | solution.py:373
  3.6 1.2 %collective-permute-start.5 = (bf16[784,256]{1,0:T(8,128)(2,1)S(1)}, bf16[784,256]{1,0:T(8,128)(2,1)S(1)}, u32[]{:S(2)}, u32[]{:S(2)}) collective-permute-start(bf16[784,256]{1,0:T(8,128)(2,1)S(1)} %get-tuple-element.41), channel_id=1, source_target_pairs={{0,4},{2,6},{4,0},{6,2},{8,12},{10,14},{12,8},{14,10},{16,20},{18,... | collective-permute-start | bytes 1204232 | tf_op jit(solution)/shard_map/ppermute | solution.py:373
  4.8 3.2 %collective-permute-start.6 = (bf16[528,256]{1,0:T(8,128)(2,1)S(1)}, bf16[528,256]{1,0:T(8,128)(2,1)S(1)}, u32[]{:S(2)}, u32[]{:S(2)}) collective-permute-start(bf16[528,256]{1,0:T(8,128)(2,1)S(1)} %get-tuple-element.39.refs_1_), channel_id=1, source_target_pairs={{0,8},{2,10},{4,12},{6,14},{8,16},{10,18},{12,20},{14,22},{16,24},... | collective-permute-start | bytes 811016 | tf_op jit(solution)/shard_map/ppermute | solution.py:376
  9.2 4.2 %collective-permute-done.6.refs_5_.refs_2_ = bf16[528,256]{1,0:T(8,128)(2,1)S(1)} collective-permute-done((bf16[528,256]{1,0:T(8,128)(2,1)S(1)}, bf16[528,256]{1,0:T(8,128)(2,1)S(1)}, u32[]{:S(2)}, u32[]{:S(2)}) %collective-permute-start.6) | collective-permute-done | bytes 270368 | tf_op jit(solution)/shard_map/ppermute | solution.py:376
  13.6 1.3 %collective-permute-start.2 = (bf16[784,256]{1,0:T(8,128)(2,1)S(1)}, bf16[784,256]{1,0:T(8,128)(2,1)S(1)}, u32[]{:S(2)}, u32[]{:S(2)}) collective-permute-start(bf16[784,256]{1,0:T(8,128)(2,1)S(1)} %get-tuple-element.33), channel_id=1, source_target_pairs={{0,6},{2,4},{4,2},{6,0},{8,14},{10,12},{12,10},{14,8},{16,22},{18,... | collective-permute-start | bytes 1204232 | tf_op jit(solution)/shard_map/ppermute | solution.py:373
  14.9 3.2 %collective-permute-start.7 = (bf16[1056,256]{1,0:T(8,128)(2,1)S(1)}, bf16[1056,256]{1,0:T(8,128)(2,1)S(1)}, u32[]{:S(2)}, u32[]{:S(2)}) collective-permute-start(bf16[1056,256]{1,0:T(8,128)(2,1)S(1)} %pad_maximum_fusion), channel_id=1, source_target_pairs={{0,8},{2,10},{4,12},{6,14},{8,16},{10,18},{12,20},{14,22},{16,24},... | collective-permute-start | bytes 1622024 | tf_op jit(solution)/shard_map/ppermute | solution.py:376
  18.1 2.1 %collective-permute-start.9 = (bf16[816,256]{1,0:T(8,128)(2,1)S(1)}, bf16[816,256]{1,0:T(8,128)(2,1)S(1)}, u32[]{:S(2)}, u32[]{:S(2)}) collective-permute-start(bf16[816,256]{1,0:T(8,128)(2,1)S(1)} %pad_maximum_fusion.1), channel_id=1, source_target_pairs={{16,8},{18,10},{20,12},{22,14},{24,16},{26,18},{28,20},{30,22},{17... | collective-permute-start | bytes 1253384 | tf_op jit(solution)/shard_map/ppermute | solution.py:379
  20.2 1.3 %collective-permute-start.3 = (bf16[128,1024]{1,0:T(8,128)(2,1)S(1)}, bf16[128,1024]{1,0:T(8,128)(2,1)S(1)}, u32[]{:S(2)}, u32[]{:S(2)}) collective-permute-start(bf16[128,1024]{1,0:T(8,128)(2,1)S(1)} %get-tuple-element.58), channel_id=1, source_target_pairs={{0,2},{2,4},{4,6},{6,0},{8,10},{10,12},{12,14},{14,8},{16,18},{18,... | collective-permute-start | bytes 786440 | tf_op jit(solution)/shard_map/ppermute | solution.py:399
  21.5 1.6 %collective-permute-done.2.refs_4_ = bf16[784,256]{1,0:T(8,128)(2,1)S(1)} collective-permute-done((bf16[784,256]{1,0:T(8,128)(2,1)S(1)}, bf16[784,256]{1,0:T(8,128)(2,1)S(1)}, u32[]{:S(2)}, u32[]{:S(2)}) %collective-permute-start.2) | collective-permute-done | bytes 401440 | tf_op jit(solution)/shard_map/ppermute | solution.py:373
  23.2 3.2 %collective-permute-start.8 = (bf16[528,256]{1,0:T(8,128)(2,1)S(1)}, bf16[528,256]{1,0:T(8,128)(2,1)S(1)}, u32[]{:S(2)}, u32[]{:S(2)}) collective-permute-start(bf16[528,256]{1,0:T(8,128)(2,1)S(1)} %slice.42), channel_id=1, source_target_pairs={{0,8},{2,10},{4,12},{6,14},{8,16},{10,18},{12,20},{14,22},{16,24},... | collective-permute-start | bytes 811016 | tf_op jit(solution)/shard_map/ppermute | solution.py:376
  26.4 3.2 %collective-permute-done.3.ring_rim = bf16[128,1024]{1,0:T(8,128)(2,1)S(1)} collective-permute-done((bf16[128,1024]{1,0:T(8,128)(2,1)S(1)}, bf16[128,1024]{1,0:T(8,128)(2,1)S(1)}, u32[]{:S(2)}, u32[]{:S(2)}) %collective-permute-start.3) | collective-permute-done | bytes 262176 | tf_op jit(solution)/shard_map/ppermute | solution.py:399
  29.6 1.9 %collective-permute-start.10 = (bf16[272,256]{1,0:T(8,128)(2,1)S(1)}, bf16[272,256]{1,0:T(8,128)(2,1)S(1)}, u32[]{:S(2)}, u32[]{:S(2)}) collective-permute-start(bf16[272,256]{1,0:T(8,128)(2,1)S(1)} %slice.39), channel_id=1, source_target_pairs={{16,8},{18,10},{20,12},{22,14},{24,16},{26,18},{28,20},{30,22},{17... | collective-permute-start | bytes 417800 | tf_op jit(solution)/shard_map/ppermute | solution.py:379
  31.5 2.2 %collective-permute-start = (bf16[128,1024]{1,0:T(8,128)(2,1)S(1)}, bf16[128,1024]{1,0:T(8,128)(2,1)S(1)}, u32[]{:S(2)}, u32[]{:S(2)}) collective-permute-start(bf16[128,1024]{1,0:T(8,128)(2,1)S(1)} %get-tuple-element.59), channel_id=1, source_target_pairs={{0,2},{2,4},{4,6},{6,8},{8,10},{10,12},{12,14},{14,16},{16,18},{18... | collective-permute-start | bytes 786440 | tf_op jit(solution)/shard_map/ppermute | solution.py:405
  33.8 3.4 %collective-permute-start.4 = (bf16[128,1024]{1,0:T(8,128)(2,1)S(1)}, bf16[128,1024]{1,0:T(8,128)(2,1)S(1)}, u32[]{:S(2)}, u32[]{:S(2)}) collective-permute-start(bf16[128,1024]{1,0:T(8,128)(2,1)S(1)} %collective-permute-done.3.ring_rim), channel_id=1, source_target_pairs={{0,8},{8,16},{16,24},{1,9},{9,17},{17,25}} | collective-permute-start | bytes 786440 | tf_op jit(solution)/shard_map/ppermute | solution.py:407
  37.2 1.8 %far.1 = bf16[272,768]{1,0:T(8,128)(2,1)S(1)} custom-call(bf16[816,256]{1,0:T(8,128)(2,1)S(1)} %collective-permute-done.9.refs_0_, bf16[272,256]{1,0:T(8,128)(2,1)S(1)} %collective-permute-done.10.refs_1_, bf16[528,256]{1,0:T(8,128)(2,1)S(1)} %collective-permute-done.6.refs_5_.refs_2_, bf16[1056,256]{1,0:T(8,128)(2,1)S(1)} %collective-permute-done.7.refs_6_.refs_3_, ...), custom_call_target="tpu_custom_call" | custom-call | flops 402653184 | bytes 2056192 | tf_op jit(solution)/shard_map/far/pallas_call | solution.py:26
  38.9 1.9 %collective-permute-start.11 = (bf16[272,768]{1,0:T(8,128)(2,1)S(1)}, bf16[272,768]{1,0:T(8,128)(2,1)S(1)}, u32[]{:S(2)}, u32[]{:S(2)}) collective-permute-start(bf16[272,768]{1,0:T(8,128)(2,1)S(1)} %far.1), channel_id=1, source_target_pairs={{8,16},{10,18},{12,20},{14,22},{16,24},{18,26},{20,28},{22,30},{9,... | collective-permute-start | bytes 1253384 | tf_op jit(solution)/shard_map/ppermute | solution.py:376
  41.2 6.0 %main.1.main_ref = f32[272,1024]{1,0:T(8,128)S(1)} custom-call(bf16[272,256]{1,0:T(8,128)(2,1)S(1)} %get-tuple-element.38.refs_0_, bf16[528,256]{1,0:T(8,128)(2,1)S(1)} %get-tuple-element.39.refs_1_, bf16[784,256]{1,0:T(8,128)(2,1)S(1)} %collective-permute-done.1.refs_2_, bf16[784,256]{1,0:T(8,128)(2,1)S(1)} %collective-permute-done.5.refs_3_, ...), custom_call_target="tpu_custom_call" | custom-call | flops 1744830464 | bytes 3809280 | tf_op jit(solution)/shard_map/main/pallas_call | solution.py:26
  47.2 3.8 %collective-permute-done.11.far_ref = bf16[272,768]{1,0:T(8,128)(2,1)S(1)} collective-permute-done((bf16[272,768]{1,0:T(8,128)(2,1)S(1)}, bf16[272,768]{1,0:T(8,128)(2,1)S(1)}, u32[]{:S(2)}, u32[]{:S(2)}) %collective-permute-start.11) | collective-permute-done | bytes 417824 | tf_op jit(solution)/shard_map/ppermute | solution.py:376
  51.6 2.5 %collective-permute-start.14 = (bf16[256,256]{1,0:T(8,128)(2,1)S(1)}, bf16[256,256]{1,0:T(8,128)(2,1)S(1)}, u32[]{:S(2)}, u32[]{:S(2)}) collective-permute-start(bf16[256,256]{1,0:T(8,128)(2,1)S(1)} %get-tuple-element.52), channel_id=1, source_target_pairs={{0,6},{2,4},{4,2},{6,0},{8,14},{10,12},{12,10},{14,8},{16,22},{18,... | collective-permute-start | bytes 393224 | tf_op jit(solution)/shard_map/ppermute | solution.py:373
  54.1 4.4 %hyena.1 = bf16[256,2048]{1,0:T(8,128)(2,1)} custom-call(bf16[256,2048]{1,0:T(8,128)(2,1)S(1)} %copy-done.2, bf16[256,2048]{1,0:T(8,128)(2,1)S(1)} %copy-done, bf16[256,2048]{1,0:T(8,128)(2,1)S(1)} %copy-done.1, bf16[128,1024]{1,0:T(8,128)(2,1)S(1)} %collective-permute-done.near_rim, bf16[128,1024]{1,0:T(8,128)(2,1)S(1)} %collective-permute-done.3.ring_rim, ...), custom_call_target="tpu_custom_call" | custom-call | flops 4294967296 | bytes 5017600 | tf_op jit(solution)/shard_map/hyena/pallas_call | solution.py:26
  58.6 3.8 %collective-permute-start.15 = (bf16[256,1024]{1,0:T(8,128)(2,1)S(1)}, bf16[256,1024]{1,0:T(8,128)(2,1)S(1)}, u32[]{:S(2)}, u32[]{:S(2)}) collective-permute-start(bf16[256,1024]{1,0:T(8,128)(2,1)S(1)} %join.1.refs_0_), channel_id=1, source_target_pairs={{0,1},{1,0},{2,3},{3,2},{4,5},{5,4},{6,7},{7,6},{8,9},{9,8},{10,11... | collective-permute-start | bytes 1572872 | tf_op jit(solution)/shard_map/ppermute | solution.py:448
  62.4 1.5 %collective-permute-done.15.refs_1_ = bf16[256,1024]{1,0:T(8,128)(2,1)S(1)} collective-permute-done((bf16[256,1024]{1,0:T(8,128)(2,1)S(1)}, bf16[256,1024]{1,0:T(8,128)(2,1)S(1)}, u32[]{:S(2)}, u32[]{:S(2)}) %collective-permute-start.15) | collective-permute-done | bytes 524320 | tf_op jit(solution)/shard_map/ppermute | solution.py:448
  64.0 3.3 %project.1 = bf16[256,2048]{1,0:T(8,128)(2,1)} custom-call(bf16[256,1024]{1,0:T(8,128)(2,1)S(1)} %join.1.refs_0_, bf16[256,1024]{1,0:T(8,128)(2,1)S(1)} %collective-permute-done.15.refs_1_, bf16[2048,2048]{1,0:T(8,128)(2,1)S(1)} %bitcast.2), custom_call_target="tpu_custom_call" | custom-call | flops 2147483648 | bytes 10485760 | tf_op jit(solution)/shard_map/project/pallas_call | solution.py:26
  (41 shorter events, 2.3 us)
Async XLA Ops:
  0.6 7.4 %copy-start = (bf16[256,2048]{1,0:T(8,128)(2,1)S(1)}, bf16[256,2048]{1,0:T(8,128)(2,1)}, u32[]{:S(2)}) copy-start(bf16[256,2048]{1,0:T(8,128)(2,1)} %k_ref.3) | copy-start | bytes 3145732
  2.3 11.2 %collective-permute-start.1 = (bf16[784,256]{1,0:T(8,128)(2,1)S(1)}, bf16[784,256]{1,0:T(8,128)(2,1)S(1)}, u32[]{:S(2)}, u32[]{:S(2)}) collective-permute-start(bf16[784,256]{1,0:T(8,128)(2,1)S(1)} %get-tuple-element.32), channel_id=1, source_target_pairs={{0,2},{2,0},{4,6},{6,4},{8,10},{10,8},{12,14},{14,12},{16,18},{18,... | collective-permute-start | bytes 1204232 | tf_op jit(solution)/shard_map/ppermute | solution.py:373
  3.6 9.9 %collective-permute-start.5 = (bf16[784,256]{1,0:T(8,128)(2,1)S(1)}, bf16[784,256]{1,0:T(8,128)(2,1)S(1)}, u32[]{:S(2)}, u32[]{:S(2)}) collective-permute-start(bf16[784,256]{1,0:T(8,128)(2,1)S(1)} %get-tuple-element.41), channel_id=1, source_target_pairs={{0,4},{2,6},{4,0},{6,2},{8,12},{10,14},{12,8},{14,10},{16,20},{18,... | collective-permute-start | bytes 1204232 | tf_op jit(solution)/shard_map/ppermute | solution.py:373
  4.8 8.6 %collective-permute-start.6 = (bf16[528,256]{1,0:T(8,128)(2,1)S(1)}, bf16[528,256]{1,0:T(8,128)(2,1)S(1)}, u32[]{:S(2)}, u32[]{:S(2)}) collective-permute-start(bf16[528,256]{1,0:T(8,128)(2,1)S(1)} %get-tuple-element.39.refs_1_), channel_id=1, source_target_pairs={{0,8},{2,10},{4,12},{6,14},{8,16},{10,18},{12,20},{14,22},{16,24},... | collective-permute-start | bytes 811016 | tf_op jit(solution)/shard_map/ppermute | solution.py:376
  13.6 9.6 %collective-permute-start.2 = (bf16[784,256]{1,0:T(8,128)(2,1)S(1)}, bf16[784,256]{1,0:T(8,128)(2,1)S(1)}, u32[]{:S(2)}, u32[]{:S(2)}) collective-permute-start(bf16[784,256]{1,0:T(8,128)(2,1)S(1)} %get-tuple-element.33), channel_id=1, source_target_pairs={{0,6},{2,4},{4,2},{6,0},{8,14},{10,12},{12,10},{14,8},{16,22},{18,... | collective-permute-start | bytes 1204232 | tf_op jit(solution)/shard_map/ppermute | solution.py:373
  14.9 22.3 %collective-permute-start.7 = (bf16[1056,256]{1,0:T(8,128)(2,1)S(1)}, bf16[1056,256]{1,0:T(8,128)(2,1)S(1)}, u32[]{:S(2)}, u32[]{:S(2)}) collective-permute-start(bf16[1056,256]{1,0:T(8,128)(2,1)S(1)} %pad_maximum_fusion), channel_id=1, source_target_pairs={{0,8},{2,10},{4,12},{6,14},{8,16},{10,18},{12,20},{14,22},{16,24},... | collective-permute-start | bytes 1622024 | tf_op jit(solution)/shard_map/ppermute | solution.py:376
  18.1 15.7 %collective-permute-start.9 = (bf16[816,256]{1,0:T(8,128)(2,1)S(1)}, bf16[816,256]{1,0:T(8,128)(2,1)S(1)}, u32[]{:S(2)}, u32[]{:S(2)}) collective-permute-start(bf16[816,256]{1,0:T(8,128)(2,1)S(1)} %pad_maximum_fusion.1), channel_id=1, source_target_pairs={{16,8},{18,10},{20,12},{22,14},{24,16},{26,18},{28,20},{30,22},{17... | collective-permute-start | bytes 1253384 | tf_op jit(solution)/shard_map/ppermute | solution.py:379
  20.2 9.3 %collective-permute-start.3 = (bf16[128,1024]{1,0:T(8,128)(2,1)S(1)}, bf16[128,1024]{1,0:T(8,128)(2,1)S(1)}, u32[]{:S(2)}, u32[]{:S(2)}) collective-permute-start(bf16[128,1024]{1,0:T(8,128)(2,1)S(1)} %get-tuple-element.58), channel_id=1, source_target_pairs={{0,2},{2,4},{4,6},{6,0},{8,10},{10,12},{12,14},{14,8},{16,18},{18,... | collective-permute-start | bytes 786440 | tf_op jit(solution)/shard_map/ppermute | solution.py:399
  23.2 14.0 %collective-permute-start.8 = (bf16[528,256]{1,0:T(8,128)(2,1)S(1)}, bf16[528,256]{1,0:T(8,128)(2,1)S(1)}, u32[]{:S(2)}, u32[]{:S(2)}) collective-permute-start(bf16[528,256]{1,0:T(8,128)(2,1)S(1)} %slice.42), channel_id=1, source_target_pairs={{0,8},{2,10},{4,12},{6,14},{8,16},{10,18},{12,20},{14,22},{16,24},... | collective-permute-start | bytes 811016 | tf_op jit(solution)/shard_map/ppermute | solution.py:376
  29.6 11.3 %copy-start.4 = (bf16[2048]{0:T(1024)(128)(2,1)S(1)}, bf16[2048]{0:T(1024)(128)(2,1)}, u32[]{:S(2)}) copy-start(bf16[2048]{0:T(1024)(128)(2,1)} %param.14) | copy-start | bytes 12292
  29.6 7.6 %collective-permute-start.10 = (bf16[272,256]{1,0:T(8,128)(2,1)S(1)}, bf16[272,256]{1,0:T(8,128)(2,1)S(1)}, u32[]{:S(2)}, u32[]{:S(2)}) collective-permute-start(bf16[272,256]{1,0:T(8,128)(2,1)S(1)} %slice.39), channel_id=1, source_target_pairs={{16,8},{18,10},{20,12},{22,14},{24,16},{26,18},{28,20},{30,22},{17... | collective-permute-start | bytes 417800 | tf_op jit(solution)/shard_map/ppermute | solution.py:379
  31.5 9.4 %collective-permute-start = (bf16[128,1024]{1,0:T(8,128)(2,1)S(1)}, bf16[128,1024]{1,0:T(8,128)(2,1)S(1)}, u32[]{:S(2)}, u32[]{:S(2)}) collective-permute-start(bf16[128,1024]{1,0:T(8,128)(2,1)S(1)} %get-tuple-element.59), channel_id=1, source_target_pairs={{0,2},{2,4},{4,6},{6,8},{8,10},{10,12},{12,14},{14,16},{16,18},{18... | collective-permute-start | bytes 786440 | tf_op jit(solution)/shard_map/ppermute | solution.py:405
  33.8 7.4 %collective-permute-start.4 = (bf16[128,1024]{1,0:T(8,128)(2,1)S(1)}, bf16[128,1024]{1,0:T(8,128)(2,1)S(1)}, u32[]{:S(2)}, u32[]{:S(2)}) collective-permute-start(bf16[128,1024]{1,0:T(8,128)(2,1)S(1)} %collective-permute-done.3.ring_rim), channel_id=1, source_target_pairs={{0,8},{8,16},{16,24},{1,9},{9,17},{17,25}} | collective-permute-start | bytes 786440 | tf_op jit(solution)/shard_map/ppermute | solution.py:407
  38.9 12.1 %collective-permute-start.11 = (bf16[272,768]{1,0:T(8,128)(2,1)S(1)}, bf16[272,768]{1,0:T(8,128)(2,1)S(1)}, u32[]{:S(2)}, u32[]{:S(2)}) collective-permute-start(bf16[272,768]{1,0:T(8,128)(2,1)S(1)} %far.1), channel_id=1, source_target_pairs={{8,16},{10,18},{12,20},{14,22},{16,24},{18,26},{20,28},{22,30},{9,... | collective-permute-start | bytes 1253384 | tf_op jit(solution)/shard_map/ppermute | solution.py:376
  41.2 12.9 %copy-start.2 = (bf16[256,2048]{1,0:T(8,128)(2,1)S(1)}, bf16[256,2048]{1,0:T(8,128)(2,1)}, u32[]{:S(2)}) copy-start(bf16[256,2048]{1,0:T(8,128)(2,1)} %q_ref.3) | copy-start | bytes 3145732
  47.2 6.9 %copy-start.1 = (bf16[256,2048]{1,0:T(8,128)(2,1)S(1)}, bf16[256,2048]{1,0:T(8,128)(2,1)}, u32[]{:S(2)}) copy-start(bf16[256,2048]{1,0:T(8,128)(2,1)} %v_ref.3) | copy-start | bytes 3145732
  47.2 6.9 %copy-start.3 = (bf16[128,128]{1,0:T(8,128)(2,1)S(1)}, bf16[128,128]{1,0:T(8,128)(2,1)}, u32[]{:S(2)}) copy-start(bf16[128,128]{1,0:T(8,128)(2,1)} %taps_ref.1) | copy-start | bytes 98308
  51.4 7.1 %collective-permute-start.12 = (bf16[256,256]{1,0:T(8,128)(2,1)S(1)}, bf16[256,256]{1,0:T(8,128)(2,1)S(1)}, u32[]{:S(2)}, u32[]{:S(2)}) collective-permute-start(bf16[256,256]{1,0:T(8,128)(2,1)S(1)} %get-tuple-element.50), channel_id=1, source_target_pairs={{0,2},{2,0},{4,6},{6,4},{8,10},{10,8},{12,14},{14,12},{16,18},{18,... | collective-permute-start | bytes 393224 | tf_op jit(solution)/shard_map/ppermute | solution.py:373
  51.5 7.0 %collective-permute-start.13 = (bf16[256,256]{1,0:T(8,128)(2,1)S(1)}, bf16[256,256]{1,0:T(8,128)(2,1)S(1)}, u32[]{:S(2)}, u32[]{:S(2)}) collective-permute-start(bf16[256,256]{1,0:T(8,128)(2,1)S(1)} %get-tuple-element.51), channel_id=1, source_target_pairs={{0,4},{2,6},{4,0},{6,2},{8,12},{10,14},{12,8},{14,10},{16,20},{18,... | collective-permute-start | bytes 393224 | tf_op jit(solution)/shard_map/ppermute | solution.py:373
  51.5 12.4 %slice-start = ((s8[8388608]{0:T(1024)(128)(4,1)}), s8[4194304]{0:T(1024)(128)(4,1)S(1)}, s32[]{:S(2)}) async-start(s8[8388608]{0:T(1024)(128)(4,1)} %bitcast.1), calls=%async_computation | async-start | bytes 8388608
  51.5 12.4 %slice-start.1 = ((s8[8388608]{0:T(1024)(128)(4,1)}), s8[4194304]{0:T(1024)(128)(4,1)S(1)}, s32[]{:S(2)}) async-start(s8[8388608]{0:T(1024)(128)(4,1)} %bitcast.1), calls=%async_computation.1 | async-start | bytes 8388608
  51.6 6.9 %collective-permute-start.14 = (bf16[256,256]{1,0:T(8,128)(2,1)S(1)}, bf16[256,256]{1,0:T(8,128)(2,1)S(1)}, u32[]{:S(2)}, u32[]{:S(2)}) collective-permute-start(bf16[256,256]{1,0:T(8,128)(2,1)S(1)} %get-tuple-element.52), channel_id=1, source_target_pairs={{0,6},{2,4},{4,2},{6,0},{8,14},{10,12},{12,10},{14,8},{16,22},{18,... | collective-permute-start | bytes 393224 | tf_op jit(solution)/shard_map/ppermute | solution.py:373
  58.6 5.4 %collective-permute-start.15 = (bf16[256,1024]{1,0:T(8,128)(2,1)S(1)}, bf16[256,1024]{1,0:T(8,128)(2,1)S(1)}, u32[]{:S(2)}, u32[]{:S(2)}) collective-permute-start(bf16[256,1024]{1,0:T(8,128)(2,1)S(1)} %join.1.refs_0_), channel_id=1, source_target_pairs={{0,1},{1,0},{2,3},{3,2},{4,5},{5,4},{6,7},{7,6},{8,9},{9,8},{10,11... | collective-permute-start | bytes 1572872 | tf_op jit(solution)/shard_map/ppermute | solution.py:448

commit v14 on v13

--- a/solution.py
+++ b/solution.py
@@ -62,7 +62,7 @@
         cols = pl.ds(begin, LANES)
         return pltpu.make_async_copy(made.at[:, cols], out_ref.at[:, cols], sent.at[tile])
 
-    @pl.loop(0, chans // LANES, unroll=4)
+    @pl.loop(0, chans // LANES, unroll=8)
     def _(tile):
         cols = pl.ds(pl.multiple_of(tile * LANES, LANES), LANES)
         rings = taps[pl.ds(pl.multiple_of(tile * per_tile, per_tile), per_tile), :]

time: 67.8 us -> 67.5 us (level)
  no operation moved by 1% of the time
where the time goes in v14:
time: 67.5 us; the launch traced here: 67.1 us
  starting transfers between devices  32.7 us (48%)
  Pallas kernels  17.2 us (25%)
  waiting for transfers between devices  14.7 us (22%)
  other arithmetic  1.24 us (2%)
  between operations  1.13 us (2%)
    pallas_call x6, Pallas kernels, kernel_call(): pl.pallas_call(kernel, in_specs=[VMEM] * len(args), out_specs=[out] * len...  15.5 us
    ppermute x4, starting transfers between devices, climb(): lax.ppermute(value, 'ctx', [(i, i + SQUAD) for i in range(first, count -...  11.5 us
    ppermute x4, waiting for transfers between devices, climb(): lax.ppermute(value, 'ctx', [(i, i + SQUAD) for i in range(first, count -...  8.01 us
    ppermute x6, starting transfers between devices, swap(): return lax.ppermute(value, 'ctx', [(i, i ^ mask) for i in range(count)])  6.46 us
    ppermute x2, starting transfers between devices, descend(): lax.ppermute(value, 'ctx', [(i, i - SQUAD) for i in range(2 * SQUAD, coun...  4 us
    ppermute x1, starting transfers between devices, turn(): lax.ppermute(value, 'tp', [(t, (t + r) % ranks) for t in range(ranks)])  3.83 us
    ppermute x1, starting transfers between devices, local(): lax.ppermute(ring, 'ctx', [(i, i + SQUAD) for i in range(0, count - SQUAD...  3.37 us
    ppermute x1, waiting for transfers between devices, local(): lax.ppermute(tail[:, half:], 'ctx', [(i, i - i % SQUAD + (i + 1) % SQUAD)...  3.2 us
  transfers between devices with their start and end apart: 16, of which 6 were waited for; matrix products, arithmetic and copies ran while one was open for 2% of the time, Pallas kernels for 18%

profile of v14, /device:TPU:17, one launch (start us, length us, event | category | flops | bytes accessed | tf_op | source)
XLA Modules:
  0.0 67.1 jit_solution(15655815832532202554)
XLA Ops:
  0.6 1.7 %deal.1 = (bf16[272,256]{1,0:T(8,128)(2,1)S(1)}, bf16[528,256]{1,0:T(8,128)(2,1)S(1)}, bf16[784,256]{1,0:T(8,128)(2,1)S(1)}, bf16[784,256]{1,0:T(8,128)(2,1)S(1)}, bf16[784,256]{1,0:T(8,128)(2,1)S(1)}) custom-call(bf16[256,1024]{1,0:T(8,128)(2,1)} %q_ref.2, bf16[256,1024]{1,0:T(8,128)(2,1)} %k_ref.2, bf16[256,1024]{1,0:T(8,128)(2,1)} %v_ref.2, s32[2,128]{1,0:T(2,128)} %bitcast.3), custom_call_target="tpu_custom_call" | custom-call | bytes 3145728 | tf_op jit(solution)/shard_map/deal/pallas_call | solution.py:160
  2.3 1.3 %collective-permute-start.1 = (bf16[784,256]{1,0:T(8,128)(2,1)S(1)}, bf16[784,256]{1,0:T(8,128)(2,1)S(1)}, u32[]{:S(2)}, u32[]{:S(2)}) collective-permute-start(bf16[784,256]{1,0:T(8,128)(2,1)S(1)} %get-tuple-element.32), channel_id=1, source_target_pairs={{0,2},{2,0},{4,6},{6,4},{8,10},{10,8},{12,14},{14,12},{16,18},{18,... | collective-permute-start | bytes 1204232 | tf_op jit(solution)/shard_map/ppermute | solution.py:373
  3.6 1.2 %collective-permute-start.5 = (bf16[784,256]{1,0:T(8,128)(2,1)S(1)}, bf16[784,256]{1,0:T(8,128)(2,1)S(1)}, u32[]{:S(2)}, u32[]{:S(2)}) collective-permute-start(bf16[784,256]{1,0:T(8,128)(2,1)S(1)} %get-tuple-element.41), channel_id=1, source_target_pairs={{0,4},{2,6},{4,0},{6,2},{8,12},{10,14},{12,8},{14,10},{16,20},{18,... | collective-permute-start | bytes 1204232 | tf_op jit(solution)/shard_map/ppermute | solution.py:373
  4.8 3.2 %collective-permute-start.6 = (bf16[528,256]{1,0:T(8,128)(2,1)S(1)}, bf16[528,256]{1,0:T(8,128)(2,1)S(1)}, u32[]{:S(2)}, u32[]{:S(2)}) collective-permute-start(bf16[528,256]{1,0:T(8,128)(2,1)S(1)} %get-tuple-element.39.refs_1_), channel_id=1, source_target_pairs={{0,8},{2,10},{4,12},{6,14},{8,16},{10,18},{12,20},{14,22},{16,24},... | collective-permute-start | bytes 811016 | tf_op jit(solution)/shard_map/ppermute | solution.py:376
  9.2 4.2 %collective-permute-done.6.refs_5_.refs_2_ = bf16[528,256]{1,0:T(8,128)(2,1)S(1)} collective-permute-done((bf16[528,256]{1,0:T(8,128)(2,1)S(1)}, bf16[528,256]{1,0:T(8,128)(2,1)S(1)}, u32[]{:S(2)}, u32[]{:S(2)}) %collective-permute-start.6) | collective-permute-done | bytes 270368 | tf_op jit(solution)/shard_map/ppermute | solution.py:376
  13.6 1.3 %collective-permute-start.2 = (bf16[784,256]{1,0:T(8,128)(2,1)S(1)}, bf16[784,256]{1,0:T(8,128)(2,1)S(1)}, u32[]{:S(2)}, u32[]{:S(2)}) collective-permute-start(bf16[784,256]{1,0:T(8,128)(2,1)S(1)} %get-tuple-element.33), channel_id=1, source_target_pairs={{0,6},{2,4},{4,2},{6,0},{8,14},{10,12},{12,10},{14,8},{16,22},{18,... | collective-permute-start | bytes 1204232 | tf_op jit(solution)/shard_map/ppermute | solution.py:373
  14.9 3.2 %collective-permute-start.7 = (bf16[1056,256]{1,0:T(8,128)(2,1)S(1)}, bf16[1056,256]{1,0:T(8,128)(2,1)S(1)}, u32[]{:S(2)}, u32[]{:S(2)}) collective-permute-start(bf16[1056,256]{1,0:T(8,128)(2,1)S(1)} %pad_maximum_fusion), channel_id=1, source_target_pairs={{0,8},{2,10},{4,12},{6,14},{8,16},{10,18},{12,20},{14,22},{16,24},... | collective-permute-start | bytes 1622024 | tf_op jit(solution)/shard_map/ppermute | solution.py:376
  18.1 2.1 %collective-permute-start.9 = (bf16[816,256]{1,0:T(8,128)(2,1)S(1)}, bf16[816,256]{1,0:T(8,128)(2,1)S(1)}, u32[]{:S(2)}, u32[]{:S(2)}) collective-permute-start(bf16[816,256]{1,0:T(8,128)(2,1)S(1)} %pad_maximum_fusion.1), channel_id=1, source_target_pairs={{16,8},{18,10},{20,12},{22,14},{24,16},{26,18},{28,20},{30,22},{17... | collective-permute-start | bytes 1253384 | tf_op jit(solution)/shard_map/ppermute | solution.py:379
  20.2 1.3 %collective-permute-start.3 = (bf16[128,1024]{1,0:T(8,128)(2,1)S(1)}, bf16[128,1024]{1,0:T(8,128)(2,1)S(1)}, u32[]{:S(2)}, u32[]{:S(2)}) collective-permute-start(bf16[128,1024]{1,0:T(8,128)(2,1)S(1)} %get-tuple-element.58), channel_id=1, source_target_pairs={{0,2},{2,4},{4,6},{6,0},{8,10},{10,12},{12,14},{14,8},{16,18},{18,... | collective-permute-start | bytes 786440 | tf_op jit(solution)/shard_map/ppermute | solution.py:399
  21.5 1.6 %collective-permute-done.2.refs_4_ = bf16[784,256]{1,0:T(8,128)(2,1)S(1)} collective-permute-done((bf16[784,256]{1,0:T(8,128)(2,1)S(1)}, bf16[784,256]{1,0:T(8,128)(2,1)S(1)}, u32[]{:S(2)}, u32[]{:S(2)}) %collective-permute-start.2) | collective-permute-done | bytes 401440 | tf_op jit(solution)/shard_map/ppermute | solution.py:373
  23.2 3.2 %collective-permute-start.8 = (bf16[528,256]{1,0:T(8,128)(2,1)S(1)}, bf16[528,256]{1,0:T(8,128)(2,1)S(1)}, u32[]{:S(2)}, u32[]{:S(2)}) collective-permute-start(bf16[528,256]{1,0:T(8,128)(2,1)S(1)} %slice.42), channel_id=1, source_target_pairs={{0,8},{2,10},{4,12},{6,14},{8,16},{10,18},{12,20},{14,22},{16,24},... | collective-permute-start | bytes 811016 | tf_op jit(solution)/shard_map/ppermute | solution.py:376
  26.4 3.2 %collective-permute-done.3.ring_rim = bf16[128,1024]{1,0:T(8,128)(2,1)S(1)} collective-permute-done((bf16[128,1024]{1,0:T(8,128)(2,1)S(1)}, bf16[128,1024]{1,0:T(8,128)(2,1)S(1)}, u32[]{:S(2)}, u32[]{:S(2)}) %collective-permute-start.3) | collective-permute-done | bytes 262176 | tf_op jit(solution)/shard_map/ppermute | solution.py:399
  29.6 1.9 %collective-permute-start.10 = (bf16[272,256]{1,0:T(8,128)(2,1)S(1)}, bf16[272,256]{1,0:T(8,128)(2,1)S(1)}, u32[]{:S(2)}, u32[]{:S(2)}) collective-permute-start(bf16[272,256]{1,0:T(8,128)(2,1)S(1)} %slice.39), channel_id=1, source_target_pairs={{16,8},{18,10},{20,12},{22,14},{24,16},{26,18},{28,20},{30,22},{17... | collective-permute-start | bytes 417800 | tf_op jit(solution)/shard_map/ppermute | solution.py:379
  31.5 2.2 %collective-permute-start = (bf16[128,1024]{1,0:T(8,128)(2,1)S(1)}, bf16[128,1024]{1,0:T(8,128)(2,1)S(1)}, u32[]{:S(2)}, u32[]{:S(2)}) collective-permute-start(bf16[128,1024]{1,0:T(8,128)(2,1)S(1)} %get-tuple-element.59), channel_id=1, source_target_pairs={{0,2},{2,4},{4,6},{6,8},{8,10},{10,12},{12,14},{14,16},{16,18},{18... | collective-permute-start | bytes 786440 | tf_op jit(solution)/shard_map/ppermute | solution.py:405
  33.8 3.4 %collective-permute-start.4 = (bf16[128,1024]{1,0:T(8,128)(2,1)S(1)}, bf16[128,1024]{1,0:T(8,128)(2,1)S(1)}, u32[]{:S(2)}, u32[]{:S(2)}) collective-permute-start(bf16[128,1024]{1,0:T(8,128)(2,1)S(1)} %collective-permute-done.3.ring_rim), channel_id=1, source_target_pairs={{0,8},{8,16},{16,24},{1,9},{9,17},{17,25}} | collective-permute-start | bytes 786440 | tf_op jit(solution)/shard_map/ppermute | solution.py:407
  37.2 1.8 %far.1 = bf16[272,768]{1,0:T(8,128)(2,1)S(1)} custom-call(bf16[816,256]{1,0:T(8,128)(2,1)S(1)} %collective-permute-done.9.refs_0_, bf16[272,256]{1,0:T(8,128)(2,1)S(1)} %collective-permute-done.10.refs_1_, bf16[528,256]{1,0:T(8,128)(2,1)S(1)} %collective-permute-done.6.refs_5_.refs_2_, bf16[1056,256]{1,0:T(8,128)(2,1)S(1)} %collective-permute-done.7.refs_6_.refs_3_, ...), custom_call_target="tpu_custom_call" | custom-call | flops 402653184 | bytes 2056192 | tf_op jit(solution)/shard_map/far/pallas_call | solution.py:26
  38.9 1.9 %collective-permute-start.11 = (bf16[272,768]{1,0:T(8,128)(2,1)S(1)}, bf16[272,768]{1,0:T(8,128)(2,1)S(1)}, u32[]{:S(2)}, u32[]{:S(2)}) collective-permute-start(bf16[272,768]{1,0:T(8,128)(2,1)S(1)} %far.1), channel_id=1, source_target_pairs={{8,16},{10,18},{12,20},{14,22},{16,24},{18,26},{20,28},{22,30},{9,... | collective-permute-start | bytes 1253384 | tf_op jit(solution)/shard_map/ppermute | solution.py:376
  41.2 6.0 %main.1.main_ref = f32[272,1024]{1,0:T(8,128)S(1)} custom-call(bf16[272,256]{1,0:T(8,128)(2,1)S(1)} %get-tuple-element.38.refs_0_, bf16[528,256]{1,0:T(8,128)(2,1)S(1)} %get-tuple-element.39.refs_1_, bf16[784,256]{1,0:T(8,128)(2,1)S(1)} %collective-permute-done.1.refs_2_, bf16[784,256]{1,0:T(8,128)(2,1)S(1)} %collective-permute-done.5.refs_3_, ...), custom_call_target="tpu_custom_call" | custom-call | flops 1744830464 | bytes 3809280 | tf_op jit(solution)/shard_map/main/pallas_call | solution.py:26
  47.2 3.8 %collective-permute-done.11.far_ref = bf16[272,768]{1,0:T(8,128)(2,1)S(1)} collective-permute-done((bf16[272,768]{1,0:T(8,128)(2,1)S(1)}, bf16[272,768]{1,0:T(8,128)(2,1)S(1)}, u32[]{:S(2)}, u32[]{:S(2)}) %collective-permute-start.11) | collective-permute-done | bytes 417824 | tf_op jit(solution)/shard_map/ppermute | solution.py:376
  51.6 2.5 %collective-permute-start.14 = (bf16[256,256]{1,0:T(8,128)(2,1)S(1)}, bf16[256,256]{1,0:T(8,128)(2,1)S(1)}, u32[]{:S(2)}, u32[]{:S(2)}) collective-permute-start(bf16[256,256]{1,0:T(8,128)(2,1)S(1)} %get-tuple-element.52), channel_id=1, source_target_pairs={{0,6},{2,4},{4,2},{6,0},{8,14},{10,12},{12,10},{14,8},{16,22},{18,... | collective-permute-start | bytes 393224 | tf_op jit(solution)/shard_map/ppermute | solution.py:373
  54.1 4.0 %hyena.1 = bf16[256,2048]{1,0:T(8,128)(2,1)} custom-call(bf16[256,2048]{1,0:T(8,128)(2,1)S(1)} %copy-done.2, bf16[256,2048]{1,0:T(8,128)(2,1)S(1)} %copy-done, bf16[256,2048]{1,0:T(8,128)(2,1)S(1)} %copy-done.1, bf16[128,1024]{1,0:T(8,128)(2,1)S(1)} %collective-permute-done.near_rim, bf16[128,1024]{1,0:T(8,128)(2,1)S(1)} %collective-permute-done.3.ring_rim, ...), custom_call_target="tpu_custom_call" | custom-call | flops 4294967296 | bytes 5017600 | tf_op jit(solution)/shard_map/hyena/pallas_call | solution.py:26
  58.2 3.8 %collective-permute-start.15 = (bf16[256,1024]{1,0:T(8,128)(2,1)S(1)}, bf16[256,1024]{1,0:T(8,128)(2,1)S(1)}, u32[]{:S(2)}, u32[]{:S(2)}) collective-permute-start(bf16[256,1024]{1,0:T(8,128)(2,1)S(1)} %join.1.refs_0_), channel_id=1, source_target_pairs={{0,1},{1,0},{2,3},{3,2},{4,5},{5,4},{6,7},{7,6},{8,9},{9,8},{10,11... | collective-permute-start | bytes 1572872 | tf_op jit(solution)/shard_map/ppermute | solution.py:448
  62.1 1.5 %collective-permute-done.15.refs_1_ = bf16[256,1024]{1,0:T(8,128)(2,1)S(1)} collective-permute-done((bf16[256,1024]{1,0:T(8,128)(2,1)S(1)}, bf16[256,1024]{1,0:T(8,128)(2,1)S(1)}, u32[]{:S(2)}, u32[]{:S(2)}) %collective-permute-start.15) | collective-permute-done | bytes 524320 | tf_op jit(solution)/shard_map/ppermute | solution.py:448
  63.6 3.3 %project.1 = bf16[256,2048]{1,0:T(8,128)(2,1)} custom-call(bf16[256,1024]{1,0:T(8,128)(2,1)S(1)} %join.1.refs_0_, bf16[256,1024]{1,0:T(8,128)(2,1)S(1)} %collective-permute-done.15.refs_1_, bf16[2048,2048]{1,0:T(8,128)(2,1)S(1)} %bitcast.2), custom_call_target="tpu_custom_call" | custom-call | flops 2147483648 | bytes 10485760 | tf_op jit(solution)/shard_map/project/pallas_call | solution.py:26
  (41 shorter events, 2.3 us)
Async XLA Ops:
  0.6 7.4 %copy-start = (bf16[256,2048]{1,0:T(8,128)(2,1)S(1)}, bf16[256,2048]{1,0:T(8,128)(2,1)}, u32[]{:S(2)}) copy-start(bf16[256,2048]{1,0:T(8,128)(2,1)} %k_ref.3) | copy-start | bytes 3145732
  2.3 11.2 %collective-permute-start.1 = (bf16[784,256]{1,0:T(8,128)(2,1)S(1)}, bf16[784,256]{1,0:T(8,128)(2,1)S(1)}, u32[]{:S(2)}, u32[]{:S(2)}) collective-permute-start(bf16[784,256]{1,0:T(8,128)(2,1)S(1)} %get-tuple-element.32), channel_id=1, source_target_pairs={{0,2},{2,0},{4,6},{6,4},{8,10},{10,8},{12,14},{14,12},{16,18},{18,... | collective-permute-start | bytes 1204232 | tf_op jit(solution)/shard_map/ppermute | solution.py:373
  3.6 9.9 %collective-permute-start.5 = (bf16[784,256]{1,0:T(8,128)(2,1)S(1)}, bf16[784,256]{1,0:T(8,128)(2,1)S(1)}, u32[]{:S(2)}, u32[]{:S(2)}) collective-permute-start(bf16[784,256]{1,0:T(8,128)(2,1)S(1)} %get-tuple-element.41), channel_id=1, source_target_pairs={{0,4},{2,6},{4,0},{6,2},{8,12},{10,14},{12,8},{14,10},{16,20},{18,... | collective-permute-start | bytes 1204232 | tf_op jit(solution)/shard_map/ppermute | solution.py:373
  4.8 8.6 %collective-permute-start.6 = (bf16[528,256]{1,0:T(8,128)(2,1)S(1)}, bf16[528,256]{1,0:T(8,128)(2,1)S(1)}, u32[]{:S(2)}, u32[]{:S(2)}) collective-permute-start(bf16[528,256]{1,0:T(8,128)(2,1)S(1)} %get-tuple-element.39.refs_1_), channel_id=1, source_target_pairs={{0,8},{2,10},{4,12},{6,14},{8,16},{10,18},{12,20},{14,22},{16,24},... | collective-permute-start | bytes 811016 | tf_op jit(solution)/shard_map/ppermute | solution.py:376
  13.6 9.6 %collective-permute-start.2 = (bf16[784,256]{1,0:T(8,128)(2,1)S(1)}, bf16[784,256]{1,0:T(8,128)(2,1)S(1)}, u32[]{:S(2)}, u32[]{:S(2)}) collective-permute-start(bf16[784,256]{1,0:T(8,128)(2,1)S(1)} %get-tuple-element.33), channel_id=1, source_target_pairs={{0,6},{2,4},{4,2},{6,0},{8,14},{10,12},{12,10},{14,8},{16,22},{18,... | collective-permute-start | bytes 1204232 | tf_op jit(solution)/shard_map/ppermute | solution.py:373
  14.9 22.3 %collective-permute-start.7 = (bf16[1056,256]{1,0:T(8,128)(2,1)S(1)}, bf16[1056,256]{1,0:T(8,128)(2,1)S(1)}, u32[]{:S(2)}, u32[]{:S(2)}) collective-permute-start(bf16[1056,256]{1,0:T(8,128)(2,1)S(1)} %pad_maximum_fusion), channel_id=1, source_target_pairs={{0,8},{2,10},{4,12},{6,14},{8,16},{10,18},{12,20},{14,22},{16,24},... | collective-permute-start | bytes 1622024 | tf_op jit(solution)/shard_map/ppermute | solution.py:376
  18.1 15.7 %collective-permute-start.9 = (bf16[816,256]{1,0:T(8,128)(2,1)S(1)}, bf16[816,256]{1,0:T(8,128)(2,1)S(1)}, u32[]{:S(2)}, u32[]{:S(2)}) collective-permute-start(bf16[816,256]{1,0:T(8,128)(2,1)S(1)} %pad_maximum_fusion.1), channel_id=1, source_target_pairs={{16,8},{18,10},{20,12},{22,14},{24,16},{26,18},{28,20},{30,22},{17... | collective-permute-start | bytes 1253384 | tf_op jit(solution)/shard_map/ppermute | solution.py:379
  20.2 9.3 %collective-permute-start.3 = (bf16[128,1024]{1,0:T(8,128)(2,1)S(1)}, bf16[128,1024]{1,0:T(8,128)(2,1)S(1)}, u32[]{:S(2)}, u32[]{:S(2)}) collective-permute-start(bf16[128,1024]{1,0:T(8,128)(2,1)S(1)} %get-tuple-element.58), channel_id=1, source_target_pairs={{0,2},{2,4},{4,6},{6,0},{8,10},{10,12},{12,14},{14,8},{16,18},{18,... | collective-permute-start | bytes 786440 | tf_op jit(solution)/shard_map/ppermute | solution.py:399
  23.2 14.0 %collective-permute-start.8 = (bf16[528,256]{1,0:T(8,128)(2,1)S(1)}, bf16[528,256]{1,0:T(8,128)(2,1)S(1)}, u32[]{:S(2)}, u32[]{:S(2)}) collective-permute-start(bf16[528,256]{1,0:T(8,128)(2,1)S(1)} %slice.42), channel_id=1, source_target_pairs={{0,8},{2,10},{4,12},{6,14},{8,16},{10,18},{12,20},{14,22},{16,24},... | collective-permute-start | bytes 811016 | tf_op jit(solution)/shard_map/ppermute | solution.py:376
  29.6 11.3 %copy-start.4 = (bf16[2048]{0:T(1024)(128)(2,1)S(1)}, bf16[2048]{0:T(1024)(128)(2,1)}, u32[]{:S(2)}) copy-start(bf16[2048]{0:T(1024)(128)(2,1)} %param.14) | copy-start | bytes 12292
  29.6 7.6 %collective-permute-start.10 = (bf16[272,256]{1,0:T(8,128)(2,1)S(1)}, bf16[272,256]{1,0:T(8,128)(2,1)S(1)}, u32[]{:S(2)}, u32[]{:S(2)}) collective-permute-start(bf16[272,256]{1,0:T(8,128)(2,1)S(1)} %slice.39), channel_id=1, source_target_pairs={{16,8},{18,10},{20,12},{22,14},{24,16},{26,18},{28,20},{30,22},{17... | collective-permute-start | bytes 417800 | tf_op jit(solution)/shard_map/ppermute | solution.py:379
  31.5 9.4 %collective-permute-start = (bf16[128,1024]{1,0:T(8,128)(2,1)S(1)}, bf16[128,1024]{1,0:T(8,128)(2,1)S(1)}, u32[]{:S(2)}, u32[]{:S(2)}) collective-permute-start(bf16[128,1024]{1,0:T(8,128)(2,1)S(1)} %get-tuple-element.59), channel_id=1, source_target_pairs={{0,2},{2,4},{4,6},{6,8},{8,10},{10,12},{12,14},{14,16},{16,18},{18... | collective-permute-start | bytes 786440 | tf_op jit(solution)/shard_map/ppermute | solution.py:405
  33.8 7.4 %collective-permute-start.4 = (bf16[128,1024]{1,0:T(8,128)(2,1)S(1)}, bf16[128,1024]{1,0:T(8,128)(2,1)S(1)}, u32[]{:S(2)}, u32[]{:S(2)}) collective-permute-start(bf16[128,1024]{1,0:T(8,128)(2,1)S(1)} %collective-permute-done.3.ring_rim), channel_id=1, source_target_pairs={{0,8},{8,16},{16,24},{1,9},{9,17},{17,25}} | collective-permute-start | bytes 786440 | tf_op jit(solution)/shard_map/ppermute | solution.py:407
  38.9 12.1 %collective-permute-start.11 = (bf16[272,768]{1,0:T(8,128)(2,1)S(1)}, bf16[272,768]{1,0:T(8,128)(2,1)S(1)}, u32[]{:S(2)}, u32[]{:S(2)}) collective-permute-start(bf16[272,768]{1,0:T(8,128)(2,1)S(1)} %far.1), channel_id=1, source_target_pairs={{8,16},{10,18},{12,20},{14,22},{16,24},{18,26},{20,28},{22,30},{9,... | collective-permute-start | bytes 1253384 | tf_op jit(solution)/shard_map/ppermute | solution.py:376
  41.2 12.9 %copy-start.2 = (bf16[256,2048]{1,0:T(8,128)(2,1)S(1)}, bf16[256,2048]{1,0:T(8,128)(2,1)}, u32[]{:S(2)}) copy-start(bf16[256,2048]{1,0:T(8,128)(2,1)} %q_ref.3) | copy-start | bytes 3145732
  47.2 6.9 %copy-start.1 = (bf16[256,2048]{1,0:T(8,128)(2,1)S(1)}, bf16[256,2048]{1,0:T(8,128)(2,1)}, u32[]{:S(2)}) copy-start(bf16[256,2048]{1,0:T(8,128)(2,1)} %v_ref.3) | copy-start | bytes 3145732
  47.2 6.9 %copy-start.3 = (bf16[128,128]{1,0:T(8,128)(2,1)S(1)}, bf16[128,128]{1,0:T(8,128)(2,1)}, u32[]{:S(2)}) copy-start(bf16[128,128]{1,0:T(8,128)(2,1)} %taps_ref.1) | copy-start | bytes 98308
  51.4 6.8 %collective-permute-start.12 = (bf16[256,256]{1,0:T(8,128)(2,1)S(1)}, bf16[256,256]{1,0:T(8,128)(2,1)S(1)}, u32[]{:S(2)}, u32[]{:S(2)}) collective-permute-start(bf16[256,256]{1,0:T(8,128)(2,1)S(1)} %get-tuple-element.50), channel_id=1, source_target_pairs={{0,2},{2,0},{4,6},{6,4},{8,10},{10,8},{12,14},{14,12},{16,18},{18,... | collective-permute-start | bytes 393224 | tf_op jit(solution)/shard_map/ppermute | solution.py:373
  51.5 6.7 %collective-permute-start.13 = (bf16[256,256]{1,0:T(8,128)(2,1)S(1)}, bf16[256,256]{1,0:T(8,128)(2,1)S(1)}, u32[]{:S(2)}, u32[]{:S(2)}) collective-permute-start(bf16[256,256]{1,0:T(8,128)(2,1)S(1)} %get-tuple-element.51), channel_id=1, source_target_pairs={{0,4},{2,6},{4,0},{6,2},{8,12},{10,14},{12,8},{14,10},{16,20},{18,... | collective-permute-start | bytes 393224 | tf_op jit(solution)/shard_map/ppermute | solution.py:373
  51.5 12.1 %slice-start = ((s8[8388608]{0:T(1024)(128)(4,1)}), s8[4194304]{0:T(1024)(128)(4,1)S(1)}, s32[]{:S(2)}) async-start(s8[8388608]{0:T(1024)(128)(4,1)} %bitcast.1), calls=%async_computation | async-start | bytes 8388608
  51.5 12.1 %slice-start.1 = ((s8[8388608]{0:T(1024)(128)(4,1)}), s8[4194304]{0:T(1024)(128)(4,1)S(1)}, s32[]{:S(2)}) async-start(s8[8388608]{0:T(1024)(128)(4,1)} %bitcast.1), calls=%async_computation.1 | async-start | bytes 8388608
  51.6 6.6 %collective-permute-start.14 = (bf16[256,256]{1,0:T(8,128)(2,1)S(1)}, bf16[256,256]{1,0:T(8,128)(2,1)S(1)}, u32[]{:S(2)}, u32[]{:S(2)}) collective-permute-start(bf16[256,256]{1,0:T(8,128)(2,1)S(1)} %get-tuple-element.52), channel_id=1, source_target_pairs={{0,6},{2,4},{4,2},{6,0},{8,14},{10,12},{12,10},{14,8},{16,22},{18,... | collective-permute-start | bytes 393224 | tf_op jit(solution)/shard_map/ppermute | solution.py:373
  58.2 5.4 %collective-permute-start.15 = (bf16[256,1024]{1,0:T(8,128)(2,1)S(1)}, bf16[256,1024]{1,0:T(8,128)(2,1)S(1)}, u32[]{:S(2)}, u32[]{:S(2)}) collective-permute-start(bf16[256,1024]{1,0:T(8,128)(2,1)S(1)} %join.1.refs_0_), channel_id=1, source_target_pairs={{0,1},{1,0},{2,3},{3,2},{4,5},{5,4},{6,7},{7,6},{8,9},{9,8},{10,11... | collective-permute-start | bytes 1572872 | tf_op jit(solution)/shard_map/ppermute | solution.py:448
